TPU v7x, 256 devices: a whole 4x4x8 slice. The times are simulated.
256 devices in a mesh: mesh: 32 (over x_hi, z, core), inst: 8 (over y, x_lo).
Axes of the slice: x: 4 (x_hi: 2, x_lo: 2; x = x_hi * 2 + x_lo), y: 4, z: 8, core: 2. Of those that a mesh axis runs over, the one named last changes fastest.
Arguments:
- displacement: float32 [16, 3, 128, 32, 128], P('inst', None, 'mesh'), may hold values from -6 to 6
- direction: float32 [16, 3, 128, 32, 128], P('inst', None, 'mesh'), may hold values from -6 to 6
- forcing: float32 [16, 3, 128, 32, 128], P('inst', None, 'mesh'), may hold values from -6 to 6
- material_ids: int32 [128, 32, 128], P('mesh'), may hold values from 0 to 15
- materials: float32 [16, 4], replicated, may hold values from 0.5 to 4
- joint_owner: int32 [65536, 1], P('mesh'), may hold values from 0 to 31, as said below
- joint_local: int32 [65536], P('mesh'), may hold values from 0 to 16383
- joint_remote: int32 [65536], P('mesh'), may hold values from 0 to 16383
- joint_kind: int32 [65536], P('mesh'), may hold values 0 or 1
Outputs:
- residual: float32 [16, 3, 128, 32, 128], P('inst', None, 'mesh')
- jacobian: float32 [16, 3, 128, 32, 128], P('inst', None, 'mesh')
Inputs may be any that keep to these rules, and one draw needn't show every extreme that they name: `joint_owner`: of the 2048 joints listed by slab p, exactly 256 have their partner in slab p, 256 in slab p + 1 and 256 in slab p - 1, 128 each in slabs p + 2 and p - 2 (slab numbers taken modulo the number of slabs), and the rest spread evenly in turn over the other slabs, in a drawn order; so no slab's list names any one slab more than 256 times.
All inputs are finite; a program needn't handle non-finite values. No bound on the sum of `joint_kind` on one device may be relied on, other than what follows from the above.
Results may differ from a plain program's by a relative error of at most 0.000088.
Values sent between devices are 32-bit elements; how exact they have to be, the bound alone decides.
No kernel may reach another device: no remote copies, remote signals or barrier semaphores. Data moves between devices by JAX's collectives and lax.ppermute only.
A program may use at most 128 MiB of HBM per device.

v0:
```python
import jax
import jax.numpy as jnp
from jax import lax
from jax.sharding import PartitionSpec as P

frequency = 0.6
damping = 0.3
bolt_stiff = 2.0
slip_force = 1.0
slip_speed = 0.5
stop_stiff = 3.0
clearance = 0.3


def extended(x, sides, width):
    for axis, dim in sides:
        size, length = (lax.axis_size(axis), x.shape[dim])
        up = [(i, (i + 1) % size) for i in range(size - 1)]
        down = [(j, i) for i, j in up]
        last = lax.slice_in_dim(x, length - width, length, axis=dim)
        first = lax.slice_in_dim(x, 0, width, axis=dim)
        before = lax.ppermute(last, axis, up)
        after = lax.ppermute(first, axis, down)
        x = jnp.concatenate([before, x, after], axis=dim)
    return x


def spectral(instance_count):
    offsets = (
        jnp.arange(instance_count, dtype=jnp.int32)[:, None]
        - jnp.arange(instance_count, dtype=jnp.int32)[None, :]
    )
    signs = jnp.where(offsets % 2 == 0, 1.0, -1.0).astype(jnp.float32)
    angles = jnp.pi * offsets.astype(jnp.float32) / instance_count
    tangent = jnp.where(offsets == 0, 1.0, jnp.tan(angles))
    first_table = jnp.where(offsets == 0, 0.0, 0.5 * signs / tangent) * frequency
    second_table = jnp.dot(first_table, first_table, precision=lax.Precision.HIGHEST)
    return (first_table, second_table)


def pad_axis(array, axis_id):
    widths = [(0, 0)] * array.ndim
    widths[axis_id] = (1, 1)
    return jnp.pad(array, widths)


def apply_stiff(fields, stiff_pad, stiff_y, stiff_z):
    centre = fields[:, 1:-1]
    stiff_x = stiff_pad[1:-1]
    summed = 0.5 * (stiff_x + stiff_pad[2:]) * (centre - fields[:, 2:])
    summed = summed + 0.5 * (stiff_x + stiff_pad[:-2]) * (centre - fields[:, :-2])
    for axis_id, stiff_axis in ((2, stiff_y), (3, stiff_z)):
        padded = pad_axis(centre, axis_id)
        padded_stiff = pad_axis(stiff_axis, axis_id - 1)
        length = centre.shape[axis_id]
        for lower in (0, 2):
            beside = lax.slice_in_dim(padded, lower, lower + length, axis=axis_id)
            stiff_beside = lax.slice_in_dim(padded_stiff, lower, lower + length, axis=axis_id - 1)
            summed = summed + 0.5 * (stiff_axis + stiff_beside) * (centre - beside)
    return summed


def joint_forces(own_side, far_side, bolted):
    gap = own_side - far_side
    slide = jnp.tanh(gap[1] / slip_speed)
    opened = jnp.tanh(gap[0] / clearance)
    friction = bolt_stiff * gap[0] + slip_force * slide
    contact = stop_stiff * (gap[0] - clearance * opened)
    joint_force = bolted * friction + (1.0 - bolted) * contact
    tangent_friction = (
        bolt_stiff * gap[2] + slip_force * (1.0 - slide * slide) / slip_speed * gap[3]
    )
    tangent_contact = stop_stiff * opened * opened * gap[2]
    joint_tangent = bolted * tangent_friction + (1.0 - bolted) * tangent_contact
    return (joint_force, joint_tangent)


def rows_forces(own_rows, far_rows, bolted, channels):
    own_cols = own_rows.T.reshape(4, channels, -1)
    far_cols = far_rows.T.reshape(4, channels, -1)
    joint_force, joint_tangent = joint_forces(own_cols, far_cols, bolted)
    return jnp.concatenate([joint_force, joint_tangent], 0).T


def on_device(
    displacement,
    direction,
    forcing,
    material_ids,
    materials,
    joint_owner,
    joint_local,
    joint_remote,
    joint_kind,
):
    local_count, components, cells_x, cells_y, cells_z = displacement.shape
    node_count = cells_x * cells_y * cells_z
    channels = local_count * components
    inst_count = lax.axis_size("inst")
    inst_index = lax.axis_index("inst")
    first_full, second_full = spectral(local_count * inst_count)
    first_rows = lax.dynamic_slice_in_dim(first_full, inst_index * local_count, local_count, 0)
    second_rows = lax.dynamic_slice_in_dim(second_full, inst_index * local_count, local_count, 0)
    highest = lax.Precision.HIGHEST

    def contract(weights, pieces):
        flat = pieces.reshape(pieces.shape[0], components, -1)
        return jnp.einsum("ts,scn->tcn", weights, flat, precision=highest)

    disp_piece = lax.all_gather(displacement, "inst", axis=0, tiled=True)
    dir_piece = lax.all_gather(direction, "inst", axis=0, tiled=True)
    rate_disp = contract(first_rows, disp_piece)
    accel_disp = contract(second_rows, disp_piece)
    rate_dir = contract(first_rows, dir_piece)
    accel_dir = contract(second_rows, dir_piece)
    matches_mat = (
        material_ids[None] == jnp.arange(materials.shape[0], dtype=jnp.int32)[:, None, None, None]
    ).astype(jnp.float32)
    properties = jnp.einsum("mp,mxyz->pxyz", materials, matches_mat, precision=highest)
    stacked = jnp.concatenate(
        [
            displacement.reshape(channels, cells_x, cells_y, cells_z),
            direction.reshape(channels, cells_x, cells_y, cells_z),
            properties[0:1],
        ],
        0,
    )
    padded = extended(stacked, (("mesh", 1),), 1)
    stiffened = apply_stiff(padded[:-1], padded[-1], properties[1], properties[2])
    stiff_disp = stiffened[:channels].reshape(local_count, components, node_count)
    stiff_dir = stiffened[channels:].reshape(local_count, components, node_count)
    masses = properties[3].reshape(node_count)
    residual = (
        masses * (accel_disp + damping * rate_disp)
        + stiff_disp
        - forcing.reshape(local_count, components, node_count)
    )
    jacobian = masses * (accel_dir + damping * rate_dir) + stiff_dir
    residual = residual.reshape(channels, node_count)
    jacobian = jacobian.reshape(channels, node_count)
    mesh_count = lax.axis_size("mesh")
    joint_count = joint_local.shape[0]
    capacity = 4 * joint_count // mesh_count
    owners = joint_owner[:, 0]
    matches = (owners[:, None] == jnp.arange(mesh_count, dtype=jnp.int32)[None, :]).astype(
        jnp.int32
    )
    within = jnp.sum(matches * (jnp.cumsum(matches, 0) - 1), 1)
    places = owners * capacity + within
    bolted = joint_kind.astype(jnp.float32)
    fields_all = jnp.stack(
        [
            displacement.reshape(channels, node_count),
            rate_disp.reshape(channels, node_count),
            direction.reshape(channels, node_count),
            rate_dir.reshape(channels, node_count),
        ]
    ).reshape(4 * channels, node_count)
    node_rows = fields_all.T
    own_rows = node_rows[joint_local]
    slot_count = mesh_count * capacity
    requested = (
        jnp.zeros((slot_count,), jnp.int32)
        .at[places]
        .set(joint_remote)
        .reshape(mesh_count, capacity)
    )
    wanted = lax.all_to_all(requested, "mesh", split_axis=0, concat_axis=0, tiled=True).reshape(-1)
    located = node_rows[wanted].reshape(mesh_count, capacity, 4 * channels)
    answer = lax.all_to_all(located, "mesh", split_axis=0, concat_axis=0, tiled=True).reshape(
        slot_count, 4 * channels
    )
    partner_rows = answer[places]
    combined_rows = rows_forces(own_rows, partner_rows, bolted, channels)
    added = jnp.zeros((node_count, 2 * channels), jnp.float32).at[joint_local].add(combined_rows)
    outgoing = jnp.zeros((slot_count, 2 * channels), jnp.float32).at[places].set(-combined_rows)
    returned = lax.all_to_all(
        outgoing.reshape(mesh_count, capacity, 2 * channels),
        "mesh",
        split_axis=0,
        concat_axis=0,
        tiled=True,
    ).reshape(slot_count, 2 * channels)
    added = added.at[wanted].add(returned)
    added_cols = added.T
    residual = residual + added_cols[:channels]
    jacobian = jacobian + added_cols[channels:]
    return (
        residual.reshape(local_count, components, cells_x, cells_y, cells_z),
        jacobian.reshape(local_count, components, cells_x, cells_y, cells_z),
    )


def solution(mesh):
    placed = (
        P("inst", None, "mesh", None, None),
        P("inst", None, "mesh", None, None),
        P("inst", None, "mesh", None, None),
        P("mesh", None, None),
        P(),
        P("mesh", None),
        P("mesh"),
        P("mesh"),
        P("mesh"),
    )
    return jax.shard_map(
        on_device,
        mesh=mesh,
        in_specs=placed,
        out_specs=(P("inst", None, "mesh", None, None), P("inst", None, "mesh", None, None)),
        check_vma=False,
    )
```

profile of v0, /device:TPU:1, one launch (start us, length us, event | category | flops | bytes accessed | tf_op | source)
XLA Modules:
  0.0 417.3 jit_solution(9758640255439083082)
XLA Ops:
  9.4 9.1 %reduce-window.6 = s32[32,16,128]{2,1,0:T(8,128)S(1)} reduce-window(s32[32,16,128]{2,1,0:T(8,128)S(1)} %fusion.31, s32[]{:T(128)} %constant.19.clone.1), window={size=1x1x128 pad=0_0x0_0x127_0}, to_apply=%region_0.1 | reduce-window | flops 8323072 | bytes 524292 | tf_op jit(solution)/shard_map/reduce-window
  20.1 8.9 %scatter_custom_fusion = s32[8192]{0:T(1024)} fusion(s32[2048]{0:T(1024)S(1)} %bitcast.121, s32[2048]{0:T(1024)} %param.16, s32[]{:T(128)} %constant.19.clone.1), kind=kCustom, calls=%fused_computation.97 | custom fusion | bytes 33280 | tf_op jit(solution)/shard_map/scatter | solution.py:165
  29.0 12.6 %all-to-all-start = ((s32[32,1,256]{2,1,0:T(1,128)}), s32[32,1,256]{2,1,0:T(1,128)S(1)}, u32[]{:S(2)}, u32[]{:S(2)}) async-start(s32[32,1,256]{2,1,0:T(1,128)} %bitcast.20), calls=%async_computation | async-start | bytes 65536 | tf_op jit(solution)/shard_map/all_to_all | solution.py:168
  46.5 3.4 collective-permute-start.1
  57.9 32.7 %all-gather.3.cloned.1.call-done = f32[16,3,4,32,128]{4,3,2,1,0:T(8,128)} async-done(((f32[2,3,4,32,128]{4,3,2,1,0:T(8,128)}), f32[16,3,4,32,128]{4,3,2,1,0:T(8,128)}) %all-gather.3.cloned.1.call-update) | async-done | bytes 3145744 | tf_op jit(solution)/shard_map/all_gather | solution.py:110
  95.3 68.3 %all-gather.5.cloned.1.call-done = f32[16,3,4,32,128]{4,3,2,1,0:T(8,128)} async-done(((f32[2,3,4,32,128]{4,3,2,1,0:T(8,128)}), f32[16,3,4,32,128]{4,3,2,1,0:T(8,128)}) %all-gather.5.cloned.1.call-update) | async-done | bytes 3145744 | tf_op jit(solution)/shard_map/all_gather | solution.py:111
  163.6 4.1 copy.147
  188.4 6.1 %copy.149 = f32[24,16384]{0,1:T(8,128)} copy(f32[24,16384]{1,0:T(8,128)} %reshape.144) | data formatting | bytes 3145728 | tf_op jit(solution)/shard_map/reshape | solution.py:158
  194.5 33.9 %gather_fusion.1 = f32[8192,24]{1,0:T(8,128)} fusion(f32[16384,24]{1,0:T(8,128)} %bitcast.95, s32[8192]{0:T(1024)} %broadcast_clamp_fusion), kind=kCustom, calls=%fused_computation.1 | custom fusion | bytes 1605632 | tf_op jit(solution)/shard_map/gather | solution.py:169
  228.4 3.5 copy.152
  232.0 10.2 %all-to-all-start.1 = ((f32[32,256,24]{1,2,0:T(8,128)}), f32[32,256,24]{1,2,0:T(8,128)}, u32[]{:S(2)}, u32[]{:S(2)}) async-start(f32[32,256,24]{1,2,0:T(8,128)} %copy.152), calls=%async_computation.1 | async-start | bytes 1572864 | tf_op jit(solution)/shard_map/all_to_all | solution.py:170
  247.6 4.1 fusion.14
  259.2 11.7 %gather_fusion = f32[2048,24]{1,0:T(8,128)} fusion(f32[16384,24]{1,0:T(8,128)} %bitcast.96, s32[2048]{0:T(1024)} %get-tuple-element.24), kind=kCustom, calls=%fused_computation | custom fusion | bytes 401408 | tf_op jit(solution)/shard_map/gather | solution.py:160
  273.1 3.6 copy.153
  276.7 10.5 %gather_fusion.2 = f32[2048,24]{1,0:T(8,128)} fusion(f32[8192,24]{1,0:T(8,128)} %bitcast.97, s32[2048]{0:T(1024)} %broadcast_clamp_fusion.1), kind=kCustom, calls=%fused_computation.2 | custom fusion | bytes 401408 | tf_op jit(solution)/shard_map/gather | solution.py:173
  294.9 8.1 %scatter_custom_fusion.2 = f32[8192,12]{1,0:T(8,128)} fusion(s32[2048]{0:T(1024)} %bitcast.123, f32[2048,12]{1,0:T(8,128)} %copy.157, f32[]{:T(128)} %constant.20.clone.1), kind=kCustom, calls=%fused_computation.19 | custom fusion | bytes 393728 | tf_op jit(solution)/shard_map/scatter | solution.py:176
  303.0 3.6 copy.158
  306.6 9.9 %all-to-all-start.2 = ((f32[32,256,12]{1,2,0:T(8,128)}), f32[32,256,12]{1,2,0:T(8,128)}, u32[]{:S(2)}, u32[]{:S(2)}) async-start(f32[32,256,12]{1,2,0:T(8,128)} %copy.158), calls=%async_computation.2 | async-start | bytes 1048576 | tf_op jit(solution)/shard_map/all_to_all | solution.py:177
  316.5 3.1 fusion.1
  320.1 4.3 %fusion.4 = f32[2,3,16384]{2,0,1:T(2,128)S(1)} fusion(f32[2,3,16384]{2,0,1:T(2,128)} %reshape.141, f32[16,3,16384]{2,0,1:T(8,128)} %reshape.137, f32[2,3,16384]{2,1,0:T(4,128)} %reshape.140, f32[2,3,16384]{2,0,1:T(2,128)} %copy-done.7, f32[16384]{0:T(1024)} %bitcast.106, f32[16,16]{1,0:T(8,128)} %fusion.56, s32[]{:T(128)S(6)} %select_n.63), kind=kOutput, calls=%fused_computation.13 | convolution fusion | flops 19365888 | bytes 4916228 | tf_op jit(solution)/shard_map/ts,scn->tcn/dot_general | solution.py:108
  325.3 15.3 %scatter_custom_fusion.1 = f32[16384,12]{1,0:T(8,128)} fusion(s32[2048]{0:T(1024)} %get-tuple-element.25, f32[2048,12]{1,0:T(8,128)S(1)} %copy.156, f32[]{:T(128)} %constant.20.clone.1), kind=kCustom, calls=%fused_computation.14 | custom fusion | flops 24576 | bytes 786944 | tf_op jit(solution)/shard_map/scatter-add | solution.py:175
  340.7 3.6 copy.167
  344.3 59.2 %scatter_fusion = f32[16384,12]{1,0:T(8,128)} fusion(f32[16384,12]{1,0:T(8,128)} %scatter_custom_fusion.1, s32[8192]{0:T(1024)S(1)} %bitcast.110, f32[8192,12]{1,0:T(8,128)} %bitcast.98), kind=kCustom, calls=%fused_computation.6 | custom fusion | flops 98304 | bytes 1212416 | tf_op jit(solution)/shard_map/scatter-add | solution.py:184
  403.5 5.2 %copy.161 = f32[16384,12]{0,1:T(8,128)S(1)} copy(f32[16384,12]{1,0:T(8,128)} %scatter_fusion) | data formatting | bytes 1572864 | tf_op jit(solution)/shard_map/scatter-add | solution.py:184
  (108 shorter events, 67.5 us)
Async XLA Ops:
  7.2 35.0 %copy-start = (f32[16,4]{0,1:T(4,128)S(1)}, f32[16,4]{0,1:T(4,128)}, u32[]{:S(2)}) copy-start(f32[16,4]{0,1:T(4,128)} %param.13) | copy-start | bytes 772
  7.2 34.7 %copy-start.5 = (f32[2,3,4,32,128]{4,3,2,1,0:T(8,128)S(1)}, f32[2,3,4,32,128]{4,3,2,1,0:T(8,128)}, u32[]{:S(2)}) copy-start(f32[2,3,4,32,128]{4,3,2,1,0:T(8,128)} %param.9) | copy-start | bytes 1179652
  7.2 34.4 %copy-start.6 = (f32[2,3,4,32,128]{4,3,2,1,0:T(8,128)S(1)}, f32[2,3,4,32,128]{4,3,2,1,0:T(8,128)}, u32[]{:S(2)}) copy-start(f32[2,3,4,32,128]{4,3,2,1,0:T(8,128)} %param.10) | copy-start | bytes 1179652
  7.2 12.8 %copy-start.16 = (s32[2048,1]{0,1:T(1,128)S(1)}, s32[2048,1]{0,1:T(1,128)}, u32[]{:S(2)}) copy-start(s32[2048,1]{0,1:T(1,128)} %param.14) | copy-start | bytes 24580
  7.2 34.9 %copy-start.17 = (s32[4,32,128]{2,1,0:T(8,128)S(1)}, s32[4,32,128]{2,1,0:T(8,128)}, u32[]{:S(2)}) copy-start(s32[4,32,128]{2,1,0:T(8,128)} %param.12) | copy-start | bytes 196612
  7.2 83.4 %all-gather.3.cloned.1.call-start = ((), (), s32[]{:S(2)}) async-start(), calls=%async_computation.3 | async-start | bytes 3538944 | tf_op jit(solution)/shard_map/all_gather | solution.py:110
  8.0 155.7 %all-gather.5.cloned.1.call-start = ((), (), s32[]{:S(2)}) async-start(), calls=%async_computation.4 | async-start | bytes 3538944 | tf_op jit(solution)/shard_map/all_gather | solution.py:111
  20.1 9.0 %copy-start.19 = (s32[2048,1]{0,1:T(1,128)}, s32[2048,1]{0,1:T(1,128)S(1)}, u32[]{:S(2)}) copy-start(s32[2048,1]{0,1:T(1,128)S(1)} %compare_select_fusion.1) | copy-start | bytes 24580
  20.1 31.7 %copy-start.18 = (s32[2048]{0:T(1024)S(1)}, s32[2048]{0:T(1024)}, u32[]{:S(2)}) copy-start(s32[2048]{0:T(1024)} %param.17) | copy-start | bytes 24580
  20.1 32.3 %copy-start.13 = (f32[2,3,4,32,128]{4,3,2,1,0:T(8,128)S(1)}, f32[2,3,4,32,128]{4,3,2,1,0:T(8,128)}, u32[]{:S(2)}) copy-start(f32[2,3,4,32,128]{4,3,2,1,0:T(8,128)} %param.11) | copy-start | bytes 1179652
  29.0 27.6 %all-to-all-start = ((s32[32,1,256]{2,1,0:T(1,128)}), s32[32,1,256]{2,1,0:T(1,128)S(1)}, u32[]{:S(2)}, u32[]{:S(2)}) async-start(s32[32,1,256]{2,1,0:T(1,128)} %bitcast.20), calls=%async_computation | async-start | bytes 65536 | tf_op jit(solution)/shard_map/all_to_all | solution.py:168
  41.9 12.4 %copy-start.3 = (f32[6,4,32,128]{3,0,2,1:T(8,128)}, f32[6,4,32,128]{3,0,2,1:T(8,128)S(1)}, u32[]{:S(2)}) copy-start(f32[6,4,32,128]{3,0,2,1:T(8,128)S(1)} %copy.138) | copy-start | bytes 1179652
  42.2 13.2 %copy-start.4 = (f32[6,4,32,128]{3,0,2,1:T(8,128)}, f32[6,4,32,128]{3,0,2,1:T(8,128)S(1)}, u32[]{:S(2)}) copy-start(f32[6,4,32,128]{3,0,2,1:T(8,128)S(1)} %copy.137) | copy-start | bytes 1179652
  43.5 11.9 %copy-start.8 = (f32[1,4,32,128]{3,0,2,1:T(1,128)}, f32[1,4,32,128]{3,0,2,1:T(1,128)S(1)}, u32[]{:S(2)}) copy-start(f32[1,4,32,128]{3,0,2,1:T(1,128)S(1)} %get-tuple-element.15) | copy-start | bytes 196612
  44.4 201.6 %collective-permute-start = (f32[13,1,32,128]{3,0,2,1:T(8,128)}, f32[13,1,32,128]{3,0,2,1:T(8,128)}, u32[]{:S(2)}, u32[]{:S(2)}) collective-permute-start(f32[13,1,32,128]{3,0,2,1:T(8,128)} %get-tuple-element.6), channel_id=1, source_target_pairs={{8,0},{16,8},{24,16},{32,24},{40,32},{48,40},{56,48},{64,56},{72,6... | collective-permute-start | bytes 638984 | tf_op jit(solution)/shard_map/ppermute | solution.py:23
  46.5 199.5 %collective-permute-start.1 = (f32[13,1,32,128]{3,0,2,1:T(8,128)}, f32[13,1,32,128]{3,0,2,1:T(8,128)}, u32[]{:S(2)}, u32[]{:S(2)}) collective-permute-start(f32[13,1,32,128]{3,0,2,1:T(8,128)} %get-tuple-element.7), channel_id=1, source_target_pairs={{0,8},{8,16},{16,24},{24,32},{32,40},{40,48},{48,56},{56,64},{64,7... | collective-permute-start | bytes 638984 | tf_op jit(solution)/shard_map/ppermute | solution.py:22
  170.6 2.5 copy-start.2
  175.4 0.8 copy-start.7
  232.0 41.2 %all-to-all-start.1 = ((f32[32,256,24]{1,2,0:T(8,128)}), f32[32,256,24]{1,2,0:T(8,128)}, u32[]{:S(2)}, u32[]{:S(2)}) async-start(f32[32,256,24]{1,2,0:T(8,128)} %copy.152), calls=%async_computation.1 | async-start | bytes 1572864 | tf_op jit(solution)/shard_map/all_to_all | solution.py:170
  306.6 34.1 %all-to-all-start.2 = ((f32[32,256,12]{1,2,0:T(8,128)}), f32[32,256,12]{1,2,0:T(8,128)}, u32[]{:S(2)}, u32[]{:S(2)}) async-start(f32[32,256,12]{1,2,0:T(8,128)} %copy.158), calls=%async_computation.2 | async-start | bytes 1048576 | tf_op jit(solution)/shard_map/all_to_all | solution.py:177
  320.1 4.8 %copy-start.10 = (f32[6,2048]{1,0:T(8,128)S(1)}, f32[6,2048]{1,0:T(8,128)}, u32[]{:S(2)}) copy-start(f32[6,2048]{1,0:T(8,128)} %copy-done.9) | copy-start | bytes 147460
  320.1 4.8 %copy-start.12 = (f32[6,2048]{1,0:T(8,128)S(1)}, f32[6,2048]{1,0:T(8,128)}, u32[]{:S(2)}) copy-start(f32[6,2048]{1,0:T(8,128)} %copy-done.11) | copy-start | bytes 147460
  340.7 3.6 copy-start.15
  403.5 7.0 %copy-start.1 = (f32[16,4]{0,1:T(4,128)S(1)}, f32[16,4]{0,1:T(4,128)}, u32[]{:S(2)}) copy-start(f32[16,4]{0,1:T(4,128)} %param.13) | copy-start | bytes 772
  (3 other events, 1.9 us)
Sparse Core Ops, SparseCore 0:
  9.8 80.7 all-gather.2
  92.4 71.1 all-gather.4
where the time goes:
time: 420 us; the launch traced here: 417 us
  local copies, waits for them, and re-layouts  143 us (34%)
  other arithmetic  105 us (25%)
  waiting for transfers between devices  102 us (24%)
  starting transfers between devices  38.3 us (9%)
  between operations  14.5 us (3%)
  matrix products  13.4 us (3%)
    all_gather x1, waiting for transfers between devices, on_device(): dir_piece = lax.all_gather(direction, 'inst', axis=0, tiled=True)  68.3 us
    scatter-add x1, other arithmetic, on_device(): added = added.at[wanted].add(returned)  59.2 us
    gather x1, local copies, waits for them, and re-layouts, on_device(): located = node_rows[wanted].reshape(mesh_count, capacity, 4 * channels)  33.9 us
    all_gather x1, waiting for transfers between devices, on_device(): disp_piece = lax.all_gather(displacement, 'inst', axis=0, tiled=True)  32.7 us
    scatter-add x1, other arithmetic, on_device(): jnp.zeros((node_count, 2 * channels), jnp.float32).at[joint_local]  15.3 us
    gather x2, local copies, waits for them, and re-layouts, on_device(): own_rows = node_rows[joint_local]  13.9 us
    gather x2, local copies, waits for them, and re-layouts, on_device(): partner_rows = answer[places]  12.8 us
    all_to_all x1, starting transfers between devices, on_device(): lax.all_to_all(requested, 'mesh', split_axis=0, concat_axis=0, tiled=True)  12.6 us
  transfers between devices with their start and end apart: 7, of which 2 were waited for; matrix products, arithmetic and copies ran while one was open for 38% of the time, Pallas kernels for 0%

commit v1 on v0

v1 whole, which is shorter than its diff:
```python
import jax
import jax.numpy as jnp
import numpy as np
from jax import lax
from jax.experimental import pallas as pl
from jax.experimental.pallas import tpu as pltpu
from jax.sharding import PartitionSpec as P

frequency = 0.6
damping = 0.3
bolt_stiff = 2.0
slip_force = 1.0
slip_speed = 0.5
stop_stiff = 3.0
clearance = 0.3

SLABS = 32
PARTS = 8
SIDE = 18
SEG = 42
f32 = jnp.float32
bf16 = jnp.bfloat16
i32 = jnp.int32


def tables(count):
    offsets = np.arange(count)[:, None] - np.arange(count)[None, :]
    tangent = np.where(offsets == 0, 1.0, np.tan(np.pi * offsets / count))
    first = np.where(offsets == 0, 0.0, 0.5 * np.where(offsets % 2 == 0, 1.0, -1.0) / tangent) * frequency
    return first, first @ first


FIRST, SECOND = tables(2 * PARTS)


def far_place(offset):
    return 8 + (offset - 3) // 3, SEG * ((offset - 3) % 3)


def place(offset):
    return {2: (6, 0), 30: (7, 0)}.get(offset) or far_place(offset)


def lane_roll(x, shift):
    shift = shift % 128
    return pltpu.roll(x, shift, x.ndim - 1) if shift else x


def lanes(rows):
    return lax.broadcasted_iota(i32, (rows, 128), 1)


def merge_far(read, rows, fill):
    lane = lanes(rows)
    tiles = []
    for k in range(9):
        parts = [lane_roll(read(3 + 3 * k + s), SEG * s) for s in range(3)]
        tile = jnp.where(lane < SEG, parts[0], jnp.where(lane < 2 * SEG, parts[1], parts[2]))
        tiles.append(jnp.where(lane < 3 * SEG, tile, fill))
    return tiles


def prep_kernel(p_ref, owner_ref, local_ref, remote_ref, kind_ref, tab_ref, chunk_ref, up_ref, down_ref):
    p = p_ref[0]
    count = owner_ref.shape[1]
    offset = (owner_ref[...] - p) & (SLABS - 1)
    hit = (lax.broadcasted_iota(i32, (SLABS, count), 0) == offset).astype(f32)
    hit16 = hit.astype(bf16)
    before = (lax.broadcasted_iota(i32, (128, 128), 0) < lax.broadcasted_iota(i32, (128, 128), 1)).astype(f32).astype(bf16)
    row = lax.broadcasted_iota(i32, (SLABS, 1), 0)
    far = row - 3
    group = (far * 171) >> 9
    start = 1024 + group * 128 + (far - 3 * group) * SEG
    for value, at in ((0, 0), (1, 256), (SLABS - 1, 512), (2, 768), (SLABS - 2, 896)):
        start = jnp.where(row == value, at, start)
    run = start.astype(f32)
    places = []
    for b in range(count // 128):
        block = hit[:, 128 * b : 128 * (b + 1)]
        earlier = jnp.dot(hit16[:, 128 * b : 128 * (b + 1)], before, preferred_element_type=f32)
        places.append(jnp.sum(block * (earlier + run), axis=0, keepdims=True))
        run = run + jnp.sum(block, axis=1, keepdims=True)
    slot = jnp.concatenate(places, axis=1).astype(i32)
    in_tile = lax.broadcasted_iota(i32, (24, count), 0) == (slot >> 7)
    in_lane = (lax.broadcasted_iota(i32, (128, count), 0) == (slot & 127)).astype(f32).astype(bf16)
    local = local_ref[...]
    remote = remote_ref[...]
    values = (local >> 7, local & 127, remote >> 7, remote & 127, kind_ref[...], jnp.ones_like(local))
    spread = jnp.concatenate([jnp.where(in_tile, v.astype(f32), 0.0) for v in values], axis=0).astype(bf16)
    got = lax.dot_general(spread, in_lane, (((1,), (1,)), ((), ())), preferred_element_type=f32)
    got = [got[24 * k : 24 * (k + 1)] for k in range(6)]
    empty = got[5] - 1.0
    tab_ref[0:24] = got[0] * 128.0 + got[1] + empty
    tab_ref[24:48] = got[2] * 128.0 + got[3] + empty
    tab_ref[48:72] = got[4]
    chunk_ref[...] = jnp.zeros(chunk_ref.shape, f32)
    for d in range(2, SLABS - 1):
        tile, seg = place(d)
        pair = jnp.concatenate([tab_ref[24 + tile : 25 + tile], tab_ref[48 + tile : 49 + tile]], axis=0)
        chunk_ref[(p + d) & (SLABS - 1), 0:2, :] = lane_roll(pair, -seg)
    for ref, tile in ((up_ref, 2), (down_ref, 4)):
        ref[0:2] = tab_ref[24 + tile : 26 + tile]
        ref[2:4] = tab_ref[48 + tile : 50 + tile]
        ref[4:8] = jnp.zeros((4, 128), f32)


def gather_rows(hi_ref, lo_ref, idx_ref, here_ref):
    def step(k, carry):
        idx = jnp.concatenate([idx_ref[pl.ds(2 * k, 1), :], idx_ref[pl.ds(2 * k + 1, 1), :]], axis=1)
        code = ((idx >> 12) << 7) | (idx & 127)
        pick = (lax.broadcasted_iota(i32, (512, 256), 0) == code).astype(f32).astype(bf16)
        rows = jnp.dot(hi_ref[...], pick, preferred_element_type=f32)
        rows = rows + jnp.dot(lo_ref[...], pick, preferred_element_type=f32)
        in_y = lax.broadcasted_iota(i32, (32, 256), 0) == ((idx >> 7) & 31)
        got = jnp.sum(jnp.where(in_y[None], rows.reshape(12, 32, 256), 0.0), axis=1)
        here_ref[2 * k] = got[:, :128]
        here_ref[2 * k + 1] = got[:, 128:]
        return carry

    lax.fori_loop(0, SIDE, step, 0)


def split_store(hi_ref, lo_ref, at_rows, at_lanes, value):
    hi = value.astype(bf16)
    hi_ref[at_rows, at_lanes] = hi
    lo_ref[at_rows, at_lanes] = (value - hi.astype(f32)).astype(bf16)


def send_rows(p, here_ref, chunk_ref, up_ref, down_ref):
    for d in (0, 1, SLABS - 1):
        chunk_ref[(p + d) & (SLABS - 1)] = jnp.zeros((24, 128), f32)
    for d in range(2, SLABS - 1):
        tile, seg = place(d)
        chunk_ref[(p + d) & (SLABS - 1), 0:12, :] = lane_roll(here_ref[tile], -seg)
        tile, seg = place(SLABS - d)
        chunk_ref[(p + d) & (SLABS - 1), 12:24, :] = lane_roll(here_ref[SIDE + tile], -seg)
    for k in range(2):
        up_ref[k] = here_ref[2 + k]
        up_ref[2 + k] = here_ref[SIDE + 4 + k]
        down_ref[k] = here_ref[4 + k]
        down_ref[2 + k] = here_ref[SIDE + 2 + k]


def there_rows(p, here_ref, chunk_ref, up_ref, down_ref):
    def listed(d):
        return chunk_ref[(p + d) & (SLABS - 1), 12:24, :]

    def asked(d):
        return chunk_ref[(p - d) & (SLABS - 1), 0:12, :]

    empty = jnp.zeros((12, 128), f32)
    out = [here_ref[SIDE], here_ref[SIDE + 1], down_ref[2], down_ref[3], up_ref[2], up_ref[3]]
    out += [listed(2), listed(SLABS - 2)] + merge_far(listed, 12, 0.0) + [empty]
    out += [here_ref[0], here_ref[1], up_ref[0], up_ref[1], down_ref[0], down_ref[1]]
    out += [asked(2), asked(SLABS - 2)] + merge_far(asked, 12, 0.0) + [empty]
    return out


def early_kernel(p_ref, tab_ref, chunk_in, up_in, down_in, disp_ref, dir_ref,
                 idx_ref, kind_ref, here_ref, chunk_ref, up_ref, down_ref, hi_ref, lo_ref):
    p = p_ref[0]

    def asked(row):
        def read(d):
            return chunk_in[(p - d) & (SLABS - 1), row : row + 1, :]

        return read

    for row, out_ref, base, fill in ((0, idx_ref, 24, -1.0), (1, kind_ref, 48, 0.0)):
        empty = jnp.full((1, 128), fill, f32)
        mine = tab_ref[base - 24 * (1 - row) : base - 24 * (1 - row) + 17]
        theirs = [tab_ref[base : base + 2], up_in[2 * row : 2 * row + 2], down_in[2 * row : 2 * row + 2]]
        read = asked(row)
        theirs += [read(2), read(SLABS - 2)] + merge_far(read, 1, fill) + [empty]
        whole = jnp.concatenate([mine, empty] + theirs + [jnp.full((4, 128), fill, f32)], axis=0)
        out_ref[...] = whole.astype(out_ref.dtype)
    for field, ref in enumerate((disp_ref, dir_ref)):
        for x in range(4):
            value = ref[:, x].reshape(6 * 32, 128)
            split_store(hi_ref, lo_ref, slice(192 * field, 192 * (field + 1)), slice(128 * x, 128 * (x + 1)), value)
    gather_rows(hi_ref, lo_ref, idx_ref, here_ref)
    send_rows(p, here_ref, chunk_ref, up_ref, down_ref)


def late_kernel(p_ref, idx_ref, rate_ref, here_ref, chunk_ref, up_ref, down_ref, hi_ref, lo_ref):
    for x in range(4):
        value = jnp.concatenate([rate_ref[2 * x], rate_ref[2 * x + 1]], axis=1).reshape(12 * 32, 128)
        split_store(hi_ref, lo_ref, slice(0, 384), slice(128 * x, 128 * (x + 1)), value)
    gather_rows(hi_ref, lo_ref, idx_ref, here_ref)
    send_rows(p_ref[0], here_ref, chunk_ref, up_ref, down_ref)


def time_kernel(in_ref, rate_ref, acc_ref):
    count = 2 * PARTS

    def step(g, carry):
        field = g // 3
        row = 6 * field + (g - 3 * field)
        x = [in_ref[t // 2, row + 3 * (t % 2)] for t in range(count)]
        for t in range(count):
            rate = None
            acc = None
            for s in range(count):
                c2 = float(SECOND[t, s])
                acc = x[s] * c2 if acc is None else acc + x[s] * c2
                c1 = float(FIRST[t, s])
                if abs(c1) > 1e-12:
                    rate = x[s] * c1 if rate is None else rate + x[s] * c1
            rate_ref[t // 2, row + 3 * (t % 2)] = rate
            acc_ref[t // 2, row + 3 * (t % 2)] = acc + damping * rate
        return carry

    lax.fori_loop(0, 6, step, 0)


def lookup(ids, mat_ref, column, count):
    out = jnp.zeros(ids.shape, f32)
    for m in range(count):
        out = jnp.where(ids == m, mat_ref[m, column], out)
    return out


def stiff_kernel(mat_ref, ids_ref, disp_ref, dir_ref, forcing_ref, low_ref, high_ref, out_ref, mass_ref, *, materials):
    ids = ids_ref[...]
    kx, ky, kz, mass = [lookup(ids, mat_ref, col, materials) for col in range(4)]
    mass_ref[...] = mass
    kx_low = lookup(low_ref[12].astype(i32) - 1, mat_ref, 0, materials)
    kx_high = lookup(high_ref[12].astype(i32) - 1, mat_ref, 0, materials)
    shape = ids.shape
    y = lax.broadcasted_iota(i32, shape, 1)
    z = lax.broadcasted_iota(i32, shape, 2)
    xm = 0.5 * (kx + jnp.concatenate([kx_low[None], kx[:-1]], axis=0))
    xp = 0.5 * (kx + jnp.concatenate([kx[1:], kx_high[None]], axis=0))
    total = xm + xp
    sides = []
    for k, pos, axis in ((ky, y, 1), (kz, z, 2)):
        size = shape[axis]
        for shift, edge in ((1, 0), (size - 1, size - 1)):
            inside = pos != edge
            near = jnp.where(inside, pltpu.roll(k, shift, axis), 0.0)
            side = 0.5 * (k + near)
            total = total + side
            sides.append((jnp.where(inside, side, 0.0), shift, axis))
    for field, ref in enumerate((disp_ref, dir_ref)):
        for c in range(6):
            w = ref[c]
            down = jnp.concatenate([low_ref[6 * field + c][None], w[:-1]], axis=0)
            up = jnp.concatenate([w[1:], high_ref[6 * field + c][None]], axis=0)
            out = total * w - xm * down - xp * up
            for side, shift, axis in sides:
                out = out - side * pltpu.roll(w, shift, axis)
            if field == 0:
                out = out - forcing_ref[c]
            out_ref[6 * field + c] = out


def final_kernel(p_ref, idx_ref, kind_ref, here0_ref, chunk0_ref, up0_ref, down0_ref, here1_ref, chunk1_ref, up1_ref, down1_ref,
                 acc_ref, lin_ref, mass_ref, res_ref, jac_ref, gap_ref, rate_ref, val_ref, sum_ref):
    p = p_ref[0]
    for out_ref, here, chunk, up, down in (
        (gap_ref, here0_ref, chunk0_ref, up0_ref, down0_ref),
        (rate_ref, here1_ref, chunk1_ref, up1_ref, down1_ref),
    ):
        for tile, other in enumerate(there_rows(p, here, chunk, up, down)):
            out_ref[tile] = here[tile] - other
    bolted = kind_ref[0 : 2 * SIDE][:, None, :]
    r = gap_ref[:, 0:6, :]
    dr = gap_ref[:, 6:12, :]
    w = rate_ref[:, 0:6, :]
    dw = rate_ref[:, 6:12, :]
    slide = jnp.tanh(w / slip_speed)
    opened = jnp.tanh(r / clearance)
    friction = bolt_stiff * r + slip_force * slide
    contact = stop_stiff * (r - clearance * opened)
    val_ref[:, 0:6, :] = bolted * friction + (1.0 - bolted) * contact
    tangent_friction = bolt_stiff * dr + slip_force * (1.0 - slide * slide) / slip_speed * dw
    tangent_contact = stop_stiff * opened * opened * dr
    val_ref[:, 6:12, :] = bolted * tangent_friction + (1.0 - bolted) * tangent_contact
    sum_ref[...] = jnp.zeros(sum_ref.shape, f32)

    def step(k, carry):
        idx = jnp.concatenate([idx_ref[pl.ds(2 * k, 1), :], idx_ref[pl.ds(2 * k + 1, 1), :]], axis=1)
        code = ((idx >> 12) << 7) | (idx & 127)
        pick = (lax.broadcasted_iota(i32, (512, 256), 0) == code).astype(f32).astype(bf16)
        in_y = lax.broadcasted_iota(i32, (32, 256), 0) == ((idx >> 7) & 31)
        value = jnp.concatenate([val_ref[2 * k], val_ref[2 * k + 1]], axis=1)
        hi = value.astype(bf16).astype(f32)
        lo = value - hi
        spread = [
            jnp.where(in_y[None], part[:, None, :], 0.0).reshape(384, 256).astype(bf16) for part in (hi, lo)
        ]
        dims = (((1,), (1,)), ((), ()))
        got = lax.dot_general(spread[0], pick, dims, preferred_element_type=f32)
        got = got + lax.dot_general(spread[1], pick, dims, preferred_element_type=f32)
        sum_ref[...] = sum_ref[...] + got
        return carry

    lax.fori_loop(0, SIDE, step, 0)
    for x in range(4):
        added = sum_ref[:, 128 * x : 128 * (x + 1)].reshape(12, 32, 128)
        acc = jnp.concatenate([acc_ref[2 * x], acc_ref[2 * x + 1]], axis=1)
        out = mass_ref[x][None] * acc + lin_ref[:, x] + added
        res_ref[:, x] = out[0:6]
        jac_ref[:, x] = out[6:12]


VMEM = 48 * 1024 * 1024


def call(kernel, outs, *args, smem=(0,), scratch=()):
    specs = [pl.BlockSpec(memory_space=pltpu.SMEM if k in smem else pltpu.VMEM) for k in range(len(args))]
    return pl.pallas_call(
        kernel,
        out_shape=[jax.ShapeDtypeStruct(s, d) for s, d in outs],
        in_specs=specs,
        out_specs=[pl.BlockSpec(memory_space=pltpu.VMEM) for _ in outs],
        scratch_shapes=list(scratch),
        compiler_params=pltpu.CompilerParams(vmem_limit_bytes=VMEM),
    )(*args)


def shift(x, by, wrap=True):
    pairs = [(i, (i + by) % SLABS) for i in range(SLABS) if wrap or 0 <= i + by < SLABS]
    return lax.ppermute(x, "mesh", pairs)


def exchange(chunk, up, down):
    chunk = lax.all_to_all(chunk, "mesh", split_axis=0, concat_axis=0, tiled=True)
    return chunk, shift(up, 1), shift(down, -1)


def on_device(displacement, direction, forcing, material_ids, materials, joint_owner, joint_local, joint_remote, joint_kind):
    shape = displacement.shape
    fields = (6, 4, 32, 128)
    disp = displacement.reshape(fields)
    dire = direction.reshape(fields)
    count = joint_local.shape[0]
    p = lax.axis_index("mesh").astype(i32).reshape(1)

    both = jnp.concatenate([disp, dire], axis=0).reshape(12, PARTS, 16, 128)
    blocks = lax.all_to_all(both.swapaxes(0, 1), "inst", split_axis=0, concat_axis=0, tiled=True)

    tab, chunk, up, down = call(
        prep_kernel,
        [((72, 128), f32), ((SLABS, 8, 128), f32), ((8, 128), f32), ((8, 128), f32)],
        p,
        joint_owner.reshape(1, count),
        joint_local.reshape(1, count),
        joint_remote.reshape(1, count),
        joint_kind.reshape(1, count),
    )
    chunk, up, down = exchange(chunk, up, down)

    ids_plus = (material_ids + 1).astype(f32)
    low = shift(jnp.concatenate([disp[:, 3], dire[:, 3], ids_plus[3:4]], axis=0), 1, wrap=False)
    high = shift(jnp.concatenate([disp[:, 0], dire[:, 0], ids_plus[0:1]], axis=0), -1, wrap=False)

    rate, acc = call(time_kernel, [((PARTS, 12, 16, 128), f32)] * 2, blocks, smem=())
    rate = lax.all_to_all(rate, "inst", split_axis=0, concat_axis=0, tiled=True)
    acc = lax.all_to_all(acc, "inst", split_axis=0, concat_axis=0, tiled=True)

    message = [((SLABS, 24, 128), f32), ((4, 12, 128), f32), ((4, 12, 128), f32)]
    split = [pltpu.VMEM((384, 512), bf16)] * 2
    rows = ((2 * SIDE, 12, 128), f32)
    idx, kind, here0, *sent0 = call(
        early_kernel,
        [((40, 128), i32), ((40, 128), f32), rows] + message,
        p, tab, chunk, up, down, disp, dire,
        scratch=split,
    )
    got0 = exchange(*sent0)

    lin, mass = call(
        lambda *refs: stiff_kernel(*refs, materials=materials.shape[0]),
        [((12, 4, 32, 128), f32), ((4, 32, 128), f32)],
        materials, material_ids, disp, dire, forcing.reshape(fields), low, high,
    )

    here1, *sent1 = call(late_kernel, [rows] + message, p, idx, rate, scratch=split)
    got1 = exchange(*sent1)

    residual, jacobian = call(
        final_kernel,
        [(fields, f32)] * 2,
        p, idx, kind, here0, *got0, here1, *got1, acc, lin, mass,
        scratch=[pltpu.VMEM((2 * SIDE, 12, 128), f32)] * 3 + [pltpu.VMEM((384, 512), f32)],
    )
    return residual.reshape(shape), jacobian.reshape(shape)


def solution(mesh):
    field = P("inst", None, "mesh", None, None)
    placed = (field, field, field, P("mesh", None, None), P(), P("mesh", None), P("mesh"), P("mesh"), P("mesh"))
    return jax.shard_map(on_device, mesh=mesh, in_specs=placed, out_specs=(field, field), check_vma=False)
```

time: 420 us -> 152 us (0.36)
  the two profiles are of different devices: /device:TPU:1 before, /device:TPU:4 now
where the time goes in v1:
time: 152 us; the launch traced here: 151 us
  starting transfers between devices  63.2 us (42%)
  Pallas kernels  31.2 us (21%)
  waiting for transfers between devices  22.2 us (15%)
  blocking collectives  17.8 us (12%)
  local copies, waits for them, and re-layouts  13.2 us (9%)
  other arithmetic  2.13 us (1%)
    pallas_call x6, Pallas kernels, call(): pl.pallas_call(kernel, out_shape=[jax.ShapeDtypeStruct(s, d) for s, d in...  31.2 us
    all_to_all x3, starting transfers between devices, exchange(): lax.all_to_all(chunk, 'mesh', split_axis=0, concat_axis=0, tiled=True)  28.9 us
    ppermute x8, starting transfers between devices, shift(): return lax.ppermute(x, 'mesh', pairs)  25.4 us
    all_to_all x3, waiting for transfers between devices, exchange(): lax.all_to_all(chunk, 'mesh', split_axis=0, concat_axis=0, tiled=True)  19 us
    all_to_all x1, blocking collectives, on_device(): rate = lax.all_to_all(rate, 'inst', split_axis=0, concat_axis=0, tiled=True)  17.8 us
    unnamed x51, local copies, waits for them, and re-layouts  13.2 us
    all_to_all x1, starting transfers between devices, on_device(): lax.all_to_all(both.swapaxes(0, 1), 'inst', split_axis=0, concat_axis=0,...  5.1 us
    all_to_all x1, starting transfers between devices, on_device(): acc = lax.all_to_all(acc, 'inst', split_axis=0, concat_axis=0, tiled=True)  3.68 us
  transfers between devices with their start and end apart: 13, of which 4 were waited for; matrix products, arithmetic and copies ran while one was open for 2% of the time, Pallas kernels for 13%

profile of v1, /device:TPU:4, one launch (start us, length us, event | category | flops | bytes accessed | tf_op | source)
XLA Modules:
  0.0 150.6 jit_solution(3319644171919225477)
XLA Ops:
  2.7 1.3 shard_map.104
  4.0 11.6 %all-to-all-start = ((f32[32,8,128]{2,1,0:T(8,128)}), f32[32,8,128]{2,1,0:T(8,128)S(1)}, u32[]{:S(2)}, u32[]{:S(2)}) async-start(f32[32,8,128]{2,1,0:T(8,128)} %get-tuple-element.23), calls=%async_computation | async-start | bytes 262144 | tf_op jit(solution)/shard_map/all_to_all | solution.py:328
  15.6 2.1 %copy_bitcast_fusion = f32[8,12,16,128]{3,2,1,0:T(8,128)} fusion(f32[6,8,16,128]{3,2,1,0:T(8,128)} %bitcast.27, f32[6,8,16,128]{3,2,1,0:T(8,128)} %bitcast.24), kind=kLoop, calls=%fused_computation.1 | loop fusion | flops 196608 | bytes 1572864 | tf_op jit(solution)/shard_map/transpose | solution.py:341
  17.7 7.0 %all-to-all-done.chunk_in = f32[32,8,128]{2,1,0:T(8,128)S(1)} async-done(((f32[32,8,128]{2,1,0:T(8,128)}), f32[32,8,128]{2,1,0:T(8,128)S(1)}, u32[]{:S(2)}, u32[]{:S(2)}) %all-to-all-start) | async-done | bytes 131104 | tf_op jit(solution)/shard_map/all_to_all | solution.py:328
  24.8 5.1 %all-to-all-start.2 = ((f32[8,12,16,128]{3,2,1,0:T(8,128)}), f32[8,12,16,128]{3,2,1,0:T(8,128)S(1)}, u32[]{:S(2)}, u32[]{:S(2)}) async-start(f32[8,12,16,128]{3,2,1,0:T(8,128)} %copy_bitcast_fusion), calls=%async_computation.2 | async-start | bytes 1572864 | tf_op jit(solution)/shard_map/all_to_all | solution.py:341
  29.9 5.4 %collective-permute-start.1 = (f32[8,128]{1,0:T(8,128)S(1)}, f32[8,128]{1,0:T(8,128)S(1)}, u32[]{:S(2)}, u32[]{:S(2)}) collective-permute-start(f32[8,128]{1,0:T(8,128)S(1)} %get-tuple-element.25), channel_id=1, source_target_pairs={{0,248},{8,0},{16,8},{24,16},{32,24},{40,32},{48,40},{56,48},{64,5... | collective-permute-start | bytes 12296 | tf_op jit(solution)/shard_map/ppermute | solution.py:324
  35.2 1.4 collective-permute-done.up_in
  36.6 8.1 %shard_map.105 = (s32[40,128]{1,0:T(8,128)S(1)}, f32[40,128]{1,0:T(8,128)S(1)}, f32[36,12,128]{2,1,0:T(8,128)S(1)}, f32[32,24,128]{2,1,0:T(8,128)}, f32[4,12,128]{2,1,0:T(8,128)}, /*index=5*/f32[4,12,128]{2,1,0:T(8,128)}) custom-call(s32[1]{0:T(128)} %bitcast.p_ref, f32[72,128]{1,0:T(8,128)S(1)} %get-tuple-element.22.tab_ref, ...), custom_call_target="tpu_custom_call" | custom-call | tf_op jit(solution)/shard_map/pallas_call | solution.py:312
  46.0 9.1 %all-to-all-start.1 = ((f32[32,24,128]{2,1,0:T(8,128)}), f32[32,24,128]{2,1,0:T(8,128)S(1)}, u32[]{:S(2)}, u32[]{:S(2)}) async-start(f32[32,24,128]{2,1,0:T(8,128)} %get-tuple-element.29), calls=%async_computation.1 | async-start | bytes 786432 | tf_op jit(solution)/shard_map/all_to_all | solution.py:328
  55.1 2.6 %shard_map.106 = (f32[8,12,16,128]{3,2,1,0:T(8,128)S(1)}, f32[8,12,16,128]{3,2,1,0:T(8,128)}) custom-call(f32[8,12,16,128]{3,2,1,0:T(8,128)S(1)} %all-to-all-done.2.in_ref), custom_call_target="tpu_custom_call" | custom-call | tf_op jit(solution)/shard_map/pallas_call | solution.py:312
  57.7 11.9 %all-to-all-done.1.chunk0_ref = f32[32,24,128]{2,1,0:T(8,128)S(1)} async-done(((f32[32,24,128]{2,1,0:T(8,128)}), f32[32,24,128]{2,1,0:T(8,128)S(1)}, u32[]{:S(2)}, u32[]{:S(2)}) %all-to-all-start.1) | async-done | bytes 393248 | tf_op jit(solution)/shard_map/all_to_all | solution.py:328
  69.7 17.8 %all_to_all.30.rate_ref = f32[8,12,16,128]{3,2,1,0:T(8,128)S(1)} all-to-all(f32[8,12,16,128]{3,2,1,0:T(8,128)S(1)} %get-tuple-element.32), channel_id=1, replica_groups=mesh['mesh'=32,'inst'=8] {'inst'}, dimensions={0} | all-to-all | bytes 1572864 | tf_op jit(solution)/shard_map/all_to_all | solution.py:359
  87.5 3.7 %all-to-all-start.5 = ((f32[8,12,16,128]{3,2,1,0:T(8,128)}), f32[8,12,16,128]{3,2,1,0:T(8,128)S(1)}, u32[]{:S(2)}, u32[]{:S(2)}) async-start(f32[8,12,16,128]{3,2,1,0:T(8,128)} %get-tuple-element.37), calls=%async_computation.5 | async-start | bytes 1572864 | tf_op jit(solution)/shard_map/all_to_all | solution.py:360
  91.2 8.0 %shard_map.107 = (f32[36,12,128]{2,1,0:T(8,128)S(1)}, f32[32,24,128]{2,1,0:T(8,128)}, f32[4,12,128]{2,1,0:T(8,128)}, f32[4,12,128]{2,1,0:T(8,128)}) custom-call(s32[1]{0:T(128)} %bitcast.p_ref, s32[40,128]{1,0:T(8,128)S(1)} %get-tuple-element.26.idx_ref, f32[8,12,16,128]{3,2,1,0:T(8,128)S(1)} %all_to_all.30.rate_ref), custom_call_target="tpu_custom_call" | custom-call | tf_op jit(solution)/shard_map/pallas_call | solution.py:312
  99.9 1.8 %all-to-all-done.5.acc_ref = f32[8,12,16,128]{3,2,1,0:T(8,128)S(1)} async-done(((f32[8,12,16,128]{3,2,1,0:T(8,128)}), f32[8,12,16,128]{3,2,1,0:T(8,128)S(1)}, u32[]{:S(2)}, u32[]{:S(2)}) %all-to-all-start.5) | async-done | bytes 786464 | tf_op jit(solution)/shard_map/all_to_all | solution.py:360
  101.7 8.2 %all-to-all-start.4 = ((f32[32,24,128]{2,1,0:T(8,128)}), f32[32,24,128]{2,1,0:T(8,128)S(1)}, u32[]{:S(2)}, u32[]{:S(2)}) async-start(f32[32,24,128]{2,1,0:T(8,128)} %get-tuple-element.34), calls=%async_computation.4 | async-start | bytes 786432 | tf_op jit(solution)/shard_map/all_to_all | solution.py:328
  110.1 2.2 %collective-permute-start.6 = (f32[13,32,128]{2,1,0:T(8,128)S(1)}, f32[13,32,128]{2,1,0:T(8,128)S(1)}, u32[]{:S(2)}, u32[]{:S(2)}) collective-permute-start(f32[13,32,128]{2,1,0:T(8,128)S(1)} %pad_maximum_fusion.1), channel_id=1, source_target_pairs={{0,8},{8,16},{16,24},{24,32},{32,40},{40,48},{48,56},{56,64},{64,7... | collective-permute-start | bytes 638984 | tf_op jit(solution)/shard_map/ppermute | solution.py:324
  112.3 7.1 %collective-permute-start.7 = (f32[13,32,128]{2,1,0:T(8,128)S(1)}, f32[13,32,128]{2,1,0:T(8,128)S(1)}, u32[]{:S(2)}, u32[]{:S(2)}) collective-permute-start(f32[13,32,128]{2,1,0:T(8,128)S(1)} %pad_maximum_fusion.2), channel_id=1, source_target_pairs={{8,0},{16,8},{24,16},{32,24},{40,32},{48,40},{56,48},{64,56},{72,6... | collective-permute-start | bytes 638984 | tf_op jit(solution)/shard_map/ppermute | solution.py:324
  119.6 5.3 %collective-permute-start.3 = (f32[4,12,128]{2,1,0:T(8,128)}, f32[4,12,128]{2,1,0:T(8,128)}, u32[]{:S(2)}, u32[]{:S(2)}) collective-permute-start(f32[4,12,128]{2,1,0:T(8,128)} %get-tuple-element.31), channel_id=1, source_target_pairs={{0,248},{8,0},{16,8},{24,16},{32,24},{40,32},{48,40},{56,48},{64,5... | collective-permute-start | bytes 73736 | tf_op jit(solution)/shard_map/ppermute | solution.py:324
  125.6 5.4 %collective-permute-start.5 = (f32[4,12,128]{2,1,0:T(8,128)}, f32[4,12,128]{2,1,0:T(8,128)}, u32[]{:S(2)}, u32[]{:S(2)}) collective-permute-start(f32[4,12,128]{2,1,0:T(8,128)} %get-tuple-element.36), channel_id=1, source_target_pairs={{0,248},{8,0},{16,8},{24,16},{32,24},{40,32},{48,40},{56,48},{64,5... | collective-permute-start | bytes 73736 | tf_op jit(solution)/shard_map/ppermute | solution.py:324
  134.4 1.6 %shard_map.108 = (f32[12,4,32,128]{3,2,1,0:T(8,128)S(1)}, f32[4,32,128]{2,1,0:T(8,128)S(1)}) custom-call(f32[16,4]{1,0:T(8,128)S(1)} %copy.24.refs_0_, s32[4,32,128]{2,1,0:T(8,128)S(1)} %copy-done.8, f32[6,4,32,128]{3,2,1,0:T(8,128)S(1)} %bitcast.26, f32[6,4,32,128]{3,2,1,0:T(8,128)S(1)} %bitcast.29, f32[6,4,32,128]{3,2,1,0:T(8,128)S(1)} %bitcast.30, ...), custom_call_target="tpu_custom_call" | custom-call | tf_op jit(solution)/shard_map/pallas_call | solution.py:312
  136.7 1.0 copy-done.4
  137.7 1.0 copy-done.6
  140.9 9.7 %shard_map.109 = (f32[6,4,32,128]{3,2,1,0:T(8,128)}, f32[6,4,32,128]{3,2,1,0:T(8,128)}) custom-call(s32[1]{0:T(128)} %bitcast.p_ref, s32[40,128]{1,0:T(8,128)S(1)} %copy-done.14, f32[40,128]{1,0:T(8,128)S(1)} %copy-done.18, f32[36,12,128]{2,1,0:T(8,128)S(1)} %copy-done.4, f32[32,24,128]{2,1,0:T(8,128)S(1)} %all-to-all-done.1.chunk0_ref, ...), custom_call_target="tpu_custom_call" | custom-call | tf_op jit(solution)/shard_map/pallas_call | solution.py:312
  (66 shorter events, 11.5 us)
Async XLA Ops:
  4.0 20.7 %all-to-all-start = ((f32[32,8,128]{2,1,0:T(8,128)}), f32[32,8,128]{2,1,0:T(8,128)S(1)}, u32[]{:S(2)}, u32[]{:S(2)}) async-start(f32[32,8,128]{2,1,0:T(8,128)} %get-tuple-element.23), calls=%async_computation | async-start | bytes 262144 | tf_op jit(solution)/shard_map/all_to_all | solution.py:328
  17.7 18.9 %copy-start = (f32[2,3,4,32,128]{4,3,2,1,0:T(8,128)S(1)}, f32[2,3,4,32,128]{4,3,2,1,0:T(8,128)}, u32[]{:S(2)}) copy-start(f32[2,3,4,32,128]{4,3,2,1,0:T(8,128)} %param.9) | copy-start | bytes 1179652
  17.7 18.9 %copy-start.1 = (f32[2,3,4,32,128]{4,3,2,1,0:T(8,128)S(1)}, f32[2,3,4,32,128]{4,3,2,1,0:T(8,128)}, u32[]{:S(2)}) copy-start(f32[2,3,4,32,128]{4,3,2,1,0:T(8,128)} %param.10) | copy-start | bytes 1179652
  24.8 21.2 %all-to-all-start.2 = ((f32[8,12,16,128]{3,2,1,0:T(8,128)}), f32[8,12,16,128]{3,2,1,0:T(8,128)S(1)}, u32[]{:S(2)}, u32[]{:S(2)}) async-start(f32[8,12,16,128]{3,2,1,0:T(8,128)} %copy_bitcast_fusion), calls=%async_computation.2 | async-start | bytes 1572864 | tf_op jit(solution)/shard_map/all_to_all | solution.py:341
  29.9 6.7 %collective-permute-start = (f32[8,128]{1,0:T(8,128)S(1)}, f32[8,128]{1,0:T(8,128)S(1)}, u32[]{:S(2)}, u32[]{:S(2)}) collective-permute-start(f32[8,128]{1,0:T(8,128)S(1)} %get-tuple-element.24), channel_id=1, source_target_pairs={{0,8},{8,16},{16,24},{24,32},{32,40},{40,48},{48,56},{56,64},{64,7... | collective-permute-start | bytes 12296 | tf_op jit(solution)/shard_map/ppermute | solution.py:324
  29.9 6.7 %collective-permute-start.1 = (f32[8,128]{1,0:T(8,128)S(1)}, f32[8,128]{1,0:T(8,128)S(1)}, u32[]{:S(2)}, u32[]{:S(2)}) collective-permute-start(f32[8,128]{1,0:T(8,128)S(1)} %get-tuple-element.25), channel_id=1, source_target_pairs={{0,248},{8,0},{16,8},{24,16},{32,24},{40,32},{48,40},{56,48},{64,5... | collective-permute-start | bytes 12296 | tf_op jit(solution)/shard_map/ppermute | solution.py:324
  46.0 45.2 %copy-start.13 = (s32[40,128]{1,0:T(8,128)}, s32[40,128]{1,0:T(8,128)S(1)}, u32[]{:S(2)}) copy-start(s32[40,128]{1,0:T(8,128)S(1)} %get-tuple-element.26.idx_ref) | copy-start | bytes 61444
  46.0 23.7 %all-to-all-start.1 = ((f32[32,24,128]{2,1,0:T(8,128)}), f32[32,24,128]{2,1,0:T(8,128)S(1)}, u32[]{:S(2)}, u32[]{:S(2)}) async-start(f32[32,24,128]{2,1,0:T(8,128)} %get-tuple-element.29), calls=%async_computation.1 | async-start | bytes 786432 | tf_op jit(solution)/shard_map/all_to_all | solution.py:328
  87.5 3.7 %copy-start.7 = (s32[4,32,128]{2,1,0:T(8,128)S(1)}, s32[4,32,128]{2,1,0:T(8,128)}, u32[]{:S(2)}) copy-start(s32[4,32,128]{2,1,0:T(8,128)} %refs_1_.1) | copy-start | bytes 196612
  87.5 14.2 %all-to-all-start.5 = ((f32[8,12,16,128]{3,2,1,0:T(8,128)}), f32[8,12,16,128]{3,2,1,0:T(8,128)S(1)}, u32[]{:S(2)}, u32[]{:S(2)}) async-start(f32[8,12,16,128]{3,2,1,0:T(8,128)} %get-tuple-element.37), calls=%async_computation.5 | async-start | bytes 1572864 | tf_op jit(solution)/shard_map/all_to_all | solution.py:360
  101.7 35.0 %all-to-all-start.4 = ((f32[32,24,128]{2,1,0:T(8,128)}), f32[32,24,128]{2,1,0:T(8,128)S(1)}, u32[]{:S(2)}, u32[]{:S(2)}) async-start(f32[32,24,128]{2,1,0:T(8,128)} %get-tuple-element.34), calls=%async_computation.4 | async-start | bytes 786432 | tf_op jit(solution)/shard_map/all_to_all | solution.py:328
  110.1 21.7 %copy-start.2 = (f32[2,3,4,32,128]{4,3,2,1,0:T(8,128)S(1)}, f32[2,3,4,32,128]{4,3,2,1,0:T(8,128)}, u32[]{:S(2)}) copy-start(f32[2,3,4,32,128]{4,3,2,1,0:T(8,128)} %param.11) | copy-start | bytes 1179652
  110.1 14.8 %collective-permute-start.6 = (f32[13,32,128]{2,1,0:T(8,128)S(1)}, f32[13,32,128]{2,1,0:T(8,128)S(1)}, u32[]{:S(2)}, u32[]{:S(2)}) collective-permute-start(f32[13,32,128]{2,1,0:T(8,128)S(1)} %pad_maximum_fusion.1), channel_id=1, source_target_pairs={{0,8},{8,16},{16,24},{24,32},{32,40},{40,48},{48,56},{56,64},{64,7... | collective-permute-start | bytes 638984 | tf_op jit(solution)/shard_map/ppermute | solution.py:324
  112.3 18.7 %collective-permute-start.7 = (f32[13,32,128]{2,1,0:T(8,128)S(1)}, f32[13,32,128]{2,1,0:T(8,128)S(1)}, u32[]{:S(2)}, u32[]{:S(2)}) collective-permute-start(f32[13,32,128]{2,1,0:T(8,128)S(1)} %pad_maximum_fusion.2), channel_id=1, source_target_pairs={{8,0},{16,8},{24,16},{32,24},{40,32},{48,40},{56,48},{64,56},{72,6... | collective-permute-start | bytes 638984 | tf_op jit(solution)/shard_map/ppermute | solution.py:324
  119.4 17.2 %collective-permute-start.2 = (f32[4,12,128]{2,1,0:T(8,128)}, f32[4,12,128]{2,1,0:T(8,128)}, u32[]{:S(2)}, u32[]{:S(2)}) collective-permute-start(f32[4,12,128]{2,1,0:T(8,128)} %get-tuple-element.30), channel_id=1, source_target_pairs={{0,8},{8,16},{16,24},{24,32},{32,40},{40,48},{48,56},{56,64},{64,7... | collective-permute-start | bytes 73736 | tf_op jit(solution)/shard_map/ppermute | solution.py:324
  119.5 11.4 %copy-start.23 = (f32[16,4]{0,1:T(4,128)S(1)}, f32[16,4]{0,1:T(4,128)}, u32[]{:S(2)}) copy-start(f32[16,4]{0,1:T(4,128)} %param.13) | copy-start | bytes 772
  119.6 17.1 %collective-permute-start.3 = (f32[4,12,128]{2,1,0:T(8,128)}, f32[4,12,128]{2,1,0:T(8,128)}, u32[]{:S(2)}, u32[]{:S(2)}) collective-permute-start(f32[4,12,128]{2,1,0:T(8,128)} %get-tuple-element.31), channel_id=1, source_target_pairs={{0,248},{8,0},{16,8},{24,16},{32,24},{40,32},{48,40},{56,48},{64,5... | collective-permute-start | bytes 73736 | tf_op jit(solution)/shard_map/ppermute | solution.py:324
  124.9 11.8 %collective-permute-start.4 = (f32[4,12,128]{2,1,0:T(8,128)}, f32[4,12,128]{2,1,0:T(8,128)}, u32[]{:S(2)}, u32[]{:S(2)}) collective-permute-start(f32[4,12,128]{2,1,0:T(8,128)} %get-tuple-element.35), channel_id=1, source_target_pairs={{0,8},{8,16},{16,24},{24,32},{32,40},{40,48},{48,56},{56,64},{64,7... | collective-permute-start | bytes 73736 | tf_op jit(solution)/shard_map/ppermute | solution.py:324
  125.6 11.1 %collective-permute-start.5 = (f32[4,12,128]{2,1,0:T(8,128)}, f32[4,12,128]{2,1,0:T(8,128)}, u32[]{:S(2)}, u32[]{:S(2)}) collective-permute-start(f32[4,12,128]{2,1,0:T(8,128)} %get-tuple-element.36), channel_id=1, source_target_pairs={{0,248},{8,0},{16,8},{24,16},{32,24},{40,32},{48,40},{56,48},{64,5... | collective-permute-start | bytes 73736 | tf_op jit(solution)/shard_map/ppermute | solution.py:324
  131.7 0.8 copy-start.8
  132.6 0.9 copy-start.10
  133.5 0.9 copy-start.12
  136.7 1.0 copy-start.4
  137.7 1.0 copy-start.6
  (13 other events, 9.1 us)

commit v2 on v1

v2 whole, which is shorter than its diff:
```python
import jax
import jax.numpy as jnp
import numpy as np
from jax import lax
from jax.experimental import pallas as pl
from jax.experimental.pallas import tpu as pltpu
from jax.sharding import PartitionSpec as P

frequency = 0.6
damping = 0.3
bolt_stiff = 2.0
slip_force = 1.0
slip_speed = 0.5
stop_stiff = 3.0
clearance = 0.3

SLABS = 32
PARTS = 8
SIDE = 18
SEG = 42
f32 = jnp.float32
bf16 = jnp.bfloat16
i32 = jnp.int32


def tables(count):
    offsets = np.arange(count)[:, None] - np.arange(count)[None, :]
    tangent = np.where(offsets == 0, 1.0, np.tan(np.pi * offsets / count))
    first = np.where(offsets == 0, 0.0, 0.5 * np.where(offsets % 2 == 0, 1.0, -1.0) / tangent) * frequency
    return first, first @ first


FIRST, SECOND = tables(2 * PARTS)
MIXED = (SECOND + damping * FIRST).astype(np.float32)
SPREAD = np.kron(FIRST, np.eye(3)).astype(np.float32)


def far_place(offset):
    return 8 + (offset - 3) // 3, SEG * ((offset - 3) % 3)


def place(offset):
    return {2: (6, 0), 30: (7, 0)}.get(offset) or far_place(offset)


def lane_roll(x, shift):
    shift = shift % 128
    return pltpu.roll(x, shift, x.ndim - 1) if shift else x


def lanes(rows):
    return lax.broadcasted_iota(i32, (rows, 128), 1)


def merge_far(read, rows, fill):
    lane = lanes(rows)
    tiles = []
    for k in range(9):
        parts = [lane_roll(read(3 + 3 * k + s), SEG * s) for s in range(3)]
        tile = jnp.where(lane < SEG, parts[0], jnp.where(lane < 2 * SEG, parts[1], parts[2]))
        tiles.append(jnp.where(lane < 3 * SEG, tile, fill))
    return tiles


def slot_tables(p, owner_ref, local_ref, remote_ref, kind_ref):
    count = owner_ref.shape[1]
    offset = (owner_ref[...] - p) & (SLABS - 1)
    hit = (lax.broadcasted_iota(i32, (SLABS, count), 0) == offset).astype(f32)
    hit16 = hit.astype(bf16)
    before = (lax.broadcasted_iota(i32, (128, 128), 0) < lax.broadcasted_iota(i32, (128, 128), 1)).astype(f32).astype(bf16)
    row = lax.broadcasted_iota(i32, (SLABS, 1), 0)
    far = row - 3
    group = (far * 171) >> 9
    start = 1024 + group * 128 + (far - 3 * group) * SEG
    for value, at in ((0, 0), (1, 256), (SLABS - 1, 512), (2, 768), (SLABS - 2, 896)):
        start = jnp.where(row == value, at, start)
    run = start.astype(f32)
    places = []
    for b in range(count // 128):
        block = hit[:, 128 * b : 128 * (b + 1)]
        earlier = jnp.dot(hit16[:, 128 * b : 128 * (b + 1)], before, preferred_element_type=f32)
        places.append(jnp.sum(block * (earlier + run), axis=0, keepdims=True))
        run = run + jnp.sum(block, axis=1, keepdims=True)
    slot = jnp.concatenate(places, axis=1).astype(i32)
    in_tile = lax.broadcasted_iota(i32, (24, count), 0) == (slot >> 7)
    in_lane = (lax.broadcasted_iota(i32, (128, count), 0) == (slot & 127)).astype(f32).astype(bf16)
    local = local_ref[...]
    remote = remote_ref[...]
    values = (local >> 7, local & 127, remote >> 7, remote & 127, kind_ref[...], jnp.ones_like(local))
    spread = jnp.concatenate([jnp.where(in_tile, v.astype(f32), 0.0) for v in values], axis=0).astype(bf16)
    got = lax.dot_general(spread, in_lane, (((1,), (1,)), ((), ())), preferred_element_type=f32)
    got = [got[24 * k : 24 * (k + 1)] for k in range(6)]
    empty = got[5] - 1.0
    return got[0] * 128.0 + got[1] + empty, got[2] * 128.0 + got[3] + empty, got[4]


def picks(idx_ref, k):
    idx = jnp.concatenate([idx_ref[pl.ds(2 * k, 1), :], idx_ref[pl.ds(2 * k + 1, 1), :]], axis=1)
    code = ((idx >> 12) << 7) | (idx & 127)
    pick = (lax.broadcasted_iota(i32, (512, 256), 0) == code).astype(f32).astype(bf16)
    return pick, lax.broadcasted_iota(i32, (32, 256), 0) == ((idx >> 7) & 31)


def split_fields(disp_ref, dir_ref, hi_ref, lo_ref):
    for field, ref in enumerate((disp_ref, dir_ref)):
        for x in range(4):
            value = ref[:, x].reshape(6 * 32, 128)
            hi = value.astype(bf16)
            at = (slice(192 * field, 192 * (field + 1)), slice(128 * x, 128 * (x + 1)))
            hi_ref[at] = hi
            lo_ref[at] = (value - hi.astype(f32)).astype(bf16)


def gather_rows(hi_ref, lo_ref, idx_ref, here_ref):
    def step(k, carry):
        pick, in_y = picks(idx_ref, k)
        rows = jnp.dot(hi_ref[...], pick, preferred_element_type=f32)
        rows = rows + jnp.dot(lo_ref[...], pick, preferred_element_type=f32)
        got = jnp.sum(jnp.where(in_y[None], rows.reshape(12, 32, 256), 0.0), axis=1)
        here_ref[2 * k, 0:12, :] = got[:, :128]
        here_ref[2 * k + 1, 0:12, :] = got[:, 128:]
        return carry

    lax.fori_loop(0, SIDE // 2, step, 0)


def scatter_rows(val_ref, idx_ref, sum_ref):
    sum_ref[...] = jnp.zeros(sum_ref.shape, f32)
    dims = (((1,), (1,)), ((), ()))

    def step(k, carry):
        pick, in_y = picks(idx_ref, k)
        value = jnp.concatenate([val_ref[2 * k], val_ref[2 * k + 1]], axis=1)
        hi = value.astype(bf16).astype(f32)
        spread = [
            jnp.where(in_y[None], part[:, None, :], 0.0).reshape(384, 256).astype(bf16) for part in (hi, value - hi)
        ]
        got = lax.dot_general(spread[0], pick, dims, preferred_element_type=f32)
        got = got + lax.dot_general(spread[1], pick, dims, preferred_element_type=f32)
        sum_ref[...] = sum_ref[...] + got
        return carry

    lax.fori_loop(0, SIDE // 2, step, 0)


def list_kernel(p_ref, owner_ref, local_ref, remote_ref, kind_ref, disp_ref, dir_ref,
                idx_ref, chunk_ref, up_ref, down_ref, self_ref, hi_ref, lo_ref, rows_ref):
    p = p_ref[0]
    split_fields(disp_ref, dir_ref, hi_ref, lo_ref)
    mine, theirs, kind = slot_tables(p, owner_ref, local_ref, remote_ref, kind_ref)
    idx_ref[...] = mine.astype(i32)
    for tile in range(SIDE):
        rows_ref[tile, 12:13, :] = theirs[tile : tile + 1]
        rows_ref[tile, 13:14, :] = kind[tile : tile + 1]
        rows_ref[tile, 14:16, :] = jnp.zeros((2, 128), f32)
    gather_rows(hi_ref, lo_ref, idx_ref, rows_ref)
    for d in (0, 1, SLABS - 1):
        chunk_ref[(p + d) & (SLABS - 1)] = jnp.zeros((16, 128), f32)
    for d in range(2, SLABS - 1):
        tile, seg = place(d)
        chunk_ref[(p + d) & (SLABS - 1)] = lane_roll(rows_ref[tile], -seg)
    self_ref[...] = rows_ref[0:2]
    up_ref[...] = rows_ref[2:4]
    down_ref[...] = rows_ref[4:6]


def gap_kernel(p_ref, chunk_ref, up_ref, down_ref, self_ref, disp_ref, dir_ref,
               idx_ref, kind_ref, gap_ref, hi_ref, lo_ref, here_ref):
    p = p_ref[0]
    split_fields(disp_ref, dir_ref, hi_ref, lo_ref)

    def asked(d):
        return chunk_ref[(p - d) & (SLABS - 1)]

    tiles = [self_ref[0], self_ref[1], up_ref[0], up_ref[1], down_ref[0], down_ref[1], asked(2), asked(SLABS - 2)]
    tiles += merge_far(asked, 16, 0.0)
    beyond = lanes(1) >= 3 * SEG
    rows = [t[12:13] for t in tiles[:8]] + [jnp.where(beyond, -1.0, t[12:13]) for t in tiles[8:]]
    idx_ref[...] = jnp.concatenate(rows + [jnp.full((7, 128), -1.0, f32)], axis=0).astype(i32)
    kind_ref[...] = jnp.concatenate([t[13:14] for t in tiles] + [jnp.zeros((7, 128), f32)], axis=0)
    gather_rows(hi_ref, lo_ref, idx_ref, here_ref)
    for tile in range(24):
        gap = tiles[tile][0:12] - here_ref[tile] if tile < 17 else jnp.zeros((12, 128), f32)
        gap_ref[tile // 3, :, 128 * (tile % 3) : 128 * (tile % 3 + 1)] = gap


def force_kernel(me_ref, kind_ref, spread_ref, gap_ref, out_ref, r_ref, d_ref, f_ref, t_ref):
    me = me_ref[0]
    for k in range(PARTS):
        r_ref[6 * k : 6 * k + 6] = gap_ref[k, 0:6, :]
        d_ref[6 * k : 6 * k + 6] = gap_ref[k, 6:12, :]
    r = r_ref[...]
    dr = d_ref[...]
    w = jnp.dot(spread_ref[...], r, precision=lax.Precision.HIGHEST, preferred_element_type=f32)
    dw = jnp.dot(spread_ref[...], dr, precision=lax.Precision.HIGHEST, preferred_element_type=f32)
    bolted = jnp.concatenate([kind_ref[pl.ds(3 * me + k, 1), :] for k in range(3)], axis=1)
    slide = jnp.tanh(w / slip_speed)
    opened = jnp.tanh(r / clearance)
    friction = bolt_stiff * r + slip_force * slide
    contact = stop_stiff * (r - clearance * opened)
    f_ref[...] = bolted * friction + (1.0 - bolted) * contact
    tangent_friction = bolt_stiff * dr + slip_force * (1.0 - slide * slide) / slip_speed * dw
    tangent_contact = stop_stiff * opened * opened * dr
    t_ref[...] = bolted * tangent_friction + (1.0 - bolted) * tangent_contact
    for k in range(PARTS):
        out_ref[k, 0:6, :] = f_ref[6 * k : 6 * k + 6]
        out_ref[k, 6:12, :] = t_ref[6 * k : 6 * k + 6]


def reply_kernel(p_ref, force_ref, chunk_ref, up_ref, down_ref, self_ref):
    p = p_ref[0]

    def force(tile):
        return force_ref[tile // 3, :, 128 * (tile % 3) : 128 * (tile % 3 + 1)]

    for d in (0, 1, SLABS - 1):
        chunk_ref[(p - d) & (SLABS - 1)] = jnp.zeros((12, 128), f32)
    for d in range(2, SLABS - 1):
        tile, seg = place(d)
        chunk_ref[(p - d) & (SLABS - 1)] = lane_roll(force(tile), -seg)
    for k in range(2):
        self_ref[k] = force(k)
        down_ref[k] = force(2 + k)
        up_ref[k] = force(4 + k)


def partner_kernel(me_ref, idx_ref, force_ref, lin_ref, mass_ref, *refs):
    acc_refs, (out_ref, val_ref, sum_ref) = refs[:PARTS], refs[PARTS:]
    for tile in range(17):
        val_ref[tile] = -force_ref[tile // 3, :, 128 * (tile % 3) : 128 * (tile % 3 + 1)]
    val_ref[17] = jnp.zeros((12, 128), f32)
    scatter_rows(val_ref, idx_ref, sum_ref)
    for x in range(4):
        out_ref[:, x] = lin_ref[:, x] + sum_ref[:, 128 * x : 128 * (x + 1)].reshape(12, 32, 128)
    me = me_ref[0]
    for k, acc in enumerate(acc_refs):
        block = me ^ k
        x = block >> 1
        rows = pl.ds(pl.multiple_of(16 * (block & 1), 16), 16)
        out_ref[:, x, rows, :] = out_ref[:, x, rows, :] + mass_ref[x, rows, :][None] * acc[...]


def final_kernel(p_ref, idx_ref, chunk_ref, up_ref, down_ref, self_ref, part_ref, res_ref, jac_ref, val_ref, sum_ref):
    p = p_ref[0]

    def listed(d):
        return chunk_ref[(p + d) & (SLABS - 1)]

    tiles = [self_ref[0], self_ref[1], down_ref[0], down_ref[1], up_ref[0], up_ref[1], listed(2), listed(SLABS - 2)]
    tiles += merge_far(listed, 12, 0.0) + [jnp.zeros((12, 128), f32)]
    for k, tile in enumerate(tiles):
        val_ref[k] = tile
    scatter_rows(val_ref, idx_ref, sum_ref)
    for x in range(4):
        out = part_ref[:, x] + sum_ref[:, 128 * x : 128 * (x + 1)].reshape(12, 32, 128)
        res_ref[:, x] = out[0:6]
        jac_ref[:, x] = out[6:12]


def piece_kernel(me_ref, disp_ref, dir_ref, *out_refs):
    me = me_ref[0]
    for k, out in enumerate(out_refs):
        block = me ^ k
        rows = pl.ds(pl.multiple_of(16 * (block & 1), 16), 16)
        out[0:6] = disp_ref[:, block >> 1, rows, :]
        out[6:12] = dir_ref[:, block >> 1, rows, :]


def time_kernel(me_ref, table_ref, *refs):
    ins, outs = refs[:PARTS], refs[PARTS:]
    me = me_ref[0]

    def step(g, carry):
        field = g // 3
        row = 6 * field + (g - 3 * field)
        x = [[ins[k][row + 3 * t] for t in range(2)] for k in range(PARTS)]
        for k in range(PARTS):
            for t in range(2):
                acc = None
                for j in range(PARTS):
                    for s in range(2):
                        term = x[j][s] * table_ref[2 * (me ^ k) + t, 2 * (me ^ j) + s]
                        acc = term if acc is None else acc + term
                outs[k][row + 3 * t] = acc
        return carry

    lax.fori_loop(0, 6, step, 0)


def lookup(ids, mat_ref, column, count):
    out = jnp.zeros(ids.shape, f32)
    for m in range(count):
        out = jnp.where(ids == m, mat_ref[m, column], out)
    return out


def stiff_kernel(mat_ref, ids_ref, disp_ref, dir_ref, forcing_ref, low_ref, high_ref, out_ref, mass_ref, *, materials):
    ids = ids_ref[...]
    kx, ky, kz, mass = [lookup(ids, mat_ref, col, materials) for col in range(4)]
    mass_ref[...] = mass
    kx_low = lookup(low_ref[12].astype(i32) - 1, mat_ref, 0, materials)
    kx_high = lookup(high_ref[12].astype(i32) - 1, mat_ref, 0, materials)
    shape = ids.shape
    y = lax.broadcasted_iota(i32, shape, 1)
    z = lax.broadcasted_iota(i32, shape, 2)
    xm = 0.5 * (kx + jnp.concatenate([kx_low[None], kx[:-1]], axis=0))
    xp = 0.5 * (kx + jnp.concatenate([kx[1:], kx_high[None]], axis=0))
    total = xm + xp
    sides = []
    for k, pos, axis in ((ky, y, 1), (kz, z, 2)):
        size = shape[axis]
        for shift, edge in ((1, 0), (size - 1, size - 1)):
            inside = pos != edge
            near = jnp.where(inside, pltpu.roll(k, shift, axis), 0.0)
            side = 0.5 * (k + near)
            total = total + side
            sides.append((jnp.where(inside, side, 0.0), shift, axis))
    for field, ref in enumerate((disp_ref, dir_ref)):
        for c in range(6):
            w = ref[c]
            down = jnp.concatenate([low_ref[6 * field + c][None], w[:-1]], axis=0)
            up = jnp.concatenate([w[1:], high_ref[6 * field + c][None]], axis=0)
            out = total * w - xm * down - xp * up
            for side, shift, axis in sides:
                out = out - side * pltpu.roll(w, shift, axis)
            if field == 0:
                out = out - forcing_ref[c]
            out_ref[6 * field + c] = out


VMEM = 48 * 1024 * 1024


def call(kernel, outs, *args, smem=(0,), scratch=()):
    specs = [pl.BlockSpec(memory_space=pltpu.SMEM if k in smem else pltpu.VMEM) for k in range(len(args))]
    return pl.pallas_call(
        kernel,
        out_shape=[jax.ShapeDtypeStruct(s, d) for s, d in outs],
        in_specs=specs,
        out_specs=[pl.BlockSpec(memory_space=pltpu.VMEM) for _ in outs],
        scratch_shapes=list(scratch),
        compiler_params=pltpu.CompilerParams(vmem_limit_bytes=VMEM),
    )(*args)


def shift(x, by, wrap=True):
    pairs = [(i, (i + by) % SLABS) for i in range(SLABS) if wrap or 0 <= i + by < SLABS]
    return lax.ppermute(x, "mesh", pairs)


def exchange(chunk, up, down):
    up, down = shift(up, 1), shift(down, -1)
    return lax.all_to_all(chunk, "mesh", split_axis=0, concat_axis=0, tiled=True), up, down


def swap(pieces):
    return [pieces[0]] + [lax.ppermute(pieces[k], "inst", [(i, i ^ k) for i in range(PARTS)]) for k in range(1, PARTS)]


def inst_split(x):
    return lax.all_to_all(x, "inst", split_axis=0, concat_axis=0, tiled=True)


def on_device(displacement, direction, forcing, material_ids, materials, joint_owner, joint_local, joint_remote, joint_kind):
    shape = displacement.shape
    fields = (6, 4, 32, 128)
    whole = (12, 4, 32, 128)
    disp = displacement.reshape(fields)
    dire = direction.reshape(fields)
    count = joint_local.shape[0]
    p = lax.axis_index("mesh").astype(i32).reshape(1)
    me = lax.axis_index("inst").astype(i32).reshape(1)
    split = [pltpu.VMEM((384, 512), bf16)] * 2
    index = ((24, 128), i32)

    own_idx, chunk, up, down, own = call(
        list_kernel,
        [index, ((SLABS, 16, 128), f32)] + [((2, 16, 128), f32)] * 3,
        p,
        joint_owner.reshape(1, count),
        joint_local.reshape(1, count),
        joint_remote.reshape(1, count),
        joint_kind.reshape(1, count),
        disp,
        dire,
        scratch=split + [pltpu.VMEM((SIDE, 16, 128), f32)],
    )
    chunk, up, down = exchange(chunk, up, down)

    pieces = swap(call(piece_kernel, [((12, 16, 128), f32)] * PARTS, me, disp, dire))
    pieces = swap(call(time_kernel, [((12, 16, 128), f32)] * PARTS, me, jnp.asarray(MIXED), *pieces, smem=(0, 1)))

    ids_plus = (material_ids + 1).astype(f32)
    low = shift(jnp.concatenate([disp[:, 3], dire[:, 3], ids_plus[3:4]], axis=0), 1, wrap=False)
    high = shift(jnp.concatenate([disp[:, 0], dire[:, 0], ids_plus[0:1]], axis=0), -1, wrap=False)
    lin, mass = call(
        lambda *refs: stiff_kernel(*refs, materials=materials.shape[0]),
        [(whole, f32), ((4, 32, 128), f32)],
        materials, material_ids, disp, dire, forcing.reshape(fields), low, high,
    )

    part = ((PARTS, 12, 384), f32)
    far_idx, kind, gap = call(
        gap_kernel,
        [index, ((24, 128), f32), part],
        p, chunk, up, down, own, disp, dire,
        scratch=split + [pltpu.VMEM((SIDE, 12, 128), f32)],
    )
    force = call(
        force_kernel, [part], me, kind, jnp.asarray(SPREAD), inst_split(gap), scratch=[pltpu.VMEM((48, 384), f32)] * 4
    )[0]
    force = inst_split(force)
    chunk, up, down, own = call(
        reply_kernel, [((SLABS, 12, 128), f32)] + [((2, 12, 128), f32)] * 3, p, force
    )
    chunk, up, down = exchange(chunk, up, down)

    adding = [pltpu.VMEM((SIDE, 12, 128), f32), pltpu.VMEM((384, 512), f32)]
    partial = call(partner_kernel, [(whole, f32)], me, far_idx, force, lin, mass, *pieces, scratch=adding)[0]
    residual, jacobian = call(
        final_kernel, [(fields, f32)] * 2, p, own_idx, chunk, up, down, own, partial, scratch=adding
    )
    return residual.reshape(shape), jacobian.reshape(shape)


def solution(mesh):
    field = P("inst", None, "mesh", None, None)
    placed = (field, field, field, P("mesh", None, None), P(), P("mesh", None), P("mesh"), P("mesh"), P("mesh"))
    return jax.shard_map(on_device, mesh=mesh, in_specs=placed, out_specs=(field, field), check_vma=False)
```

time: 152 us -> 120 us (0.79)
  blocking collectives: 17.8 us -> 0 us
  local copies, waits for them, and re-layouts: 13.2 us -> 4.26 us
  Pallas kernels: 31.2 us -> 25.4 us
  starting transfers between devices: 63.2 us -> 68.2 us
  other arithmetic: 2.13 us -> 0.04 us
  waiting for transfers between devices: 22.2 us -> 20.5 us
    ppermute x0 -> x14, starting transfers between devices: none -> 25.5 us  [swap(): lax.ppermute(pieces[k], 'inst', [(i, i ^ k) for i in range(PARTS)])]
    all_to_all x3 -> x2, waiting for transfers between devices: 19 us -> 0.01 us  [exchange(): lax.all_to_all(chunk, 'mesh', split_axis=0, concat_axis=0, tiled=True)]
    all_to_all x1 -> x0, blocking collectives: 17.8 us -> none  [on_device(): rate = lax.all_to_all(rate, 'inst', split_axis=0, concat_axis=0, tiled=True)]
    all_to_all x2, waiting for transfers between devices: 1.8 us -> 13.8 us  [inst_split(): return lax.all_to_all(x, 'inst', split_axis=0, concat_axis=0, tiled=True)]
    all_to_all x3 -> x2, starting transfers between devices: 28.9 us -> 19.1 us  [exchange(): lax.all_to_all(chunk, 'mesh', split_axis=0, concat_axis=0, tiled=True)]
    ppermute x8 -> x6, starting transfers between devices: 25.4 us -> 16 us  [shift(): return lax.ppermute(x, 'mesh', pairs)]
    unnamed x51 -> x28, local copies, waits for them, and re-layouts: 13.2 us -> 4.22 us
    pallas_call x6 -> x9, Pallas kernels: 31.2 us -> 25.4 us  [call(): pl.pallas_call(kernel, out_shape=[jax.ShapeDtypeStruct(s, d) for s, d in...]
  transfers between devices with their start and end apart: 13 -> 24, of which waited for: 4 -> 6; matrix products, arithmetic and copies ran while one was open for 2% -> 0% of each run, Pallas kernels for 13% -> 13%
where the time goes in v2:
time: 120 us; the launch traced here: 119 us
  starting transfers between devices  68.2 us (57%)
  Pallas kernels  25.4 us (21%)
  waiting for transfers between devices  20.5 us (17%)
  local copies, waits for them, and re-layouts  4.26 us (4%)
    ppermute x14, starting transfers between devices, swap(): lax.ppermute(pieces[k], 'inst', [(i, i ^ k) for i in range(PARTS)])  25.5 us
    pallas_call x9, Pallas kernels, call(): pl.pallas_call(kernel, out_shape=[jax.ShapeDtypeStruct(s, d) for s, d in...  25.4 us
    all_to_all x2, starting transfers between devices, exchange(): lax.all_to_all(chunk, 'mesh', split_axis=0, concat_axis=0, tiled=True)  19.1 us
    ppermute x6, starting transfers between devices, shift(): return lax.ppermute(x, 'mesh', pairs)  16 us
    all_to_all x2, waiting for transfers between devices, inst_split(): return lax.all_to_all(x, 'inst', split_axis=0, concat_axis=0, tiled=True)  13.8 us
    all_to_all x2, starting transfers between devices, inst_split(): return lax.all_to_all(x, 'inst', split_axis=0, concat_axis=0, tiled=True)  7.57 us
    ppermute x14, waiting for transfers between devices, swap(): lax.ppermute(pieces[k], 'inst', [(i, i ^ k) for i in range(PARTS)])  5.32 us
    unnamed x28, local copies, waits for them, and re-layouts  4.22 us
  transfers between devices with their start and end apart: 24, of which 6 were waited for; matrix products, arithmetic and copies ran while one was open for 0% of the time, Pallas kernels for 13%

profile of v2, /device:TPU:4, one launch (start us, length us, event | category | flops | bytes accessed | tf_op | source)
XLA Modules:
  0.0 119.4 jit_solution(6661777209852968969)
XLA Ops:
  4.7 4.9 %shard_map.122 = (s32[24,128]{1,0:T(8,128)S(1)}, f32[32,16,128]{2,1,0:T(8,128)}, f32[2,16,128]{2,1,0:T(8,128)S(1)}, f32[2,16,128]{2,1,0:T(8,128)S(1)}, f32[2,16,128]{2,1,0:T(8,128)S(1)}) custom-call(s32[1]{0:T(128)} %bitcast.p_ref, s32[1,2048]{1,0:T(1,128)S(1)} %bitcast.32, s32[1,2048]{1,0:T(1,128)S(1)} %bitcast.33, s32[1,2048]{1,0:T(1,128)S(1)} %bitcast.34, ...), custom_call_target="tpu_custom_call" | custom-call | tf_op jit(solution)/shard_map/pallas_call | solution.py:336
  9.7 11.7 %all-to-all-start = ((f32[32,16,128]{2,1,0:T(8,128)}), f32[32,16,128]{2,1,0:T(8,128)S(1)}, u32[]{:S(2)}, u32[]{:S(2)}) async-start(f32[32,16,128]{2,1,0:T(8,128)} %get-tuple-element.35), calls=%async_computation | async-start | bytes 524288 | tf_op jit(solution)/shard_map/all_to_all | solution.py:353
  21.5 3.9 %collective-permute-start.10 = (f32[12,16,128]{2,1,0:T(8,128)S(1)}, f32[12,16,128]{2,1,0:T(8,128)S(1)}, u32[]{:S(2)}, u32[]{:S(2)}) collective-permute-start(f32[12,16,128]{2,1,0:T(8,128)S(1)} %get-tuple-element.53), channel_id=1, source_target_pairs={{0,5},{1,4},{2,7},{3,6},{4,1},{5,0},{6,3},{7,2},{8,13},{9,12},{10,... | collective-permute-start | bytes 294920 | tf_op jit(solution)/shard_map/ppermute | solution.py:357
  26.5 2.4 %collective-permute-start.12 = (f32[12,16,128]{2,1,0:T(8,128)S(1)}, f32[12,16,128]{2,1,0:T(8,128)S(1)}, u32[]{:S(2)}, u32[]{:S(2)}) collective-permute-start(f32[12,16,128]{2,1,0:T(8,128)S(1)} %get-tuple-element.55), channel_id=1, source_target_pairs={{0,7},{1,6},{2,5},{3,4},{4,3},{5,2},{6,1},{7,0},{8,15},{9,14},{10,... | collective-permute-start | bytes 294920 | tf_op jit(solution)/shard_map/ppermute | solution.py:357
  28.9 5.4 %collective-permute-start.1 = (f32[2,16,128]{2,1,0:T(8,128)S(1)}, f32[2,16,128]{2,1,0:T(8,128)S(1)}, u32[]{:S(2)}, u32[]{:S(2)}) collective-permute-start(f32[2,16,128]{2,1,0:T(8,128)S(1)} %get-tuple-element.37), channel_id=1, source_target_pairs={{0,248},{8,0},{16,8},{24,16},{32,24},{40,32},{48,40},{56,48},{64,5... | collective-permute-start | bytes 49160 | tf_op jit(solution)/shard_map/ppermute | solution.py:348
  36.9 4.4 %shard_map.123 = (s32[24,128]{1,0:T(8,128)S(1)}, f32[24,128]{1,0:T(8,128)S(1)}, f32[8,12,384]{2,1,0:T(8,128)}) custom-call(s32[1]{0:T(128)} %bitcast.p_ref, f32[32,16,128]{2,1,0:T(8,128)S(1)} %all-to-all-done.chunk_ref, f32[2,16,128]{2,1,0:T(8,128)S(1)} %collective-permute-done.up_ref, f32[2,16,128]{2,1,0:T(8,128)S(1)} %collective-permute-done.1.down_ref, ...), custom_call_target="tpu_custom_call" | custom-call | tf_op jit(solution)/shard_map/pallas_call | solution.py:336
  41.3 4.2 %all-to-all-start.1 = ((f32[8,12,384]{2,1,0:T(8,128)}), f32[8,12,384]{2,1,0:T(8,128)S(1)}, u32[]{:S(2)}, u32[]{:S(2)}) async-start(f32[8,12,384]{2,1,0:T(8,128)} %get-tuple-element.40), calls=%async_computation.1 | async-start | bytes 393216 | tf_op jit(solution)/shard_map/all_to_all | solution.py:361
  45.5 6.9 %all-to-all-done.1.gap_ref = f32[8,12,384]{2,1,0:T(8,128)S(1)} async-done(((f32[8,12,384]{2,1,0:T(8,128)}), f32[8,12,384]{2,1,0:T(8,128)S(1)}, u32[]{:S(2)}, u32[]{:S(2)}) %all-to-all-start.1) | async-done | bytes 147488 | tf_op jit(solution)/shard_map/all_to_all | solution.py:361
  53.4 3.4 %all-to-all-start.2 = ((f32[8,12,384]{2,1,0:T(8,128)}), f32[8,12,384]{2,1,0:T(8,128)S(1)}, u32[]{:S(2)}, u32[]{:S(2)}) async-start(f32[8,12,384]{2,1,0:T(8,128)} %shard_map.124), calls=%async_computation.2 | async-start | bytes 393216 | tf_op jit(solution)/shard_map/all_to_all | solution.py:361
  56.8 6.9 %all-to-all-done.2.force_ref = f32[8,12,384]{2,1,0:T(8,128)S(1)} async-done(((f32[8,12,384]{2,1,0:T(8,128)}), f32[8,12,384]{2,1,0:T(8,128)S(1)}, u32[]{:S(2)}, u32[]{:S(2)}) %all-to-all-start.2) | async-done | bytes 147488 | tf_op jit(solution)/shard_map/all_to_all | solution.py:361
  64.5 7.4 %all-to-all-start.3 = ((f32[32,12,128]{2,1,0:T(8,128)}), f32[32,12,128]{2,1,0:T(8,128)S(1)}, u32[]{:S(2)}, u32[]{:S(2)}) async-start(f32[32,12,128]{2,1,0:T(8,128)} %get-tuple-element.41), calls=%async_computation.3 | async-start | bytes 524288 | tf_op jit(solution)/shard_map/all_to_all | solution.py:353
  72.9 2.0 %collective-permute-start.9 = (f32[12,16,128]{2,1,0:T(8,128)S(1)}, f32[12,16,128]{2,1,0:T(8,128)S(1)}, u32[]{:S(2)}, u32[]{:S(2)}) collective-permute-start(f32[12,16,128]{2,1,0:T(8,128)S(1)} %get-tuple-element.52), channel_id=1, source_target_pairs={{0,4},{1,5},{2,6},{3,7},{4,0},{5,1},{6,2},{7,3},{8,12},{9,13},{10,... | collective-permute-start | bytes 294920 | tf_op jit(solution)/shard_map/ppermute | solution.py:357
  74.9 1.9 %collective-permute-start.4 = (f32[13,32,128]{2,1,0:T(8,128)S(1)}, f32[13,32,128]{2,1,0:T(8,128)S(1)}, u32[]{:S(2)}, u32[]{:S(2)}) collective-permute-start(f32[13,32,128]{2,1,0:T(8,128)S(1)} %pad_maximum_fusion), channel_id=1, source_target_pairs={{0,8},{8,16},{16,24},{24,32},{32,40},{40,48},{48,56},{56,64},{64,7... | collective-permute-start | bytes 638984 | tf_op jit(solution)/shard_map/ppermute | solution.py:348
  76.9 2.1 %collective-permute-done.8.refs_3_ = f32[12,16,128]{2,1,0:T(8,128)S(1)} collective-permute-done((f32[12,16,128]{2,1,0:T(8,128)S(1)}, f32[12,16,128]{2,1,0:T(8,128)S(1)}, u32[]{:S(2)}, u32[]{:S(2)}) %collective-permute-start.8) | collective-permute-done | bytes 98336 | tf_op jit(solution)/shard_map/ppermute | solution.py:357
  80.4 3.3 %shard_map.128 = (f32[12,16,128]{2,1,0:T(8,128)S(1)}, f32[12,16,128]{2,1,0:T(8,128)S(1)}, f32[12,16,128]{2,1,0:T(8,128)S(1)}, f32[12,16,128]{2,1,0:T(8,128)S(1)}...) custom-call(s32[1]{0:T(128)} %bitcast.8.me_ref, ...), custom_call_target="tpu_custom_call" | custom-call | tf_op jit(solution)/shard_map/pallas_call | solution.py:336
  84.8 3.3 %collective-permute-start.5 = (f32[13,32,128]{2,1,0:T(8,128)S(1)}, f32[13,32,128]{2,1,0:T(8,128)S(1)}, u32[]{:S(2)}, u32[]{:S(2)}) collective-permute-start(f32[13,32,128]{2,1,0:T(8,128)S(1)} %pad_maximum_fusion.1), channel_id=1, source_target_pairs={{8,0},{16,8},{24,16},{32,24},{40,32},{48,40},{56,48},{64,56},{72,6... | collective-permute-start | bytes 638984 | tf_op jit(solution)/shard_map/ppermute | solution.py:348
  88.6 2.9 %collective-permute-start.15 = (f32[12,16,128]{2,1,0:T(8,128)S(1)}, f32[12,16,128]{2,1,0:T(8,128)S(1)}, u32[]{:S(2)}, u32[]{:S(2)}) collective-permute-start(f32[12,16,128]{2,1,0:T(8,128)S(1)} %get-tuple-element.59), channel_id=1, source_target_pairs={{0,3},{1,2},{2,1},{3,0},{4,7},{5,6},{6,5},{7,4},{8,11},{9,10},{10,... | collective-permute-start | bytes 294920 | tf_op jit(solution)/shard_map/ppermute | solution.py:357
  93.2 1.7 %collective-permute-done.14.refs_2_ = f32[12,16,128]{2,1,0:T(8,128)S(1)} collective-permute-done((f32[12,16,128]{2,1,0:T(8,128)S(1)}, f32[12,16,128]{2,1,0:T(8,128)S(1)}, u32[]{:S(2)}, u32[]{:S(2)}) %collective-permute-start.14) | collective-permute-done | bytes 98336 | tf_op jit(solution)/shard_map/ppermute | solution.py:357
  95.0 2.1 %collective-permute-start.17 = (f32[12,16,128]{2,1,0:T(8,128)S(1)}, f32[12,16,128]{2,1,0:T(8,128)S(1)}, u32[]{:S(2)}, u32[]{:S(2)}) collective-permute-start(f32[12,16,128]{2,1,0:T(8,128)S(1)} %get-tuple-element.61), channel_id=1, source_target_pairs={{0,5},{1,4},{2,7},{3,6},{4,1},{5,0},{6,3},{7,2},{8,13},{9,12},{10,... | collective-permute-start | bytes 294920 | tf_op jit(solution)/shard_map/ppermute | solution.py:357
  97.1 3.8 %collective-permute-start.18 = (f32[12,16,128]{2,1,0:T(8,128)S(1)}, f32[12,16,128]{2,1,0:T(8,128)S(1)}, u32[]{:S(2)}, u32[]{:S(2)}) collective-permute-start(f32[12,16,128]{2,1,0:T(8,128)S(1)} %get-tuple-element.62), channel_id=1, source_target_pairs={{0,6},{1,7},{2,4},{3,5},{4,2},{5,3},{6,0},{7,1},{8,14},{9,15},{10,... | collective-permute-start | bytes 294920 | tf_op jit(solution)/shard_map/ppermute | solution.py:357
  101.0 1.8 %collective-permute-start.19 = (f32[12,16,128]{2,1,0:T(8,128)S(1)}, f32[12,16,128]{2,1,0:T(8,128)S(1)}, u32[]{:S(2)}, u32[]{:S(2)}) collective-permute-start(f32[12,16,128]{2,1,0:T(8,128)S(1)} %get-tuple-element.63), channel_id=1, source_target_pairs={{0,7},{1,6},{2,5},{3,4},{4,3},{5,2},{6,1},{7,0},{8,15},{9,14},{10,... | collective-permute-start | bytes 294920 | tf_op jit(solution)/shard_map/ppermute | solution.py:357
  102.8 5.4 %collective-permute-start.3 = (f32[2,12,128]{2,1,0:T(8,128)S(1)}, f32[2,12,128]{2,1,0:T(8,128)S(1)}, u32[]{:S(2)}, u32[]{:S(2)}) collective-permute-start(f32[2,12,128]{2,1,0:T(8,128)S(1)} %get-tuple-element.43), channel_id=1, source_target_pairs={{0,248},{8,0},{16,8},{24,16},{32,24},{40,32},{48,40},{56,48},{64,5... | collective-permute-start | bytes 36872 | tf_op jit(solution)/shard_map/ppermute | solution.py:348
  109.9 4.3 %shard_map.129.part_ref = f32[12,4,32,128]{3,2,1,0:T(8,128)S(1)} custom-call(s32[1]{0:T(128)} %bitcast.8.me_ref, s32[24,128]{1,0:T(8,128)S(1)} %get-tuple-element.45.idx_ref, f32[8,12,384]{2,1,0:T(8,128)S(1)} %all-to-all-done.2.force_ref, f32[12,4,32,128]{3,2,1,0:T(8,128)S(1)} %get-tuple-element.46.lin_ref, f32[4,32,128]{2,1,0:T(8,128)S(1)} %get-tuple-element.47.mass_ref, ...), custom_call_target="tpu_custom_call" | custom-call | tf_op jit(solution)/shard_map/pallas_call | solution.py:336
  114.2 5.1 %shard_map.130 = (f32[6,4,32,128]{3,2,1,0:T(8,128)}, f32[6,4,32,128]{3,2,1,0:T(8,128)}) custom-call(s32[1]{0:T(128)} %bitcast.p_ref, s32[24,128]{1,0:T(8,128)S(1)} %get-tuple-element.34.idx_ref, f32[32,12,128]{2,1,0:T(8,128)S(1)} %all-to-all-done.3.chunk_ref, f32[2,12,128]{2,1,0:T(8,128)S(1)} %collective-permute-done.2.up_ref, ...), custom_call_target="tpu_custom_call" | custom-call | tf_op jit(solution)/shard_map/pallas_call | solution.py:336
  (67 shorter events, 17.1 us)
Async XLA Ops:
  9.7 27.2 %all-to-all-start = ((f32[32,16,128]{2,1,0:T(8,128)}), f32[32,16,128]{2,1,0:T(8,128)S(1)}, u32[]{:S(2)}, u32[]{:S(2)}) async-start(f32[32,16,128]{2,1,0:T(8,128)} %get-tuple-element.35), calls=%async_computation | async-start | bytes 524288 | tf_op jit(solution)/shard_map/all_to_all | solution.py:353
  21.5 50.4 %collective-permute-start.10 = (f32[12,16,128]{2,1,0:T(8,128)S(1)}, f32[12,16,128]{2,1,0:T(8,128)S(1)}, u32[]{:S(2)}, u32[]{:S(2)}) collective-permute-start(f32[12,16,128]{2,1,0:T(8,128)S(1)} %get-tuple-element.53), channel_id=1, source_target_pairs={{0,5},{1,4},{2,7},{3,6},{4,1},{5,0},{6,3},{7,2},{8,13},{9,12},{10,... | collective-permute-start | bytes 294920 | tf_op jit(solution)/shard_map/ppermute | solution.py:357
  25.4 47.4 %collective-permute-start.11 = (f32[12,16,128]{2,1,0:T(8,128)S(1)}, f32[12,16,128]{2,1,0:T(8,128)S(1)}, u32[]{:S(2)}, u32[]{:S(2)}) collective-permute-start(f32[12,16,128]{2,1,0:T(8,128)S(1)} %get-tuple-element.54), channel_id=1, source_target_pairs={{0,6},{1,7},{2,4},{3,5},{4,2},{5,3},{6,0},{7,1},{8,14},{9,15},{10,... | collective-permute-start | bytes 294920 | tf_op jit(solution)/shard_map/ppermute | solution.py:357
  26.5 48.4 %collective-permute-start.12 = (f32[12,16,128]{2,1,0:T(8,128)S(1)}, f32[12,16,128]{2,1,0:T(8,128)S(1)}, u32[]{:S(2)}, u32[]{:S(2)}) collective-permute-start(f32[12,16,128]{2,1,0:T(8,128)S(1)} %get-tuple-element.55), channel_id=1, source_target_pairs={{0,7},{1,6},{2,5},{3,4},{4,3},{5,2},{6,1},{7,0},{8,15},{9,14},{10,... | collective-permute-start | bytes 294920 | tf_op jit(solution)/shard_map/ppermute | solution.py:357
  28.9 6.8 %collective-permute-start = (f32[2,16,128]{2,1,0:T(8,128)S(1)}, f32[2,16,128]{2,1,0:T(8,128)S(1)}, u32[]{:S(2)}, u32[]{:S(2)}) collective-permute-start(f32[2,16,128]{2,1,0:T(8,128)S(1)} %get-tuple-element.36), channel_id=1, source_target_pairs={{0,8},{8,16},{16,24},{24,32},{32,40},{40,48},{48,56},{56,64},{64,7... | collective-permute-start | bytes 49160 | tf_op jit(solution)/shard_map/ppermute | solution.py:348
  28.9 8.0 %collective-permute-start.1 = (f32[2,16,128]{2,1,0:T(8,128)S(1)}, f32[2,16,128]{2,1,0:T(8,128)S(1)}, u32[]{:S(2)}, u32[]{:S(2)}) collective-permute-start(f32[2,16,128]{2,1,0:T(8,128)S(1)} %get-tuple-element.37), channel_id=1, source_target_pairs={{0,248},{8,0},{16,8},{24,16},{32,24},{40,32},{48,40},{56,48},{64,5... | collective-permute-start | bytes 49160 | tf_op jit(solution)/shard_map/ppermute | solution.py:348
  35.7 41.1 %collective-permute-start.6 = (f32[12,16,128]{2,1,0:T(8,128)S(1)}, f32[12,16,128]{2,1,0:T(8,128)S(1)}, u32[]{:S(2)}, u32[]{:S(2)}) collective-permute-start(f32[12,16,128]{2,1,0:T(8,128)S(1)} %get-tuple-element.49), channel_id=1, source_target_pairs={{0,1},{1,0},{2,3},{3,2},{4,5},{5,4},{6,7},{7,6},{8,9},{9,8},{10,11... | collective-permute-start | bytes 294920 | tf_op jit(solution)/shard_map/ppermute | solution.py:357
  36.9 40.0 %collective-permute-start.7 = (f32[12,16,128]{2,1,0:T(8,128)S(1)}, f32[12,16,128]{2,1,0:T(8,128)S(1)}, u32[]{:S(2)}, u32[]{:S(2)}) collective-permute-start(f32[12,16,128]{2,1,0:T(8,128)S(1)} %get-tuple-element.50), channel_id=1, source_target_pairs={{0,2},{1,3},{2,0},{3,1},{4,6},{5,7},{6,4},{7,5},{8,10},{9,11},{10,... | collective-permute-start | bytes 294920 | tf_op jit(solution)/shard_map/ppermute | solution.py:357
  41.3 11.1 %all-to-all-start.1 = ((f32[8,12,384]{2,1,0:T(8,128)}), f32[8,12,384]{2,1,0:T(8,128)S(1)}, u32[]{:S(2)}, u32[]{:S(2)}) async-start(f32[8,12,384]{2,1,0:T(8,128)} %get-tuple-element.40), calls=%async_computation.1 | async-start | bytes 393216 | tf_op jit(solution)/shard_map/all_to_all | solution.py:361
  53.4 10.3 %all-to-all-start.2 = ((f32[8,12,384]{2,1,0:T(8,128)}), f32[8,12,384]{2,1,0:T(8,128)S(1)}, u32[]{:S(2)}, u32[]{:S(2)}) async-start(f32[8,12,384]{2,1,0:T(8,128)} %shard_map.124), calls=%async_computation.2 | async-start | bytes 393216 | tf_op jit(solution)/shard_map/all_to_all | solution.py:361
  64.5 49.7 %all-to-all-start.3 = ((f32[32,12,128]{2,1,0:T(8,128)}), f32[32,12,128]{2,1,0:T(8,128)S(1)}, u32[]{:S(2)}, u32[]{:S(2)}) async-start(f32[32,12,128]{2,1,0:T(8,128)} %get-tuple-element.41), calls=%async_computation.3 | async-start | bytes 524288 | tf_op jit(solution)/shard_map/all_to_all | solution.py:353
  71.9 7.0 %collective-permute-start.8 = (f32[12,16,128]{2,1,0:T(8,128)S(1)}, f32[12,16,128]{2,1,0:T(8,128)S(1)}, u32[]{:S(2)}, u32[]{:S(2)}) collective-permute-start(f32[12,16,128]{2,1,0:T(8,128)S(1)} %get-tuple-element.51), channel_id=1, source_target_pairs={{0,3},{1,2},{2,1},{3,0},{4,7},{5,6},{6,5},{7,4},{8,11},{9,10},{10,... | collective-permute-start | bytes 294920 | tf_op jit(solution)/shard_map/ppermute | solution.py:357
  72.9 7.6 %collective-permute-start.9 = (f32[12,16,128]{2,1,0:T(8,128)S(1)}, f32[12,16,128]{2,1,0:T(8,128)S(1)}, u32[]{:S(2)}, u32[]{:S(2)}) collective-permute-start(f32[12,16,128]{2,1,0:T(8,128)S(1)} %get-tuple-element.52), channel_id=1, source_target_pairs={{0,4},{1,5},{2,6},{3,7},{4,0},{5,1},{6,2},{7,3},{8,12},{9,13},{10,... | collective-permute-start | bytes 294920 | tf_op jit(solution)/shard_map/ppermute | solution.py:357
  74.9 27.9 %collective-permute-start.4 = (f32[13,32,128]{2,1,0:T(8,128)S(1)}, f32[13,32,128]{2,1,0:T(8,128)S(1)}, u32[]{:S(2)}, u32[]{:S(2)}) collective-permute-start(f32[13,32,128]{2,1,0:T(8,128)S(1)} %pad_maximum_fusion), channel_id=1, source_target_pairs={{0,8},{8,16},{16,24},{24,32},{32,40},{40,48},{48,56},{56,64},{64,7... | collective-permute-start | bytes 638984 | tf_op jit(solution)/shard_map/ppermute | solution.py:348
  83.7 7.8 %collective-permute-start.13 = (f32[12,16,128]{2,1,0:T(8,128)S(1)}, f32[12,16,128]{2,1,0:T(8,128)S(1)}, u32[]{:S(2)}, u32[]{:S(2)}) collective-permute-start(f32[12,16,128]{2,1,0:T(8,128)S(1)} %get-tuple-element.57), channel_id=1, source_target_pairs={{0,1},{1,0},{2,3},{3,2},{4,5},{5,4},{6,7},{7,6},{8,9},{9,8},{10,11... | collective-permute-start | bytes 294920 | tf_op jit(solution)/shard_map/ppermute | solution.py:357
  84.8 18.0 %collective-permute-start.5 = (f32[13,32,128]{2,1,0:T(8,128)S(1)}, f32[13,32,128]{2,1,0:T(8,128)S(1)}, u32[]{:S(2)}, u32[]{:S(2)}) collective-permute-start(f32[13,32,128]{2,1,0:T(8,128)S(1)} %pad_maximum_fusion.1), channel_id=1, source_target_pairs={{8,0},{16,8},{24,16},{32,24},{40,32},{48,40},{56,48},{64,56},{72,6... | collective-permute-start | bytes 638984 | tf_op jit(solution)/shard_map/ppermute | solution.py:348
  88.1 6.8 %collective-permute-start.14 = (f32[12,16,128]{2,1,0:T(8,128)S(1)}, f32[12,16,128]{2,1,0:T(8,128)S(1)}, u32[]{:S(2)}, u32[]{:S(2)}) collective-permute-start(f32[12,16,128]{2,1,0:T(8,128)S(1)} %get-tuple-element.58), channel_id=1, source_target_pairs={{0,2},{1,3},{2,0},{3,1},{4,6},{5,7},{6,4},{7,5},{8,10},{9,11},{10,... | collective-permute-start | bytes 294920 | tf_op jit(solution)/shard_map/ppermute | solution.py:357
  88.6 8.5 %collective-permute-start.15 = (f32[12,16,128]{2,1,0:T(8,128)S(1)}, f32[12,16,128]{2,1,0:T(8,128)S(1)}, u32[]{:S(2)}, u32[]{:S(2)}) collective-permute-start(f32[12,16,128]{2,1,0:T(8,128)S(1)} %get-tuple-element.59), channel_id=1, source_target_pairs={{0,3},{1,2},{2,1},{3,0},{4,7},{5,6},{6,5},{7,4},{8,11},{9,10},{10,... | collective-permute-start | bytes 294920 | tf_op jit(solution)/shard_map/ppermute | solution.py:357
  91.5 9.4 %collective-permute-start.16 = (f32[12,16,128]{2,1,0:T(8,128)S(1)}, f32[12,16,128]{2,1,0:T(8,128)S(1)}, u32[]{:S(2)}, u32[]{:S(2)}) collective-permute-start(f32[12,16,128]{2,1,0:T(8,128)S(1)} %get-tuple-element.60), channel_id=1, source_target_pairs={{0,4},{1,5},{2,6},{3,7},{4,0},{5,1},{6,2},{7,3},{8,12},{9,13},{10,... | collective-permute-start | bytes 294920 | tf_op jit(solution)/shard_map/ppermute | solution.py:357
  95.0 14.9 %collective-permute-start.17 = (f32[12,16,128]{2,1,0:T(8,128)S(1)}, f32[12,16,128]{2,1,0:T(8,128)S(1)}, u32[]{:S(2)}, u32[]{:S(2)}) collective-permute-start(f32[12,16,128]{2,1,0:T(8,128)S(1)} %get-tuple-element.61), channel_id=1, source_target_pairs={{0,5},{1,4},{2,7},{3,6},{4,1},{5,0},{6,3},{7,2},{8,13},{9,12},{10,... | collective-permute-start | bytes 294920 | tf_op jit(solution)/shard_map/ppermute | solution.py:357
  97.1 12.8 %collective-permute-start.18 = (f32[12,16,128]{2,1,0:T(8,128)S(1)}, f32[12,16,128]{2,1,0:T(8,128)S(1)}, u32[]{:S(2)}, u32[]{:S(2)}) collective-permute-start(f32[12,16,128]{2,1,0:T(8,128)S(1)} %get-tuple-element.62), channel_id=1, source_target_pairs={{0,6},{1,7},{2,4},{3,5},{4,2},{5,3},{6,0},{7,1},{8,14},{9,15},{10,... | collective-permute-start | bytes 294920 | tf_op jit(solution)/shard_map/ppermute | solution.py:357
  101.0 8.9 %collective-permute-start.19 = (f32[12,16,128]{2,1,0:T(8,128)S(1)}, f32[12,16,128]{2,1,0:T(8,128)S(1)}, u32[]{:S(2)}, u32[]{:S(2)}) collective-permute-start(f32[12,16,128]{2,1,0:T(8,128)S(1)} %get-tuple-element.63), channel_id=1, source_target_pairs={{0,7},{1,6},{2,5},{3,4},{4,3},{5,2},{6,1},{7,0},{8,15},{9,14},{10,... | collective-permute-start | bytes 294920 | tf_op jit(solution)/shard_map/ppermute | solution.py:357
  102.8 11.4 %collective-permute-start.2 = (f32[2,12,128]{2,1,0:T(8,128)S(1)}, f32[2,12,128]{2,1,0:T(8,128)S(1)}, u32[]{:S(2)}, u32[]{:S(2)}) collective-permute-start(f32[2,12,128]{2,1,0:T(8,128)S(1)} %get-tuple-element.42), channel_id=1, source_target_pairs={{0,8},{8,16},{16,24},{24,32},{32,40},{40,48},{48,56},{56,64},{64,7... | collective-permute-start | bytes 36872 | tf_op jit(solution)/shard_map/ppermute | solution.py:348
  102.8 11.4 %collective-permute-start.3 = (f32[2,12,128]{2,1,0:T(8,128)S(1)}, f32[2,12,128]{2,1,0:T(8,128)S(1)}, u32[]{:S(2)}, u32[]{:S(2)}) collective-permute-start(f32[2,12,128]{2,1,0:T(8,128)S(1)} %get-tuple-element.43), channel_id=1, source_target_pairs={{0,248},{8,0},{16,8},{24,16},{32,24},{40,32},{48,40},{56,48},{64,5... | collective-permute-start | bytes 36872 | tf_op jit(solution)/shard_map/ppermute | solution.py:348
  (13 other events, 81.7 us)

commit v3 on v2

--- a/solution.py
+++ b/solution.py
@@ -143,16 +143,36 @@
     lax.fori_loop(0, SIDE // 2, step, 0)
 
 
-def list_kernel(p_ref, owner_ref, local_ref, remote_ref, kind_ref, disp_ref, dir_ref,
-                idx_ref, chunk_ref, up_ref, down_ref, self_ref, hi_ref, lo_ref, rows_ref):
+def list_kernel(p_ref, me_ref, owner_hbm, local_hbm, remote_hbm, kind_hbm, disp_hbm, dir_hbm, ids_hbm,
+                idx_ref, chunk_ref, up_ref, down_ref, self_ref, same_ref, other_ref,
+                hi_ref, lo_ref, rows_ref, owner_ref, local_ref, remote_ref, kind_ref, disp_ref, dir_ref, ids_ref, sems):
     p = p_ref[0]
-    split_fields(disp_ref, dir_ref, hi_ref, lo_ref)
+    pairs = ((owner_hbm, owner_ref), (local_hbm, local_ref), (remote_hbm, remote_ref), (kind_hbm, kind_ref),
+             (disp_hbm, disp_ref), (dir_hbm, dir_ref), (ids_hbm, ids_ref))
+    copies = [pltpu.make_async_copy(a, b, sems.at[k]) for k, (a, b) in enumerate(pairs)]
+    for copy in copies:
+        copy.start()
+    for copy in copies[:4]:
+        copy.wait()
     mine, theirs, kind = slot_tables(p, owner_ref, local_ref, remote_ref, kind_ref)
     idx_ref[...] = mine.astype(i32)
     for tile in range(SIDE):
         rows_ref[tile, 12:13, :] = theirs[tile : tile + 1]
         rows_ref[tile, 13:14, :] = kind[tile : tile + 1]
         rows_ref[tile, 14:16, :] = jnp.zeros((2, 128), f32)
+    for copy in copies[4:]:
+        copy.wait()
+    split_fields(disp_ref, dir_ref, hi_ref, lo_ref)
+    for ref, x in ((up_ref, 3), (down_ref, 0)):
+        ref[2:14] = disp_ref[:, x].reshape(12, 16, 128)
+        ref[14:26] = dir_ref[:, x].reshape(12, 16, 128)
+        ref[26:28] = (ids_ref[x] + 1).astype(f32).reshape(2, 16, 128)
+    for k in range(PARTS):
+        block = me_ref[0] ^ k
+        rows = pl.ds(pl.multiple_of(16 * (block & 1), 16), 16)
+        out = (same_ref, other_ref)[k % 2].at[k // 2]
+        out[0:6] = disp_ref[:, block >> 1, rows, :]
+        out[6:12] = dir_ref[:, block >> 1, rows, :]
     gather_rows(hi_ref, lo_ref, idx_ref, rows_ref)
     for d in (0, 1, SLABS - 1):
         chunk_ref[(p + d) & (SLABS - 1)] = jnp.zeros((16, 128), f32)
@@ -160,11 +180,11 @@
         tile, seg = place(d)
         chunk_ref[(p + d) & (SLABS - 1)] = lane_roll(rows_ref[tile], -seg)
     self_ref[...] = rows_ref[0:2]
-    up_ref[...] = rows_ref[2:4]
-    down_ref[...] = rows_ref[4:6]
-
-
-def gap_kernel(p_ref, chunk_ref, up_ref, down_ref, self_ref, disp_ref, dir_ref,
+    up_ref[0:2] = rows_ref[2:4]
+    down_ref[0:2] = rows_ref[4:6]
+
+
+def gap_kernel(p_ref, chunk_ref, up_ref, down_ref, self_ref, disp_ref, dir_ref, after_ref,
                idx_ref, kind_ref, gap_ref, hi_ref, lo_ref, here_ref):
     p = p_ref[0]
     split_fields(disp_ref, dir_ref, hi_ref, lo_ref)
@@ -184,7 +204,7 @@
         gap_ref[tile // 3, :, 128 * (tile % 3) : 128 * (tile % 3 + 1)] = gap
 
 
-def force_kernel(me_ref, kind_ref, spread_ref, gap_ref, out_ref, r_ref, d_ref, f_ref, t_ref):
+def force_kernel(me_ref, kind_ref, spread_ref, gap_ref, after_ref, out_ref, r_ref, d_ref, f_ref, t_ref):
     me = me_ref[0]
     for k in range(PARTS):
         r_ref[6 * k : 6 * k + 6] = gap_ref[k, 0:6, :]
@@ -207,7 +227,7 @@
         out_ref[k, 6:12, :] = t_ref[6 * k : 6 * k + 6]
 
 
-def reply_kernel(p_ref, force_ref, chunk_ref, up_ref, down_ref, self_ref):
+def reply_kernel(p_ref, force_ref, after1, after2, after3, chunk_ref, up_ref, down_ref, self_ref):
     p = p_ref[0]
 
     def force(tile):
@@ -224,8 +244,8 @@
         up_ref[k] = force(4 + k)
 
 
-def partner_kernel(me_ref, idx_ref, force_ref, lin_ref, mass_ref, *refs):
-    acc_refs, (out_ref, val_ref, sum_ref) = refs[:PARTS], refs[PARTS:]
+def partner_kernel(me_ref, idx_ref, force_ref, lin_ref, mass_ref, own_ref, y1_ref, y2_ref, y3_ref, x_ref,
+                   out_ref, val_ref, sum_ref):
     for tile in range(17):
         val_ref[tile] = -force_ref[tile // 3, :, 128 * (tile % 3) : 128 * (tile % 3 + 1)]
     val_ref[17] = jnp.zeros((12, 128), f32)
@@ -233,11 +253,12 @@
     for x in range(4):
         out_ref[:, x] = lin_ref[:, x] + sum_ref[:, 128 * x : 128 * (x + 1)].reshape(12, 32, 128)
     me = me_ref[0]
-    for k, acc in enumerate(acc_refs):
+    for k in range(PARTS):
+        acc = x_ref[k // 2] if k % 2 else (own_ref, y1_ref, y2_ref, y3_ref)[k // 2][0]
         block = me ^ k
         x = block >> 1
         rows = pl.ds(pl.multiple_of(16 * (block & 1), 16), 16)
-        out_ref[:, x, rows, :] = out_ref[:, x, rows, :] + mass_ref[x, rows, :][None] * acc[...]
+        out_ref[:, x, rows, :] = out_ref[:, x, rows, :] + mass_ref[x, rows, :][None] * acc
 
 
 def final_kernel(p_ref, idx_ref, chunk_ref, up_ref, down_ref, self_ref, part_ref, res_ref, jac_ref, val_ref, sum_ref):
@@ -257,18 +278,20 @@
         jac_ref[:, x] = out[6:12]
 
 
-def piece_kernel(me_ref, disp_ref, dir_ref, *out_refs):
+def join_kernel(same_ref, other_ref, *out_refs):
+    for k, out in enumerate(out_refs):
+        out[0] = same_ref[k + 1]
+        out[1] = other_ref[k + 1]
+
+
+def turn_kernel(own_ref, y1_ref, y2_ref, y3_ref, out_ref):
+    for k, ref in enumerate((own_ref, y1_ref, y2_ref, y3_ref)):
+        out_ref[k] = ref[1]
+
+
+def time_kernel(me_ref, table_ref, same_ref, other_ref, y1_ref, y2_ref, y3_ref, *outs):
     me = me_ref[0]
-    for k, out in enumerate(out_refs):
-        block = me ^ k
-        rows = pl.ds(pl.multiple_of(16 * (block & 1), 16), 16)
-        out[0:6] = disp_ref[:, block >> 1, rows, :]
-        out[6:12] = dir_ref[:, block >> 1, rows, :]
-
-
-def time_kernel(me_ref, table_ref, *refs):
-    ins, outs = refs[:PARTS], refs[PARTS:]
-    me = me_ref[0]
+    ins = [same_ref.at[0], other_ref.at[0]] + [ref.at[b] for ref in (y1_ref, y2_ref, y3_ref) for b in range(2)]
 
     def step(g, carry):
         field = g // 3
@@ -281,7 +304,7 @@
                     for s in range(2):
                         term = x[j][s] * table_ref[2 * (me ^ k) + t, 2 * (me ^ j) + s]
                         acc = term if acc is None else acc + term
-                outs[k][row + 3 * t] = acc
+                outs[k // 2][k % 2, row + 3 * t] = acc
         return carry
 
     lax.fori_loop(0, 6, step, 0)
@@ -294,12 +317,15 @@
     return out
 
 
-def stiff_kernel(mat_ref, ids_ref, disp_ref, dir_ref, forcing_ref, low_ref, high_ref, out_ref, mass_ref, *, materials):
+def stiff_kernel(p_ref, mat_ref, ids_ref, disp_ref, dir_ref, forcing_ref, up_ref, down_ref, out_ref, mass_ref, *, materials):
+    p = p_ref[0]
+    low = jnp.where(p > 0, up_ref[2:28], 0.0).reshape(13, 32, 128)
+    high = jnp.where(p < SLABS - 1, down_ref[2:28], 0.0).reshape(13, 32, 128)
     ids = ids_ref[...]
     kx, ky, kz, mass = [lookup(ids, mat_ref, col, materials) for col in range(4)]
     mass_ref[...] = mass
-    kx_low = lookup(low_ref[12].astype(i32) - 1, mat_ref, 0, materials)
-    kx_high = lookup(high_ref[12].astype(i32) - 1, mat_ref, 0, materials)
+    kx_low = lookup(low[12].astype(i32) - 1, mat_ref, 0, materials)
+    kx_high = lookup(high[12].astype(i32) - 1, mat_ref, 0, materials)
     shape = ids.shape
     y = lax.broadcasted_iota(i32, shape, 1)
     z = lax.broadcasted_iota(i32, shape, 2)
@@ -318,8 +344,8 @@
     for field, ref in enumerate((disp_ref, dir_ref)):
         for c in range(6):
             w = ref[c]
-            down = jnp.concatenate([low_ref[6 * field + c][None], w[:-1]], axis=0)
-            up = jnp.concatenate([w[1:], high_ref[6 * field + c][None]], axis=0)
+            down = jnp.concatenate([low[6 * field + c][None], w[:-1]], axis=0)
+            up = jnp.concatenate([w[1:], high[6 * field + c][None]], axis=0)
             out = total * w - xm * down - xp * up
             for side, shift, axis in sides:
                 out = out - side * pltpu.roll(w, shift, axis)
@@ -328,24 +354,24 @@
             out_ref[6 * field + c] = out
 
 
-VMEM = 48 * 1024 * 1024
-
-
-def call(kernel, outs, *args, smem=(0,), scratch=()):
-    specs = [pl.BlockSpec(memory_space=pltpu.SMEM if k in smem else pltpu.VMEM) for k in range(len(args))]
+VMEM = 24 * 1024 * 1024
+
+
+def call(kernel, outs, *args, smem=(0,), away=(), scratch=(), limit=VMEM):
+    spaces = [pltpu.SMEM if k in smem else pl.ANY if k in away else pltpu.VMEM for k in range(len(args))]
+    specs = [pl.BlockSpec(memory_space=space) for space in spaces]
     return pl.pallas_call(
         kernel,
         out_shape=[jax.ShapeDtypeStruct(s, d) for s, d in outs],
         in_specs=specs,
         out_specs=[pl.BlockSpec(memory_space=pltpu.VMEM) for _ in outs],
         scratch_shapes=list(scratch),
-        compiler_params=pltpu.CompilerParams(vmem_limit_bytes=VMEM),
+        compiler_params=pltpu.CompilerParams(vmem_limit_bytes=limit),
     )(*args)
 
 
-def shift(x, by, wrap=True):
-    pairs = [(i, (i + by) % SLABS) for i in range(SLABS) if wrap or 0 <= i + by < SLABS]
-    return lax.ppermute(x, "mesh", pairs)
+def shift(x, by):
+    return lax.ppermute(x, "mesh", [(i, (i + by) % SLABS) for i in range(SLABS)])
 
 
 def exchange(chunk, up, down):
@@ -353,8 +379,8 @@
     return lax.all_to_all(chunk, "mesh", split_axis=0, concat_axis=0, tiled=True), up, down
 
 
-def swap(pieces):
-    return [pieces[0]] + [lax.ppermute(pieces[k], "inst", [(i, i ^ k) for i in range(PARTS)]) for k in range(1, PARTS)]
+def swap(x, bit):
+    return lax.ppermute(x, "inst", [(i, i ^ bit) for i in range(PARTS)])
 
 
 def inst_split(x):
@@ -372,53 +398,69 @@
     me = lax.axis_index("inst").astype(i32).reshape(1)
     split = [pltpu.VMEM((384, 512), bf16)] * 2
     index = ((24, 128), i32)
-
-    own_idx, chunk, up, down, own = call(
+    half = ((4, 12, 16, 128), f32)
+
+    own_idx, chunk, up, down, own, same, other = call(
         list_kernel,
-        [index, ((SLABS, 16, 128), f32)] + [((2, 16, 128), f32)] * 3,
+        [index, ((SLABS, 16, 128), f32), ((28, 16, 128), f32), ((28, 16, 128), f32), ((2, 16, 128), f32), half, half],
         p,
+        me,
         joint_owner.reshape(1, count),
         joint_local.reshape(1, count),
         joint_remote.reshape(1, count),
         joint_kind.reshape(1, count),
         disp,
         dire,
-        scratch=split + [pltpu.VMEM((SIDE, 16, 128), f32)],
+        material_ids,
+        smem=(0, 1),
+        away=range(2, 9),
+        limit=60 * 1024 * 1024,
+        scratch=split
+        + [pltpu.VMEM((SIDE, 16, 128), f32)]
+        + [pltpu.VMEM((1, count), i32)] * 4
+        + [pltpu.VMEM(fields, f32)] * 2
+        + [pltpu.VMEM((4, 32, 128), i32), pltpu.SemaphoreType.DMA((7,))],
     )
     chunk, up, down = exchange(chunk, up, down)
 
-    pieces = swap(call(piece_kernel, [((12, 16, 128), f32)] * PARTS, me, disp, dire))
-    pieces = swap(call(time_kernel, [((12, 16, 128), f32)] * PARTS, me, jnp.asarray(MIXED), *pieces, smem=(0, 1)))
-
-    ids_plus = (material_ids + 1).astype(f32)
-    low = shift(jnp.concatenate([disp[:, 3], dire[:, 3], ids_plus[3:4]], axis=0), 1, wrap=False)
-    high = shift(jnp.concatenate([disp[:, 0], dire[:, 0], ids_plus[0:1]], axis=0), -1, wrap=False)
-    lin, mass = call(
-        lambda *refs: stiff_kernel(*refs, materials=materials.shape[0]),
-        [(whole, f32), ((4, 32, 128), f32)],
-        materials, material_ids, disp, dire, forcing.reshape(fields), low, high,
-    )
+    pair = ((2, 12, 16, 128), f32)
+    other = swap(other, 1)
+    joined = call(join_kernel, [pair] * 3, same, other, smem=())
+    turned = [swap(x, 2 * k + 2) for k, x in enumerate(joined)]
+    inertia = call(time_kernel, [pair] * 4, me, jnp.asarray(MIXED), same, other, *turned, smem=(0, 1))
 
     part = ((PARTS, 12, 384), f32)
     far_idx, kind, gap = call(
         gap_kernel,
         [index, ((24, 128), f32), part],
-        p, chunk, up, down, own, disp, dire,
+        p, chunk, up, down, own, disp, dire, joined[0],
+        away=(7,),
         scratch=split + [pltpu.VMEM((SIDE, 12, 128), f32)],
     )
     force = call(
-        force_kernel, [part], me, kind, jnp.asarray(SPREAD), inst_split(gap), scratch=[pltpu.VMEM((48, 384), f32)] * 4
+        force_kernel,
+        [part],
+        me, kind, jnp.asarray(SPREAD), inst_split(gap), inertia[0],
+        away=(4,),
+        scratch=[pltpu.VMEM((48, 384), f32)] * 4,
     )[0]
     force = inst_split(force)
-    chunk, up, down, own = call(
-        reply_kernel, [((SLABS, 12, 128), f32)] + [((2, 12, 128), f32)] * 3, p, force
+    turned = [inertia[0]] + [swap(inertia[k], 2 * k) for k in (1, 2, 3)]
+    messages = [((SLABS, 12, 128), f32)] + [((2, 12, 128), f32)] * 3
+    chunk, up2, down2, own = call(reply_kernel, messages, p, force, *turned[1:], away=(2, 3, 4))
+    chunk, up2, down2 = exchange(chunk, up2, down2)
+
+    lin, mass = call(
+        lambda *refs: stiff_kernel(*refs, materials=materials.shape[0]),
+        [(whole, f32), ((4, 32, 128), f32)],
+        p, materials, material_ids, disp, dire, forcing.reshape(fields), up, down,
+        smem=(0, 1),
     )
-    chunk, up, down = exchange(chunk, up, down)
-
+    other = swap(call(turn_kernel, [half], *turned, smem=())[0], 1)
     adding = [pltpu.VMEM((SIDE, 12, 128), f32), pltpu.VMEM((384, 512), f32)]
-    partial = call(partner_kernel, [(whole, f32)], me, far_idx, force, lin, mass, *pieces, scratch=adding)[0]
+    partial = call(partner_kernel, [(whole, f32)], me, far_idx, force, lin, mass, *turned, other, scratch=adding)[0]
     residual, jacobian = call(
-        final_kernel, [(fields, f32)] * 2, p, own_idx, chunk, up, down, own, partial, scratch=adding
+        final_kernel, [(fields, f32)] * 2, p, own_idx, chunk, up2, down2, own, partial, scratch=adding
     )
     return residual.reshape(shape), jacobian.reshape(shape)
 

time: 120 us -> 93.5 us (0.78)
  the two profiles are of different devices: /device:TPU:4 before, /device:TPU:1 now
where the time goes in v3:
time: 93.5 us; the launch traced here: 93 us
  starting transfers between devices  46.1 us (49%)
  Pallas kernels  28.8 us (31%)
  waiting for transfers between devices  17.2 us (18%)
    pallas_call x10, Pallas kernels, call(): pl.pallas_call(kernel, out_shape=[jax.ShapeDtypeStruct(s, d) for s, d in...  28.8 us
    all_to_all x2, starting transfers between devices, exchange(): lax.all_to_all(chunk, 'mesh', split_axis=0, concat_axis=0, tiled=True)  21.9 us
    ppermute x8, starting transfers between devices, swap(): return lax.ppermute(x, 'inst', [(i, i ^ bit) for i in range(PARTS)])  11.4 us
    all_to_all x2, starting transfers between devices, inst_split(): return lax.all_to_all(x, 'inst', split_axis=0, concat_axis=0, tiled=True)  9.16 us
    all_to_all x2, waiting for transfers between devices, exchange(): lax.all_to_all(chunk, 'mesh', split_axis=0, concat_axis=0, tiled=True)  7.53 us
    ppermute x4, waiting for transfers between devices, shift(): lax.ppermute(x, 'mesh', [(i, (i + by) % SLABS) for i in range(SLABS)])  5.04 us
    ppermute x8, waiting for transfers between devices, swap(): return lax.ppermute(x, 'inst', [(i, i ^ bit) for i in range(PARTS)])  4.61 us
    ppermute x4, starting transfers between devices, shift(): lax.ppermute(x, 'mesh', [(i, (i + by) % SLABS) for i in range(SLABS)])  3.53 us
  transfers between devices with their start and end apart: 16, of which 7 were waited for; matrix products, arithmetic and copies ran while one was open for 0% of the time, Pallas kernels for 19%

profile of v3, /device:TPU:1, one launch (start us, length us, event | category | flops | bytes accessed | tf_op | source)
XLA Modules:
  0.0 93.0 jit_solution(3322530614577033986)
XLA Ops:
  0.6 6.2 %shard_map.122 = (s32[24,128]{1,0:T(8,128)}, f32[32,16,128]{2,1,0:T(8,128)}, f32[28,16,128]{2,1,0:T(8,128)}, f32[28,16,128]{2,1,0:T(8,128)}, f32[2,16,128]{2,1,0...) custom-call(s32[1]{0:T(128)} %bitcast.p_ref.refs_0_, s32[1]{0:T(128)} %bitcast.1.me_ref, ...), custom_call_target="tpu_custom_call" | custom-call | tf_op jit(solution)/shard_map/pallas_call | solution.py:363
  6.8 2.1 %collective-permute-start.2 = (f32[4,12,16,128]{3,2,1,0:T(8,128)}, f32[4,12,16,128]{3,2,1,0:T(8,128)S(1)}, u32[]{:S(2)}, u32[]{:S(2)}) collective-permute-start(f32[4,12,16,128]{3,2,1,0:T(8,128)} %get-tuple-element.33), channel_id=1, source_target_pairs={{0,1},{1,0},{2,3},{3,2},{4,5},{5,4},{6,7},{7,6},{8,9},{9,8},{10,11... | collective-permute-start | bytes 1179656 | tf_op jit(solution)/shard_map/ppermute | solution.py:383
  8.9 11.9 %all-to-all-start = ((f32[32,16,128]{2,1,0:T(8,128)}), f32[32,16,128]{2,1,0:T(8,128)S(1)}, u32[]{:S(2)}, u32[]{:S(2)}) async-start(f32[32,16,128]{2,1,0:T(8,128)} %get-tuple-element.28), calls=%async_computation | async-start | bytes 524288 | tf_op jit(solution)/shard_map/all_to_all | solution.py:379
  20.8 1.7 %collective-permute-start = (f32[28,16,128]{2,1,0:T(8,128)}, f32[28,16,128]{2,1,0:T(8,128)S(1)}, u32[]{:S(2)}, u32[]{:S(2)}) collective-permute-start(f32[28,16,128]{2,1,0:T(8,128)} %get-tuple-element.29), channel_id=1, source_target_pairs={{0,8},{8,16},{16,24},{24,32},{32,40},{40,48},{48,56},{56,64},{64,7... | collective-permute-start | bytes 688136 | tf_op jit(solution)/shard_map/ppermute | solution.py:374
  23.3 1.3 %collective-permute-start.3 = (f32[2,12,16,128]{3,2,1,0:T(8,128)S(1)}, f32[2,12,16,128]{3,2,1,0:T(8,128)S(1)}, u32[]{:S(2)}, u32[]{:S(2)}) collective-permute-start(f32[2,12,16,128]{3,2,1,0:T(8,128)S(1)} %get-tuple-element.34.after_ref), channel_id=1, source_target_pairs={{0,2},{1,3},{2,0},{3,1},{4,6},{5,7},{6,4},{7,5},{8,10},{9,11},{10,... | collective-permute-start | bytes 589832 | tf_op jit(solution)/shard_map/ppermute | solution.py:383
  24.6 2.6 %collective-permute-start.4 = (f32[2,12,16,128]{3,2,1,0:T(8,128)}, f32[2,12,16,128]{3,2,1,0:T(8,128)S(1)}, u32[]{:S(2)}, u32[]{:S(2)}) collective-permute-start(f32[2,12,16,128]{3,2,1,0:T(8,128)} %get-tuple-element.37), channel_id=1, source_target_pairs={{0,4},{1,5},{2,6},{3,7},{4,0},{5,1},{6,2},{7,3},{8,12},{9,13},{10,... | collective-permute-start | bytes 589832 | tf_op jit(solution)/shard_map/ppermute | solution.py:383
  27.2 2.3 %collective-permute-done.up_ref.refs_6_ = f32[28,16,128]{2,1,0:T(8,128)S(1)} collective-permute-done((f32[28,16,128]{2,1,0:T(8,128)}, f32[28,16,128]{2,1,0:T(8,128)S(1)}, u32[]{:S(2)}, u32[]{:S(2)}) %collective-permute-start) | collective-permute-done | bytes 229408 | tf_op jit(solution)/shard_map/ppermute | solution.py:374
  29.6 2.1 %collective-permute-done.1.down_ref.refs_7_ = f32[28,16,128]{2,1,0:T(8,128)S(1)} collective-permute-done((f32[28,16,128]{2,1,0:T(8,128)}, f32[28,16,128]{2,1,0:T(8,128)S(1)}, u32[]{:S(2)}, u32[]{:S(2)}) %collective-permute-start.1) | collective-permute-done | bytes 229408 | tf_op jit(solution)/shard_map/ppermute | solution.py:374
  31.6 2.6 %all-to-all-done.chunk_ref = f32[32,16,128]{2,1,0:T(8,128)S(1)} async-done(((f32[32,16,128]{2,1,0:T(8,128)}), f32[32,16,128]{2,1,0:T(8,128)S(1)}, u32[]{:S(2)}, u32[]{:S(2)}) %all-to-all-start) | async-done | bytes 262176 | tf_op jit(solution)/shard_map/all_to_all | solution.py:379
  34.3 4.4 %shard_map.124 = (s32[24,128]{1,0:T(8,128)S(1)}, f32[24,128]{1,0:T(8,128)S(1)}, f32[8,12,384]{2,1,0:T(8,128)}) custom-call(s32[1]{0:T(128)} %bitcast.p_ref.refs_0_, f32[32,16,128]{2,1,0:T(8,128)S(1)} %all-to-all-done.chunk_ref, f32[28,16,128]{2,1,0:T(8,128)S(1)} %collective-permute-done.up_ref.refs_6_, ...), custom_call_target="tpu_custom_call" | custom-call | tf_op jit(solution)/shard_map/pallas_call | solution.py:363
  38.6 4.3 %all-to-all-start.1 = ((f32[8,12,384]{2,1,0:T(8,128)}), f32[8,12,384]{2,1,0:T(8,128)S(1)}, u32[]{:S(2)}, u32[]{:S(2)}) async-start(f32[8,12,384]{2,1,0:T(8,128)} %get-tuple-element.36), calls=%async_computation.1 | async-start | bytes 393216 | tf_op jit(solution)/shard_map/all_to_all | solution.py:387
  43.0 3.9 %shard_map.125 = (f32[2,12,16,128]{3,2,1,0:T(8,128)S(1)}, f32[2,12,16,128]{3,2,1,0:T(8,128)}, f32[2,12,16,128]{3,2,1,0:T(8,128)}, f32[2,12,16,128]{3,2,1,0:T(8,128)S(1)}) custom-call(s32[1]{0:T(128)} %bitcast.1.me_ref, f32[16,16]{1,0:T(8,128)S(1)} %copy-done.8, f32[4,12,16,128]{3,2,1,0:T(8,128)S(1)} %copy-done.2, ...), custom_call_target="tpu_custom_call" | custom-call | tf_op jit(solution)/shard_map/pallas_call | solution.py:363
  46.9 1.5 %collective-permute-start.6 = (f32[2,12,16,128]{3,2,1,0:T(8,128)}, f32[2,12,16,128]{3,2,1,0:T(8,128)S(1)}, u32[]{:S(2)}, u32[]{:S(2)}) collective-permute-start(f32[2,12,16,128]{3,2,1,0:T(8,128)} %get-tuple-element.40), channel_id=1, source_target_pairs={{0,2},{1,3},{2,0},{3,1},{4,6},{5,7},{6,4},{7,5},{8,10},{9,11},{10,... | collective-permute-start | bytes 589832 | tf_op jit(solution)/shard_map/ppermute | solution.py:383
  48.4 2.4 %collective-permute-start.7 = (f32[2,12,16,128]{3,2,1,0:T(8,128)}, f32[2,12,16,128]{3,2,1,0:T(8,128)S(1)}, u32[]{:S(2)}, u32[]{:S(2)}) collective-permute-start(f32[2,12,16,128]{3,2,1,0:T(8,128)} %get-tuple-element.41), channel_id=1, source_target_pairs={{0,4},{1,5},{2,6},{3,7},{4,0},{5,1},{6,2},{7,3},{8,12},{9,13},{10,... | collective-permute-start | bytes 589832 | tf_op jit(solution)/shard_map/ppermute | solution.py:383
  51.8 4.8 %all-to-all-start.2 = ((f32[8,12,384]{2,1,0:T(8,128)}), f32[8,12,384]{2,1,0:T(8,128)S(1)}, u32[]{:S(2)}, u32[]{:S(2)}) async-start(f32[8,12,384]{2,1,0:T(8,128)} %shard_map.126), calls=%async_computation.2 | async-start | bytes 393216 | tf_op jit(solution)/shard_map/all_to_all | solution.py:387
  56.6 1.2 %collective-permute-done.7.after2.y2_ref = f32[2,12,16,128]{3,2,1,0:T(8,128)S(1)} collective-permute-done((f32[2,12,16,128]{3,2,1,0:T(8,128)}, f32[2,12,16,128]{3,2,1,0:T(8,128)S(1)}, u32[]{:S(2)}, u32[]{:S(2)}) %collective-permute-start.7) | collective-permute-done | bytes 196640 | tf_op jit(solution)/shard_map/ppermute | solution.py:383
  57.8 3.4 %collective-permute-done.8.after3.y3_ref = f32[2,12,16,128]{3,2,1,0:T(8,128)S(1)} collective-permute-done((f32[2,12,16,128]{3,2,1,0:T(8,128)S(1)}, f32[2,12,16,128]{3,2,1,0:T(8,128)S(1)}, u32[]{:S(2)}, u32[]{:S(2)}) %collective-permute-start.8) | collective-permute-done | bytes 196640 | tf_op jit(solution)/shard_map/ppermute | solution.py:383
  62.0 1.5 %collective-permute-start.11 = (f32[4,12,16,128]{3,2,1,0:T(8,128)}, f32[4,12,16,128]{3,2,1,0:T(8,128)S(1)}, u32[]{:S(2)}, u32[]{:S(2)}) collective-permute-start(f32[4,12,16,128]{3,2,1,0:T(8,128)} %shard_map.129), channel_id=1, source_target_pairs={{0,1},{1,0},{2,3},{3,2},{4,5},{5,4},{6,7},{7,6},{8,9},{9,8},{10,11... | collective-permute-start | bytes 1179656 | tf_op jit(solution)/shard_map/ppermute | solution.py:383
  64.4 10.1 %all-to-all-start.3 = ((f32[32,12,128]{2,1,0:T(8,128)}), f32[32,12,128]{2,1,0:T(8,128)S(1)}, u32[]{:S(2)}, u32[]{:S(2)}) async-start(f32[32,12,128]{2,1,0:T(8,128)} %get-tuple-element.43), calls=%async_computation.3 | async-start | bytes 524288 | tf_op jit(solution)/shard_map/all_to_all | solution.py:379
  74.7 1.5 %collective-permute-start.9 = (f32[2,12,128]{2,1,0:T(8,128)S(1)}, f32[2,12,128]{2,1,0:T(8,128)S(1)}, u32[]{:S(2)}, u32[]{:S(2)}) collective-permute-start(f32[2,12,128]{2,1,0:T(8,128)S(1)} %get-tuple-element.44), channel_id=1, source_target_pairs={{0,8},{8,16},{16,24},{24,32},{32,40},{40,48},{48,56},{56,64},{64,7... | collective-permute-start | bytes 36872 | tf_op jit(solution)/shard_map/ppermute | solution.py:374
  76.3 1.6 %shard_map.128 = (f32[12,4,32,128]{3,2,1,0:T(8,128)S(1)}, f32[4,32,128]{2,1,0:T(8,128)S(1)}) custom-call(s32[1]{0:T(128)} %bitcast.p_ref.refs_0_, f32[16,4]{1,0:T(8,128)S(1)} %copy.13.refs_1_, s32[4,32,128]{2,1,0:T(8,128)S(1)} %copy-done.4, f32[6,4,32,128]{3,2,1,0:T(8,128)S(1)} %bitcast.13, f32[6,4,32,128]{3,2,1,0:T(8,128)S(1)} %bitcast.16, ...), custom_call_target="tpu_custom_call" | custom-call | tf_op jit(solution)/shard_map/pallas_call | solution.py:363
  78.0 4.3 %shard_map.130.part_ref = f32[12,4,32,128]{3,2,1,0:T(8,128)S(1)} custom-call(s32[1]{0:T(128)} %bitcast.1.me_ref, s32[24,128]{1,0:T(8,128)S(1)} %get-tuple-element.47.idx_ref, f32[8,12,384]{2,1,0:T(8,128)S(1)} %all-to-all-done.2.force_ref, f32[12,4,32,128]{3,2,1,0:T(8,128)S(1)} %get-tuple-element.48.lin_ref, f32[4,32,128]{2,1,0:T(8,128)S(1)} %get-tuple-element.49.mass_ref, ...), custom_call_target="tpu_custom_call" | custom-call | tf_op jit(solution)/shard_map/pallas_call | solution.py:363
  82.9 4.9 %all-to-all-done.3.chunk_ref = f32[32,12,128]{2,1,0:T(8,128)S(1)} async-done(((f32[32,12,128]{2,1,0:T(8,128)}), f32[32,12,128]{2,1,0:T(8,128)S(1)}, u32[]{:S(2)}, u32[]{:S(2)}) %all-to-all-start.3) | async-done | bytes 196640 | tf_op jit(solution)/shard_map/all_to_all | solution.py:379
  87.8 5.1 %shard_map.131 = (f32[6,4,32,128]{3,2,1,0:T(8,128)}, f32[6,4,32,128]{3,2,1,0:T(8,128)}) custom-call(s32[1]{0:T(128)} %bitcast.p_ref.refs_0_, s32[24,128]{1,0:T(8,128)S(1)} %copy-done.7, f32[32,12,128]{2,1,0:T(8,128)S(1)} %all-to-all-done.3.chunk_ref, f32[2,12,128]{2,1,0:T(8,128)S(1)} %collective-permute-done.9.up_ref, ...), custom_call_target="tpu_custom_call" | custom-call | tf_op jit(solution)/shard_map/pallas_call | solution.py:363
  (39 shorter events, 4.4 us)
Async XLA Ops:
  6.8 15.7 %copy-start.2 = (f32[4,12,16,128]{3,2,1,0:T(8,128)S(1)}, f32[4,12,16,128]{3,2,1,0:T(8,128)}, u32[]{:S(2)}) copy-start(f32[4,12,16,128]{3,2,1,0:T(8,128)} %get-tuple-element.32.same_ref) | copy-start | bytes 1179652
  6.8 15.7 %collective-permute-start.2 = (f32[4,12,16,128]{3,2,1,0:T(8,128)}, f32[4,12,16,128]{3,2,1,0:T(8,128)S(1)}, u32[]{:S(2)}, u32[]{:S(2)}) collective-permute-start(f32[4,12,16,128]{3,2,1,0:T(8,128)} %get-tuple-element.33), channel_id=1, source_target_pairs={{0,1},{1,0},{2,3},{3,2},{4,5},{5,4},{6,7},{7,6},{8,9},{9,8},{10,11... | collective-permute-start | bytes 1179656 | tf_op jit(solution)/shard_map/ppermute | solution.py:383
  8.9 25.3 %copy-start.6 = (f32[2,16,128]{2,1,0:T(8,128)S(1)}, f32[2,16,128]{2,1,0:T(8,128)}, u32[]{:S(2)}) copy-start(f32[2,16,128]{2,1,0:T(8,128)} %get-tuple-element.31.self_ref) | copy-start | bytes 49156
  8.9 25.3 %all-to-all-start = ((f32[32,16,128]{2,1,0:T(8,128)}), f32[32,16,128]{2,1,0:T(8,128)S(1)}, u32[]{:S(2)}, u32[]{:S(2)}) async-start(f32[32,16,128]{2,1,0:T(8,128)} %get-tuple-element.28), calls=%async_computation | async-start | bytes 524288 | tf_op jit(solution)/shard_map/all_to_all | solution.py:379
  20.8 8.7 %collective-permute-start = (f32[28,16,128]{2,1,0:T(8,128)}, f32[28,16,128]{2,1,0:T(8,128)S(1)}, u32[]{:S(2)}, u32[]{:S(2)}) collective-permute-start(f32[28,16,128]{2,1,0:T(8,128)} %get-tuple-element.29), channel_id=1, source_target_pairs={{0,8},{8,16},{16,24},{24,32},{32,40},{40,48},{48,56},{56,64},{64,7... | collective-permute-start | bytes 688136 | tf_op jit(solution)/shard_map/ppermute | solution.py:374
  22.5 9.1 %collective-permute-start.1 = (f32[28,16,128]{2,1,0:T(8,128)}, f32[28,16,128]{2,1,0:T(8,128)S(1)}, u32[]{:S(2)}, u32[]{:S(2)}) collective-permute-start(f32[28,16,128]{2,1,0:T(8,128)} %get-tuple-element.30), channel_id=1, source_target_pairs={{0,248},{8,0},{16,8},{24,16},{32,24},{40,32},{48,40},{56,48},{64,5... | collective-permute-start | bytes 688136 | tf_op jit(solution)/shard_map/ppermute | solution.py:374
  22.5 11.7 %copy-start = (f32[2,3,4,32,128]{4,3,2,1,0:T(8,128)S(1)}, f32[2,3,4,32,128]{4,3,2,1,0:T(8,128)}, u32[]{:S(2)}) copy-start(f32[2,3,4,32,128]{4,3,2,1,0:T(8,128)} %param.11) | copy-start | bytes 1179652
  22.6 11.7 %copy-start.1 = (f32[2,3,4,32,128]{4,3,2,1,0:T(8,128)S(1)}, f32[2,3,4,32,128]{4,3,2,1,0:T(8,128)}, u32[]{:S(2)}) copy-start(f32[2,3,4,32,128]{4,3,2,1,0:T(8,128)} %param.12) | copy-start | bytes 1179652
  23.3 19.7 %collective-permute-start.3 = (f32[2,12,16,128]{3,2,1,0:T(8,128)S(1)}, f32[2,12,16,128]{3,2,1,0:T(8,128)S(1)}, u32[]{:S(2)}, u32[]{:S(2)}) collective-permute-start(f32[2,12,16,128]{3,2,1,0:T(8,128)S(1)} %get-tuple-element.34.after_ref), channel_id=1, source_target_pairs={{0,2},{1,3},{2,0},{3,1},{4,6},{5,7},{6,4},{7,5},{8,10},{9,11},{10,... | collective-permute-start | bytes 589832 | tf_op jit(solution)/shard_map/ppermute | solution.py:383
  24.6 18.4 %collective-permute-start.4 = (f32[2,12,16,128]{3,2,1,0:T(8,128)}, f32[2,12,16,128]{3,2,1,0:T(8,128)S(1)}, u32[]{:S(2)}, u32[]{:S(2)}) collective-permute-start(f32[2,12,16,128]{3,2,1,0:T(8,128)} %get-tuple-element.37), channel_id=1, source_target_pairs={{0,4},{1,5},{2,6},{3,7},{4,0},{5,1},{6,2},{7,3},{8,12},{9,13},{10,... | collective-permute-start | bytes 589832 | tf_op jit(solution)/shard_map/ppermute | solution.py:383
  27.2 15.8 %collective-permute-start.5 = (f32[2,12,16,128]{3,2,1,0:T(8,128)S(1)}, f32[2,12,16,128]{3,2,1,0:T(8,128)S(1)}, u32[]{:S(2)}, u32[]{:S(2)}) collective-permute-start(f32[2,12,16,128]{3,2,1,0:T(8,128)S(1)} %get-tuple-element.38), channel_id=1, source_target_pairs={{0,6},{1,7},{2,4},{3,5},{4,2},{5,3},{6,0},{7,1},{8,14},{9,15},{10,... | collective-permute-start | bytes 589832 | tf_op jit(solution)/shard_map/ppermute | solution.py:383
  38.6 12.2 %all-to-all-start.1 = ((f32[8,12,384]{2,1,0:T(8,128)}), f32[8,12,384]{2,1,0:T(8,128)S(1)}, u32[]{:S(2)}, u32[]{:S(2)}) async-start(f32[8,12,384]{2,1,0:T(8,128)} %get-tuple-element.36), calls=%async_computation.1 | async-start | bytes 393216 | tf_op jit(solution)/shard_map/all_to_all | solution.py:387
  43.0 7.8 %copy-start.5 = (f32[48,48]{1,0:T(8,128)S(1)}, f32[48,48]{1,0:T(8,128)}, u32[]{:S(2)}) copy-start(f32[48,48]{1,0:T(8,128)} %constant.14.clone.spread_ref) | copy-start | bytes 27652
  46.9 9.7 %collective-permute-start.6 = (f32[2,12,16,128]{3,2,1,0:T(8,128)}, f32[2,12,16,128]{3,2,1,0:T(8,128)S(1)}, u32[]{:S(2)}, u32[]{:S(2)}) collective-permute-start(f32[2,12,16,128]{3,2,1,0:T(8,128)} %get-tuple-element.40), channel_id=1, source_target_pairs={{0,2},{1,3},{2,0},{3,1},{4,6},{5,7},{6,4},{7,5},{8,10},{9,11},{10,... | collective-permute-start | bytes 589832 | tf_op jit(solution)/shard_map/ppermute | solution.py:383
  48.4 9.4 %collective-permute-start.7 = (f32[2,12,16,128]{3,2,1,0:T(8,128)}, f32[2,12,16,128]{3,2,1,0:T(8,128)S(1)}, u32[]{:S(2)}, u32[]{:S(2)}) collective-permute-start(f32[2,12,16,128]{3,2,1,0:T(8,128)} %get-tuple-element.41), channel_id=1, source_target_pairs={{0,4},{1,5},{2,6},{3,7},{4,0},{5,1},{6,2},{7,3},{8,12},{9,13},{10,... | collective-permute-start | bytes 589832 | tf_op jit(solution)/shard_map/ppermute | solution.py:383
  50.8 10.4 %collective-permute-start.8 = (f32[2,12,16,128]{3,2,1,0:T(8,128)S(1)}, f32[2,12,16,128]{3,2,1,0:T(8,128)S(1)}, u32[]{:S(2)}, u32[]{:S(2)}) collective-permute-start(f32[2,12,16,128]{3,2,1,0:T(8,128)S(1)} %get-tuple-element.42), channel_id=1, source_target_pairs={{0,6},{1,7},{2,4},{3,5},{4,2},{5,3},{6,0},{7,1},{8,14},{9,15},{10,... | collective-permute-start | bytes 589832 | tf_op jit(solution)/shard_map/ppermute | solution.py:383
  51.8 11.8 %all-to-all-start.2 = ((f32[8,12,384]{2,1,0:T(8,128)}), f32[8,12,384]{2,1,0:T(8,128)S(1)}, u32[]{:S(2)}, u32[]{:S(2)}) async-start(f32[8,12,384]{2,1,0:T(8,128)} %shard_map.126), calls=%async_computation.2 | async-start | bytes 393216 | tf_op jit(solution)/shard_map/all_to_all | solution.py:387
  62.0 16.0 %collective-permute-start.11 = (f32[4,12,16,128]{3,2,1,0:T(8,128)}, f32[4,12,16,128]{3,2,1,0:T(8,128)S(1)}, u32[]{:S(2)}, u32[]{:S(2)}) collective-permute-start(f32[4,12,16,128]{3,2,1,0:T(8,128)} %shard_map.129), channel_id=1, source_target_pairs={{0,1},{1,0},{2,3},{3,2},{4,5},{5,4},{6,7},{7,6},{8,9},{9,8},{10,11... | collective-permute-start | bytes 1179656 | tf_op jit(solution)/shard_map/ppermute | solution.py:383
  64.4 12.0 %copy-start.3 = (f32[2,3,4,32,128]{4,3,2,1,0:T(8,128)S(1)}, f32[2,3,4,32,128]{4,3,2,1,0:T(8,128)}, u32[]{:S(2)}) copy-start(f32[2,3,4,32,128]{4,3,2,1,0:T(8,128)} %param.13) | copy-start | bytes 1179652
  64.4 12.0 %copy-start.4 = (s32[4,32,128]{2,1,0:T(8,128)S(1)}, s32[4,32,128]{2,1,0:T(8,128)}, u32[]{:S(2)}) copy-start(s32[4,32,128]{2,1,0:T(8,128)} %refs_2_.1) | copy-start | bytes 196612
  64.4 23.5 %all-to-all-start.3 = ((f32[32,12,128]{2,1,0:T(8,128)}), f32[32,12,128]{2,1,0:T(8,128)S(1)}, u32[]{:S(2)}, u32[]{:S(2)}) async-start(f32[32,12,128]{2,1,0:T(8,128)} %get-tuple-element.43), calls=%async_computation.3 | async-start | bytes 524288 | tf_op jit(solution)/shard_map/all_to_all | solution.py:379
  74.4 8.5 %collective-permute-start.10 = (f32[2,12,128]{2,1,0:T(8,128)S(1)}, f32[2,12,128]{2,1,0:T(8,128)S(1)}, u32[]{:S(2)}, u32[]{:S(2)}) collective-permute-start(f32[2,12,128]{2,1,0:T(8,128)S(1)} %get-tuple-element.45), channel_id=1, source_target_pairs={{0,248},{8,0},{16,8},{24,16},{32,24},{40,32},{48,40},{56,48},{64,5... | collective-permute-start | bytes 36872 | tf_op jit(solution)/shard_map/ppermute | solution.py:374
  74.7 8.2 %collective-permute-start.9 = (f32[2,12,128]{2,1,0:T(8,128)S(1)}, f32[2,12,128]{2,1,0:T(8,128)S(1)}, u32[]{:S(2)}, u32[]{:S(2)}) collective-permute-start(f32[2,12,128]{2,1,0:T(8,128)S(1)} %get-tuple-element.44), channel_id=1, source_target_pairs={{0,8},{8,16},{16,24},{24,32},{32,40},{40,48},{48,56},{56,64},{64,7... | collective-permute-start | bytes 36872 | tf_op jit(solution)/shard_map/ppermute | solution.py:374
  78.0 9.9 %copy-start.7 = (s32[24,128]{1,0:T(8,128)S(1)}, s32[24,128]{1,0:T(8,128)}, u32[]{:S(2)}) copy-start(s32[24,128]{1,0:T(8,128)} %get-tuple-element.27.idx_ref) | copy-start | bytes 36868
  (2 other events, 6.2 us)

commit v4 on v3

--- a/solution.py
+++ b/solution.py
@@ -101,27 +101,31 @@
     return pick, lax.broadcasted_iota(i32, (32, 256), 0) == ((idx >> 7) & 31)
 
 
-def split_fields(disp_ref, dir_ref, hi_ref, lo_ref):
+def split_fields(disp_ref, dir_ref, parts_ref):
     for field, ref in enumerate((disp_ref, dir_ref)):
         for x in range(4):
             value = ref[:, x].reshape(6 * 32, 128)
             hi = value.astype(bf16)
-            at = (slice(192 * field, 192 * (field + 1)), slice(128 * x, 128 * (x + 1)))
-            hi_ref[at] = hi
-            lo_ref[at] = (value - hi.astype(f32)).astype(bf16)
-
-
-def gather_rows(hi_ref, lo_ref, idx_ref, here_ref):
+            cols = slice(128 * x, 128 * (x + 1))
+            parts_ref[192 * field : 192 * (field + 1), cols] = hi
+            parts_ref[384 + 192 * field : 384 + 192 * (field + 1), cols] = (value - hi.astype(f32)).astype(bf16)
+
+
+def split_kernel(disp_ref, dir_ref, parts_ref):
+    split_fields(disp_ref, dir_ref, parts_ref)
+
+
+def gather_rows(parts_ref, idx_ref, here_ref):
     def step(k, carry):
         pick, in_y = picks(idx_ref, k)
-        rows = jnp.dot(hi_ref[...], pick, preferred_element_type=f32)
-        rows = rows + jnp.dot(lo_ref[...], pick, preferred_element_type=f32)
-        got = jnp.sum(jnp.where(in_y[None], rows.reshape(12, 32, 256), 0.0), axis=1)
+        rows = jnp.dot(parts_ref[...], pick, preferred_element_type=f32)
+        rows = (rows[:384] + rows[384:]).reshape(12, 32, 256)
+        got = jnp.sum(jnp.where(in_y[None], rows, 0.0), axis=1)
         here_ref[2 * k, 0:12, :] = got[:, :128]
         here_ref[2 * k + 1, 0:12, :] = got[:, 128:]
         return carry
 
-    lax.fori_loop(0, SIDE // 2, step, 0)
+    lax.fori_loop(0, SIDE // 2, step, 0, unroll=3)
 
 
 def scatter_rows(val_ref, idx_ref, sum_ref):
@@ -140,18 +144,31 @@
         sum_ref[...] = sum_ref[...] + got
         return carry
 
-    lax.fori_loop(0, SIDE // 2, step, 0)
+    lax.fori_loop(0, SIDE // 2, step, 0, unroll=3)
 
 
 def list_kernel(p_ref, me_ref, owner_hbm, local_hbm, remote_hbm, kind_hbm, disp_hbm, dir_hbm, ids_hbm,
-                idx_ref, chunk_ref, up_ref, down_ref, self_ref, same_ref, other_ref,
-                hi_ref, lo_ref, rows_ref, owner_ref, local_ref, remote_ref, kind_ref, disp_ref, dir_ref, ids_ref, sems):
+                idx_ref, chunk_ref, up_hbm, down_hbm, self_ref, same_hbm, other_hbm,
+                parts_ref, rows_ref, owner_ref, local_ref, remote_ref, kind_ref, disp_ref, dir_ref, ids_ref, near_ref,
+                sems, more_sems):
     p = p_ref[0]
     pairs = ((owner_hbm, owner_ref), (local_hbm, local_ref), (remote_hbm, remote_ref), (kind_hbm, kind_ref),
              (disp_hbm, disp_ref), (dir_hbm, dir_ref), (ids_hbm, ids_ref))
     copies = [pltpu.make_async_copy(a, b, sems.at[k]) for k, (a, b) in enumerate(pairs)]
     for copy in copies:
         copy.start()
+    moves = []
+    for field, hbm in enumerate((disp_hbm, dir_hbm)):
+        part = pl.ds(6 * field, 6)
+        for k in range(PARTS):
+            block = me_ref[0] ^ k
+            rows = pl.ds(pl.multiple_of(16 * (block & 1), 16), 16)
+            moves.append((hbm.at[:, block >> 1, rows, :], (same_hbm, other_hbm)[k % 2].at[k // 2, part]))
+        moves.append((hbm.at[:, 3], up_hbm.at[pl.ds(1 + 6 * field, 6)]))
+        moves.append((hbm.at[:, 0], down_hbm.at[pl.ds(1 + 6 * field, 6)]))
+    moves = [pltpu.make_async_copy(a, b, more_sems.at[k]) for k, (a, b) in enumerate(moves)]
+    for move in moves:
+        move.start()
     for copy in copies[:4]:
         copy.wait()
     mine, theirs, kind = slot_tables(p, owner_ref, local_ref, remote_ref, kind_ref)
@@ -162,43 +179,42 @@
         rows_ref[tile, 14:16, :] = jnp.zeros((2, 128), f32)
     for copy in copies[4:]:
         copy.wait()
-    split_fields(disp_ref, dir_ref, hi_ref, lo_ref)
-    for ref, x in ((up_ref, 3), (down_ref, 0)):
-        ref[2:14] = disp_ref[:, x].reshape(12, 16, 128)
-        ref[14:26] = dir_ref[:, x].reshape(12, 16, 128)
-        ref[26:28] = (ids_ref[x] + 1).astype(f32).reshape(2, 16, 128)
-    for k in range(PARTS):
-        block = me_ref[0] ^ k
-        rows = pl.ds(pl.multiple_of(16 * (block & 1), 16), 16)
-        out = (same_ref, other_ref)[k % 2].at[k // 2]
-        out[0:6] = disp_ref[:, block >> 1, rows, :]
-        out[6:12] = dir_ref[:, block >> 1, rows, :]
-    gather_rows(hi_ref, lo_ref, idx_ref, rows_ref)
+    split_fields(disp_ref, dir_ref, parts_ref)
+    near_ref[2] = (ids_ref[3] + 1).astype(f32)
+    near_ref[3] = (ids_ref[0] + 1).astype(f32)
+    gather_rows(parts_ref, idx_ref, rows_ref)
+    for k in range(2):
+        near_ref[k] = rows_ref[2 + 2 * k : 4 + 2 * k].reshape(32, 128)
+    ends = ((near_ref.at[0], up_hbm.at[0]), (near_ref.at[1], down_hbm.at[0]),
+            (near_ref.at[2], up_hbm.at[13]), (near_ref.at[3], down_hbm.at[13]))
+    ends = [pltpu.make_async_copy(a, b, sems.at[7 + k]) for k, (a, b) in enumerate(ends)]
+    for end in ends:
+        end.start()
     for d in (0, 1, SLABS - 1):
         chunk_ref[(p + d) & (SLABS - 1)] = jnp.zeros((16, 128), f32)
     for d in range(2, SLABS - 1):
         tile, seg = place(d)
         chunk_ref[(p + d) & (SLABS - 1)] = lane_roll(rows_ref[tile], -seg)
     self_ref[...] = rows_ref[0:2]
-    up_ref[0:2] = rows_ref[2:4]
-    down_ref[0:2] = rows_ref[4:6]
-
-
-def gap_kernel(p_ref, chunk_ref, up_ref, down_ref, self_ref, disp_ref, dir_ref, after_ref,
-               idx_ref, kind_ref, gap_ref, hi_ref, lo_ref, here_ref):
+    for move in moves + ends:
+        move.wait()
+
+
+def gap_kernel(p_ref, chunk_ref, up_ref, down_ref, self_ref, parts_ref, after_ref,
+               idx_ref, kind_ref, gap_ref, here_ref):
     p = p_ref[0]
-    split_fields(disp_ref, dir_ref, hi_ref, lo_ref)
 
     def asked(d):
         return chunk_ref[(p - d) & (SLABS - 1)]
 
-    tiles = [self_ref[0], self_ref[1], up_ref[0], up_ref[1], down_ref[0], down_ref[1], asked(2), asked(SLABS - 2)]
+    near = [ref[0, 16 * k : 16 * (k + 1), :] for ref in (up_ref, down_ref) for k in range(2)]
+    tiles = [self_ref[0], self_ref[1]] + near + [asked(2), asked(SLABS - 2)]
     tiles += merge_far(asked, 16, 0.0)
     beyond = lanes(1) >= 3 * SEG
     rows = [t[12:13] for t in tiles[:8]] + [jnp.where(beyond, -1.0, t[12:13]) for t in tiles[8:]]
     idx_ref[...] = jnp.concatenate(rows + [jnp.full((7, 128), -1.0, f32)], axis=0).astype(i32)
     kind_ref[...] = jnp.concatenate([t[13:14] for t in tiles] + [jnp.zeros((7, 128), f32)], axis=0)
-    gather_rows(hi_ref, lo_ref, idx_ref, here_ref)
+    gather_rows(parts_ref, idx_ref, here_ref)
     for tile in range(24):
         gap = tiles[tile][0:12] - here_ref[tile] if tile < 17 else jnp.zeros((12, 128), f32)
         gap_ref[tile // 3, :, 128 * (tile % 3) : 128 * (tile % 3 + 1)] = gap
@@ -289,25 +305,30 @@
         out_ref[k] = ref[1]
 
 
-def time_kernel(me_ref, table_ref, same_ref, other_ref, y1_ref, y2_ref, y3_ref, *outs):
+def time_kernel(me_ref, same_ref, other_ref, y1_ref, y2_ref, y3_ref, *refs):
+    outs, in_ref, out_ref = refs[:4], refs[4], refs[5]
     me = me_ref[0]
-    ins = [same_ref.at[0], other_ref.at[0]] + [ref.at[b] for ref in (y1_ref, y2_ref, y3_ref) for b in range(2)]
+    in_ref[0] = same_ref[0]
+    in_ref[1] = other_ref[0]
+    for k, ref in enumerate((y1_ref, y2_ref, y3_ref)):
+        in_ref[2 * k + 2 : 2 * k + 4] = ref[...]
+    at = [me ^ ((me + k) & (PARTS - 1)) for k in range(PARTS)]
+    count = 2 * PARTS
 
     def step(g, carry):
         field = g // 3
         row = 6 * field + (g - 3 * field)
-        x = [[ins[k][row + 3 * t] for t in range(2)] for k in range(PARTS)]
-        for k in range(PARTS):
-            for t in range(2):
-                acc = None
-                for j in range(PARTS):
-                    for s in range(2):
-                        term = x[j][s] * table_ref[2 * (me ^ k) + t, 2 * (me ^ j) + s]
-                        acc = term if acc is None else acc + term
-                outs[k // 2][k % 2, row + 3 * t] = acc
+        x = [in_ref[at[t // 2], row + 3 * (t % 2)] for t in range(count)]
+        for t in range(count):
+            acc = x[0] * float(MIXED[t, 0])
+            for s in range(1, count):
+                acc = acc + x[s] * float(MIXED[(t - s) % count, 0])
+            out_ref[at[t // 2], row + 3 * (t % 2)] = acc
         return carry
 
     lax.fori_loop(0, 6, step, 0)
+    for k, out in enumerate(outs):
+        out[...] = out_ref[2 * k : 2 * k + 2]
 
 
 def lookup(ids, mat_ref, column, count):
@@ -319,8 +340,8 @@
 
 def stiff_kernel(p_ref, mat_ref, ids_ref, disp_ref, dir_ref, forcing_ref, up_ref, down_ref, out_ref, mass_ref, *, materials):
     p = p_ref[0]
-    low = jnp.where(p > 0, up_ref[2:28], 0.0).reshape(13, 32, 128)
-    high = jnp.where(p < SLABS - 1, down_ref[2:28], 0.0).reshape(13, 32, 128)
+    low = jnp.where(p > 0, up_ref[1:14], 0.0)
+    high = jnp.where(p < SLABS - 1, down_ref[1:14], 0.0)
     ids = ids_ref[...]
     kx, ky, kz, mass = [lookup(ids, mat_ref, col, materials) for col in range(4)]
     mass_ref[...] = mass
@@ -354,17 +375,17 @@
             out_ref[6 * field + c] = out
 
 
-VMEM = 24 * 1024 * 1024
-
-
-def call(kernel, outs, *args, smem=(0,), away=(), scratch=(), limit=VMEM):
+VMEM = 16 * 1024 * 1024
+
+
+def call(kernel, outs, *args, smem=(0,), away=(), scratch=(), kept=(), limit=VMEM):
     spaces = [pltpu.SMEM if k in smem else pl.ANY if k in away else pltpu.VMEM for k in range(len(args))]
     specs = [pl.BlockSpec(memory_space=space) for space in spaces]
     return pl.pallas_call(
         kernel,
         out_shape=[jax.ShapeDtypeStruct(s, d) for s, d in outs],
         in_specs=specs,
-        out_specs=[pl.BlockSpec(memory_space=pltpu.VMEM) for _ in outs],
+        out_specs=[pl.BlockSpec(memory_space=pl.ANY if k in kept else pltpu.VMEM) for k in range(len(outs))],
         scratch_shapes=list(scratch),
         compiler_params=pltpu.CompilerParams(vmem_limit_bytes=limit),
     )(*args)
@@ -396,13 +417,14 @@
     count = joint_local.shape[0]
     p = lax.axis_index("mesh").astype(i32).reshape(1)
     me = lax.axis_index("inst").astype(i32).reshape(1)
-    split = [pltpu.VMEM((384, 512), bf16)] * 2
+    parts = (768, 512)
     index = ((24, 128), i32)
     half = ((4, 12, 16, 128), f32)
+    near = ((14, 32, 128), f32)
 
     own_idx, chunk, up, down, own, same, other = call(
         list_kernel,
-        [index, ((SLABS, 16, 128), f32), ((28, 16, 128), f32), ((28, 16, 128), f32), ((2, 16, 128), f32), half, half],
+        [index, ((SLABS, 16, 128), f32), near, near, ((2, 16, 128), f32), half, half],
         p,
         me,
         joint_owner.reshape(1, count),
@@ -415,11 +437,12 @@
         smem=(0, 1),
         away=range(2, 9),
         limit=60 * 1024 * 1024,
-        scratch=split
-        + [pltpu.VMEM((SIDE, 16, 128), f32)]
+        kept=(2, 3, 5, 6),
+        scratch=[pltpu.VMEM(parts, bf16), pltpu.VMEM((SIDE, 16, 128), f32)]
         + [pltpu.VMEM((1, count), i32)] * 4
         + [pltpu.VMEM(fields, f32)] * 2
-        + [pltpu.VMEM((4, 32, 128), i32), pltpu.SemaphoreType.DMA((7,))],
+        + [pltpu.VMEM((4, 32, 128), i32), pltpu.VMEM((4, 32, 128), f32)]
+        + [pltpu.SemaphoreType.DMA((11,)), pltpu.SemaphoreType.DMA((20,))],
     )
     chunk, up, down = exchange(chunk, up, down)
 
@@ -427,15 +450,17 @@
     other = swap(other, 1)
     joined = call(join_kernel, [pair] * 3, same, other, smem=())
     turned = [swap(x, 2 * k + 2) for k, x in enumerate(joined)]
-    inertia = call(time_kernel, [pair] * 4, me, jnp.asarray(MIXED), same, other, *turned, smem=(0, 1))
+    blocks = [pltpu.VMEM((PARTS, 12, 16, 128), f32)] * 2
+    inertia = call(time_kernel, [pair] * 4, me, same, other, *turned, scratch=blocks)
 
     part = ((PARTS, 12, 384), f32)
+    fields_parts = call(split_kernel, [(parts, bf16)], disp, dire, smem=())[0]
     far_idx, kind, gap = call(
         gap_kernel,
         [index, ((24, 128), f32), part],
-        p, chunk, up, down, own, disp, dire, joined[0],
-        away=(7,),
-        scratch=split + [pltpu.VMEM((SIDE, 12, 128), f32)],
+        p, chunk, up, down, own, fields_parts, joined[0],
+        away=(6,),
+        scratch=[pltpu.VMEM((SIDE, 12, 128), f32)],
     )
     force = call(
         force_kernel,

time: 93.5 us -> 122 us (1.30)
  Pallas kernels: 28.8 us -> 53.7 us
  local copies, waits for them, and re-layouts: 0.13 us -> 2.39 us
    pallas_call x10 -> x11, Pallas kernels: 28.8 us -> 53.7 us  [call(): pl.pallas_call(kernel, out_shape=[jax.ShapeDtypeStruct(s, d) for s, d in...]
    unnamed x21 -> x25, local copies, waits for them, and re-layouts: 0.13 us -> 2.39 us
  transfers between devices with their start and end apart: 16 -> 16, of which waited for: 7 -> 7; matrix products, arithmetic and copies ran while one was open for 0% -> 0% of each run, Pallas kernels for 19% -> 10%
where the time goes in v4:
time: 122 us; the launch traced here: 121 us
  Pallas kernels  53.7 us (44%)
  starting transfers between devices  46.5 us (38%)
  waiting for transfers between devices  18.2 us (15%)
  local copies, waits for them, and re-layouts  2.39 us (2%)
    pallas_call x11, Pallas kernels, call(): pl.pallas_call(kernel, out_shape=[jax.ShapeDtypeStruct(s, d) for s, d in...  53.7 us
    all_to_all x2, starting transfers between devices, exchange(): lax.all_to_all(chunk, 'mesh', split_axis=0, concat_axis=0, tiled=True)  22.4 us
    ppermute x8, starting transfers between devices, swap(): return lax.ppermute(x, 'inst', [(i, i ^ bit) for i in range(PARTS)])  11.4 us
    all_to_all x2, starting transfers between devices, inst_split(): return lax.all_to_all(x, 'inst', split_axis=0, concat_axis=0, tiled=True)  8.95 us
    all_to_all x2, waiting for transfers between devices, exchange(): lax.all_to_all(chunk, 'mesh', split_axis=0, concat_axis=0, tiled=True)  7.53 us
    ppermute x4, waiting for transfers between devices, shift(): lax.ppermute(x, 'mesh', [(i, (i + by) % SLABS) for i in range(SLABS)])  6.21 us
    ppermute x8, waiting for transfers between devices, swap(): return lax.ppermute(x, 'inst', [(i, i ^ bit) for i in range(PARTS)])  4.41 us
    ppermute x4, starting transfers between devices, shift(): lax.ppermute(x, 'mesh', [(i, (i + by) % SLABS) for i in range(SLABS)])  3.69 us
  transfers between devices with their start and end apart: 16, of which 7 were waited for; matrix products, arithmetic and copies ran while one was open for 0% of the time, Pallas kernels for 10%

profile of v4, /device:TPU:1, one launch (start us, length us, event | category | flops | bytes accessed | tf_op | source)
XLA Modules:
  0.0 121.5 jit_solution(10066948795525552859)
XLA Ops:
  0.6 37.9 %shard_map.113 = (s32[24,128]{1,0:T(8,128)}, f32[32,16,128]{2,1,0:T(8,128)}, f32[14,32,128]{2,1,0:T(8,128)}, f32[14,32,128]{2,1,0:T(8,128)}, f32[2,16,128]{2,1,0...) custom-call(s32[1]{0:T(128)} %bitcast.p_ref.refs_0_, s32[1]{0:T(128)} %bitcast.1.me_ref, ...), custom_call_target="tpu_custom_call" | custom-call | tf_op jit(solution)/shard_map/pallas_call | solution.py:384
  38.5 2.1 %collective-permute-start.2 = (f32[4,12,16,128]{3,2,1,0:T(8,128)}, f32[4,12,16,128]{3,2,1,0:T(8,128)S(1)}, u32[]{:S(2)}, u32[]{:S(2)}) collective-permute-start(f32[4,12,16,128]{3,2,1,0:T(8,128)} %get-tuple-element.33), channel_id=1, source_target_pairs={{0,1},{1,0},{2,3},{3,2},{4,5},{5,4},{6,7},{7,6},{8,9},{9,8},{10,11... | collective-permute-start | bytes 1179656 | tf_op jit(solution)/shard_map/ppermute | solution.py:404
  40.6 11.7 %all-to-all-start = ((f32[32,16,128]{2,1,0:T(8,128)}), f32[32,16,128]{2,1,0:T(8,128)S(1)}, u32[]{:S(2)}, u32[]{:S(2)}) async-start(f32[32,16,128]{2,1,0:T(8,128)} %get-tuple-element.28), calls=%async_computation | async-start | bytes 524288 | tf_op jit(solution)/shard_map/all_to_all | solution.py:400
  52.4 1.7 %collective-permute-start = (f32[14,32,128]{2,1,0:T(8,128)}, f32[14,32,128]{2,1,0:T(8,128)S(1)}, u32[]{:S(2)}, u32[]{:S(2)}) collective-permute-start(f32[14,32,128]{2,1,0:T(8,128)} %get-tuple-element.29), channel_id=1, source_target_pairs={{0,8},{8,16},{16,24},{24,32},{32,40},{40,48},{48,56},{56,64},{64,7... | collective-permute-start | bytes 688136 | tf_op jit(solution)/shard_map/ppermute | solution.py:395
  55.0 1.3 %collective-permute-start.3 = (f32[2,12,16,128]{3,2,1,0:T(8,128)}, f32[2,12,16,128]{3,2,1,0:T(8,128)S(1)}, u32[]{:S(2)}, u32[]{:S(2)}) collective-permute-start(f32[2,12,16,128]{3,2,1,0:T(8,128)} %get-tuple-element.34.after_ref), channel_id=1, source_target_pairs={{0,2},{1,3},{2,0},{3,1},{4,6},{5,7},{6,4},{7,5},{8,10},{9,11},{10,... | collective-permute-start | bytes 589832 | tf_op jit(solution)/shard_map/ppermute | solution.py:404
  56.3 2.6 %collective-permute-start.4 = (f32[2,12,16,128]{3,2,1,0:T(8,128)}, f32[2,12,16,128]{3,2,1,0:T(8,128)S(1)}, u32[]{:S(2)}, u32[]{:S(2)}) collective-permute-start(f32[2,12,16,128]{3,2,1,0:T(8,128)} %get-tuple-element.37), channel_id=1, source_target_pairs={{0,4},{1,5},{2,6},{3,7},{4,0},{5,1},{6,2},{7,3},{8,12},{9,13},{10,... | collective-permute-start | bytes 589832 | tf_op jit(solution)/shard_map/ppermute | solution.py:404
  59.1 2.1 %collective-permute-done.up_ref.refs_6_ = f32[14,32,128]{2,1,0:T(8,128)S(1)} collective-permute-done((f32[14,32,128]{2,1,0:T(8,128)}, f32[14,32,128]{2,1,0:T(8,128)S(1)}, u32[]{:S(2)}, u32[]{:S(2)}) %collective-permute-start) | collective-permute-done | bytes 229408 | tf_op jit(solution)/shard_map/ppermute | solution.py:395
  61.1 2.1 %collective-permute-done.1.down_ref.refs_7_ = f32[14,32,128]{2,1,0:T(8,128)S(1)} collective-permute-done((f32[14,32,128]{2,1,0:T(8,128)}, f32[14,32,128]{2,1,0:T(8,128)S(1)}, u32[]{:S(2)}, u32[]{:S(2)}) %collective-permute-start.1) | collective-permute-done | bytes 229408 | tf_op jit(solution)/shard_map/ppermute | solution.py:395
  63.2 2.6 %all-to-all-done.chunk_ref = f32[32,16,128]{2,1,0:T(8,128)S(1)} async-done(((f32[32,16,128]{2,1,0:T(8,128)}), f32[32,16,128]{2,1,0:T(8,128)S(1)}, u32[]{:S(2)}, u32[]{:S(2)}) %all-to-all-start) | async-done | bytes 262176 | tf_op jit(solution)/shard_map/all_to_all | solution.py:400
  65.8 2.5 %shard_map.116 = (s32[24,128]{1,0:T(8,128)S(1)}, f32[24,128]{1,0:T(8,128)S(1)}, f32[8,12,384]{2,1,0:T(8,128)S(1)}) custom-call(s32[1]{0:T(128)} %bitcast.p_ref.refs_0_, f32[32,16,128]{2,1,0:T(8,128)S(1)} %all-to-all-done.chunk_ref, f32[14,32,128]{2,1,0:T(8,128)S(1)} %collective-permute-done.up_ref.refs_6_, ...), custom_call_target="tpu_custom_call" | custom-call | tf_op jit(solution)/shard_map/pallas_call | solution.py:384
  69.0 4.2 %all-to-all-start.1 = ((f32[8,12,384]{2,1,0:T(8,128)}), f32[8,12,384]{2,1,0:T(8,128)S(1)}, u32[]{:S(2)}, u32[]{:S(2)}) async-start(f32[8,12,384]{2,1,0:T(8,128)} %copy-done.7), calls=%async_computation.1 | async-start | bytes 393216 | tf_op jit(solution)/shard_map/all_to_all | solution.py:408
  74.8 2.0 %shard_map.117 = (f32[2,12,16,128]{3,2,1,0:T(8,128)S(1)}, f32[2,12,16,128]{3,2,1,0:T(8,128)S(1)}, f32[2,12,16,128]{3,2,1,0:T(8,128)S(1)}, f32[2,12,16,128]{3,2,1,0:T(8,128)S(1)}) custom-call(s32[1]{0:T(128)} %bitcast.1.me_ref, f32[4,12,16,128]{3,2,1,0:T(8,128)S(1)} %copy-done.2, f32[4,12,16,128]{3,2,1,0:T(8,128)S(1)} %collective-permute-done.2.other_ref, ...), custom_call_target="tpu_custom_call" | custom-call | tf_op jit(solution)/shard_map/pallas_call | solution.py:384
  76.8 1.5 %collective-permute-start.6 = (f32[2,12,16,128]{3,2,1,0:T(8,128)S(1)}, f32[2,12,16,128]{3,2,1,0:T(8,128)S(1)}, u32[]{:S(2)}, u32[]{:S(2)}) collective-permute-start(f32[2,12,16,128]{3,2,1,0:T(8,128)S(1)} %get-tuple-element.40), channel_id=1, source_target_pairs={{0,2},{1,3},{2,0},{3,1},{4,6},{5,7},{6,4},{7,5},{8,10},{9,11},{10,... | collective-permute-start | bytes 589832 | tf_op jit(solution)/shard_map/ppermute | solution.py:404
  78.3 2.4 %collective-permute-start.7 = (f32[2,12,16,128]{3,2,1,0:T(8,128)S(1)}, f32[2,12,16,128]{3,2,1,0:T(8,128)S(1)}, u32[]{:S(2)}, u32[]{:S(2)}) collective-permute-start(f32[2,12,16,128]{3,2,1,0:T(8,128)S(1)} %get-tuple-element.41), channel_id=1, source_target_pairs={{0,4},{1,5},{2,6},{3,7},{4,0},{5,1},{6,2},{7,3},{8,12},{9,13},{10,... | collective-permute-start | bytes 589832 | tf_op jit(solution)/shard_map/ppermute | solution.py:404
  81.8 4.8 %all-to-all-start.2 = ((f32[8,12,384]{2,1,0:T(8,128)}), f32[8,12,384]{2,1,0:T(8,128)S(1)}, u32[]{:S(2)}, u32[]{:S(2)}) async-start(f32[8,12,384]{2,1,0:T(8,128)} %shard_map.118), calls=%async_computation.2 | async-start | bytes 393216 | tf_op jit(solution)/shard_map/all_to_all | solution.py:408
  87.5 3.4 %collective-permute-done.8.after3.y3_ref = f32[2,12,16,128]{3,2,1,0:T(8,128)S(1)} collective-permute-done((f32[2,12,16,128]{3,2,1,0:T(8,128)S(1)}, f32[2,12,16,128]{3,2,1,0:T(8,128)S(1)}, u32[]{:S(2)}, u32[]{:S(2)}) %collective-permute-start.8) | collective-permute-done | bytes 196640 | tf_op jit(solution)/shard_map/ppermute | solution.py:404
  91.7 1.3 %collective-permute-start.11 = (f32[4,12,16,128]{3,2,1,0:T(8,128)}, f32[4,12,16,128]{3,2,1,0:T(8,128)S(1)}, u32[]{:S(2)}, u32[]{:S(2)}) collective-permute-start(f32[4,12,16,128]{3,2,1,0:T(8,128)} %shard_map.121), channel_id=1, source_target_pairs={{0,1},{1,0},{2,3},{3,2},{4,5},{5,4},{6,7},{7,6},{8,9},{9,8},{10,11... | collective-permute-start | bytes 1179656 | tf_op jit(solution)/shard_map/ppermute | solution.py:404
  93.9 10.7 %all-to-all-start.3 = ((f32[32,12,128]{2,1,0:T(8,128)}), f32[32,12,128]{2,1,0:T(8,128)S(1)}, u32[]{:S(2)}, u32[]{:S(2)}) async-start(f32[32,12,128]{2,1,0:T(8,128)} %get-tuple-element.43), calls=%async_computation.3 | async-start | bytes 524288 | tf_op jit(solution)/shard_map/all_to_all | solution.py:400
  104.9 1.7 %collective-permute-start.9 = (f32[2,12,128]{2,1,0:T(8,128)S(1)}, f32[2,12,128]{2,1,0:T(8,128)S(1)}, u32[]{:S(2)}, u32[]{:S(2)}) collective-permute-start(f32[2,12,128]{2,1,0:T(8,128)S(1)} %get-tuple-element.44), channel_id=1, source_target_pairs={{0,8},{8,16},{16,24},{24,32},{32,40},{40,48},{48,56},{56,64},{64,7... | collective-permute-start | bytes 36872 | tf_op jit(solution)/shard_map/ppermute | solution.py:395
  106.6 1.6 %shard_map.120 = (f32[12,4,32,128]{3,2,1,0:T(8,128)S(1)}, f32[4,32,128]{2,1,0:T(8,128)S(1)}) custom-call(s32[1]{0:T(128)} %bitcast.p_ref.refs_0_, f32[16,4]{1,0:T(8,128)S(1)} %copy.12.refs_1_, s32[4,32,128]{2,1,0:T(8,128)S(1)} %copy-done.4, f32[6,4,32,128]{3,2,1,0:T(8,128)S(1)} %bitcast.13, f32[6,4,32,128]{3,2,1,0:T(8,128)S(1)} %bitcast.16, ...), custom_call_target="tpu_custom_call" | custom-call | tf_op jit(solution)/shard_map/pallas_call | solution.py:384
  108.3 2.7 %shard_map.122.part_ref = f32[12,4,32,128]{3,2,1,0:T(8,128)S(1)} custom-call(s32[1]{0:T(128)} %bitcast.1.me_ref, s32[24,128]{1,0:T(8,128)S(1)} %get-tuple-element.47.idx_ref, f32[8,12,384]{2,1,0:T(8,128)S(1)} %all-to-all-done.2.force_ref, f32[12,4,32,128]{3,2,1,0:T(8,128)S(1)} %get-tuple-element.48.lin_ref, f32[4,32,128]{2,1,0:T(8,128)S(1)} %get-tuple-element.49.mass_ref, ...), custom_call_target="tpu_custom_call" | custom-call | tf_op jit(solution)/shard_map/pallas_call | solution.py:384
  111.0 2.1 %collective-permute-done.10.down_ref = f32[2,12,128]{2,1,0:T(8,128)S(1)} collective-permute-done((f32[2,12,128]{2,1,0:T(8,128)S(1)}, f32[2,12,128]{2,1,0:T(8,128)S(1)}, u32[]{:S(2)}, u32[]{:S(2)}) %collective-permute-start.10) | collective-permute-done | bytes 12320 | tf_op jit(solution)/shard_map/ppermute | solution.py:395
  113.1 4.9 %all-to-all-done.3.chunk_ref = f32[32,12,128]{2,1,0:T(8,128)S(1)} async-done(((f32[32,12,128]{2,1,0:T(8,128)}), f32[32,12,128]{2,1,0:T(8,128)S(1)}, u32[]{:S(2)}, u32[]{:S(2)}) %all-to-all-start.3) | async-done | bytes 196640 | tf_op jit(solution)/shard_map/all_to_all | solution.py:400
  118.0 3.5 %shard_map.123 = (f32[6,4,32,128]{3,2,1,0:T(8,128)}, f32[6,4,32,128]{3,2,1,0:T(8,128)}) custom-call(s32[1]{0:T(128)} %bitcast.p_ref.refs_0_, s32[24,128]{1,0:T(8,128)S(1)} %copy-done.10, f32[32,12,128]{2,1,0:T(8,128)S(1)} %all-to-all-done.3.chunk_ref, f32[2,12,128]{2,1,0:T(8,128)S(1)} %collective-permute-done.9.up_ref, ...), custom_call_target="tpu_custom_call" | custom-call | tf_op jit(solution)/shard_map/pallas_call | solution.py:384
  (44 shorter events, 7.3 us)
Async XLA Ops:
  38.5 15.6 %copy-start.2 = (f32[4,12,16,128]{3,2,1,0:T(8,128)S(1)}, f32[4,12,16,128]{3,2,1,0:T(8,128)}, u32[]{:S(2)}) copy-start(f32[4,12,16,128]{3,2,1,0:T(8,128)} %get-tuple-element.32.same_ref) | copy-start | bytes 1179652
  38.5 15.6 %collective-permute-start.2 = (f32[4,12,16,128]{3,2,1,0:T(8,128)}, f32[4,12,16,128]{3,2,1,0:T(8,128)S(1)}, u32[]{:S(2)}, u32[]{:S(2)}) collective-permute-start(f32[4,12,16,128]{3,2,1,0:T(8,128)} %get-tuple-element.33), channel_id=1, source_target_pairs={{0,1},{1,0},{2,3},{3,2},{4,5},{5,4},{6,7},{7,6},{8,9},{9,8},{10,11... | collective-permute-start | bytes 1179656 | tf_op jit(solution)/shard_map/ppermute | solution.py:404
  40.6 25.2 %all-to-all-start = ((f32[32,16,128]{2,1,0:T(8,128)}), f32[32,16,128]{2,1,0:T(8,128)S(1)}, u32[]{:S(2)}, u32[]{:S(2)}) async-start(f32[32,16,128]{2,1,0:T(8,128)} %get-tuple-element.28), calls=%async_computation | async-start | bytes 524288 | tf_op jit(solution)/shard_map/all_to_all | solution.py:400
  52.4 8.7 %collective-permute-start = (f32[14,32,128]{2,1,0:T(8,128)}, f32[14,32,128]{2,1,0:T(8,128)S(1)}, u32[]{:S(2)}, u32[]{:S(2)}) collective-permute-start(f32[14,32,128]{2,1,0:T(8,128)} %get-tuple-element.29), channel_id=1, source_target_pairs={{0,8},{8,16},{16,24},{24,32},{32,40},{40,48},{48,56},{56,64},{64,7... | collective-permute-start | bytes 688136 | tf_op jit(solution)/shard_map/ppermute | solution.py:395
  54.1 9.1 %collective-permute-start.1 = (f32[14,32,128]{2,1,0:T(8,128)}, f32[14,32,128]{2,1,0:T(8,128)S(1)}, u32[]{:S(2)}, u32[]{:S(2)}) collective-permute-start(f32[14,32,128]{2,1,0:T(8,128)} %get-tuple-element.30), channel_id=1, source_target_pairs={{0,248},{8,0},{16,8},{24,16},{32,24},{40,32},{48,40},{56,48},{64,5... | collective-permute-start | bytes 688136 | tf_op jit(solution)/shard_map/ppermute | solution.py:395
  54.1 4.8 %copy-start = (f32[2,3,4,32,128]{4,3,2,1,0:T(8,128)S(1)}, f32[2,3,4,32,128]{4,3,2,1,0:T(8,128)}, u32[]{:S(2)}) copy-start(f32[2,3,4,32,128]{4,3,2,1,0:T(8,128)} %param.10) | copy-start | bytes 1179652
  54.1 4.8 %copy-start.1 = (f32[2,3,4,32,128]{4,3,2,1,0:T(8,128)S(1)}, f32[2,3,4,32,128]{4,3,2,1,0:T(8,128)}, u32[]{:S(2)}) copy-start(f32[2,3,4,32,128]{4,3,2,1,0:T(8,128)} %param.11) | copy-start | bytes 1179652
  55.0 18.2 %collective-permute-start.3 = (f32[2,12,16,128]{3,2,1,0:T(8,128)}, f32[2,12,16,128]{3,2,1,0:T(8,128)S(1)}, u32[]{:S(2)}, u32[]{:S(2)}) collective-permute-start(f32[2,12,16,128]{3,2,1,0:T(8,128)} %get-tuple-element.34.after_ref), channel_id=1, source_target_pairs={{0,2},{1,3},{2,0},{3,1},{4,6},{5,7},{6,4},{7,5},{8,10},{9,11},{10,... | collective-permute-start | bytes 589832 | tf_op jit(solution)/shard_map/ppermute | solution.py:404
  56.3 16.9 %collective-permute-start.4 = (f32[2,12,16,128]{3,2,1,0:T(8,128)}, f32[2,12,16,128]{3,2,1,0:T(8,128)S(1)}, u32[]{:S(2)}, u32[]{:S(2)}) collective-permute-start(f32[2,12,16,128]{3,2,1,0:T(8,128)} %get-tuple-element.37), channel_id=1, source_target_pairs={{0,4},{1,5},{2,6},{3,7},{4,0},{5,1},{6,2},{7,3},{8,12},{9,13},{10,... | collective-permute-start | bytes 589832 | tf_op jit(solution)/shard_map/ppermute | solution.py:404
  58.9 6.9 %copy-start.9 = (f32[2,16,128]{2,1,0:T(8,128)S(1)}, f32[2,16,128]{2,1,0:T(8,128)}, u32[]{:S(2)}) copy-start(f32[2,16,128]{2,1,0:T(8,128)} %get-tuple-element.31.self_ref) | copy-start | bytes 49156
  58.9 15.0 %collective-permute-start.5 = (f32[2,12,16,128]{3,2,1,0:T(8,128)}, f32[2,12,16,128]{3,2,1,0:T(8,128)}, u32[]{:S(2)}, u32[]{:S(2)}) collective-permute-start(f32[2,12,16,128]{3,2,1,0:T(8,128)} %get-tuple-element.38), channel_id=1, source_target_pairs={{0,6},{1,7},{2,4},{3,5},{4,2},{5,3},{6,0},{7,1},{8,14},{9,15},{10,... | collective-permute-start | bytes 589832 | tf_op jit(solution)/shard_map/ppermute | solution.py:404
  69.0 11.8 %all-to-all-start.1 = ((f32[8,12,384]{2,1,0:T(8,128)}), f32[8,12,384]{2,1,0:T(8,128)S(1)}, u32[]{:S(2)}, u32[]{:S(2)}) async-start(f32[8,12,384]{2,1,0:T(8,128)} %copy-done.7), calls=%async_computation.1 | async-start | bytes 393216 | tf_op jit(solution)/shard_map/all_to_all | solution.py:408
  74.8 6.0 %copy-start.8 = (f32[48,48]{1,0:T(8,128)S(1)}, f32[48,48]{1,0:T(8,128)}, u32[]{:S(2)}) copy-start(f32[48,48]{1,0:T(8,128)} %constant.11.clone.spread_ref) | copy-start | bytes 27652
  76.8 9.8 %collective-permute-start.6 = (f32[2,12,16,128]{3,2,1,0:T(8,128)S(1)}, f32[2,12,16,128]{3,2,1,0:T(8,128)S(1)}, u32[]{:S(2)}, u32[]{:S(2)}) collective-permute-start(f32[2,12,16,128]{3,2,1,0:T(8,128)S(1)} %get-tuple-element.40), channel_id=1, source_target_pairs={{0,2},{1,3},{2,0},{3,1},{4,6},{5,7},{6,4},{7,5},{8,10},{9,11},{10,... | collective-permute-start | bytes 589832 | tf_op jit(solution)/shard_map/ppermute | solution.py:404
  78.3 9.2 %collective-permute-start.7 = (f32[2,12,16,128]{3,2,1,0:T(8,128)S(1)}, f32[2,12,16,128]{3,2,1,0:T(8,128)S(1)}, u32[]{:S(2)}, u32[]{:S(2)}) collective-permute-start(f32[2,12,16,128]{3,2,1,0:T(8,128)S(1)} %get-tuple-element.41), channel_id=1, source_target_pairs={{0,4},{1,5},{2,6},{3,7},{4,0},{5,1},{6,2},{7,3},{8,12},{9,13},{10,... | collective-permute-start | bytes 589832 | tf_op jit(solution)/shard_map/ppermute | solution.py:404
  80.7 10.2 %collective-permute-start.8 = (f32[2,12,16,128]{3,2,1,0:T(8,128)S(1)}, f32[2,12,16,128]{3,2,1,0:T(8,128)S(1)}, u32[]{:S(2)}, u32[]{:S(2)}) collective-permute-start(f32[2,12,16,128]{3,2,1,0:T(8,128)S(1)} %get-tuple-element.42), channel_id=1, source_target_pairs={{0,6},{1,7},{2,4},{3,5},{4,2},{5,3},{6,0},{7,1},{8,14},{9,15},{10,... | collective-permute-start | bytes 589832 | tf_op jit(solution)/shard_map/ppermute | solution.py:404
  81.8 11.3 %all-to-all-start.2 = ((f32[8,12,384]{2,1,0:T(8,128)}), f32[8,12,384]{2,1,0:T(8,128)S(1)}, u32[]{:S(2)}, u32[]{:S(2)}) async-start(f32[8,12,384]{2,1,0:T(8,128)} %shard_map.118), calls=%async_computation.2 | async-start | bytes 393216 | tf_op jit(solution)/shard_map/all_to_all | solution.py:408
  91.7 16.5 %collective-permute-start.11 = (f32[4,12,16,128]{3,2,1,0:T(8,128)}, f32[4,12,16,128]{3,2,1,0:T(8,128)S(1)}, u32[]{:S(2)}, u32[]{:S(2)}) collective-permute-start(f32[4,12,16,128]{3,2,1,0:T(8,128)} %shard_map.121), channel_id=1, source_target_pairs={{0,1},{1,0},{2,3},{3,2},{4,5},{5,4},{6,7},{7,6},{8,9},{9,8},{10,11... | collective-permute-start | bytes 1179656 | tf_op jit(solution)/shard_map/ppermute | solution.py:404
  93.9 12.8 %copy-start.3 = (f32[2,3,4,32,128]{4,3,2,1,0:T(8,128)S(1)}, f32[2,3,4,32,128]{4,3,2,1,0:T(8,128)}, u32[]{:S(2)}) copy-start(f32[2,3,4,32,128]{4,3,2,1,0:T(8,128)} %param.12) | copy-start | bytes 1179652
  93.9 12.8 %copy-start.4 = (s32[4,32,128]{2,1,0:T(8,128)S(1)}, s32[4,32,128]{2,1,0:T(8,128)}, u32[]{:S(2)}) copy-start(s32[4,32,128]{2,1,0:T(8,128)} %refs_2_.1) | copy-start | bytes 196612
  93.9 24.1 %all-to-all-start.3 = ((f32[32,12,128]{2,1,0:T(8,128)}), f32[32,12,128]{2,1,0:T(8,128)S(1)}, u32[]{:S(2)}, u32[]{:S(2)}) async-start(f32[32,12,128]{2,1,0:T(8,128)} %get-tuple-element.43), calls=%async_computation.3 | async-start | bytes 524288 | tf_op jit(solution)/shard_map/all_to_all | solution.py:400
  104.6 8.5 %collective-permute-start.10 = (f32[2,12,128]{2,1,0:T(8,128)S(1)}, f32[2,12,128]{2,1,0:T(8,128)S(1)}, u32[]{:S(2)}, u32[]{:S(2)}) collective-permute-start(f32[2,12,128]{2,1,0:T(8,128)S(1)} %get-tuple-element.45), channel_id=1, source_target_pairs={{0,248},{8,0},{16,8},{24,16},{32,24},{40,32},{48,40},{56,48},{64,5... | collective-permute-start | bytes 36872 | tf_op jit(solution)/shard_map/ppermute | solution.py:395
  104.9 8.2 %collective-permute-start.9 = (f32[2,12,128]{2,1,0:T(8,128)S(1)}, f32[2,12,128]{2,1,0:T(8,128)S(1)}, u32[]{:S(2)}, u32[]{:S(2)}) collective-permute-start(f32[2,12,128]{2,1,0:T(8,128)S(1)} %get-tuple-element.44), channel_id=1, source_target_pairs={{0,8},{8,16},{16,24},{24,32},{32,40},{40,48},{48,56},{56,64},{64,7... | collective-permute-start | bytes 36872 | tf_op jit(solution)/shard_map/ppermute | solution.py:395
  108.3 9.7 %copy-start.10 = (s32[24,128]{1,0:T(8,128)S(1)}, s32[24,128]{1,0:T(8,128)}, u32[]{:S(2)}) copy-start(s32[24,128]{1,0:T(8,128)} %get-tuple-element.27.idx_ref) | copy-start | bytes 36868
  (4 other events, 4.3 us)

commit v5 on v4

--- a/solution.py
+++ b/solution.py
@@ -157,18 +157,6 @@
     copies = [pltpu.make_async_copy(a, b, sems.at[k]) for k, (a, b) in enumerate(pairs)]
     for copy in copies:
         copy.start()
-    moves = []
-    for field, hbm in enumerate((disp_hbm, dir_hbm)):
-        part = pl.ds(6 * field, 6)
-        for k in range(PARTS):
-            block = me_ref[0] ^ k
-            rows = pl.ds(pl.multiple_of(16 * (block & 1), 16), 16)
-            moves.append((hbm.at[:, block >> 1, rows, :], (same_hbm, other_hbm)[k % 2].at[k // 2, part]))
-        moves.append((hbm.at[:, 3], up_hbm.at[pl.ds(1 + 6 * field, 6)]))
-        moves.append((hbm.at[:, 0], down_hbm.at[pl.ds(1 + 6 * field, 6)]))
-    moves = [pltpu.make_async_copy(a, b, more_sems.at[k]) for k, (a, b) in enumerate(moves)]
-    for move in moves:
-        move.start()
     for copy in copies[:4]:
         copy.wait()
     mine, theirs, kind = slot_tables(p, owner_ref, local_ref, remote_ref, kind_ref)
@@ -179,6 +167,18 @@
         rows_ref[tile, 14:16, :] = jnp.zeros((2, 128), f32)
     for copy in copies[4:]:
         copy.wait()
+    moves = []
+    for field, ref in enumerate((disp_ref, dir_ref)):
+        part = pl.ds(6 * field, 6)
+        for k in range(PARTS):
+            block = me_ref[0] ^ k
+            rows = pl.ds(pl.multiple_of(16 * (block & 1), 16), 16)
+            moves.append((ref.at[:, block >> 1, rows, :], (same_hbm, other_hbm)[k % 2].at[k // 2, part]))
+        moves.append((ref.at[:, 3], up_hbm.at[pl.ds(1 + 6 * field, 6)]))
+        moves.append((ref.at[:, 0], down_hbm.at[pl.ds(1 + 6 * field, 6)]))
+    moves = [pltpu.make_async_copy(a, b, more_sems.at[k]) for k, (a, b) in enumerate(moves)]
+    for move in moves:
+        move.start()
     split_fields(disp_ref, dir_ref, parts_ref)
     near_ref[2] = (ids_ref[3] + 1).astype(f32)
     near_ref[3] = (ids_ref[0] + 1).astype(f32)
@@ -243,7 +243,7 @@
         out_ref[k, 6:12, :] = t_ref[6 * k : 6 * k + 6]
 
 
-def reply_kernel(p_ref, force_ref, after1, after2, after3, chunk_ref, up_ref, down_ref, self_ref):
+def reply_kernel(p_ref, force_ref, chunk_ref, up_ref, down_ref, self_ref):
     p = p_ref[0]
 
     def force(tile):
@@ -260,24 +260,17 @@
         up_ref[k] = force(4 + k)
 
 
-def partner_kernel(me_ref, idx_ref, force_ref, lin_ref, mass_ref, own_ref, y1_ref, y2_ref, y3_ref, x_ref,
-                   out_ref, val_ref, sum_ref):
+def partner_kernel(idx_ref, force_ref, lin_ref, out_ref, val_ref, sum_ref):
     for tile in range(17):
         val_ref[tile] = -force_ref[tile // 3, :, 128 * (tile % 3) : 128 * (tile % 3 + 1)]
     val_ref[17] = jnp.zeros((12, 128), f32)
     scatter_rows(val_ref, idx_ref, sum_ref)
     for x in range(4):
         out_ref[:, x] = lin_ref[:, x] + sum_ref[:, 128 * x : 128 * (x + 1)].reshape(12, 32, 128)
-    me = me_ref[0]
-    for k in range(PARTS):
-        acc = x_ref[k // 2] if k % 2 else (own_ref, y1_ref, y2_ref, y3_ref)[k // 2][0]
-        block = me ^ k
-        x = block >> 1
-        rows = pl.ds(pl.multiple_of(16 * (block & 1), 16), 16)
-        out_ref[:, x, rows, :] = out_ref[:, x, rows, :] + mass_ref[x, rows, :][None] * acc
-
-
-def final_kernel(p_ref, idx_ref, chunk_ref, up_ref, down_ref, self_ref, part_ref, res_ref, jac_ref, val_ref, sum_ref):
+
+
+def final_kernel(p_ref, me_ref, idx_ref, chunk_ref, up_ref, down_ref, self_ref, part_ref, mass_ref,
+                 own_ref, y1_ref, y2_ref, y3_ref, x_ref, res_ref, jac_ref, val_ref, sum_ref, acc_ref):
     p = p_ref[0]
 
     def listed(d):
@@ -287,9 +280,14 @@
     tiles += merge_far(listed, 12, 0.0) + [jnp.zeros((12, 128), f32)]
     for k, tile in enumerate(tiles):
         val_ref[k] = tile
+    for k in range(PARTS):
+        acc = x_ref[k // 2] if k % 2 else (own_ref, y1_ref, y2_ref, y3_ref)[k // 2][0]
+        acc_ref[me_ref[0] ^ k] = acc
     scatter_rows(val_ref, idx_ref, sum_ref)
     for x in range(4):
-        out = part_ref[:, x] + sum_ref[:, 128 * x : 128 * (x + 1)].reshape(12, 32, 128)
+        acc = jnp.concatenate([acc_ref[2 * x], acc_ref[2 * x + 1]], axis=1)
+        added = sum_ref[:, 128 * x : 128 * (x + 1)].reshape(12, 32, 128)
+        out = part_ref[:, x] + mass_ref[x][None] * acc + added
         res_ref[:, x] = out[0:6]
         jac_ref[:, x] = out[6:12]
 
@@ -472,7 +470,7 @@
     force = inst_split(force)
     turned = [inertia[0]] + [swap(inertia[k], 2 * k) for k in (1, 2, 3)]
     messages = [((SLABS, 12, 128), f32)] + [((2, 12, 128), f32)] * 3
-    chunk, up2, down2, own = call(reply_kernel, messages, p, force, *turned[1:], away=(2, 3, 4))
+    chunk, up2, down2, own = call(reply_kernel, messages, p, force)
     chunk, up2, down2 = exchange(chunk, up2, down2)
 
     lin, mass = call(
@@ -483,9 +481,13 @@
     )
     other = swap(call(turn_kernel, [half], *turned, smem=())[0], 1)
     adding = [pltpu.VMEM((SIDE, 12, 128), f32), pltpu.VMEM((384, 512), f32)]
-    partial = call(partner_kernel, [(whole, f32)], me, far_idx, force, lin, mass, *turned, other, scratch=adding)[0]
+    partial = call(partner_kernel, [(whole, f32)], far_idx, force, lin, smem=(), scratch=adding)[0]
     residual, jacobian = call(
-        final_kernel, [(fields, f32)] * 2, p, own_idx, chunk, up2, down2, own, partial, scratch=adding
+        final_kernel,
+        [(fields, f32)] * 2,
+        p, me, own_idx, chunk, up2, down2, own, partial, mass, *turned, other,
+        smem=(0, 1),
+        scratch=adding + blocks[:1],
     )
     return residual.reshape(shape), jacobian.reshape(shape)
 

time: 122 us -> 89.8 us (0.74)
  Pallas kernels: 53.7 us -> 21.5 us
    pallas_call x11, Pallas kernels: 53.7 us -> 21.5 us  [call(): pl.pallas_call(kernel, out_shape=[jax.ShapeDtypeStruct(s, d) for s, d in...]
    all_to_all x2, waiting for transfers between devices: 0.01 us -> 3.53 us  [inst_split(): return lax.all_to_all(x, 'inst', split_axis=0, concat_axis=0, tiled=True)]
    ppermute x8, waiting for transfers between devices: 4.41 us -> 1.07 us  [swap(): return lax.ppermute(x, 'inst', [(i, i ^ bit) for i in range(PARTS)])]
  transfers between devices with their start and end apart: 16 -> 16, of which waited for: 7 -> 7; matrix products, arithmetic and copies ran while one was open for 0% -> 0% of each run, Pallas kernels for 10% -> 13%
where the time goes in v5:
time: 89.8 us; the launch traced here: 89.3 us
  starting transfers between devices  45.8 us (51%)
  Pallas kernels  21.5 us (24%)
  waiting for transfers between devices  18.7 us (21%)
  local copies, waits for them, and re-layouts  2.39 us (3%)
    all_to_all x2, starting transfers between devices, exchange(): lax.all_to_all(chunk, 'mesh', split_axis=0, concat_axis=0, tiled=True)  22.2 us
    pallas_call x11, Pallas kernels, call(): pl.pallas_call(kernel, out_shape=[jax.ShapeDtypeStruct(s, d) for s, d in...  21.5 us
    ppermute x8, starting transfers between devices, swap(): return lax.ppermute(x, 'inst', [(i, i ^ bit) for i in range(PARTS)])  11.3 us
    all_to_all x2, starting transfers between devices, inst_split(): return lax.all_to_all(x, 'inst', split_axis=0, concat_axis=0, tiled=True)  8.94 us
    all_to_all x2, waiting for transfers between devices, exchange(): lax.all_to_all(chunk, 'mesh', split_axis=0, concat_axis=0, tiled=True)  7.54 us
    ppermute x4, waiting for transfers between devices, shift(): lax.ppermute(x, 'mesh', [(i, (i + by) % SLABS) for i in range(SLABS)])  6.58 us
    all_to_all x2, waiting for transfers between devices, inst_split(): return lax.all_to_all(x, 'inst', split_axis=0, concat_axis=0, tiled=True)  3.53 us
    ppermute x4, starting transfers between devices, shift(): lax.ppermute(x, 'mesh', [(i, (i + by) % SLABS) for i in range(SLABS)])  3.42 us
  transfers between devices with their start and end apart: 16, of which 7 were waited for; matrix products, arithmetic and copies ran while one was open for 0% of the time, Pallas kernels for 13%

profile of v5, /device:TPU:1, one launch (start us, length us, event | category | flops | bytes accessed | tf_op | source)
XLA Modules:
  0.0 89.3 jit_solution(14172537502830190448)
XLA Ops:
  0.6 5.4 %shard_map.113 = (s32[24,128]{1,0:T(8,128)}, f32[32,16,128]{2,1,0:T(8,128)}, f32[14,32,128]{2,1,0:T(8,128)}, f32[14,32,128]{2,1,0:T(8,128)}, f32[2,16,128]{2,1,0...) custom-call(s32[1]{0:T(128)} %bitcast.p_ref.refs_0_, s32[1]{0:T(128)} %bitcast.1.me_ref, ...), custom_call_target="tpu_custom_call" | custom-call | tf_op jit(solution)/shard_map/pallas_call | solution.py:382
  6.1 2.1 %collective-permute-start.2 = (f32[4,12,16,128]{3,2,1,0:T(8,128)}, f32[4,12,16,128]{3,2,1,0:T(8,128)S(1)}, u32[]{:S(2)}, u32[]{:S(2)}) collective-permute-start(f32[4,12,16,128]{3,2,1,0:T(8,128)} %get-tuple-element.33), channel_id=1, source_target_pairs={{0,1},{1,0},{2,3},{3,2},{4,5},{5,4},{6,7},{7,6},{8,9},{9,8},{10,11... | collective-permute-start | bytes 1179656 | tf_op jit(solution)/shard_map/ppermute | solution.py:402
  8.2 11.7 %all-to-all-start = ((f32[32,16,128]{2,1,0:T(8,128)}), f32[32,16,128]{2,1,0:T(8,128)S(1)}, u32[]{:S(2)}, u32[]{:S(2)}) async-start(f32[32,16,128]{2,1,0:T(8,128)} %get-tuple-element.28), calls=%async_computation | async-start | bytes 524288 | tf_op jit(solution)/shard_map/all_to_all | solution.py:398
  20.0 1.7 %collective-permute-start = (f32[14,32,128]{2,1,0:T(8,128)}, f32[14,32,128]{2,1,0:T(8,128)S(1)}, u32[]{:S(2)}, u32[]{:S(2)}) collective-permute-start(f32[14,32,128]{2,1,0:T(8,128)} %get-tuple-element.29), channel_id=1, source_target_pairs={{0,8},{8,16},{16,24},{24,32},{32,40},{40,48},{48,56},{56,64},{64,7... | collective-permute-start | bytes 688136 | tf_op jit(solution)/shard_map/ppermute | solution.py:393
  22.6 1.3 %collective-permute-start.3 = (f32[2,12,16,128]{3,2,1,0:T(8,128)}, f32[2,12,16,128]{3,2,1,0:T(8,128)S(1)}, u32[]{:S(2)}, u32[]{:S(2)}) collective-permute-start(f32[2,12,16,128]{3,2,1,0:T(8,128)} %get-tuple-element.34.after_ref), channel_id=1, source_target_pairs={{0,2},{1,3},{2,0},{3,1},{4,6},{5,7},{6,4},{7,5},{8,10},{9,11},{10,... | collective-permute-start | bytes 589832 | tf_op jit(solution)/shard_map/ppermute | solution.py:402
  23.9 2.6 %collective-permute-start.4 = (f32[2,12,16,128]{3,2,1,0:T(8,128)}, f32[2,12,16,128]{3,2,1,0:T(8,128)S(1)}, u32[]{:S(2)}, u32[]{:S(2)}) collective-permute-start(f32[2,12,16,128]{3,2,1,0:T(8,128)} %get-tuple-element.37), channel_id=1, source_target_pairs={{0,4},{1,5},{2,6},{3,7},{4,0},{5,1},{6,2},{7,3},{8,12},{9,13},{10,... | collective-permute-start | bytes 589832 | tf_op jit(solution)/shard_map/ppermute | solution.py:402
  26.6 2.1 %collective-permute-done.up_ref.refs_6_ = f32[14,32,128]{2,1,0:T(8,128)S(1)} collective-permute-done((f32[14,32,128]{2,1,0:T(8,128)}, f32[14,32,128]{2,1,0:T(8,128)S(1)}, u32[]{:S(2)}, u32[]{:S(2)}) %collective-permute-start) | collective-permute-done | bytes 229408 | tf_op jit(solution)/shard_map/ppermute | solution.py:393
  28.7 2.1 %collective-permute-done.1.down_ref.refs_7_ = f32[14,32,128]{2,1,0:T(8,128)S(1)} collective-permute-done((f32[14,32,128]{2,1,0:T(8,128)}, f32[14,32,128]{2,1,0:T(8,128)S(1)}, u32[]{:S(2)}, u32[]{:S(2)}) %collective-permute-start.1) | collective-permute-done | bytes 229408 | tf_op jit(solution)/shard_map/ppermute | solution.py:393
  30.8 2.6 %all-to-all-done.chunk_ref = f32[32,16,128]{2,1,0:T(8,128)S(1)} async-done(((f32[32,16,128]{2,1,0:T(8,128)}), f32[32,16,128]{2,1,0:T(8,128)S(1)}, u32[]{:S(2)}, u32[]{:S(2)}) %all-to-all-start) | async-done | bytes 262176 | tf_op jit(solution)/shard_map/all_to_all | solution.py:398
  33.4 2.5 %shard_map.116 = (s32[24,128]{1,0:T(8,128)S(1)}, f32[24,128]{1,0:T(8,128)S(1)}, f32[8,12,384]{2,1,0:T(8,128)S(1)}) custom-call(s32[1]{0:T(128)} %bitcast.p_ref.refs_0_, f32[32,16,128]{2,1,0:T(8,128)S(1)} %all-to-all-done.chunk_ref, f32[14,32,128]{2,1,0:T(8,128)S(1)} %collective-permute-done.up_ref.refs_6_, ...), custom_call_target="tpu_custom_call" | custom-call | tf_op jit(solution)/shard_map/pallas_call | solution.py:382
  36.6 4.2 %all-to-all-start.1 = ((f32[8,12,384]{2,1,0:T(8,128)}), f32[8,12,384]{2,1,0:T(8,128)S(1)}, u32[]{:S(2)}, u32[]{:S(2)}) async-start(f32[8,12,384]{2,1,0:T(8,128)} %copy-done.7), calls=%async_computation.1 | async-start | bytes 393216 | tf_op jit(solution)/shard_map/all_to_all | solution.py:406
  42.4 2.0 %shard_map.117 = (f32[2,12,16,128]{3,2,1,0:T(8,128)S(1)}, f32[2,12,16,128]{3,2,1,0:T(8,128)S(1)}, f32[2,12,16,128]{3,2,1,0:T(8,128)S(1)}, f32[2,12,16,128]{3,2,1,0:T(8,128)S(1)}) custom-call(s32[1]{0:T(128)} %bitcast.1.me_ref, f32[4,12,16,128]{3,2,1,0:T(8,128)S(1)} %copy-done.2, f32[4,12,16,128]{3,2,1,0:T(8,128)S(1)} %collective-permute-done.2.other_ref, ...), custom_call_target="tpu_custom_call" | custom-call | tf_op jit(solution)/shard_map/pallas_call | solution.py:382
  44.4 2.8 %collective-permute-start.10 = (f32[2,12,16,128]{3,2,1,0:T(8,128)S(1)}, f32[2,12,16,128]{3,2,1,0:T(8,128)S(1)}, u32[]{:S(2)}, u32[]{:S(2)}) collective-permute-start(f32[2,12,16,128]{3,2,1,0:T(8,128)S(1)} %get-tuple-element.49), channel_id=1, source_target_pairs={{0,6},{1,7},{2,4},{3,5},{4,2},{5,3},{6,0},{7,1},{8,14},{9,15},{10,... | collective-permute-start | bytes 589832 | tf_op jit(solution)/shard_map/ppermute | solution.py:402
  47.1 1.3 %collective-permute-start.9 = (f32[2,12,16,128]{3,2,1,0:T(8,128)S(1)}, f32[2,12,16,128]{3,2,1,0:T(8,128)S(1)}, u32[]{:S(2)}, u32[]{:S(2)}) collective-permute-start(f32[2,12,16,128]{3,2,1,0:T(8,128)S(1)} %get-tuple-element.48), channel_id=1, source_target_pairs={{0,4},{1,5},{2,6},{3,7},{4,0},{5,1},{6,2},{7,3},{8,12},{9,13},{10,... | collective-permute-start | bytes 589832 | tf_op jit(solution)/shard_map/ppermute | solution.py:402
  49.4 4.7 %all-to-all-start.2 = ((f32[8,12,384]{2,1,0:T(8,128)}), f32[8,12,384]{2,1,0:T(8,128)S(1)}, u32[]{:S(2)}, u32[]{:S(2)}) async-start(f32[8,12,384]{2,1,0:T(8,128)} %shard_map.118), calls=%async_computation.2 | async-start | bytes 393216 | tf_op jit(solution)/shard_map/all_to_all | solution.py:406
  55.2 1.2 %collective-permute-start.11 = (f32[4,12,16,128]{3,2,1,0:T(8,128)S(1)}, f32[4,12,16,128]{3,2,1,0:T(8,128)}, u32[]{:S(2)}, u32[]{:S(2)}) collective-permute-start(f32[4,12,16,128]{3,2,1,0:T(8,128)S(1)} %shard_map.122), channel_id=1, source_target_pairs={{0,1},{1,0},{2,3},{3,2},{4,5},{5,4},{6,7},{7,6},{8,9},{9,8},{10,11... | collective-permute-start | bytes 1179656 | tf_op jit(solution)/shard_map/ppermute | solution.py:402
  56.4 3.5 %all-to-all-done.2.force_ref = f32[8,12,384]{2,1,0:T(8,128)S(1)} async-done(((f32[8,12,384]{2,1,0:T(8,128)}), f32[8,12,384]{2,1,0:T(8,128)S(1)}, u32[]{:S(2)}, u32[]{:S(2)}) %all-to-all-start.2) | async-done | bytes 147488 | tf_op jit(solution)/shard_map/all_to_all | solution.py:406
  60.8 10.4 %all-to-all-start.3 = ((f32[32,12,128]{2,1,0:T(8,128)}), f32[32,12,128]{2,1,0:T(8,128)S(1)}, u32[]{:S(2)}, u32[]{:S(2)}) async-start(f32[32,12,128]{2,1,0:T(8,128)} %get-tuple-element.40), calls=%async_computation.3 | async-start | bytes 524288 | tf_op jit(solution)/shard_map/all_to_all | solution.py:398
  71.2 1.7 %collective-permute-start.6 = (f32[2,12,128]{2,1,0:T(8,128)S(1)}, f32[2,12,128]{2,1,0:T(8,128)S(1)}, u32[]{:S(2)}, u32[]{:S(2)}) collective-permute-start(f32[2,12,128]{2,1,0:T(8,128)S(1)} %get-tuple-element.41), channel_id=1, source_target_pairs={{0,8},{8,16},{16,24},{24,32},{32,40},{40,48},{48,56},{56,64},{64,7... | collective-permute-start | bytes 36872 | tf_op jit(solution)/shard_map/ppermute | solution.py:393
  73.0 1.6 %shard_map.120 = (f32[12,4,32,128]{3,2,1,0:T(8,128)S(1)}, f32[4,32,128]{2,1,0:T(8,128)S(1)}) custom-call(s32[1]{0:T(128)} %bitcast.p_ref.refs_0_, f32[16,4]{1,0:T(8,128)S(1)} %copy.12.refs_1_, s32[4,32,128]{2,1,0:T(8,128)S(1)} %copy-done.4, f32[6,4,32,128]{3,2,1,0:T(8,128)S(1)} %bitcast.13, f32[6,4,32,128]{3,2,1,0:T(8,128)S(1)} %bitcast.16, ...), custom_call_target="tpu_custom_call" | custom-call | tf_op jit(solution)/shard_map/pallas_call | solution.py:382
  74.7 2.6 %shard_map.121.part_ref = f32[12,4,32,128]{3,2,1,0:T(8,128)S(1)} custom-call(s32[24,128]{1,0:T(8,128)S(1)} %get-tuple-element.44.idx_ref, f32[8,12,384]{2,1,0:T(8,128)S(1)} %all-to-all-done.2.force_ref, f32[12,4,32,128]{3,2,1,0:T(8,128)S(1)} %get-tuple-element.45.lin_ref), custom_call_target="tpu_custom_call" | custom-call | tf_op jit(solution)/shard_map/pallas_call | solution.py:382
  77.3 2.5 %collective-permute-done.7.down_ref = f32[2,12,128]{2,1,0:T(8,128)S(1)} collective-permute-done((f32[2,12,128]{2,1,0:T(8,128)S(1)}, f32[2,12,128]{2,1,0:T(8,128)S(1)}, u32[]{:S(2)}, u32[]{:S(2)}) %collective-permute-start.7) | collective-permute-done | bytes 12320 | tf_op jit(solution)/shard_map/ppermute | solution.py:393
  79.7 4.9 %all-to-all-done.3.chunk_ref = f32[32,12,128]{2,1,0:T(8,128)S(1)} async-done(((f32[32,12,128]{2,1,0:T(8,128)}), f32[32,12,128]{2,1,0:T(8,128)S(1)}, u32[]{:S(2)}, u32[]{:S(2)}) %all-to-all-start.3) | async-done | bytes 196640 | tf_op jit(solution)/shard_map/all_to_all | solution.py:398
  84.6 4.6 %shard_map.123 = (f32[6,4,32,128]{3,2,1,0:T(8,128)}, f32[6,4,32,128]{3,2,1,0:T(8,128)}) custom-call(s32[1]{0:T(128)} %bitcast.p_ref.refs_0_, s32[1]{0:T(128)} %bitcast.1.me_ref, s32[24,128]{1,0:T(8,128)S(1)} %copy-done.10, f32[32,12,128]{2,1,0:T(8,128)S(1)} %all-to-all-done.3.chunk_ref, f32[2,12,128]{2,1,0:T(8,128)S(1)} %collective-permute-done.6.up_ref, ...), custom_call_target="tpu_custom_call" | custom-call | tf_op jit(solution)/shard_map/pallas_call | solution.py:382
  (44 shorter events, 6.3 us)
Async XLA Ops:
  6.1 15.6 %copy-start.2 = (f32[4,12,16,128]{3,2,1,0:T(8,128)S(1)}, f32[4,12,16,128]{3,2,1,0:T(8,128)}, u32[]{:S(2)}) copy-start(f32[4,12,16,128]{3,2,1,0:T(8,128)} %get-tuple-element.32.same_ref) | copy-start | bytes 1179652
  6.1 15.6 %collective-permute-start.2 = (f32[4,12,16,128]{3,2,1,0:T(8,128)}, f32[4,12,16,128]{3,2,1,0:T(8,128)S(1)}, u32[]{:S(2)}, u32[]{:S(2)}) collective-permute-start(f32[4,12,16,128]{3,2,1,0:T(8,128)} %get-tuple-element.33), channel_id=1, source_target_pairs={{0,1},{1,0},{2,3},{3,2},{4,5},{5,4},{6,7},{7,6},{8,9},{9,8},{10,11... | collective-permute-start | bytes 1179656 | tf_op jit(solution)/shard_map/ppermute | solution.py:402
  8.2 25.2 %all-to-all-start = ((f32[32,16,128]{2,1,0:T(8,128)}), f32[32,16,128]{2,1,0:T(8,128)S(1)}, u32[]{:S(2)}, u32[]{:S(2)}) async-start(f32[32,16,128]{2,1,0:T(8,128)} %get-tuple-element.28), calls=%async_computation | async-start | bytes 524288 | tf_op jit(solution)/shard_map/all_to_all | solution.py:398
  20.0 8.7 %collective-permute-start = (f32[14,32,128]{2,1,0:T(8,128)}, f32[14,32,128]{2,1,0:T(8,128)S(1)}, u32[]{:S(2)}, u32[]{:S(2)}) collective-permute-start(f32[14,32,128]{2,1,0:T(8,128)} %get-tuple-element.29), channel_id=1, source_target_pairs={{0,8},{8,16},{16,24},{24,32},{32,40},{40,48},{48,56},{56,64},{64,7... | collective-permute-start | bytes 688136 | tf_op jit(solution)/shard_map/ppermute | solution.py:393
  21.7 9.1 %collective-permute-start.1 = (f32[14,32,128]{2,1,0:T(8,128)}, f32[14,32,128]{2,1,0:T(8,128)S(1)}, u32[]{:S(2)}, u32[]{:S(2)}) collective-permute-start(f32[14,32,128]{2,1,0:T(8,128)} %get-tuple-element.30), channel_id=1, source_target_pairs={{0,248},{8,0},{16,8},{24,16},{32,24},{40,32},{48,40},{56,48},{64,5... | collective-permute-start | bytes 688136 | tf_op jit(solution)/shard_map/ppermute | solution.py:393
  21.7 4.8 %copy-start = (f32[2,3,4,32,128]{4,3,2,1,0:T(8,128)S(1)}, f32[2,3,4,32,128]{4,3,2,1,0:T(8,128)}, u32[]{:S(2)}) copy-start(f32[2,3,4,32,128]{4,3,2,1,0:T(8,128)} %param.10) | copy-start | bytes 1179652
  21.7 4.8 %copy-start.1 = (f32[2,3,4,32,128]{4,3,2,1,0:T(8,128)S(1)}, f32[2,3,4,32,128]{4,3,2,1,0:T(8,128)}, u32[]{:S(2)}) copy-start(f32[2,3,4,32,128]{4,3,2,1,0:T(8,128)} %param.11) | copy-start | bytes 1179652
  22.6 18.2 %collective-permute-start.3 = (f32[2,12,16,128]{3,2,1,0:T(8,128)}, f32[2,12,16,128]{3,2,1,0:T(8,128)S(1)}, u32[]{:S(2)}, u32[]{:S(2)}) collective-permute-start(f32[2,12,16,128]{3,2,1,0:T(8,128)} %get-tuple-element.34.after_ref), channel_id=1, source_target_pairs={{0,2},{1,3},{2,0},{3,1},{4,6},{5,7},{6,4},{7,5},{8,10},{9,11},{10,... | collective-permute-start | bytes 589832 | tf_op jit(solution)/shard_map/ppermute | solution.py:402
  23.9 16.9 %collective-permute-start.4 = (f32[2,12,16,128]{3,2,1,0:T(8,128)}, f32[2,12,16,128]{3,2,1,0:T(8,128)S(1)}, u32[]{:S(2)}, u32[]{:S(2)}) collective-permute-start(f32[2,12,16,128]{3,2,1,0:T(8,128)} %get-tuple-element.37), channel_id=1, source_target_pairs={{0,4},{1,5},{2,6},{3,7},{4,0},{5,1},{6,2},{7,3},{8,12},{9,13},{10,... | collective-permute-start | bytes 589832 | tf_op jit(solution)/shard_map/ppermute | solution.py:402
  26.5 6.9 %copy-start.9 = (f32[2,16,128]{2,1,0:T(8,128)S(1)}, f32[2,16,128]{2,1,0:T(8,128)}, u32[]{:S(2)}) copy-start(f32[2,16,128]{2,1,0:T(8,128)} %get-tuple-element.31.self_ref) | copy-start | bytes 49156
  26.5 15.0 %collective-permute-start.5 = (f32[2,12,16,128]{3,2,1,0:T(8,128)}, f32[2,12,16,128]{3,2,1,0:T(8,128)}, u32[]{:S(2)}, u32[]{:S(2)}) collective-permute-start(f32[2,12,16,128]{3,2,1,0:T(8,128)} %get-tuple-element.38), channel_id=1, source_target_pairs={{0,6},{1,7},{2,4},{3,5},{4,2},{5,3},{6,0},{7,1},{8,14},{9,15},{10,... | collective-permute-start | bytes 589832 | tf_op jit(solution)/shard_map/ppermute | solution.py:402
  36.6 11.8 %all-to-all-start.1 = ((f32[8,12,384]{2,1,0:T(8,128)}), f32[8,12,384]{2,1,0:T(8,128)S(1)}, u32[]{:S(2)}, u32[]{:S(2)}) async-start(f32[8,12,384]{2,1,0:T(8,128)} %copy-done.7), calls=%async_computation.1 | async-start | bytes 393216 | tf_op jit(solution)/shard_map/all_to_all | solution.py:406
  42.4 6.0 %copy-start.8 = (f32[48,48]{1,0:T(8,128)S(1)}, f32[48,48]{1,0:T(8,128)}, u32[]{:S(2)}) copy-start(f32[48,48]{1,0:T(8,128)} %constant.11.clone.spread_ref) | copy-start | bytes 27652
  44.4 9.8 %collective-permute-start.10 = (f32[2,12,16,128]{3,2,1,0:T(8,128)S(1)}, f32[2,12,16,128]{3,2,1,0:T(8,128)S(1)}, u32[]{:S(2)}, u32[]{:S(2)}) collective-permute-start(f32[2,12,16,128]{3,2,1,0:T(8,128)S(1)} %get-tuple-element.49), channel_id=1, source_target_pairs={{0,6},{1,7},{2,4},{3,5},{4,2},{5,3},{6,0},{7,1},{8,14},{9,15},{10,... | collective-permute-start | bytes 589832 | tf_op jit(solution)/shard_map/ppermute | solution.py:402
  47.1 7.0 %collective-permute-start.8 = (f32[2,12,16,128]{3,2,1,0:T(8,128)S(1)}, f32[2,12,16,128]{3,2,1,0:T(8,128)S(1)}, u32[]{:S(2)}, u32[]{:S(2)}) collective-permute-start(f32[2,12,16,128]{3,2,1,0:T(8,128)S(1)} %get-tuple-element.47), channel_id=1, source_target_pairs={{0,2},{1,3},{2,0},{3,1},{4,6},{5,7},{6,4},{7,5},{8,10},{9,11},{10,... | collective-permute-start | bytes 589832 | tf_op jit(solution)/shard_map/ppermute | solution.py:402
  47.1 8.1 %collective-permute-start.9 = (f32[2,12,16,128]{3,2,1,0:T(8,128)S(1)}, f32[2,12,16,128]{3,2,1,0:T(8,128)S(1)}, u32[]{:S(2)}, u32[]{:S(2)}) collective-permute-start(f32[2,12,16,128]{3,2,1,0:T(8,128)S(1)} %get-tuple-element.48), channel_id=1, source_target_pairs={{0,4},{1,5},{2,6},{3,7},{4,0},{5,1},{6,2},{7,3},{8,12},{9,13},{10,... | collective-permute-start | bytes 589832 | tf_op jit(solution)/shard_map/ppermute | solution.py:402
  49.4 10.6 %all-to-all-start.2 = ((f32[8,12,384]{2,1,0:T(8,128)}), f32[8,12,384]{2,1,0:T(8,128)S(1)}, u32[]{:S(2)}, u32[]{:S(2)}) async-start(f32[8,12,384]{2,1,0:T(8,128)} %shard_map.118), calls=%async_computation.2 | async-start | bytes 393216 | tf_op jit(solution)/shard_map/all_to_all | solution.py:406
  55.2 17.8 %copy-start.3 = (f32[2,3,4,32,128]{4,3,2,1,0:T(8,128)S(1)}, f32[2,3,4,32,128]{4,3,2,1,0:T(8,128)}, u32[]{:S(2)}) copy-start(f32[2,3,4,32,128]{4,3,2,1,0:T(8,128)} %param.12) | copy-start | bytes 1179652
  55.2 29.4 %collective-permute-start.11 = (f32[4,12,16,128]{3,2,1,0:T(8,128)S(1)}, f32[4,12,16,128]{3,2,1,0:T(8,128)}, u32[]{:S(2)}, u32[]{:S(2)}) collective-permute-start(f32[4,12,16,128]{3,2,1,0:T(8,128)S(1)} %shard_map.122), channel_id=1, source_target_pairs={{0,1},{1,0},{2,3},{3,2},{4,5},{5,4},{6,7},{7,6},{8,9},{9,8},{10,11... | collective-permute-start | bytes 1179656 | tf_op jit(solution)/shard_map/ppermute | solution.py:402
  60.8 12.3 %copy-start.4 = (s32[4,32,128]{2,1,0:T(8,128)S(1)}, s32[4,32,128]{2,1,0:T(8,128)}, u32[]{:S(2)}) copy-start(s32[4,32,128]{2,1,0:T(8,128)} %refs_2_.1) | copy-start | bytes 196612
  60.8 23.9 %all-to-all-start.3 = ((f32[32,12,128]{2,1,0:T(8,128)}), f32[32,12,128]{2,1,0:T(8,128)S(1)}, u32[]{:S(2)}, u32[]{:S(2)}) async-start(f32[32,12,128]{2,1,0:T(8,128)} %get-tuple-element.40), calls=%async_computation.3 | async-start | bytes 524288 | tf_op jit(solution)/shard_map/all_to_all | solution.py:398
  71.2 6.0 %collective-permute-start.6 = (f32[2,12,128]{2,1,0:T(8,128)S(1)}, f32[2,12,128]{2,1,0:T(8,128)S(1)}, u32[]{:S(2)}, u32[]{:S(2)}) collective-permute-start(f32[2,12,128]{2,1,0:T(8,128)S(1)} %get-tuple-element.41), channel_id=1, source_target_pairs={{0,8},{8,16},{16,24},{24,32},{32,40},{40,48},{48,56},{56,64},{64,7... | collective-permute-start | bytes 36872 | tf_op jit(solution)/shard_map/ppermute | solution.py:393
  72.9 6.8 %collective-permute-start.7 = (f32[2,12,128]{2,1,0:T(8,128)S(1)}, f32[2,12,128]{2,1,0:T(8,128)S(1)}, u32[]{:S(2)}, u32[]{:S(2)}) collective-permute-start(f32[2,12,128]{2,1,0:T(8,128)S(1)} %get-tuple-element.42), channel_id=1, source_target_pairs={{0,248},{8,0},{16,8},{24,16},{32,24},{40,32},{48,40},{56,48},{64,5... | collective-permute-start | bytes 36872 | tf_op jit(solution)/shard_map/ppermute | solution.py:393
  74.6 10.0 %copy-start.10 = (s32[24,128]{1,0:T(8,128)S(1)}, s32[24,128]{1,0:T(8,128)}, u32[]{:S(2)}) copy-start(s32[24,128]{1,0:T(8,128)} %get-tuple-element.27.idx_ref) | copy-start | bytes 36868
  (4 other events, 4.0 us)

commit v6 on v5

--- a/solution.py
+++ b/solution.py
@@ -39,8 +39,12 @@
     return 8 + (offset - 3) // 3, SEG * ((offset - 3) % 3)
 
 
-def place(offset):
-    return {2: (6, 0), 30: (7, 0)}.get(offset) or far_place(offset)
+def pack(rows, seg):
+    return jnp.where(lanes(8) < 64, lane_roll(rows[:8], -seg), lane_roll(rows[8:], 64 - seg))
+
+
+def unpack(chunk):
+    return jnp.concatenate([chunk, lane_roll(chunk, 64)], axis=0)
 
 
 def lane_roll(x, shift):
@@ -148,7 +152,7 @@
 
 
 def list_kernel(p_ref, me_ref, owner_hbm, local_hbm, remote_hbm, kind_hbm, disp_hbm, dir_hbm, ids_hbm,
-                idx_ref, chunk_ref, up_hbm, down_hbm, self_ref, same_hbm, other_hbm,
+                idx_ref, chunk_ref, up_hbm, down_hbm, up2_ref, down2_ref, self_ref, same_hbm, other_hbm,
                 parts_ref, rows_ref, owner_ref, local_ref, remote_ref, kind_ref, disp_ref, dir_ref, ids_ref, near_ref,
                 sems, more_sems):
     p = p_ref[0]
@@ -190,25 +194,27 @@
     ends = [pltpu.make_async_copy(a, b, sems.at[7 + k]) for k, (a, b) in enumerate(ends)]
     for end in ends:
         end.start()
-    for d in (0, 1, SLABS - 1):
-        chunk_ref[(p + d) & (SLABS - 1)] = jnp.zeros((16, 128), f32)
-    for d in range(2, SLABS - 1):
-        tile, seg = place(d)
-        chunk_ref[(p + d) & (SLABS - 1)] = lane_roll(rows_ref[tile], -seg)
+    for d in (0, 1, 2, SLABS - 2, SLABS - 1):
+        chunk_ref[(p + d) & (SLABS - 1)] = jnp.zeros((8, 128), f32)
+    for d in range(3, SLABS - 2):
+        tile, seg = far_place(d)
+        chunk_ref[(p + d) & (SLABS - 1)] = pack(rows_ref[tile], seg)
+    up2_ref[...] = rows_ref[6]
+    down2_ref[...] = rows_ref[7]
     self_ref[...] = rows_ref[0:2]
     for move in moves + ends:
         move.wait()
 
 
-def gap_kernel(p_ref, chunk_ref, up_ref, down_ref, self_ref, parts_ref, after_ref,
+def gap_kernel(p_ref, chunk_ref, up_ref, down_ref, up2_ref, down2_ref, self_ref, parts_ref, after_ref,
                idx_ref, kind_ref, gap_ref, here_ref):
     p = p_ref[0]
 
     def asked(d):
-        return chunk_ref[(p - d) & (SLABS - 1)]
+        return unpack(chunk_ref[(p - d) & (SLABS - 1)])
 
     near = [ref[0, 16 * k : 16 * (k + 1), :] for ref in (up_ref, down_ref) for k in range(2)]
-    tiles = [self_ref[0], self_ref[1]] + near + [asked(2), asked(SLABS - 2)]
+    tiles = [self_ref[0], self_ref[1]] + near + [up2_ref[...], down2_ref[...]]
     tiles += merge_far(asked, 16, 0.0)
     beyond = lanes(1) >= 3 * SEG
     rows = [t[12:13] for t in tiles[:8]] + [jnp.where(beyond, -1.0, t[12:13]) for t in tiles[8:]]
@@ -251,8 +257,10 @@
 
     for d in (0, 1, SLABS - 1):
         chunk_ref[(p - d) & (SLABS - 1)] = jnp.zeros((12, 128), f32)
-    for d in range(2, SLABS - 1):
-        tile, seg = place(d)
+    for d, tile in ((2, 6), (SLABS - 2, 7)):
+        chunk_ref[(p - d) & (SLABS - 1)] = force(tile)
+    for d in range(3, SLABS - 2):
+        tile, seg = far_place(d)
         chunk_ref[(p - d) & (SLABS - 1)] = lane_roll(force(tile), -seg)
     for k in range(2):
         self_ref[k] = force(k)
@@ -270,8 +278,14 @@
 
 
 def final_kernel(p_ref, me_ref, idx_ref, chunk_ref, up_ref, down_ref, self_ref, part_ref, mass_ref,
-                 own_ref, y1_ref, y2_ref, y3_ref, x_ref, res_ref, jac_ref, val_ref, sum_ref, acc_ref):
+                 own_ref, y1_ref, y2_ref, y3_ref, x_ref, res_ref, jac_ref, val_ref, sum_ref, acc_ref, sems):
     p = p_ref[0]
+    copies = []
+    for k in range(PARTS):
+        source = x_ref.at[k // 2] if k % 2 else (own_ref, y1_ref, y2_ref, y3_ref)[k // 2].at[0]
+        copies.append(pltpu.make_async_copy(source, acc_ref.at[me_ref[0] ^ k], sems.at[k]))
+    for copy in copies:
+        copy.start()
 
     def listed(d):
         return chunk_ref[(p + d) & (SLABS - 1)]
@@ -280,10 +294,9 @@
     tiles += merge_far(listed, 12, 0.0) + [jnp.zeros((12, 128), f32)]
     for k, tile in enumerate(tiles):
         val_ref[k] = tile
-    for k in range(PARTS):
-        acc = x_ref[k // 2] if k % 2 else (own_ref, y1_ref, y2_ref, y3_ref)[k // 2][0]
-        acc_ref[me_ref[0] ^ k] = acc
     scatter_rows(val_ref, idx_ref, sum_ref)
+    for copy in copies:
+        copy.wait()
     for x in range(4):
         acc = jnp.concatenate([acc_ref[2 * x], acc_ref[2 * x + 1]], axis=1)
         added = sum_ref[:, 128 * x : 128 * (x + 1)].reshape(12, 32, 128)
@@ -304,12 +317,15 @@
 
 
 def time_kernel(me_ref, same_ref, other_ref, y1_ref, y2_ref, y3_ref, *refs):
-    outs, in_ref, out_ref = refs[:4], refs[4], refs[5]
+    outs, in_ref, out_ref, sems = refs[:4], refs[4], refs[5], refs[6]
     me = me_ref[0]
-    in_ref[0] = same_ref[0]
-    in_ref[1] = other_ref[0]
-    for k, ref in enumerate((y1_ref, y2_ref, y3_ref)):
-        in_ref[2 * k + 2 : 2 * k + 4] = ref[...]
+    pairs = [(same_ref.at[0], in_ref.at[0]), (other_ref.at[0], in_ref.at[1])]
+    pairs += [(ref, in_ref.at[pl.ds(2 * k + 2, 2)]) for k, ref in enumerate((y1_ref, y2_ref, y3_ref))]
+    copies = [pltpu.make_async_copy(a, b, sems.at[k]) for k, (a, b) in enumerate(pairs)]
+    for copy in copies:
+        copy.start()
+    for copy in copies:
+        copy.wait()
     at = [me ^ ((me + k) & (PARTS - 1)) for k in range(PARTS)]
     count = 2 * PARTS
 
@@ -393,9 +409,9 @@
     return lax.ppermute(x, "mesh", [(i, (i + by) % SLABS) for i in range(SLABS)])
 
 
-def exchange(chunk, up, down):
-    up, down = shift(up, 1), shift(down, -1)
-    return lax.all_to_all(chunk, "mesh", split_axis=0, concat_axis=0, tiled=True), up, down
+def exchange(chunk, *near):
+    near = [shift(x, by) for x, by in zip(near, (1, -1, 2, -2))]
+    return lax.all_to_all(chunk, "mesh", split_axis=0, concat_axis=0, tiled=True), *near
 
 
 def swap(x, bit):
@@ -419,10 +435,11 @@
     index = ((24, 128), i32)
     half = ((4, 12, 16, 128), f32)
     near = ((14, 32, 128), f32)
-
-    own_idx, chunk, up, down, own, same, other = call(
+    tile = ((16, 128), f32)
+
+    own_idx, chunk, *sides, own, same, other = call(
         list_kernel,
-        [index, ((SLABS, 16, 128), f32), near, near, ((2, 16, 128), f32), half, half],
+        [index, ((SLABS, 8, 128), f32), near, near, tile, tile, ((2, 16, 128), f32), half, half],
         p,
         me,
         joint_owner.reshape(1, count),
@@ -435,29 +452,29 @@
         smem=(0, 1),
         away=range(2, 9),
         limit=60 * 1024 * 1024,
-        kept=(2, 3, 5, 6),
+        kept=(2, 3, 7, 8),
         scratch=[pltpu.VMEM(parts, bf16), pltpu.VMEM((SIDE, 16, 128), f32)]
         + [pltpu.VMEM((1, count), i32)] * 4
         + [pltpu.VMEM(fields, f32)] * 2
         + [pltpu.VMEM((4, 32, 128), i32), pltpu.VMEM((4, 32, 128), f32)]
         + [pltpu.SemaphoreType.DMA((11,)), pltpu.SemaphoreType.DMA((20,))],
     )
-    chunk, up, down = exchange(chunk, up, down)
+    chunk, *sides = exchange(chunk, *sides)
 
     pair = ((2, 12, 16, 128), f32)
     other = swap(other, 1)
     joined = call(join_kernel, [pair] * 3, same, other, smem=())
     turned = [swap(x, 2 * k + 2) for k, x in enumerate(joined)]
     blocks = [pltpu.VMEM((PARTS, 12, 16, 128), f32)] * 2
-    inertia = call(time_kernel, [pair] * 4, me, same, other, *turned, scratch=blocks)
+    inertia = call(time_kernel, [pair] * 4, me, same, other, *turned, away=range(1, 6), scratch=blocks + [pltpu.SemaphoreType.DMA((5,))])
 
     part = ((PARTS, 12, 384), f32)
     fields_parts = call(split_kernel, [(parts, bf16)], disp, dire, smem=())[0]
     far_idx, kind, gap = call(
         gap_kernel,
         [index, ((24, 128), f32), part],
-        p, chunk, up, down, own, fields_parts, joined[0],
-        away=(6,),
+        p, chunk, *sides, own, fields_parts, joined[0],
+        away=(8,),
         scratch=[pltpu.VMEM((SIDE, 12, 128), f32)],
     )
     force = call(
@@ -469,14 +486,14 @@
     )[0]
     force = inst_split(force)
     turned = [inertia[0]] + [swap(inertia[k], 2 * k) for k in (1, 2, 3)]
-    messages = [((SLABS, 12, 128), f32)] + [((2, 12, 128), f32)] * 3
-    chunk, up2, down2, own = call(reply_kernel, messages, p, force)
-    chunk, up2, down2 = exchange(chunk, up2, down2)
+    two = ((2, 12, 128), f32)
+    chunk, *replies, own = call(reply_kernel, [((SLABS, 12, 128), f32), two, two, two], p, force)
+    chunk, *replies = exchange(chunk, *replies)
 
     lin, mass = call(
         lambda *refs: stiff_kernel(*refs, materials=materials.shape[0]),
         [(whole, f32), ((4, 32, 128), f32)],
-        p, materials, material_ids, disp, dire, forcing.reshape(fields), up, down,
+        p, materials, material_ids, disp, dire, forcing.reshape(fields), *sides[:2],
         smem=(0, 1),
     )
     other = swap(call(turn_kernel, [half], *turned, smem=())[0], 1)
@@ -485,9 +502,10 @@
     residual, jacobian = call(
         final_kernel,
         [(fields, f32)] * 2,
-        p, me, own_idx, chunk, up2, down2, own, partial, mass, *turned, other,
+        p, me, own_idx, chunk, *replies, own, partial, mass, *turned, other,
         smem=(0, 1),
-        scratch=adding + blocks[:1],
+        away=range(9, 14),
+        scratch=adding + blocks[:1] + [pltpu.SemaphoreType.DMA((PARTS,))],
     )
     return residual.reshape(shape), jacobian.reshape(shape)
 

time: 89.8 us -> 91.3 us (1.017)
  starting transfers between devices: 45.8 us -> 52.9 us
  waiting for transfers between devices: 18.7 us -> 12.6 us
    ppermute x4 -> x6, starting transfers between devices: 3.42 us -> 8.68 us  [shift(): lax.ppermute(x, 'mesh', [(i, (i + by) % SLABS) for i in range(SLABS)])]
    ppermute x4 -> x6, waiting for transfers between devices: 6.58 us -> 2.46 us  [shift(): lax.ppermute(x, 'mesh', [(i, (i + by) % SLABS) for i in range(SLABS)])]
    all_to_all x2, waiting for transfers between devices: 7.54 us -> 4.91 us  [exchange(): lax.all_to_all(chunk, 'mesh', split_axis=0, concat_axis=0, tiled=True)]
    ppermute x8, starting transfers between devices: 11.3 us -> 13 us  [swap(): return lax.ppermute(x, 'inst', [(i, i ^ bit) for i in range(PARTS)])]
    ppermute x8, waiting for transfers between devices: 1.07 us -> 2.04 us  [swap(): return lax.ppermute(x, 'inst', [(i, i ^ bit) for i in range(PARTS)])]
    unnamed x25 -> x27, local copies, waits for them, and re-layouts: 2.39 us -> 2.31 us
  transfers between devices with their start and end apart: 16 -> 18, of which waited for: 7 -> 6; matrix products, arithmetic and copies ran while one was open for 0% -> 0% of each run, Pallas kernels for 13% -> 14%
where the time goes in v6:
time: 91.3 us; the launch traced here: 90.6 us
  starting transfers between devices  52.9 us (58%)
  Pallas kernels  21.9 us (24%)
  waiting for transfers between devices  12.6 us (14%)
  local copies, waits for them, and re-layouts  2.31 us (3%)
  between operations  1.02 us (1%)
    all_to_all x2, starting transfers between devices, exchange(): lax.all_to_all(chunk, 'mesh', split_axis=0, concat_axis=0, tiled=True)  23 us
    pallas_call x11, Pallas kernels, call(): pl.pallas_call(kernel, out_shape=[jax.ShapeDtypeStruct(s, d) for s, d in...  21.9 us
    ppermute x8, starting transfers between devices, swap(): return lax.ppermute(x, 'inst', [(i, i ^ bit) for i in range(PARTS)])  13 us
    ppermute x6, starting transfers between devices, shift(): lax.ppermute(x, 'mesh', [(i, (i + by) % SLABS) for i in range(SLABS)])  8.68 us
    all_to_all x2, starting transfers between devices, inst_split(): return lax.all_to_all(x, 'inst', split_axis=0, concat_axis=0, tiled=True)  8.29 us
    all_to_all x2, waiting for transfers between devices, exchange(): lax.all_to_all(chunk, 'mesh', split_axis=0, concat_axis=0, tiled=True)  4.91 us
    all_to_all x2, waiting for transfers between devices, inst_split(): return lax.all_to_all(x, 'inst', split_axis=0, concat_axis=0, tiled=True)  3.16 us
    ppermute x6, waiting for transfers between devices, shift(): lax.ppermute(x, 'mesh', [(i, (i + by) % SLABS) for i in range(SLABS)])  2.46 us
  transfers between devices with their start and end apart: 18, of which 6 were waited for; matrix products, arithmetic and copies ran while one was open for 0% of the time, Pallas kernels for 14%

profile of v6, /device:TPU:1, one launch (start us, length us, event | category | flops | bytes accessed | tf_op | source)
XLA Modules:
  0.0 90.6 jit_solution(14841608054338781882)
XLA Ops:
  0.6 5.4 %shard_map.113 = (s32[24,128]{1,0:T(8,128)}, f32[32,8,128]{2,1,0:T(8,128)}, f32[14,32,128]{2,1,0:T(8,128)}, f32[14,32,128]{2,1,0:T(8,128)}, f32[16,128]{1,0:T(8,...) custom-call(s32[1]{0:T(128)} %bitcast.p_ref.refs_0_, ...), custom_call_target="tpu_custom_call" | custom-call | tf_op jit(solution)/shard_map/pallas_call | solution.py:398
  6.0 2.1 %collective-permute-start.4 = (f32[4,12,16,128]{3,2,1,0:T(8,128)}, f32[4,12,16,128]{3,2,1,0:T(8,128)S(1)}, u32[]{:S(2)}, u32[]{:S(2)}) collective-permute-start(f32[4,12,16,128]{3,2,1,0:T(8,128)} %get-tuple-element.37), channel_id=1, source_target_pairs={{0,1},{1,0},{2,3},{3,2},{4,5},{5,4},{6,7},{7,6},{8,9},{9,8},{10,11... | collective-permute-start | bytes 1179656 | tf_op jit(solution)/shard_map/ppermute | solution.py:418
  8.2 11.9 %all-to-all-start = ((f32[32,8,128]{2,1,0:T(8,128)}), f32[32,8,128]{2,1,0:T(8,128)S(1)}, u32[]{:S(2)}, u32[]{:S(2)}) async-start(f32[32,8,128]{2,1,0:T(8,128)} %get-tuple-element.30), calls=%async_computation | async-start | bytes 262144 | tf_op jit(solution)/shard_map/all_to_all | solution.py:414
  20.1 1.7 %collective-permute-start = (f32[14,32,128]{2,1,0:T(8,128)}, f32[14,32,128]{2,1,0:T(8,128)S(1)}, u32[]{:S(2)}, u32[]{:S(2)}) collective-permute-start(f32[14,32,128]{2,1,0:T(8,128)} %get-tuple-element.31), channel_id=1, source_target_pairs={{0,8},{8,16},{16,24},{24,32},{32,40},{40,48},{48,56},{56,64},{64,7... | collective-permute-start | bytes 688136 | tf_op jit(solution)/shard_map/ppermute | solution.py:409
  21.8 1.2 %collective-permute-start.2 = (f32[16,128]{1,0:T(8,128)S(1)}, f32[16,128]{1,0:T(8,128)S(1)}, u32[]{:S(2)}, u32[]{:S(2)}) collective-permute-start(f32[16,128]{1,0:T(8,128)S(1)} %copy-done.12), channel_id=1, source_target_pairs={{0,16},{8,24},{16,32},{24,40},{32,48},{40,56},{48,64},{56,72},{64,... | collective-permute-start | bytes 24584 | tf_op jit(solution)/shard_map/ppermute | solution.py:409
  23.0 3.9 %collective-permute-start.3 = (f32[16,128]{1,0:T(8,128)S(1)}, f32[16,128]{1,0:T(8,128)S(1)}, u32[]{:S(2)}, u32[]{:S(2)}) collective-permute-start(f32[16,128]{1,0:T(8,128)S(1)} %copy-done.11), channel_id=1, source_target_pairs={{0,240},{8,248},{16,0},{24,8},{32,16},{40,24},{48,32},{56,40},{64,... | collective-permute-start | bytes 24584 | tf_op jit(solution)/shard_map/ppermute | solution.py:409
  28.7 2.9 %collective-permute-start.6 = (f32[2,12,16,128]{3,2,1,0:T(8,128)}, f32[2,12,16,128]{3,2,1,0:T(8,128)S(1)}, u32[]{:S(2)}, u32[]{:S(2)}) collective-permute-start(f32[2,12,16,128]{3,2,1,0:T(8,128)} %get-tuple-element.41), channel_id=1, source_target_pairs={{0,4},{1,5},{2,6},{3,7},{4,0},{5,1},{6,2},{7,3},{8,12},{9,13},{10,... | collective-permute-start | bytes 589832 | tf_op jit(solution)/shard_map/ppermute | solution.py:418
  31.8 2.7 %collective-permute-start.7 = (f32[2,12,16,128]{3,2,1,0:T(8,128)}, f32[2,12,16,128]{3,2,1,0:T(8,128)S(1)}, u32[]{:S(2)}, u32[]{:S(2)}) collective-permute-start(f32[2,12,16,128]{3,2,1,0:T(8,128)} %get-tuple-element.42), channel_id=1, source_target_pairs={{0,6},{1,7},{2,4},{3,5},{4,2},{5,3},{6,0},{7,1},{8,14},{9,15},{10,... | collective-permute-start | bytes 589832 | tf_op jit(solution)/shard_map/ppermute | solution.py:418
  35.3 2.5 %shard_map.116 = (s32[24,128]{1,0:T(8,128)S(1)}, f32[24,128]{1,0:T(8,128)S(1)}, f32[8,12,384]{2,1,0:T(8,128)S(1)}) custom-call(s32[1]{0:T(128)} %bitcast.p_ref.refs_0_, f32[32,8,128]{2,1,0:T(8,128)S(1)} %all-to-all-done.chunk_ref, f32[14,32,128]{2,1,0:T(8,128)S(1)} %collective-permute-done.up_ref.refs_6_, ...), custom_call_target="tpu_custom_call" | custom-call | tf_op jit(solution)/shard_map/pallas_call | solution.py:398
  38.5 3.5 %all-to-all-start.1 = ((f32[8,12,384]{2,1,0:T(8,128)}), f32[8,12,384]{2,1,0:T(8,128)S(1)}, u32[]{:S(2)}, u32[]{:S(2)}) async-start(f32[8,12,384]{2,1,0:T(8,128)} %copy-done.6), calls=%async_computation.1 | async-start | bytes 393216 | tf_op jit(solution)/shard_map/all_to_all | solution.py:422
  42.1 2.7 %shard_map.117 = (f32[2,12,16,128]{3,2,1,0:T(8,128)S(1)}, f32[2,12,16,128]{3,2,1,0:T(8,128)}, f32[2,12,16,128]{3,2,1,0:T(8,128)}, f32[2,12,16,128]{3,2,1,0:T(8,128)S(1)}) custom-call(s32[1]{0:T(128)} %bitcast.1.me_ref, f32[4,12,16,128]{3,2,1,0:T(8,128)S(1)} %copy-done.3, f32[4,12,16,128]{3,2,1,0:T(8,128)S(1)} %collective-permute-done.4.other_ref, ...), custom_call_target="tpu_custom_call" | custom-call | tf_op jit(solution)/shard_map/pallas_call | solution.py:398
  44.8 1.4 %collective-permute-start.10 = (f32[2,12,16,128]{3,2,1,0:T(8,128)}, f32[2,12,16,128]{3,2,1,0:T(8,128)S(1)}, u32[]{:S(2)}, u32[]{:S(2)}) collective-permute-start(f32[2,12,16,128]{3,2,1,0:T(8,128)} %get-tuple-element.51), channel_id=1, source_target_pairs={{0,2},{1,3},{2,0},{3,1},{4,6},{5,7},{6,4},{7,5},{8,10},{9,11},{10,... | collective-permute-start | bytes 589832 | tf_op jit(solution)/shard_map/ppermute | solution.py:418
  46.3 2.4 %collective-permute-start.11 = (f32[2,12,16,128]{3,2,1,0:T(8,128)}, f32[2,12,16,128]{3,2,1,0:T(8,128)S(1)}, u32[]{:S(2)}, u32[]{:S(2)}) collective-permute-start(f32[2,12,16,128]{3,2,1,0:T(8,128)} %get-tuple-element.52), channel_id=1, source_target_pairs={{0,4},{1,5},{2,6},{3,7},{4,0},{5,1},{6,2},{7,3},{8,12},{9,13},{10,... | collective-permute-start | bytes 589832 | tf_op jit(solution)/shard_map/ppermute | solution.py:418
  49.8 4.8 %all-to-all-start.2 = ((f32[8,12,384]{2,1,0:T(8,128)}), f32[8,12,384]{2,1,0:T(8,128)S(1)}, u32[]{:S(2)}, u32[]{:S(2)}) async-start(f32[8,12,384]{2,1,0:T(8,128)} %shard_map.118), calls=%async_computation.2 | async-start | bytes 393216 | tf_op jit(solution)/shard_map/all_to_all | solution.py:422
  55.5 1.0 %collective-permute-done.12.y3_ref = f32[2,12,16,128]{3,2,1,0:T(8,128)S(1)} collective-permute-done((f32[2,12,16,128]{3,2,1,0:T(8,128)S(1)}, f32[2,12,16,128]{3,2,1,0:T(8,128)S(1)}, u32[]{:S(2)}, u32[]{:S(2)}) %collective-permute-start.12) | collective-permute-done | bytes 196640 | tf_op jit(solution)/shard_map/ppermute | solution.py:418
  56.6 1.2 %collective-permute-start.13 = (f32[4,12,16,128]{3,2,1,0:T(8,128)S(1)}, f32[4,12,16,128]{3,2,1,0:T(8,128)}, u32[]{:S(2)}, u32[]{:S(2)}) collective-permute-start(f32[4,12,16,128]{3,2,1,0:T(8,128)S(1)} %shard_map.122), channel_id=1, source_target_pairs={{0,1},{1,0},{2,3},{3,2},{4,5},{5,4},{6,7},{7,6},{8,9},{9,8},{10,11... | collective-permute-start | bytes 1179656 | tf_op jit(solution)/shard_map/ppermute | solution.py:418
  57.8 3.2 %all-to-all-done.2.force_ref = f32[8,12,384]{2,1,0:T(8,128)S(1)} async-done(((f32[8,12,384]{2,1,0:T(8,128)}), f32[8,12,384]{2,1,0:T(8,128)S(1)}, u32[]{:S(2)}, u32[]{:S(2)}) %all-to-all-start.2) | async-done | bytes 147488 | tf_op jit(solution)/shard_map/all_to_all | solution.py:422
  61.8 11.1 %all-to-all-start.3 = ((f32[32,12,128]{2,1,0:T(8,128)}), f32[32,12,128]{2,1,0:T(8,128)S(1)}, u32[]{:S(2)}, u32[]{:S(2)}) async-start(f32[32,12,128]{2,1,0:T(8,128)} %get-tuple-element.44), calls=%async_computation.3 | async-start | bytes 524288 | tf_op jit(solution)/shard_map/all_to_all | solution.py:414
  72.9 1.9 %collective-permute-start.8 = (f32[2,12,128]{2,1,0:T(8,128)S(1)}, f32[2,12,128]{2,1,0:T(8,128)S(1)}, u32[]{:S(2)}, u32[]{:S(2)}) collective-permute-start(f32[2,12,128]{2,1,0:T(8,128)S(1)} %get-tuple-element.45), channel_id=1, source_target_pairs={{0,8},{8,16},{16,24},{24,32},{32,40},{40,48},{48,56},{56,64},{64,7... | collective-permute-start | bytes 36872 | tf_op jit(solution)/shard_map/ppermute | solution.py:409
  74.9 1.6 %shard_map.120 = (f32[12,4,32,128]{3,2,1,0:T(8,128)S(1)}, f32[4,32,128]{2,1,0:T(8,128)S(1)}) custom-call(s32[1]{0:T(128)} %bitcast.p_ref.refs_0_, f32[16,4]{1,0:T(8,128)S(1)} %copy.12.refs_1_, s32[4,32,128]{2,1,0:T(8,128)S(1)} %copy-done.5, f32[6,4,32,128]{3,2,1,0:T(8,128)S(1)} %bitcast.13, f32[6,4,32,128]{3,2,1,0:T(8,128)S(1)} %bitcast.16, ...), custom_call_target="tpu_custom_call" | custom-call | tf_op jit(solution)/shard_map/pallas_call | solution.py:398
  76.5 2.6 %shard_map.121.part_ref = f32[12,4,32,128]{3,2,1,0:T(8,128)S(1)} custom-call(s32[24,128]{1,0:T(8,128)S(1)} %get-tuple-element.48.idx_ref, f32[8,12,384]{2,1,0:T(8,128)S(1)} %all-to-all-done.2.force_ref, f32[12,4,32,128]{3,2,1,0:T(8,128)S(1)} %get-tuple-element.49.lin_ref), custom_call_target="tpu_custom_call" | custom-call | tf_op jit(solution)/shard_map/pallas_call | solution.py:398
  79.1 2.3 %collective-permute-done.9.down_ref = f32[2,12,128]{2,1,0:T(8,128)S(1)} collective-permute-done((f32[2,12,128]{2,1,0:T(8,128)S(1)}, f32[2,12,128]{2,1,0:T(8,128)S(1)}, u32[]{:S(2)}, u32[]{:S(2)}) %collective-permute-start.9) | collective-permute-done | bytes 12320 | tf_op jit(solution)/shard_map/ppermute | solution.py:409
  81.4 4.9 %all-to-all-done.3.chunk_ref = f32[32,12,128]{2,1,0:T(8,128)S(1)} async-done(((f32[32,12,128]{2,1,0:T(8,128)}), f32[32,12,128]{2,1,0:T(8,128)S(1)}, u32[]{:S(2)}, u32[]{:S(2)}) %all-to-all-start.3) | async-done | bytes 196640 | tf_op jit(solution)/shard_map/all_to_all | solution.py:414
  86.3 4.2 %shard_map.123 = (f32[6,4,32,128]{3,2,1,0:T(8,128)}, f32[6,4,32,128]{3,2,1,0:T(8,128)}) custom-call(s32[1]{0:T(128)} %bitcast.p_ref.refs_0_, s32[1]{0:T(128)} %bitcast.1.me_ref, s32[24,128]{1,0:T(8,128)S(1)} %copy-done.9, f32[32,12,128]{2,1,0:T(8,128)S(1)} %all-to-all-done.3.chunk_ref, f32[2,12,128]{2,1,0:T(8,128)S(1)} %collective-permute-done.8.up_ref, ...), custom_call_target="tpu_custom_call" | custom-call | tf_op jit(solution)/shard_map/pallas_call | solution.py:398
  (50 shorter events, 6.4 us)
Async XLA Ops:
  6.0 20.8 %collective-permute-start.4 = (f32[4,12,16,128]{3,2,1,0:T(8,128)}, f32[4,12,16,128]{3,2,1,0:T(8,128)S(1)}, u32[]{:S(2)}, u32[]{:S(2)}) collective-permute-start(f32[4,12,16,128]{3,2,1,0:T(8,128)} %get-tuple-element.37), channel_id=1, source_target_pairs={{0,1},{1,0},{2,3},{3,2},{4,5},{5,4},{6,7},{7,6},{8,9},{9,8},{10,11... | collective-permute-start | bytes 1179656 | tf_op jit(solution)/shard_map/ppermute | solution.py:418
  8.2 13.6 %copy-start.12 = (f32[16,128]{1,0:T(8,128)S(1)}, f32[16,128]{1,0:T(8,128)}, u32[]{:S(2)}) copy-start(f32[16,128]{1,0:T(8,128)} %get-tuple-element.33) | copy-start | bytes 24580
  8.2 14.8 %copy-start.11 = (f32[16,128]{1,0:T(8,128)S(1)}, f32[16,128]{1,0:T(8,128)}, u32[]{:S(2)}) copy-start(f32[16,128]{1,0:T(8,128)} %get-tuple-element.34) | copy-start | bytes 24580
  8.2 26.5 %all-to-all-start = ((f32[32,8,128]{2,1,0:T(8,128)}), f32[32,8,128]{2,1,0:T(8,128)S(1)}, u32[]{:S(2)}, u32[]{:S(2)}) async-start(f32[32,8,128]{2,1,0:T(8,128)} %get-tuple-element.30), calls=%async_computation | async-start | bytes 262144 | tf_op jit(solution)/shard_map/all_to_all | solution.py:414
  20.1 14.6 %collective-permute-start = (f32[14,32,128]{2,1,0:T(8,128)}, f32[14,32,128]{2,1,0:T(8,128)S(1)}, u32[]{:S(2)}, u32[]{:S(2)}) collective-permute-start(f32[14,32,128]{2,1,0:T(8,128)} %get-tuple-element.31), channel_id=1, source_target_pairs={{0,8},{8,16},{16,24},{24,32},{32,40},{40,48},{48,56},{56,64},{64,7... | collective-permute-start | bytes 688136 | tf_op jit(solution)/shard_map/ppermute | solution.py:409
  21.8 12.9 %collective-permute-start.1 = (f32[14,32,128]{2,1,0:T(8,128)}, f32[14,32,128]{2,1,0:T(8,128)S(1)}, u32[]{:S(2)}, u32[]{:S(2)}) collective-permute-start(f32[14,32,128]{2,1,0:T(8,128)} %get-tuple-element.32), channel_id=1, source_target_pairs={{0,248},{8,0},{16,8},{24,16},{32,24},{40,32},{48,40},{56,48},{64,5... | collective-permute-start | bytes 688136 | tf_op jit(solution)/shard_map/ppermute | solution.py:409
  21.8 10.0 %collective-permute-start.2 = (f32[16,128]{1,0:T(8,128)S(1)}, f32[16,128]{1,0:T(8,128)S(1)}, u32[]{:S(2)}, u32[]{:S(2)}) collective-permute-start(f32[16,128]{1,0:T(8,128)S(1)} %copy-done.12), channel_id=1, source_target_pairs={{0,16},{8,24},{16,32},{24,40},{32,48},{40,56},{48,64},{56,72},{64,... | collective-permute-start | bytes 24584 | tf_op jit(solution)/shard_map/ppermute | solution.py:409
  23.0 11.6 %collective-permute-start.3 = (f32[16,128]{1,0:T(8,128)S(1)}, f32[16,128]{1,0:T(8,128)S(1)}, u32[]{:S(2)}, u32[]{:S(2)}) collective-permute-start(f32[16,128]{1,0:T(8,128)S(1)} %copy-done.11), channel_id=1, source_target_pairs={{0,240},{8,248},{16,0},{24,8},{32,16},{40,24},{48,32},{56,40},{64,... | collective-permute-start | bytes 24584 | tf_op jit(solution)/shard_map/ppermute | solution.py:409
  28.7 13.3 %collective-permute-start.6 = (f32[2,12,16,128]{3,2,1,0:T(8,128)}, f32[2,12,16,128]{3,2,1,0:T(8,128)S(1)}, u32[]{:S(2)}, u32[]{:S(2)}) collective-permute-start(f32[2,12,16,128]{3,2,1,0:T(8,128)} %get-tuple-element.41), channel_id=1, source_target_pairs={{0,4},{1,5},{2,6},{3,7},{4,0},{5,1},{6,2},{7,3},{8,12},{9,13},{10,... | collective-permute-start | bytes 589832 | tf_op jit(solution)/shard_map/ppermute | solution.py:418
  31.8 10.2 %collective-permute-start.7 = (f32[2,12,16,128]{3,2,1,0:T(8,128)}, f32[2,12,16,128]{3,2,1,0:T(8,128)S(1)}, u32[]{:S(2)}, u32[]{:S(2)}) collective-permute-start(f32[2,12,16,128]{3,2,1,0:T(8,128)} %get-tuple-element.42), channel_id=1, source_target_pairs={{0,6},{1,7},{2,4},{3,5},{4,2},{5,3},{6,0},{7,1},{8,14},{9,15},{10,... | collective-permute-start | bytes 589832 | tf_op jit(solution)/shard_map/ppermute | solution.py:418
  34.5 7.5 %collective-permute-start.5 = (f32[2,12,16,128]{3,2,1,0:T(8,128)}, f32[2,12,16,128]{3,2,1,0:T(8,128)S(1)}, u32[]{:S(2)}, u32[]{:S(2)}) collective-permute-start(f32[2,12,16,128]{3,2,1,0:T(8,128)} %get-tuple-element.38.after_ref), channel_id=1, source_target_pairs={{0,2},{1,3},{2,0},{3,1},{4,6},{5,7},{6,4},{7,5},{8,10},{9,11},{10,... | collective-permute-start | bytes 589832 | tf_op jit(solution)/shard_map/ppermute | solution.py:418
  38.5 10.3 %all-to-all-start.1 = ((f32[8,12,384]{2,1,0:T(8,128)}), f32[8,12,384]{2,1,0:T(8,128)S(1)}, u32[]{:S(2)}, u32[]{:S(2)}) async-start(f32[8,12,384]{2,1,0:T(8,128)} %copy-done.6), calls=%async_computation.1 | async-start | bytes 393216 | tf_op jit(solution)/shard_map/all_to_all | solution.py:422
  42.0 6.7 %copy-start.7 = (f32[48,48]{1,0:T(8,128)S(1)}, f32[48,48]{1,0:T(8,128)}, u32[]{:S(2)}) copy-start(f32[48,48]{1,0:T(8,128)} %constant.11.clone.spread_ref) | copy-start | bytes 27652
  44.8 9.7 %collective-permute-start.10 = (f32[2,12,16,128]{3,2,1,0:T(8,128)}, f32[2,12,16,128]{3,2,1,0:T(8,128)S(1)}, u32[]{:S(2)}, u32[]{:S(2)}) collective-permute-start(f32[2,12,16,128]{3,2,1,0:T(8,128)} %get-tuple-element.51), channel_id=1, source_target_pairs={{0,2},{1,3},{2,0},{3,1},{4,6},{5,7},{6,4},{7,5},{8,10},{9,11},{10,... | collective-permute-start | bytes 589832 | tf_op jit(solution)/shard_map/ppermute | solution.py:418
  46.3 9.3 %collective-permute-start.11 = (f32[2,12,16,128]{3,2,1,0:T(8,128)}, f32[2,12,16,128]{3,2,1,0:T(8,128)S(1)}, u32[]{:S(2)}, u32[]{:S(2)}) collective-permute-start(f32[2,12,16,128]{3,2,1,0:T(8,128)} %get-tuple-element.52), channel_id=1, source_target_pairs={{0,4},{1,5},{2,6},{3,7},{4,0},{5,1},{6,2},{7,3},{8,12},{9,13},{10,... | collective-permute-start | bytes 589832 | tf_op jit(solution)/shard_map/ppermute | solution.py:418
  48.7 7.9 %collective-permute-start.12 = (f32[2,12,16,128]{3,2,1,0:T(8,128)S(1)}, f32[2,12,16,128]{3,2,1,0:T(8,128)S(1)}, u32[]{:S(2)}, u32[]{:S(2)}) collective-permute-start(f32[2,12,16,128]{3,2,1,0:T(8,128)S(1)} %get-tuple-element.53), channel_id=1, source_target_pairs={{0,6},{1,7},{2,4},{3,5},{4,2},{5,3},{6,0},{7,1},{8,14},{9,15},{10,... | collective-permute-start | bytes 589832 | tf_op jit(solution)/shard_map/ppermute | solution.py:418
  49.8 11.2 %all-to-all-start.2 = ((f32[8,12,384]{2,1,0:T(8,128)}), f32[8,12,384]{2,1,0:T(8,128)S(1)}, u32[]{:S(2)}, u32[]{:S(2)}) async-start(f32[8,12,384]{2,1,0:T(8,128)} %shard_map.118), calls=%async_computation.2 | async-start | bytes 393216 | tf_op jit(solution)/shard_map/all_to_all | solution.py:422
  56.6 18.3 %copy-start.4 = (f32[2,3,4,32,128]{4,3,2,1,0:T(8,128)S(1)}, f32[2,3,4,32,128]{4,3,2,1,0:T(8,128)}, u32[]{:S(2)}) copy-start(f32[2,3,4,32,128]{4,3,2,1,0:T(8,128)} %param.12) | copy-start | bytes 1179652
  56.6 29.7 %collective-permute-start.13 = (f32[4,12,16,128]{3,2,1,0:T(8,128)S(1)}, f32[4,12,16,128]{3,2,1,0:T(8,128)}, u32[]{:S(2)}, u32[]{:S(2)}) collective-permute-start(f32[4,12,16,128]{3,2,1,0:T(8,128)S(1)} %shard_map.122), channel_id=1, source_target_pairs={{0,1},{1,0},{2,3},{3,2},{4,5},{5,4},{6,7},{7,6},{8,9},{9,8},{10,11... | collective-permute-start | bytes 1179656 | tf_op jit(solution)/shard_map/ppermute | solution.py:418
  61.8 13.1 %copy-start.5 = (s32[4,32,128]{2,1,0:T(8,128)S(1)}, s32[4,32,128]{2,1,0:T(8,128)}, u32[]{:S(2)}) copy-start(s32[4,32,128]{2,1,0:T(8,128)} %refs_2_.1) | copy-start | bytes 196612
  61.8 24.5 %all-to-all-start.3 = ((f32[32,12,128]{2,1,0:T(8,128)}), f32[32,12,128]{2,1,0:T(8,128)S(1)}, u32[]{:S(2)}, u32[]{:S(2)}) async-start(f32[32,12,128]{2,1,0:T(8,128)} %get-tuple-element.44), calls=%async_computation.3 | async-start | bytes 524288 | tf_op jit(solution)/shard_map/all_to_all | solution.py:414
  72.9 6.2 %collective-permute-start.8 = (f32[2,12,128]{2,1,0:T(8,128)S(1)}, f32[2,12,128]{2,1,0:T(8,128)S(1)}, u32[]{:S(2)}, u32[]{:S(2)}) collective-permute-start(f32[2,12,128]{2,1,0:T(8,128)S(1)} %get-tuple-element.45), channel_id=1, source_target_pairs={{0,8},{8,16},{16,24},{24,32},{32,40},{40,48},{48,56},{56,64},{64,7... | collective-permute-start | bytes 36872 | tf_op jit(solution)/shard_map/ppermute | solution.py:409
  74.8 6.6 %collective-permute-start.9 = (f32[2,12,128]{2,1,0:T(8,128)S(1)}, f32[2,12,128]{2,1,0:T(8,128)S(1)}, u32[]{:S(2)}, u32[]{:S(2)}) collective-permute-start(f32[2,12,128]{2,1,0:T(8,128)S(1)} %get-tuple-element.46), channel_id=1, source_target_pairs={{0,248},{8,0},{16,8},{24,16},{32,24},{40,32},{48,40},{56,48},{64,5... | collective-permute-start | bytes 36872 | tf_op jit(solution)/shard_map/ppermute | solution.py:409
  76.5 9.8 %copy-start.9 = (s32[24,128]{1,0:T(8,128)S(1)}, s32[24,128]{1,0:T(8,128)}, u32[]{:S(2)}) copy-start(s32[24,128]{1,0:T(8,128)} %get-tuple-element.29.idx_ref) | copy-start | bytes 36868
  (7 other events, 21.2 us)

commit v7 on v6

--- a/solution.py
+++ b/solution.py
@@ -37,14 +37,6 @@
 
 def far_place(offset):
     return 8 + (offset - 3) // 3, SEG * ((offset - 3) % 3)
-
-
-def pack(rows, seg):
-    return jnp.where(lanes(8) < 64, lane_roll(rows[:8], -seg), lane_roll(rows[8:], 64 - seg))
-
-
-def unpack(chunk):
-    return jnp.concatenate([chunk, lane_roll(chunk, 64)], axis=0)
 
 
 def lane_roll(x, shift):
@@ -152,8 +144,8 @@
 
 
 def list_kernel(p_ref, me_ref, owner_hbm, local_hbm, remote_hbm, kind_hbm, disp_hbm, dir_hbm, ids_hbm,
-                idx_ref, chunk_ref, up_hbm, down_hbm, up2_ref, down2_ref, self_ref, same_hbm, other_hbm,
-                parts_ref, rows_ref, owner_ref, local_ref, remote_ref, kind_ref, disp_ref, dir_ref, ids_ref, near_ref,
+                idx_ref, chunk_ref, up_ref, down_ref, self_ref, same_hbm, other_hbm, high_hbm, low_hbm,
+                parts_ref, rows_ref, owner_ref, local_ref, remote_ref, kind_ref, disp_ref, dir_ref, ids_ref, edge_ref,
                 sems, more_sems):
     p = p_ref[0]
     pairs = ((owner_hbm, owner_ref), (local_hbm, local_ref), (remote_hbm, remote_ref), (kind_hbm, kind_ref),
@@ -178,43 +170,41 @@
             block = me_ref[0] ^ k
             rows = pl.ds(pl.multiple_of(16 * (block & 1), 16), 16)
             moves.append((ref.at[:, block >> 1, rows, :], (same_hbm, other_hbm)[k % 2].at[k // 2, part]))
-        moves.append((ref.at[:, 3], up_hbm.at[pl.ds(1 + 6 * field, 6)]))
-        moves.append((ref.at[:, 0], down_hbm.at[pl.ds(1 + 6 * field, 6)]))
+        moves.append((ref.at[:, 3], high_hbm.at[pl.ds(6 * field, 6)]))
+        moves.append((ref.at[:, 0], low_hbm.at[pl.ds(6 * field, 6)]))
     moves = [pltpu.make_async_copy(a, b, more_sems.at[k]) for k, (a, b) in enumerate(moves)]
     for move in moves:
         move.start()
     split_fields(disp_ref, dir_ref, parts_ref)
-    near_ref[2] = (ids_ref[3] + 1).astype(f32)
-    near_ref[3] = (ids_ref[0] + 1).astype(f32)
-    gather_rows(parts_ref, idx_ref, rows_ref)
-    for k in range(2):
-        near_ref[k] = rows_ref[2 + 2 * k : 4 + 2 * k].reshape(32, 128)
-    ends = ((near_ref.at[0], up_hbm.at[0]), (near_ref.at[1], down_hbm.at[0]),
-            (near_ref.at[2], up_hbm.at[13]), (near_ref.at[3], down_hbm.at[13]))
-    ends = [pltpu.make_async_copy(a, b, sems.at[7 + k]) for k, (a, b) in enumerate(ends)]
+    ends = []
+    for k, (x, hbm) in enumerate(((3, high_hbm), (0, low_hbm))):
+        edge_ref[k] = (ids_ref[x] + 1).astype(f32)
+        ends.append(pltpu.make_async_copy(edge_ref.at[k], hbm.at[12], sems.at[7 + k]))
     for end in ends:
         end.start()
-    for d in (0, 1, 2, SLABS - 2, SLABS - 1):
-        chunk_ref[(p + d) & (SLABS - 1)] = jnp.zeros((8, 128), f32)
+    gather_rows(parts_ref, idx_ref, rows_ref)
+    for d in (0, 1, SLABS - 1):
+        chunk_ref[(p + d) & (SLABS - 1)] = jnp.zeros((16, 128), f32)
+    for d, tile in ((2, 6), (SLABS - 2, 7)):
+        chunk_ref[(p + d) & (SLABS - 1)] = rows_ref[tile]
     for d in range(3, SLABS - 2):
         tile, seg = far_place(d)
-        chunk_ref[(p + d) & (SLABS - 1)] = pack(rows_ref[tile], seg)
-    up2_ref[...] = rows_ref[6]
-    down2_ref[...] = rows_ref[7]
+        chunk_ref[(p + d) & (SLABS - 1)] = lane_roll(rows_ref[tile], -seg)
     self_ref[...] = rows_ref[0:2]
+    up_ref[...] = rows_ref[2:4]
+    down_ref[...] = rows_ref[4:6]
     for move in moves + ends:
         move.wait()
 
 
-def gap_kernel(p_ref, chunk_ref, up_ref, down_ref, up2_ref, down2_ref, self_ref, parts_ref, after_ref,
+def gap_kernel(p_ref, chunk_ref, up_ref, down_ref, self_ref, parts_ref, after_ref,
                idx_ref, kind_ref, gap_ref, here_ref):
     p = p_ref[0]
 
     def asked(d):
-        return unpack(chunk_ref[(p - d) & (SLABS - 1)])
-
-    near = [ref[0, 16 * k : 16 * (k + 1), :] for ref in (up_ref, down_ref) for k in range(2)]
-    tiles = [self_ref[0], self_ref[1]] + near + [up2_ref[...], down2_ref[...]]
+        return chunk_ref[(p - d) & (SLABS - 1)]
+
+    tiles = [self_ref[0], self_ref[1], up_ref[0], up_ref[1], down_ref[0], down_ref[1], asked(2), asked(SLABS - 2)]
     tiles += merge_far(asked, 16, 0.0)
     beyond = lanes(1) >= 3 * SEG
     rows = [t[12:13] for t in tiles[:8]] + [jnp.where(beyond, -1.0, t[12:13]) for t in tiles[8:]]
@@ -352,10 +342,10 @@
     return out
 
 
-def stiff_kernel(p_ref, mat_ref, ids_ref, disp_ref, dir_ref, forcing_ref, up_ref, down_ref, out_ref, mass_ref, *, materials):
+def stiff_kernel(p_ref, mat_ref, ids_ref, disp_ref, dir_ref, forcing_ref, low_ref, high_ref, out_ref, mass_ref, *, materials):
     p = p_ref[0]
-    low = jnp.where(p > 0, up_ref[1:14], 0.0)
-    high = jnp.where(p < SLABS - 1, down_ref[1:14], 0.0)
+    low = jnp.where(p > 0, low_ref[...], 0.0)
+    high = jnp.where(p < SLABS - 1, high_ref[...], 0.0)
     ids = ids_ref[...]
     kx, ky, kz, mass = [lookup(ids, mat_ref, col, materials) for col in range(4)]
     mass_ref[...] = mass
@@ -405,12 +395,13 @@
     )(*args)
 
 
-def shift(x, by):
-    return lax.ppermute(x, "mesh", [(i, (i + by) % SLABS) for i in range(SLABS)])
+def shift(x, by, wrap=True):
+    pairs = [(i, (i + by) % SLABS) for i in range(SLABS) if wrap or 0 <= i + by < SLABS]
+    return lax.ppermute(x, "mesh", pairs)
 
 
 def exchange(chunk, *near):
-    near = [shift(x, by) for x, by in zip(near, (1, -1, 2, -2))]
+    near = [shift(x, by) for x, by in zip(near, (1, -1))]
     return lax.all_to_all(chunk, "mesh", split_axis=0, concat_axis=0, tiled=True), *near
 
 
@@ -434,12 +425,11 @@
     parts = (768, 512)
     index = ((24, 128), i32)
     half = ((4, 12, 16, 128), f32)
-    near = ((14, 32, 128), f32)
-    tile = ((16, 128), f32)
-
-    own_idx, chunk, *sides, own, same, other = call(
+    halo = ((13, 32, 128), f32)
+
+    own_idx, chunk, up, down, own, same, other, high, low = call(
         list_kernel,
-        [index, ((SLABS, 8, 128), f32), near, near, tile, tile, ((2, 16, 128), f32), half, half],
+        [index, ((SLABS, 16, 128), f32)] + [((2, 16, 128), f32)] * 3 + [half, half, halo, halo],
         p,
         me,
         joint_owner.reshape(1, count),
@@ -452,14 +442,14 @@
         smem=(0, 1),
         away=range(2, 9),
         limit=60 * 1024 * 1024,
-        kept=(2, 3, 7, 8),
+        kept=(5, 6, 7, 8),
         scratch=[pltpu.VMEM(parts, bf16), pltpu.VMEM((SIDE, 16, 128), f32)]
         + [pltpu.VMEM((1, count), i32)] * 4
         + [pltpu.VMEM(fields, f32)] * 2
-        + [pltpu.VMEM((4, 32, 128), i32), pltpu.VMEM((4, 32, 128), f32)]
-        + [pltpu.SemaphoreType.DMA((11,)), pltpu.SemaphoreType.DMA((20,))],
+        + [pltpu.VMEM((4, 32, 128), i32), pltpu.VMEM((2, 32, 128), f32)]
+        + [pltpu.SemaphoreType.DMA((9,)), pltpu.SemaphoreType.DMA((20,))],
     )
-    chunk, *sides = exchange(chunk, *sides)
+    chunk, up, down = exchange(chunk, up, down)
 
     pair = ((2, 12, 16, 128), f32)
     other = swap(other, 1)
@@ -473,8 +463,8 @@
     far_idx, kind, gap = call(
         gap_kernel,
         [index, ((24, 128), f32), part],
-        p, chunk, *sides, own, fields_parts, joined[0],
-        away=(8,),
+        p, chunk, up, down, own, fields_parts, joined[0],
+        away=(6,),
         scratch=[pltpu.VMEM((SIDE, 12, 128), f32)],
     )
     force = call(
@@ -493,7 +483,7 @@
     lin, mass = call(
         lambda *refs: stiff_kernel(*refs, materials=materials.shape[0]),
         [(whole, f32), ((4, 32, 128), f32)],
-        p, materials, material_ids, disp, dire, forcing.reshape(fields), *sides[:2],
+        p, materials, material_ids, disp, dire, forcing.reshape(fields), shift(high, 1, False), shift(low, -1, False),
         smem=(0, 1),
     )
     other = swap(call(turn_kernel, [half], *turned, smem=())[0], 1)

time: 91.3 us -> 96.8 us (1.060)
  the two profiles are of different devices: /device:TPU:1 before, /device:TPU:4 now
where the time goes in v7:
time: 96.8 us; the launch traced here: 96.1 us
  starting transfers between devices  61.8 us (64%)
  Pallas kernels  22.1 us (23%)
  waiting for transfers between devices  7.88 us (8%)
  local copies, waits for them, and re-layouts  3.3 us (3%)
  between operations  1.1 us (1%)
    pallas_call x11, Pallas kernels, call(): pl.pallas_call(kernel, out_shape=[jax.ShapeDtypeStruct(s, d) for s, d in...  22.1 us
    ppermute x6, starting transfers between devices, shift(): return lax.ppermute(x, 'mesh', pairs)  20 us
    all_to_all x2, starting transfers between devices, exchange(): lax.all_to_all(chunk, 'mesh', split_axis=0, concat_axis=0, tiled=True)  19.7 us
    ppermute x8, starting transfers between devices, swap(): return lax.ppermute(x, 'inst', [(i, i ^ bit) for i in range(PARTS)])  12.4 us
    all_to_all x2, starting transfers between devices, inst_split(): return lax.all_to_all(x, 'inst', split_axis=0, concat_axis=0, tiled=True)  9.78 us
    ppermute x8, waiting for transfers between devices, swap(): return lax.ppermute(x, 'inst', [(i, i ^ bit) for i in range(PARTS)])  4.39 us
    unnamed x35, local copies, waits for them, and re-layouts  3.3 us
    all_to_all x2, waiting for transfers between devices, inst_split(): return lax.all_to_all(x, 'inst', split_axis=0, concat_axis=0, tiled=True)  2.17 us
  transfers between devices with their start and end apart: 18, of which 5 were waited for; matrix products, arithmetic and copies ran while one was open for 1% of the time, Pallas kernels for 12%

profile of v7, /device:TPU:4, one launch (start us, length us, event | category | flops | bytes accessed | tf_op | source)
XLA Modules:
  0.0 96.1 jit_solution(10325555009263694080)
XLA Ops:
  0.6 4.9 %shard_map.113 = (s32[24,128]{1,0:T(8,128)}, f32[32,16,128]{2,1,0:T(8,128)}, f32[2,16,128]{2,1,0:T(8,128)}, f32[2,16,128]{2,1,0:T(8,128)}, f32[2,16,128]{2,1,0:T...) custom-call(s32[1]{0:T(128)} %bitcast.p_ref.refs_0_, ...), custom_call_target="tpu_custom_call" | custom-call | tf_op jit(solution)/shard_map/pallas_call | solution.py:388
  5.6 1.3 %collective-permute-start.2 = (f32[4,12,16,128]{3,2,1,0:T(8,128)}, f32[4,12,16,128]{3,2,1,0:T(8,128)S(1)}, u32[]{:S(2)}, u32[]{:S(2)}) collective-permute-start(f32[4,12,16,128]{3,2,1,0:T(8,128)} %get-tuple-element.35), channel_id=1, source_target_pairs={{0,1},{1,0},{2,3},{3,2},{4,5},{5,4},{6,7},{7,6},{8,9},{9,8},{10,11... | collective-permute-start | bytes 1179656 | tf_op jit(solution)/shard_map/ppermute | solution.py:409
  6.9 11.7 %all-to-all-start = ((f32[32,16,128]{2,1,0:T(8,128)}), f32[32,16,128]{2,1,0:T(8,128)S(1)}, u32[]{:S(2)}, u32[]{:S(2)}) async-start(f32[32,16,128]{2,1,0:T(8,128)} %get-tuple-element.30), calls=%async_computation | async-start | bytes 524288 | tf_op jit(solution)/shard_map/all_to_all | solution.py:405
  19.4 1.6 %collective-permute-start.3 = (f32[2,12,16,128]{3,2,1,0:T(8,128)S(1)}, f32[2,12,16,128]{3,2,1,0:T(8,128)S(1)}, u32[]{:S(2)}, u32[]{:S(2)}) collective-permute-start(f32[2,12,16,128]{3,2,1,0:T(8,128)S(1)} %get-tuple-element.36.after_ref), channel_id=1, source_target_pairs={{0,2},{1,3},{2,0},{3,1},{4,6},{5,7},{6,4},{7,5},{8,10},{9,11},{10,... | collective-permute-start | bytes 589832 | tf_op jit(solution)/shard_map/ppermute | solution.py:409
  21.0 2.9 %collective-permute-start.4 = (f32[2,12,16,128]{3,2,1,0:T(8,128)}, f32[2,12,16,128]{3,2,1,0:T(8,128)S(1)}, u32[]{:S(2)}, u32[]{:S(2)}) collective-permute-start(f32[2,12,16,128]{3,2,1,0:T(8,128)} %get-tuple-element.39), channel_id=1, source_target_pairs={{0,4},{1,5},{2,6},{3,7},{4,0},{5,1},{6,2},{7,3},{8,12},{9,13},{10,... | collective-permute-start | bytes 589832 | tf_op jit(solution)/shard_map/ppermute | solution.py:409
  24.2 5.3 %collective-permute-start.1 = (f32[2,16,128]{2,1,0:T(8,128)S(1)}, f32[2,16,128]{2,1,0:T(8,128)S(1)}, u32[]{:S(2)}, u32[]{:S(2)}) collective-permute-start(f32[2,16,128]{2,1,0:T(8,128)S(1)} %copy-done.15), channel_id=1, source_target_pairs={{0,248},{8,0},{16,8},{24,16},{32,24},{40,32},{48,40},{56,48},{64,5... | collective-permute-start | bytes 49160 | tf_op jit(solution)/shard_map/ppermute | solution.py:400
  29.7 1.3 %collective-permute-done.up_ref = f32[2,16,128]{2,1,0:T(8,128)S(1)} collective-permute-done((f32[2,16,128]{2,1,0:T(8,128)S(1)}, f32[2,16,128]{2,1,0:T(8,128)S(1)}, u32[]{:S(2)}, u32[]{:S(2)}) %collective-permute-start) | collective-permute-done | bytes 16416 | tf_op jit(solution)/shard_map/ppermute | solution.py:400
  31.0 2.5 %shard_map.116 = (s32[24,128]{1,0:T(8,128)S(1)}, f32[24,128]{1,0:T(8,128)S(1)}, f32[8,12,384]{2,1,0:T(8,128)S(1)}) custom-call(s32[1]{0:T(128)} %bitcast.p_ref.refs_0_, f32[32,16,128]{2,1,0:T(8,128)S(1)} %all-to-all-done.chunk_ref, f32[2,16,128]{2,1,0:T(8,128)S(1)} %collective-permute-done.up_ref, f32[2,16,128]{2,1,0:T(8,128)S(1)} %collective-permute-done.1.down_ref, ...), custom_call_target="tpu_custom_call" | custom-call | tf_op jit(solution)/shard_map/pallas_call | solution.py:388
  34.8 4.6 %all-to-all-start.1 = ((f32[8,12,384]{2,1,0:T(8,128)}), f32[8,12,384]{2,1,0:T(8,128)S(1)}, u32[]{:S(2)}, u32[]{:S(2)}) async-start(f32[8,12,384]{2,1,0:T(8,128)} %copy-done.5), calls=%async_computation.1 | async-start | bytes 393216 | tf_op jit(solution)/shard_map/all_to_all | solution.py:413
  39.3 2.0 %shard_map.117 = (f32[2,12,16,128]{3,2,1,0:T(8,128)S(1)}, f32[2,12,16,128]{3,2,1,0:T(8,128)S(1)}, f32[2,12,16,128]{3,2,1,0:T(8,128)S(1)}, f32[2,12,16,128]{3,2,1,0:T(8,128)S(1)}) custom-call(s32[1]{0:T(128)} %bitcast.1.me_ref, f32[4,12,16,128]{3,2,1,0:T(8,128)S(1)} %copy-done.2, f32[4,12,16,128]{3,2,1,0:T(8,128)S(1)} %collective-permute-done.2.other_ref, ...), custom_call_target="tpu_custom_call" | custom-call | tf_op jit(solution)/shard_map/pallas_call | solution.py:388
  41.4 2.1 %collective-permute-start.10 = (f32[2,12,16,128]{3,2,1,0:T(8,128)S(1)}, f32[2,12,16,128]{3,2,1,0:T(8,128)S(1)}, u32[]{:S(2)}, u32[]{:S(2)}) collective-permute-start(f32[2,12,16,128]{3,2,1,0:T(8,128)S(1)} %get-tuple-element.51), channel_id=1, source_target_pairs={{0,2},{1,3},{2,0},{3,1},{4,6},{5,7},{6,4},{7,5},{8,10},{9,11},{10,... | collective-permute-start | bytes 589832 | tf_op jit(solution)/shard_map/ppermute | solution.py:409
  43.5 2.7 %collective-permute-start.11 = (f32[2,12,16,128]{3,2,1,0:T(8,128)S(1)}, f32[2,12,16,128]{3,2,1,0:T(8,128)S(1)}, u32[]{:S(2)}, u32[]{:S(2)}) collective-permute-start(f32[2,12,16,128]{3,2,1,0:T(8,128)S(1)} %get-tuple-element.52), channel_id=1, source_target_pairs={{0,4},{1,5},{2,6},{3,7},{4,0},{5,1},{6,2},{7,3},{8,12},{9,13},{10,... | collective-permute-start | bytes 589832 | tf_op jit(solution)/shard_map/ppermute | solution.py:409
  47.4 5.2 %all-to-all-start.2 = ((f32[8,12,384]{2,1,0:T(8,128)}), f32[8,12,384]{2,1,0:T(8,128)S(1)}, u32[]{:S(2)}, u32[]{:S(2)}) async-start(f32[8,12,384]{2,1,0:T(8,128)} %shard_map.118), calls=%async_computation.2 | async-start | bytes 393216 | tf_op jit(solution)/shard_map/all_to_all | solution.py:413
  52.6 1.7 %collective-permute-done.11.y2_ref = f32[2,12,16,128]{3,2,1,0:T(8,128)S(1)} collective-permute-done((f32[2,12,16,128]{3,2,1,0:T(8,128)S(1)}, f32[2,12,16,128]{3,2,1,0:T(8,128)S(1)}, u32[]{:S(2)}, u32[]{:S(2)}) %collective-permute-start.11) | collective-permute-done | bytes 196640 | tf_op jit(solution)/shard_map/ppermute | solution.py:409
  54.2 2.7 %collective-permute-done.12.y3_ref = f32[2,12,16,128]{3,2,1,0:T(8,128)S(1)} collective-permute-done((f32[2,12,16,128]{3,2,1,0:T(8,128)S(1)}, f32[2,12,16,128]{3,2,1,0:T(8,128)S(1)}, u32[]{:S(2)}, u32[]{:S(2)}) %collective-permute-start.12) | collective-permute-done | bytes 196640 | tf_op jit(solution)/shard_map/ppermute | solution.py:409
  57.0 1.6 %collective-permute-start.13 = (f32[4,12,16,128]{3,2,1,0:T(8,128)S(1)}, f32[4,12,16,128]{3,2,1,0:T(8,128)S(1)}, u32[]{:S(2)}, u32[]{:S(2)}) collective-permute-start(f32[4,12,16,128]{3,2,1,0:T(8,128)S(1)} %shard_map.122), channel_id=1, source_target_pairs={{0,1},{1,0},{2,3},{3,2},{4,5},{5,4},{6,7},{7,6},{8,9},{9,8},{10,11... | collective-permute-start | bytes 1179656 | tf_op jit(solution)/shard_map/ppermute | solution.py:409
  58.5 2.1 %all-to-all-done.2.force_ref = f32[8,12,384]{2,1,0:T(8,128)S(1)} async-done(((f32[8,12,384]{2,1,0:T(8,128)}), f32[8,12,384]{2,1,0:T(8,128)S(1)}, u32[]{:S(2)}, u32[]{:S(2)}) %all-to-all-start.2) | async-done | bytes 147488 | tf_op jit(solution)/shard_map/all_to_all | solution.py:413
  62.0 7.9 %all-to-all-start.3 = ((f32[32,12,128]{2,1,0:T(8,128)}), f32[32,12,128]{2,1,0:T(8,128)S(1)}, u32[]{:S(2)}, u32[]{:S(2)}) async-start(f32[32,12,128]{2,1,0:T(8,128)} %get-tuple-element.42), calls=%async_computation.3 | async-start | bytes 524288 | tf_op jit(solution)/shard_map/all_to_all | solution.py:405
  70.0 2.1 %collective-permute-start.8 = (f32[13,32,128]{2,1,0:T(8,128)}, f32[13,32,128]{2,1,0:T(8,128)S(1)}, u32[]{:S(2)}, u32[]{:S(2)}) collective-permute-start(f32[13,32,128]{2,1,0:T(8,128)} %get-tuple-element.47), channel_id=1, source_target_pairs={{0,8},{8,16},{16,24},{24,32},{32,40},{40,48},{48,56},{56,64},{64,7... | collective-permute-start | bytes 638984 | tf_op jit(solution)/shard_map/ppermute | solution.py:400
  72.1 7.1 %collective-permute-start.9 = (f32[13,32,128]{2,1,0:T(8,128)}, f32[13,32,128]{2,1,0:T(8,128)}, u32[]{:S(2)}, u32[]{:S(2)}) collective-permute-start(f32[13,32,128]{2,1,0:T(8,128)} %get-tuple-element.48), channel_id=1, source_target_pairs={{8,0},{16,8},{24,16},{32,24},{40,32},{48,40},{56,48},{64,56},{72,6... | collective-permute-start | bytes 638984 | tf_op jit(solution)/shard_map/ppermute | solution.py:400
  79.3 5.3 %collective-permute-start.7 = (f32[2,12,128]{2,1,0:T(8,128)}, f32[2,12,128]{2,1,0:T(8,128)}, u32[]{:S(2)}, u32[]{:S(2)}) collective-permute-start(f32[2,12,128]{2,1,0:T(8,128)} %get-tuple-element.44), channel_id=1, source_target_pairs={{0,248},{8,0},{16,8},{24,16},{32,24},{40,32},{48,40},{56,48},{64,5... | collective-permute-start | bytes 36872 | tf_op jit(solution)/shard_map/ppermute | solution.py:400
  86.0 1.9 %shard_map.120 = (f32[12,4,32,128]{3,2,1,0:T(8,128)S(1)}, f32[4,32,128]{2,1,0:T(8,128)S(1)}) custom-call(s32[1]{0:T(128)} %bitcast.p_ref.refs_0_, f32[16,4]{1,0:T(8,128)S(1)} %copy-done.6, s32[4,32,128]{2,1,0:T(8,128)S(1)} %copy-done.4, f32[6,4,32,128]{3,2,1,0:T(8,128)S(1)} %bitcast.13, f32[6,4,32,128]{3,2,1,0:T(8,128)S(1)} %bitcast.16, ...), custom_call_target="tpu_custom_call" | custom-call | tf_op jit(solution)/shard_map/pallas_call | solution.py:388
  87.9 2.6 %shard_map.121.part_ref = f32[12,4,32,128]{3,2,1,0:T(8,128)S(1)} custom-call(s32[24,128]{1,0:T(8,128)S(1)} %copy-done.13, f32[8,12,384]{2,1,0:T(8,128)S(1)} %all-to-all-done.2.force_ref, f32[12,4,32,128]{3,2,1,0:T(8,128)S(1)} %get-tuple-element.49.lin_ref), custom_call_target="tpu_custom_call" | custom-call | tf_op jit(solution)/shard_map/pallas_call | solution.py:388
  90.6 5.4 %shard_map.123 = (f32[6,4,32,128]{3,2,1,0:T(8,128)}, f32[6,4,32,128]{3,2,1,0:T(8,128)}) custom-call(s32[1]{0:T(128)} %bitcast.p_ref.refs_0_, s32[1]{0:T(128)} %bitcast.1.me_ref, s32[24,128]{1,0:T(8,128)S(1)} %copy-done.11, f32[32,12,128]{2,1,0:T(8,128)S(1)} %all-to-all-done.3.chunk_ref, f32[2,12,128]{2,1,0:T(8,128)} %collective-permute-done.6.up_ref, ...), custom_call_target="tpu_custom_call" | custom-call | tf_op jit(solution)/shard_map/pallas_call | solution.py:388
  (58 shorter events, 6.6 us)
Async XLA Ops:
  5.6 13.0 %copy-start.2 = (f32[4,12,16,128]{3,2,1,0:T(8,128)S(1)}, f32[4,12,16,128]{3,2,1,0:T(8,128)}, u32[]{:S(2)}) copy-start(f32[4,12,16,128]{3,2,1,0:T(8,128)} %get-tuple-element.34.same_ref) | copy-start | bytes 1179652
  5.6 13.0 %collective-permute-start.2 = (f32[4,12,16,128]{3,2,1,0:T(8,128)}, f32[4,12,16,128]{3,2,1,0:T(8,128)S(1)}, u32[]{:S(2)}, u32[]{:S(2)}) collective-permute-start(f32[4,12,16,128]{3,2,1,0:T(8,128)} %get-tuple-element.35), channel_id=1, source_target_pairs={{0,1},{1,0},{2,3},{3,2},{4,5},{5,4},{6,7},{7,6},{8,9},{9,8},{10,11... | collective-permute-start | bytes 1179656 | tf_op jit(solution)/shard_map/ppermute | solution.py:409
  6.9 17.3 %copy-start.16 = (f32[2,16,128]{2,1,0:T(8,128)S(1)}, f32[2,16,128]{2,1,0:T(8,128)}, u32[]{:S(2)}) copy-start(f32[2,16,128]{2,1,0:T(8,128)} %get-tuple-element.31) | copy-start | bytes 49156
  6.9 17.3 %copy-start.15 = (f32[2,16,128]{2,1,0:T(8,128)S(1)}, f32[2,16,128]{2,1,0:T(8,128)}, u32[]{:S(2)}) copy-start(f32[2,16,128]{2,1,0:T(8,128)} %get-tuple-element.32) | copy-start | bytes 49156
  6.9 24.1 %all-to-all-start = ((f32[32,16,128]{2,1,0:T(8,128)}), f32[32,16,128]{2,1,0:T(8,128)S(1)}, u32[]{:S(2)}, u32[]{:S(2)}) async-start(f32[32,16,128]{2,1,0:T(8,128)} %get-tuple-element.30), calls=%async_computation | async-start | bytes 524288 | tf_op jit(solution)/shard_map/all_to_all | solution.py:405
  19.4 19.9 %collective-permute-start.3 = (f32[2,12,16,128]{3,2,1,0:T(8,128)S(1)}, f32[2,12,16,128]{3,2,1,0:T(8,128)S(1)}, u32[]{:S(2)}, u32[]{:S(2)}) collective-permute-start(f32[2,12,16,128]{3,2,1,0:T(8,128)S(1)} %get-tuple-element.36.after_ref), channel_id=1, source_target_pairs={{0,2},{1,3},{2,0},{3,1},{4,6},{5,7},{6,4},{7,5},{8,10},{9,11},{10,... | collective-permute-start | bytes 589832 | tf_op jit(solution)/shard_map/ppermute | solution.py:409
  21.0 18.3 %collective-permute-start.4 = (f32[2,12,16,128]{3,2,1,0:T(8,128)}, f32[2,12,16,128]{3,2,1,0:T(8,128)S(1)}, u32[]{:S(2)}, u32[]{:S(2)}) collective-permute-start(f32[2,12,16,128]{3,2,1,0:T(8,128)} %get-tuple-element.39), channel_id=1, source_target_pairs={{0,4},{1,5},{2,6},{3,7},{4,0},{5,1},{6,2},{7,3},{8,12},{9,13},{10,... | collective-permute-start | bytes 589832 | tf_op jit(solution)/shard_map/ppermute | solution.py:409
  23.9 15.4 %collective-permute-start.5 = (f32[2,12,16,128]{3,2,1,0:T(8,128)}, f32[2,12,16,128]{3,2,1,0:T(8,128)S(1)}, u32[]{:S(2)}, u32[]{:S(2)}) collective-permute-start(f32[2,12,16,128]{3,2,1,0:T(8,128)} %get-tuple-element.40), channel_id=1, source_target_pairs={{0,6},{1,7},{2,4},{3,5},{4,2},{5,3},{6,0},{7,1},{8,14},{9,15},{10,... | collective-permute-start | bytes 589832 | tf_op jit(solution)/shard_map/ppermute | solution.py:409
  24.1 6.8 %collective-permute-start = (f32[2,16,128]{2,1,0:T(8,128)S(1)}, f32[2,16,128]{2,1,0:T(8,128)S(1)}, u32[]{:S(2)}, u32[]{:S(2)}) collective-permute-start(f32[2,16,128]{2,1,0:T(8,128)S(1)} %copy-done.16), channel_id=1, source_target_pairs={{0,8},{8,16},{16,24},{24,32},{32,40},{40,48},{48,56},{56,64},{64,7... | collective-permute-start | bytes 49160 | tf_op jit(solution)/shard_map/ppermute | solution.py:400
  24.2 6.8 %collective-permute-start.1 = (f32[2,16,128]{2,1,0:T(8,128)S(1)}, f32[2,16,128]{2,1,0:T(8,128)S(1)}, u32[]{:S(2)}, u32[]{:S(2)}) collective-permute-start(f32[2,16,128]{2,1,0:T(8,128)S(1)} %copy-done.15), channel_id=1, source_target_pairs={{0,248},{8,0},{16,8},{24,16},{32,24},{40,32},{48,40},{56,48},{64,5... | collective-permute-start | bytes 49160 | tf_op jit(solution)/shard_map/ppermute | solution.py:400
  34.8 11.6 %all-to-all-start.1 = ((f32[8,12,384]{2,1,0:T(8,128)}), f32[8,12,384]{2,1,0:T(8,128)S(1)}, u32[]{:S(2)}, u32[]{:S(2)}) async-start(f32[8,12,384]{2,1,0:T(8,128)} %copy-done.5), calls=%async_computation.1 | async-start | bytes 393216 | tf_op jit(solution)/shard_map/all_to_all | solution.py:413
  41.4 11.2 %collective-permute-start.10 = (f32[2,12,16,128]{3,2,1,0:T(8,128)S(1)}, f32[2,12,16,128]{3,2,1,0:T(8,128)S(1)}, u32[]{:S(2)}, u32[]{:S(2)}) collective-permute-start(f32[2,12,16,128]{3,2,1,0:T(8,128)S(1)} %get-tuple-element.51), channel_id=1, source_target_pairs={{0,2},{1,3},{2,0},{3,1},{4,6},{5,7},{6,4},{7,5},{8,10},{9,11},{10,... | collective-permute-start | bytes 589832 | tf_op jit(solution)/shard_map/ppermute | solution.py:409
  43.5 10.7 %collective-permute-start.11 = (f32[2,12,16,128]{3,2,1,0:T(8,128)S(1)}, f32[2,12,16,128]{3,2,1,0:T(8,128)S(1)}, u32[]{:S(2)}, u32[]{:S(2)}) collective-permute-start(f32[2,12,16,128]{3,2,1,0:T(8,128)S(1)} %get-tuple-element.52), channel_id=1, source_target_pairs={{0,4},{1,5},{2,6},{3,7},{4,0},{5,1},{6,2},{7,3},{8,12},{9,13},{10,... | collective-permute-start | bytes 589832 | tf_op jit(solution)/shard_map/ppermute | solution.py:409
  46.2 10.8 %collective-permute-start.12 = (f32[2,12,16,128]{3,2,1,0:T(8,128)S(1)}, f32[2,12,16,128]{3,2,1,0:T(8,128)S(1)}, u32[]{:S(2)}, u32[]{:S(2)}) collective-permute-start(f32[2,12,16,128]{3,2,1,0:T(8,128)S(1)} %get-tuple-element.53), channel_id=1, source_target_pairs={{0,6},{1,7},{2,4},{3,5},{4,2},{5,3},{6,0},{7,1},{8,14},{9,15},{10,... | collective-permute-start | bytes 589832 | tf_op jit(solution)/shard_map/ppermute | solution.py:409
  47.4 13.3 %all-to-all-start.2 = ((f32[8,12,384]{2,1,0:T(8,128)}), f32[8,12,384]{2,1,0:T(8,128)S(1)}, u32[]{:S(2)}, u32[]{:S(2)}) async-start(f32[8,12,384]{2,1,0:T(8,128)} %shard_map.118), calls=%async_computation.2 | async-start | bytes 393216 | tf_op jit(solution)/shard_map/all_to_all | solution.py:413
  57.0 28.3 %copy-start.3 = (f32[2,3,4,32,128]{4,3,2,1,0:T(8,128)S(1)}, f32[2,3,4,32,128]{4,3,2,1,0:T(8,128)}, u32[]{:S(2)}) copy-start(f32[2,3,4,32,128]{4,3,2,1,0:T(8,128)} %param.12) | copy-start | bytes 1179652
  57.0 33.6 %collective-permute-start.13 = (f32[4,12,16,128]{3,2,1,0:T(8,128)S(1)}, f32[4,12,16,128]{3,2,1,0:T(8,128)S(1)}, u32[]{:S(2)}, u32[]{:S(2)}) collective-permute-start(f32[4,12,16,128]{3,2,1,0:T(8,128)S(1)} %shard_map.122), channel_id=1, source_target_pairs={{0,1},{1,0},{2,3},{3,2},{4,5},{5,4},{6,7},{7,6},{8,9},{9,8},{10,11... | collective-permute-start | bytes 1179656 | tf_op jit(solution)/shard_map/ppermute | solution.py:409
  62.0 23.3 %copy-start.4 = (s32[4,32,128]{2,1,0:T(8,128)S(1)}, s32[4,32,128]{2,1,0:T(8,128)}, u32[]{:S(2)}) copy-start(s32[4,32,128]{2,1,0:T(8,128)} %refs_2_.1) | copy-start | bytes 196612
  62.0 28.5 %all-to-all-start.3 = ((f32[32,12,128]{2,1,0:T(8,128)}), f32[32,12,128]{2,1,0:T(8,128)S(1)}, u32[]{:S(2)}, u32[]{:S(2)}) async-start(f32[32,12,128]{2,1,0:T(8,128)} %get-tuple-element.42), calls=%async_computation.3 | async-start | bytes 524288 | tf_op jit(solution)/shard_map/all_to_all | solution.py:405
  70.0 15.3 %collective-permute-start.8 = (f32[13,32,128]{2,1,0:T(8,128)}, f32[13,32,128]{2,1,0:T(8,128)S(1)}, u32[]{:S(2)}, u32[]{:S(2)}) collective-permute-start(f32[13,32,128]{2,1,0:T(8,128)} %get-tuple-element.47), channel_id=1, source_target_pairs={{0,8},{8,16},{16,24},{24,32},{32,40},{40,48},{48,56},{56,64},{64,7... | collective-permute-start | bytes 638984 | tf_op jit(solution)/shard_map/ppermute | solution.py:400
  72.0 12.6 %copy-start.14 = (f32[16,4]{0,1:T(4,128)S(1)}, f32[16,4]{0,1:T(4,128)}, u32[]{:S(2)}) copy-start(f32[16,4]{0,1:T(4,128)} %param.14) | copy-start | bytes 772
  72.1 13.3 %collective-permute-start.9 = (f32[13,32,128]{2,1,0:T(8,128)}, f32[13,32,128]{2,1,0:T(8,128)}, u32[]{:S(2)}, u32[]{:S(2)}) collective-permute-start(f32[13,32,128]{2,1,0:T(8,128)} %get-tuple-element.48), channel_id=1, source_target_pairs={{8,0},{16,8},{24,16},{32,24},{40,32},{48,40},{56,48},{64,56},{72,6... | collective-permute-start | bytes 638984 | tf_op jit(solution)/shard_map/ppermute | solution.py:400
  79.2 11.4 %collective-permute-start.6 = (f32[2,12,128]{2,1,0:T(8,128)}, f32[2,12,128]{2,1,0:T(8,128)}, u32[]{:S(2)}, u32[]{:S(2)}) collective-permute-start(f32[2,12,128]{2,1,0:T(8,128)} %get-tuple-element.43), channel_id=1, source_target_pairs={{0,8},{8,16},{16,24},{24,32},{32,40},{40,48},{48,56},{56,64},{64,7... | collective-permute-start | bytes 36872 | tf_op jit(solution)/shard_map/ppermute | solution.py:400
  79.3 11.3 %collective-permute-start.7 = (f32[2,12,128]{2,1,0:T(8,128)}, f32[2,12,128]{2,1,0:T(8,128)}, u32[]{:S(2)}, u32[]{:S(2)}) collective-permute-start(f32[2,12,128]{2,1,0:T(8,128)} %get-tuple-element.44), channel_id=1, source_target_pairs={{0,248},{8,0},{16,8},{24,16},{32,24},{40,32},{48,40},{56,48},{64,5... | collective-permute-start | bytes 36872 | tf_op jit(solution)/shard_map/ppermute | solution.py:400
  (11 other events, 45.4 us)

commit v8 on v5

--- a/solution.py
+++ b/solution.py
@@ -39,8 +39,18 @@
     return 8 + (offset - 3) // 3, SEG * ((offset - 3) % 3)
 
 
-def place(offset):
-    return {2: (6, 0), 30: (7, 0)}.get(offset) or far_place(offset)
+def fold(rows):
+    return jnp.concatenate([rows[0:4], rows[4:8], rows[8:12]], axis=1)
+
+
+def unfold(rows):
+    width = rows.shape[1] // 3
+    return jnp.concatenate([rows[:, width * k : width * (k + 1)] for k in range(3)], axis=0)
+
+
+def part_tile(ref, tile):
+    at = 128 * (tile % 3)
+    return jnp.concatenate([ref[tile // 3, :, 384 * k + at : 384 * k + at + 128] for k in range(3)], axis=0)
 
 
 def lane_roll(x, shift):
@@ -192,8 +202,10 @@
         end.start()
     for d in (0, 1, SLABS - 1):
         chunk_ref[(p + d) & (SLABS - 1)] = jnp.zeros((16, 128), f32)
-    for d in range(2, SLABS - 1):
-        tile, seg = place(d)
+    for d, tile in ((2, 6), (SLABS - 2, 7)):
+        chunk_ref[(p + d) & (SLABS - 1)] = rows_ref[tile]
+    for d in range(3, SLABS - 2):
+        tile, seg = far_place(d)
         chunk_ref[(p + d) & (SLABS - 1)] = lane_roll(rows_ref[tile], -seg)
     self_ref[...] = rows_ref[0:2]
     for move in moves + ends:
@@ -217,14 +229,17 @@
     gather_rows(parts_ref, idx_ref, here_ref)
     for tile in range(24):
         gap = tiles[tile][0:12] - here_ref[tile] if tile < 17 else jnp.zeros((12, 128), f32)
-        gap_ref[tile // 3, :, 128 * (tile % 3) : 128 * (tile % 3 + 1)] = gap
+        at = 128 * (tile % 3)
+        for k in range(3):
+            gap_ref[tile // 3, :, 384 * k + at : 384 * k + at + 128] = gap[4 * k : 4 * k + 4]
 
 
 def force_kernel(me_ref, kind_ref, spread_ref, gap_ref, after_ref, out_ref, r_ref, d_ref, f_ref, t_ref):
     me = me_ref[0]
     for k in range(PARTS):
-        r_ref[6 * k : 6 * k + 6] = gap_ref[k, 0:6, :]
-        d_ref[6 * k : 6 * k + 6] = gap_ref[k, 6:12, :]
+        gap = unfold(gap_ref[k])
+        r_ref[6 * k : 6 * k + 6] = gap[0:6]
+        d_ref[6 * k : 6 * k + 6] = gap[6:12]
     r = r_ref[...]
     dr = d_ref[...]
     w = jnp.dot(spread_ref[...], r, precision=lax.Precision.HIGHEST, preferred_element_type=f32)
@@ -239,30 +254,27 @@
     tangent_contact = stop_stiff * opened * opened * dr
     t_ref[...] = bolted * tangent_friction + (1.0 - bolted) * tangent_contact
     for k in range(PARTS):
-        out_ref[k, 0:6, :] = f_ref[6 * k : 6 * k + 6]
-        out_ref[k, 6:12, :] = t_ref[6 * k : 6 * k + 6]
+        out_ref[k] = fold(jnp.concatenate([f_ref[6 * k : 6 * k + 6], t_ref[6 * k : 6 * k + 6]], axis=0))
 
 
 def reply_kernel(p_ref, force_ref, chunk_ref, up_ref, down_ref, self_ref):
     p = p_ref[0]
-
-    def force(tile):
-        return force_ref[tile // 3, :, 128 * (tile % 3) : 128 * (tile % 3 + 1)]
-
     for d in (0, 1, SLABS - 1):
-        chunk_ref[(p - d) & (SLABS - 1)] = jnp.zeros((12, 128), f32)
-    for d in range(2, SLABS - 1):
-        tile, seg = place(d)
-        chunk_ref[(p - d) & (SLABS - 1)] = lane_roll(force(tile), -seg)
+        chunk_ref[(p - d) & (SLABS - 1)] = jnp.zeros((4, 384), f32)
+    for d, tile in ((2, 6), (SLABS - 2, 7)):
+        chunk_ref[(p - d) & (SLABS - 1)] = fold(part_tile(force_ref, tile))
+    for d in range(3, SLABS - 2):
+        tile, seg = far_place(d)
+        chunk_ref[(p - d) & (SLABS - 1)] = fold(lane_roll(part_tile(force_ref, tile), -seg))
     for k in range(2):
-        self_ref[k] = force(k)
-        down_ref[k] = force(2 + k)
-        up_ref[k] = force(4 + k)
+        self_ref[k] = part_tile(force_ref, k)
+        down_ref[k] = part_tile(force_ref, 2 + k)
+        up_ref[k] = part_tile(force_ref, 4 + k)
 
 
 def partner_kernel(idx_ref, force_ref, lin_ref, out_ref, val_ref, sum_ref):
     for tile in range(17):
-        val_ref[tile] = -force_ref[tile // 3, :, 128 * (tile % 3) : 128 * (tile % 3 + 1)]
+        val_ref[tile] = -part_tile(force_ref, tile)
     val_ref[17] = jnp.zeros((12, 128), f32)
     scatter_rows(val_ref, idx_ref, sum_ref)
     for x in range(4):
@@ -270,20 +282,25 @@
 
 
 def final_kernel(p_ref, me_ref, idx_ref, chunk_ref, up_ref, down_ref, self_ref, part_ref, mass_ref,
-                 own_ref, y1_ref, y2_ref, y3_ref, x_ref, res_ref, jac_ref, val_ref, sum_ref, acc_ref):
+                 own_ref, y1_ref, y2_ref, y3_ref, x_ref, res_ref, jac_ref, val_ref, sum_ref, acc_ref, sems):
     p = p_ref[0]
+    copies = []
+    for k in range(PARTS):
+        source = x_ref.at[k // 2] if k % 2 else (own_ref, y1_ref, y2_ref, y3_ref)[k // 2].at[0]
+        copies.append(pltpu.make_async_copy(source, acc_ref.at[me_ref[0] ^ k], sems.at[k]))
+    for copy in copies:
+        copy.start()
 
     def listed(d):
-        return chunk_ref[(p + d) & (SLABS - 1)]
+        return unfold(chunk_ref[(p + d) & (SLABS - 1)])
 
     tiles = [self_ref[0], self_ref[1], down_ref[0], down_ref[1], up_ref[0], up_ref[1], listed(2), listed(SLABS - 2)]
     tiles += merge_far(listed, 12, 0.0) + [jnp.zeros((12, 128), f32)]
     for k, tile in enumerate(tiles):
         val_ref[k] = tile
-    for k in range(PARTS):
-        acc = x_ref[k // 2] if k % 2 else (own_ref, y1_ref, y2_ref, y3_ref)[k // 2][0]
-        acc_ref[me_ref[0] ^ k] = acc
     scatter_rows(val_ref, idx_ref, sum_ref)
+    for copy in copies:
+        copy.wait()
     for x in range(4):
         acc = jnp.concatenate([acc_ref[2 * x], acc_ref[2 * x + 1]], axis=1)
         added = sum_ref[:, 128 * x : 128 * (x + 1)].reshape(12, 32, 128)
@@ -304,12 +321,15 @@
 
 
 def time_kernel(me_ref, same_ref, other_ref, y1_ref, y2_ref, y3_ref, *refs):
-    outs, in_ref, out_ref = refs[:4], refs[4], refs[5]
+    outs, in_ref, out_ref, sems = refs[:4], refs[4], refs[5], refs[6]
     me = me_ref[0]
-    in_ref[0] = same_ref[0]
-    in_ref[1] = other_ref[0]
-    for k, ref in enumerate((y1_ref, y2_ref, y3_ref)):
-        in_ref[2 * k + 2 : 2 * k + 4] = ref[...]
+    pairs = [(same_ref.at[0], in_ref.at[0]), (other_ref.at[0], in_ref.at[1])]
+    pairs += [(ref, in_ref.at[pl.ds(2 * k + 2, 2)]) for k, ref in enumerate((y1_ref, y2_ref, y3_ref))]
+    copies = [pltpu.make_async_copy(a, b, sems.at[k]) for k, (a, b) in enumerate(pairs)]
+    for copy in copies:
+        copy.start()
+    for copy in copies:
+        copy.wait()
     at = [me ^ ((me + k) & (PARTS - 1)) for k in range(PARTS)]
     count = 2 * PARTS
 
@@ -449,9 +469,9 @@
     joined = call(join_kernel, [pair] * 3, same, other, smem=())
     turned = [swap(x, 2 * k + 2) for k, x in enumerate(joined)]
     blocks = [pltpu.VMEM((PARTS, 12, 16, 128), f32)] * 2
-    inertia = call(time_kernel, [pair] * 4, me, same, other, *turned, scratch=blocks)
-
-    part = ((PARTS, 12, 384), f32)
+    inertia = call(time_kernel, [pair] * 4, me, same, other, *turned, away=range(1, 6), scratch=blocks + [pltpu.SemaphoreType.DMA((5,))])
+
+    part = ((PARTS, 4, 1152), f32)
     fields_parts = call(split_kernel, [(parts, bf16)], disp, dire, smem=())[0]
     far_idx, kind, gap = call(
         gap_kernel,
@@ -469,8 +489,8 @@
     )[0]
     force = inst_split(force)
     turned = [inertia[0]] + [swap(inertia[k], 2 * k) for k in (1, 2, 3)]
-    messages = [((SLABS, 12, 128), f32)] + [((2, 12, 128), f32)] * 3
-    chunk, up2, down2, own = call(reply_kernel, messages, p, force)
+    two = ((2, 12, 128), f32)
+    chunk, up2, down2, own = call(reply_kernel, [((SLABS, 4, 384), f32), two, two, two], p, force)
     chunk, up2, down2 = exchange(chunk, up2, down2)
 
     lin, mass = call(
@@ -487,7 +507,8 @@
         [(fields, f32)] * 2,
         p, me, own_idx, chunk, up2, down2, own, partial, mass, *turned, other,
         smem=(0, 1),
-        scratch=adding + blocks[:1],
+        away=range(9, 14),
+        scratch=adding + blocks[:1] + [pltpu.SemaphoreType.DMA((PARTS,))],
     )
     return residual.reshape(shape), jacobian.reshape(shape)
 

time: 89.8 us -> 87.3 us (0.972)
  waiting for transfers between devices: 18.7 us -> 17 us
  local copies, waits for them, and re-layouts: 2.39 us -> 0.78 us
  Pallas kernels: 21.5 us -> 22.4 us
    ppermute x8, waiting for transfers between devices: 1.07 us -> 4.62 us  [swap(): return lax.ppermute(x, 'inst', [(i, i ^ bit) for i in range(PARTS)])]
    all_to_all x2, waiting for transfers between devices: 3.53 us -> 0.01 us  [inst_split(): return lax.all_to_all(x, 'inst', split_axis=0, concat_axis=0, tiled=True)]
    unnamed x25 -> x21, local copies, waits for them, and re-layouts: 2.39 us -> 0.78 us
    ppermute x4, waiting for transfers between devices: 6.58 us -> 5.17 us  [shift(): lax.ppermute(x, 'mesh', [(i, (i + by) % SLABS) for i in range(SLABS)])]
    pallas_call x11, Pallas kernels: 21.5 us -> 22.4 us  [call(): pl.pallas_call(kernel, out_shape=[jax.ShapeDtypeStruct(s, d) for s, d in...]
  transfers between devices with their start and end apart: 16 -> 16, of which waited for: 7 -> 7; matrix products, arithmetic and copies ran while one was open for 0% -> 0% of each run, Pallas kernels for 13% -> 15%
where the time goes in v8:
time: 87.3 us; the launch traced here: 86.8 us
  starting transfers between devices  45.6 us (52%)
  Pallas kernels  22.4 us (26%)
  waiting for transfers between devices  17 us (19%)
  between operations  0.98 us (1%)
    pallas_call x11, Pallas kernels, call(): pl.pallas_call(kernel, out_shape=[jax.ShapeDtypeStruct(s, d) for s, d in...  22.4 us
    all_to_all x2, starting transfers between devices, exchange(): lax.all_to_all(chunk, 'mesh', split_axis=0, concat_axis=0, tiled=True)  21.6 us
    ppermute x8, starting transfers between devices, swap(): return lax.ppermute(x, 'inst', [(i, i ^ bit) for i in range(PARTS)])  11.6 us
    all_to_all x2, starting transfers between devices, inst_split(): return lax.all_to_all(x, 'inst', split_axis=0, concat_axis=0, tiled=True)  8.95 us
    all_to_all x2, waiting for transfers between devices, exchange(): lax.all_to_all(chunk, 'mesh', split_axis=0, concat_axis=0, tiled=True)  7.22 us
    ppermute x4, waiting for transfers between devices, shift(): lax.ppermute(x, 'mesh', [(i, (i + by) % SLABS) for i in range(SLABS)])  5.17 us
    ppermute x8, waiting for transfers between devices, swap(): return lax.ppermute(x, 'inst', [(i, i ^ bit) for i in range(PARTS)])  4.62 us
    ppermute x4, starting transfers between devices, shift(): lax.ppermute(x, 'mesh', [(i, (i + by) % SLABS) for i in range(SLABS)])  3.42 us
  transfers between devices with their start and end apart: 16, of which 7 were waited for; matrix products, arithmetic and copies ran while one was open for 0% of the time, Pallas kernels for 15%

profile of v8, /device:TPU:1, one launch (start us, length us, event | category | flops | bytes accessed | tf_op | source)
XLA Modules:
  0.0 86.8 jit_solution(7264422901870923092)
XLA Ops:
  0.6 5.4 %shard_map.113 = (s32[24,128]{1,0:T(8,128)}, f32[32,16,128]{2,1,0:T(8,128)}, f32[14,32,128]{2,1,0:T(8,128)}, f32[14,32,128]{2,1,0:T(8,128)}, f32[2,16,128]{2,1,0...) custom-call(s32[1]{0:T(128)} %bitcast.p_ref.refs_0_, s32[1]{0:T(128)} %bitcast.1.me_ref, ...), custom_call_target="tpu_custom_call" | custom-call | tf_op jit(solution)/shard_map/pallas_call | solution.py:402
  6.1 2.1 %collective-permute-start.2 = (f32[4,12,16,128]{3,2,1,0:T(8,128)}, f32[4,12,16,128]{3,2,1,0:T(8,128)S(1)}, u32[]{:S(2)}, u32[]{:S(2)}) collective-permute-start(f32[4,12,16,128]{3,2,1,0:T(8,128)} %get-tuple-element.33), channel_id=1, source_target_pairs={{0,1},{1,0},{2,3},{3,2},{4,5},{5,4},{6,7},{7,6},{8,9},{9,8},{10,11... | collective-permute-start | bytes 1179656 | tf_op jit(solution)/shard_map/ppermute | solution.py:422
  8.2 11.7 %all-to-all-start = ((f32[32,16,128]{2,1,0:T(8,128)}), f32[32,16,128]{2,1,0:T(8,128)S(1)}, u32[]{:S(2)}, u32[]{:S(2)}) async-start(f32[32,16,128]{2,1,0:T(8,128)} %get-tuple-element.28), calls=%async_computation | async-start | bytes 524288 | tf_op jit(solution)/shard_map/all_to_all | solution.py:418
  19.9 1.7 %collective-permute-start = (f32[14,32,128]{2,1,0:T(8,128)}, f32[14,32,128]{2,1,0:T(8,128)S(1)}, u32[]{:S(2)}, u32[]{:S(2)}) collective-permute-start(f32[14,32,128]{2,1,0:T(8,128)} %get-tuple-element.29), channel_id=1, source_target_pairs={{0,8},{8,16},{16,24},{24,32},{32,40},{40,48},{48,56},{56,64},{64,7... | collective-permute-start | bytes 688136 | tf_op jit(solution)/shard_map/ppermute | solution.py:413
  22.6 1.3 %collective-permute-start.3 = (f32[2,12,16,128]{3,2,1,0:T(8,128)}, f32[2,12,16,128]{3,2,1,0:T(8,128)S(1)}, u32[]{:S(2)}, u32[]{:S(2)}) collective-permute-start(f32[2,12,16,128]{3,2,1,0:T(8,128)} %get-tuple-element.34.after_ref), channel_id=1, source_target_pairs={{0,2},{1,3},{2,0},{3,1},{4,6},{5,7},{6,4},{7,5},{8,10},{9,11},{10,... | collective-permute-start | bytes 589832 | tf_op jit(solution)/shard_map/ppermute | solution.py:422
  23.8 2.6 %collective-permute-start.4 = (f32[2,12,16,128]{3,2,1,0:T(8,128)}, f32[2,12,16,128]{3,2,1,0:T(8,128)S(1)}, u32[]{:S(2)}, u32[]{:S(2)}) collective-permute-start(f32[2,12,16,128]{3,2,1,0:T(8,128)} %get-tuple-element.37), channel_id=1, source_target_pairs={{0,4},{1,5},{2,6},{3,7},{4,0},{5,1},{6,2},{7,3},{8,12},{9,13},{10,... | collective-permute-start | bytes 589832 | tf_op jit(solution)/shard_map/ppermute | solution.py:422
  26.6 2.1 %collective-permute-done.up_ref.refs_6_ = f32[14,32,128]{2,1,0:T(8,128)S(1)} collective-permute-done((f32[14,32,128]{2,1,0:T(8,128)}, f32[14,32,128]{2,1,0:T(8,128)S(1)}, u32[]{:S(2)}, u32[]{:S(2)}) %collective-permute-start) | collective-permute-done | bytes 229408 | tf_op jit(solution)/shard_map/ppermute | solution.py:413
  28.7 2.1 %collective-permute-done.1.down_ref.refs_7_ = f32[14,32,128]{2,1,0:T(8,128)S(1)} collective-permute-done((f32[14,32,128]{2,1,0:T(8,128)}, f32[14,32,128]{2,1,0:T(8,128)S(1)}, u32[]{:S(2)}, u32[]{:S(2)}) %collective-permute-start.1) | collective-permute-done | bytes 229408 | tf_op jit(solution)/shard_map/ppermute | solution.py:413
  30.7 2.6 %all-to-all-done.chunk_ref = f32[32,16,128]{2,1,0:T(8,128)S(1)} async-done(((f32[32,16,128]{2,1,0:T(8,128)}), f32[32,16,128]{2,1,0:T(8,128)S(1)}, u32[]{:S(2)}, u32[]{:S(2)}) %all-to-all-start) | async-done | bytes 262176 | tf_op jit(solution)/shard_map/all_to_all | solution.py:418
  33.4 2.5 %shard_map.116 = (s32[24,128]{1,0:T(8,128)S(1)}, f32[24,128]{1,0:T(8,128)S(1)}, f32[8,4,1152]{2,1,0:T(4,128)S(1)}) custom-call(s32[1]{0:T(128)} %bitcast.p_ref.refs_0_, f32[32,16,128]{2,1,0:T(8,128)S(1)} %all-to-all-done.chunk_ref, f32[14,32,128]{2,1,0:T(8,128)S(1)} %collective-permute-done.up_ref.refs_6_, ...), custom_call_target="tpu_custom_call" | custom-call | tf_op jit(solution)/shard_map/pallas_call | solution.py:402
  36.5 4.2 %all-to-all-start.1 = ((f32[8,4,1152]{2,1,0:T(4,128)}), f32[8,4,1152]{2,1,0:T(4,128)S(1)}, u32[]{:S(2)}, u32[]{:S(2)}) async-start(f32[8,4,1152]{2,1,0:T(4,128)} %copy-done.5), calls=%async_computation.1 | async-start | bytes 294912 | tf_op jit(solution)/shard_map/all_to_all | solution.py:426
  40.8 3.4 %shard_map.117 = (f32[2,12,16,128]{3,2,1,0:T(8,128)S(1)}, f32[2,12,16,128]{3,2,1,0:T(8,128)}, f32[2,12,16,128]{3,2,1,0:T(8,128)}, f32[2,12,16,128]{3,2,1,0:T(8,128)S(1)}) custom-call(s32[1]{0:T(128)} %bitcast.1.me_ref, f32[4,12,16,128]{3,2,1,0:T(8,128)S(1)} %copy-done.2, f32[4,12,16,128]{3,2,1,0:T(8,128)S(1)} %collective-permute-done.2.other_ref, ...), custom_call_target="tpu_custom_call" | custom-call | tf_op jit(solution)/shard_map/pallas_call | solution.py:402
  44.2 1.5 %collective-permute-start.8 = (f32[2,12,16,128]{3,2,1,0:T(8,128)}, f32[2,12,16,128]{3,2,1,0:T(8,128)S(1)}, u32[]{:S(2)}, u32[]{:S(2)}) collective-permute-start(f32[2,12,16,128]{3,2,1,0:T(8,128)} %get-tuple-element.47), channel_id=1, source_target_pairs={{0,2},{1,3},{2,0},{3,1},{4,6},{5,7},{6,4},{7,5},{8,10},{9,11},{10,... | collective-permute-start | bytes 589832 | tf_op jit(solution)/shard_map/ppermute | solution.py:422
  45.7 2.4 %collective-permute-start.9 = (f32[2,12,16,128]{3,2,1,0:T(8,128)}, f32[2,12,16,128]{3,2,1,0:T(8,128)S(1)}, u32[]{:S(2)}, u32[]{:S(2)}) collective-permute-start(f32[2,12,16,128]{3,2,1,0:T(8,128)} %get-tuple-element.48), channel_id=1, source_target_pairs={{0,4},{1,5},{2,6},{3,7},{4,0},{5,1},{6,2},{7,3},{8,12},{9,13},{10,... | collective-permute-start | bytes 589832 | tf_op jit(solution)/shard_map/ppermute | solution.py:422
  49.2 4.8 %all-to-all-start.2 = ((f32[8,4,1152]{2,1,0:T(4,128)}), f32[8,4,1152]{2,1,0:T(4,128)S(1)}, u32[]{:S(2)}, u32[]{:S(2)}) async-start(f32[8,4,1152]{2,1,0:T(4,128)} %shard_map.118), calls=%async_computation.2 | async-start | bytes 294912 | tf_op jit(solution)/shard_map/all_to_all | solution.py:426
  53.9 1.2 %collective-permute-done.9.y2_ref = f32[2,12,16,128]{3,2,1,0:T(8,128)S(1)} collective-permute-done((f32[2,12,16,128]{3,2,1,0:T(8,128)}, f32[2,12,16,128]{3,2,1,0:T(8,128)S(1)}, u32[]{:S(2)}, u32[]{:S(2)}) %collective-permute-start.9) | collective-permute-done | bytes 196640 | tf_op jit(solution)/shard_map/ppermute | solution.py:422
  55.1 3.4 %collective-permute-done.10.y3_ref = f32[2,12,16,128]{3,2,1,0:T(8,128)S(1)} collective-permute-done((f32[2,12,16,128]{3,2,1,0:T(8,128)S(1)}, f32[2,12,16,128]{3,2,1,0:T(8,128)S(1)}, u32[]{:S(2)}, u32[]{:S(2)}) %collective-permute-start.10) | collective-permute-done | bytes 196640 | tf_op jit(solution)/shard_map/ppermute | solution.py:422
  58.6 1.6 %collective-permute-start.11 = (f32[4,12,16,128]{3,2,1,0:T(8,128)S(1)}, f32[4,12,16,128]{3,2,1,0:T(8,128)}, u32[]{:S(2)}, u32[]{:S(2)}) collective-permute-start(f32[4,12,16,128]{3,2,1,0:T(8,128)S(1)} %shard_map.122), channel_id=1, source_target_pairs={{0,1},{1,0},{2,3},{3,2},{4,5},{5,4},{6,7},{7,6},{8,9},{9,8},{10,11... | collective-permute-start | bytes 1179656 | tf_op jit(solution)/shard_map/ppermute | solution.py:422
  61.0 9.8 %all-to-all-start.3 = ((f32[32,4,384]{2,1,0:T(4,128)}), f32[32,4,384]{2,1,0:T(4,128)S(1)}, u32[]{:S(2)}, u32[]{:S(2)}) async-start(f32[32,4,384]{2,1,0:T(4,128)} %get-tuple-element.40), calls=%async_computation.3 | async-start | bytes 393216 | tf_op jit(solution)/shard_map/all_to_all | solution.py:418
  70.8 1.7 %collective-permute-start.6 = (f32[2,12,128]{2,1,0:T(8,128)S(1)}, f32[2,12,128]{2,1,0:T(8,128)S(1)}, u32[]{:S(2)}, u32[]{:S(2)}) collective-permute-start(f32[2,12,128]{2,1,0:T(8,128)S(1)} %get-tuple-element.41), channel_id=1, source_target_pairs={{0,8},{8,16},{16,24},{24,32},{32,40},{40,48},{48,56},{56,64},{64,7... | collective-permute-start | bytes 36872 | tf_op jit(solution)/shard_map/ppermute | solution.py:413
  72.6 1.6 %shard_map.120 = (f32[12,4,32,128]{3,2,1,0:T(8,128)S(1)}, f32[4,32,128]{2,1,0:T(8,128)S(1)}) custom-call(s32[1]{0:T(128)} %bitcast.p_ref.refs_0_, f32[16,4]{1,0:T(8,128)S(1)} %copy.12.refs_1_, s32[4,32,128]{2,1,0:T(8,128)S(1)} %copy-done.4, f32[6,4,32,128]{3,2,1,0:T(8,128)S(1)} %bitcast.13, f32[6,4,32,128]{3,2,1,0:T(8,128)S(1)} %bitcast.16, ...), custom_call_target="tpu_custom_call" | custom-call | tf_op jit(solution)/shard_map/pallas_call | solution.py:402
  74.2 2.6 %shard_map.121.part_ref = f32[12,4,32,128]{3,2,1,0:T(8,128)S(1)} custom-call(s32[24,128]{1,0:T(8,128)S(1)} %get-tuple-element.44.idx_ref, f32[8,4,1152]{2,1,0:T(4,128)S(1)} %all-to-all-done.2.force_ref, f32[12,4,32,128]{3,2,1,0:T(8,128)S(1)} %get-tuple-element.45.lin_ref), custom_call_target="tpu_custom_call" | custom-call | tf_op jit(solution)/shard_map/pallas_call | solution.py:402
  77.9 4.6 %all-to-all-done.3.chunk_ref = f32[32,4,384]{2,1,0:T(4,128)S(1)} async-done(((f32[32,4,384]{2,1,0:T(4,128)}), f32[32,4,384]{2,1,0:T(4,128)S(1)}, u32[]{:S(2)}, u32[]{:S(2)}) %all-to-all-start.3) | async-done | bytes 196640 | tf_op jit(solution)/shard_map/all_to_all | solution.py:418
  82.5 4.1 %shard_map.123 = (f32[6,4,32,128]{3,2,1,0:T(8,128)}, f32[6,4,32,128]{3,2,1,0:T(8,128)}) custom-call(s32[1]{0:T(128)} %bitcast.p_ref.refs_0_, s32[1]{0:T(128)} %bitcast.1.me_ref, s32[24,128]{1,0:T(8,128)S(1)} %copy-done.8, f32[32,4,384]{2,1,0:T(4,128)S(1)} %all-to-all-done.3.chunk_ref, f32[2,12,128]{2,1,0:T(8,128)S(1)} %collective-permute-done.6.up_ref, ...), custom_call_target="tpu_custom_call" | custom-call | tf_op jit(solution)/shard_map/pallas_call | solution.py:402
  (40 shorter events, 4.7 us)
Async XLA Ops:
  6.1 15.6 %copy-start.2 = (f32[4,12,16,128]{3,2,1,0:T(8,128)S(1)}, f32[4,12,16,128]{3,2,1,0:T(8,128)}, u32[]{:S(2)}) copy-start(f32[4,12,16,128]{3,2,1,0:T(8,128)} %get-tuple-element.32.same_ref) | copy-start | bytes 1179652
  6.1 15.6 %collective-permute-start.2 = (f32[4,12,16,128]{3,2,1,0:T(8,128)}, f32[4,12,16,128]{3,2,1,0:T(8,128)S(1)}, u32[]{:S(2)}, u32[]{:S(2)}) collective-permute-start(f32[4,12,16,128]{3,2,1,0:T(8,128)} %get-tuple-element.33), channel_id=1, source_target_pairs={{0,1},{1,0},{2,3},{3,2},{4,5},{5,4},{6,7},{7,6},{8,9},{9,8},{10,11... | collective-permute-start | bytes 1179656 | tf_op jit(solution)/shard_map/ppermute | solution.py:422
  8.2 25.2 %all-to-all-start = ((f32[32,16,128]{2,1,0:T(8,128)}), f32[32,16,128]{2,1,0:T(8,128)S(1)}, u32[]{:S(2)}, u32[]{:S(2)}) async-start(f32[32,16,128]{2,1,0:T(8,128)} %get-tuple-element.28), calls=%async_computation | async-start | bytes 524288 | tf_op jit(solution)/shard_map/all_to_all | solution.py:418
  19.9 8.7 %collective-permute-start = (f32[14,32,128]{2,1,0:T(8,128)}, f32[14,32,128]{2,1,0:T(8,128)S(1)}, u32[]{:S(2)}, u32[]{:S(2)}) collective-permute-start(f32[14,32,128]{2,1,0:T(8,128)} %get-tuple-element.29), channel_id=1, source_target_pairs={{0,8},{8,16},{16,24},{24,32},{32,40},{40,48},{48,56},{56,64},{64,7... | collective-permute-start | bytes 688136 | tf_op jit(solution)/shard_map/ppermute | solution.py:413
  21.7 9.1 %collective-permute-start.1 = (f32[14,32,128]{2,1,0:T(8,128)}, f32[14,32,128]{2,1,0:T(8,128)S(1)}, u32[]{:S(2)}, u32[]{:S(2)}) collective-permute-start(f32[14,32,128]{2,1,0:T(8,128)} %get-tuple-element.30), channel_id=1, source_target_pairs={{0,248},{8,0},{16,8},{24,16},{32,24},{40,32},{48,40},{56,48},{64,5... | collective-permute-start | bytes 688136 | tf_op jit(solution)/shard_map/ppermute | solution.py:413
  21.7 4.8 %copy-start = (f32[2,3,4,32,128]{4,3,2,1,0:T(8,128)S(1)}, f32[2,3,4,32,128]{4,3,2,1,0:T(8,128)}, u32[]{:S(2)}) copy-start(f32[2,3,4,32,128]{4,3,2,1,0:T(8,128)} %param.10) | copy-start | bytes 1179652
  21.7 4.8 %copy-start.1 = (f32[2,3,4,32,128]{4,3,2,1,0:T(8,128)S(1)}, f32[2,3,4,32,128]{4,3,2,1,0:T(8,128)}, u32[]{:S(2)}) copy-start(f32[2,3,4,32,128]{4,3,2,1,0:T(8,128)} %param.11) | copy-start | bytes 1179652
  22.6 18.2 %collective-permute-start.3 = (f32[2,12,16,128]{3,2,1,0:T(8,128)}, f32[2,12,16,128]{3,2,1,0:T(8,128)S(1)}, u32[]{:S(2)}, u32[]{:S(2)}) collective-permute-start(f32[2,12,16,128]{3,2,1,0:T(8,128)} %get-tuple-element.34.after_ref), channel_id=1, source_target_pairs={{0,2},{1,3},{2,0},{3,1},{4,6},{5,7},{6,4},{7,5},{8,10},{9,11},{10,... | collective-permute-start | bytes 589832 | tf_op jit(solution)/shard_map/ppermute | solution.py:422
  23.8 16.9 %collective-permute-start.4 = (f32[2,12,16,128]{3,2,1,0:T(8,128)}, f32[2,12,16,128]{3,2,1,0:T(8,128)S(1)}, u32[]{:S(2)}, u32[]{:S(2)}) collective-permute-start(f32[2,12,16,128]{3,2,1,0:T(8,128)} %get-tuple-element.37), channel_id=1, source_target_pairs={{0,4},{1,5},{2,6},{3,7},{4,0},{5,1},{6,2},{7,3},{8,12},{9,13},{10,... | collective-permute-start | bytes 589832 | tf_op jit(solution)/shard_map/ppermute | solution.py:422
  26.5 6.9 %copy-start.7 = (f32[2,16,128]{2,1,0:T(8,128)S(1)}, f32[2,16,128]{2,1,0:T(8,128)}, u32[]{:S(2)}) copy-start(f32[2,16,128]{2,1,0:T(8,128)} %get-tuple-element.31.self_ref) | copy-start | bytes 49156
  26.5 14.3 %collective-permute-start.5 = (f32[2,12,16,128]{3,2,1,0:T(8,128)}, f32[2,12,16,128]{3,2,1,0:T(8,128)}, u32[]{:S(2)}, u32[]{:S(2)}) collective-permute-start(f32[2,12,16,128]{3,2,1,0:T(8,128)} %get-tuple-element.38), channel_id=1, source_target_pairs={{0,6},{1,7},{2,4},{3,5},{4,2},{5,3},{6,0},{7,1},{8,14},{9,15},{10,... | collective-permute-start | bytes 589832 | tf_op jit(solution)/shard_map/ppermute | solution.py:422
  36.5 11.7 %all-to-all-start.1 = ((f32[8,4,1152]{2,1,0:T(4,128)}), f32[8,4,1152]{2,1,0:T(4,128)S(1)}, u32[]{:S(2)}, u32[]{:S(2)}) async-start(f32[8,4,1152]{2,1,0:T(4,128)} %copy-done.5), calls=%async_computation.1 | async-start | bytes 294912 | tf_op jit(solution)/shard_map/all_to_all | solution.py:426
  40.8 7.4 %copy-start.6 = (f32[48,48]{1,0:T(8,128)S(1)}, f32[48,48]{1,0:T(8,128)}, u32[]{:S(2)}) copy-start(f32[48,48]{1,0:T(8,128)} %constant.11.clone.spread_ref) | copy-start | bytes 27652
  44.2 9.8 %collective-permute-start.8 = (f32[2,12,16,128]{3,2,1,0:T(8,128)}, f32[2,12,16,128]{3,2,1,0:T(8,128)S(1)}, u32[]{:S(2)}, u32[]{:S(2)}) collective-permute-start(f32[2,12,16,128]{3,2,1,0:T(8,128)} %get-tuple-element.47), channel_id=1, source_target_pairs={{0,2},{1,3},{2,0},{3,1},{4,6},{5,7},{6,4},{7,5},{8,10},{9,11},{10,... | collective-permute-start | bytes 589832 | tf_op jit(solution)/shard_map/ppermute | solution.py:422
  45.7 9.4 %collective-permute-start.9 = (f32[2,12,16,128]{3,2,1,0:T(8,128)}, f32[2,12,16,128]{3,2,1,0:T(8,128)S(1)}, u32[]{:S(2)}, u32[]{:S(2)}) collective-permute-start(f32[2,12,16,128]{3,2,1,0:T(8,128)} %get-tuple-element.48), channel_id=1, source_target_pairs={{0,4},{1,5},{2,6},{3,7},{4,0},{5,1},{6,2},{7,3},{8,12},{9,13},{10,... | collective-permute-start | bytes 589832 | tf_op jit(solution)/shard_map/ppermute | solution.py:422
  48.1 10.4 %collective-permute-start.10 = (f32[2,12,16,128]{3,2,1,0:T(8,128)S(1)}, f32[2,12,16,128]{3,2,1,0:T(8,128)S(1)}, u32[]{:S(2)}, u32[]{:S(2)}) collective-permute-start(f32[2,12,16,128]{3,2,1,0:T(8,128)S(1)} %get-tuple-element.49), channel_id=1, source_target_pairs={{0,6},{1,7},{2,4},{3,5},{4,2},{5,3},{6,0},{7,1},{8,14},{9,15},{10,... | collective-permute-start | bytes 589832 | tf_op jit(solution)/shard_map/ppermute | solution.py:422
  49.2 11.0 %all-to-all-start.2 = ((f32[8,4,1152]{2,1,0:T(4,128)}), f32[8,4,1152]{2,1,0:T(4,128)S(1)}, u32[]{:S(2)}, u32[]{:S(2)}) async-start(f32[8,4,1152]{2,1,0:T(4,128)} %shard_map.118), calls=%async_computation.2 | async-start | bytes 294912 | tf_op jit(solution)/shard_map/all_to_all | solution.py:426
  58.6 14.0 %copy-start.3 = (f32[2,3,4,32,128]{4,3,2,1,0:T(8,128)S(1)}, f32[2,3,4,32,128]{4,3,2,1,0:T(8,128)}, u32[]{:S(2)}) copy-start(f32[2,3,4,32,128]{4,3,2,1,0:T(8,128)} %param.12) | copy-start | bytes 1179652
  58.6 23.9 %collective-permute-start.11 = (f32[4,12,16,128]{3,2,1,0:T(8,128)S(1)}, f32[4,12,16,128]{3,2,1,0:T(8,128)}, u32[]{:S(2)}, u32[]{:S(2)}) collective-permute-start(f32[4,12,16,128]{3,2,1,0:T(8,128)S(1)} %shard_map.122), channel_id=1, source_target_pairs={{0,1},{1,0},{2,3},{3,2},{4,5},{5,4},{6,7},{7,6},{8,9},{9,8},{10,11... | collective-permute-start | bytes 1179656 | tf_op jit(solution)/shard_map/ppermute | solution.py:422
  61.0 11.7 %copy-start.4 = (s32[4,32,128]{2,1,0:T(8,128)S(1)}, s32[4,32,128]{2,1,0:T(8,128)}, u32[]{:S(2)}) copy-start(s32[4,32,128]{2,1,0:T(8,128)} %refs_2_.1) | copy-start | bytes 196612
  61.0 21.5 %all-to-all-start.3 = ((f32[32,4,384]{2,1,0:T(4,128)}), f32[32,4,384]{2,1,0:T(4,128)S(1)}, u32[]{:S(2)}, u32[]{:S(2)}) async-start(f32[32,4,384]{2,1,0:T(4,128)} %get-tuple-element.40), calls=%async_computation.3 | async-start | bytes 393216 | tf_op jit(solution)/shard_map/all_to_all | solution.py:418
  70.8 6.0 %collective-permute-start.6 = (f32[2,12,128]{2,1,0:T(8,128)S(1)}, f32[2,12,128]{2,1,0:T(8,128)S(1)}, u32[]{:S(2)}, u32[]{:S(2)}) collective-permute-start(f32[2,12,128]{2,1,0:T(8,128)S(1)} %get-tuple-element.41), channel_id=1, source_target_pairs={{0,8},{8,16},{16,24},{24,32},{32,40},{40,48},{48,56},{56,64},{64,7... | collective-permute-start | bytes 36872 | tf_op jit(solution)/shard_map/ppermute | solution.py:413
  72.5 5.4 %collective-permute-start.7 = (f32[2,12,128]{2,1,0:T(8,128)S(1)}, f32[2,12,128]{2,1,0:T(8,128)S(1)}, u32[]{:S(2)}, u32[]{:S(2)}) collective-permute-start(f32[2,12,128]{2,1,0:T(8,128)S(1)} %get-tuple-element.42), channel_id=1, source_target_pairs={{0,248},{8,0},{16,8},{24,16},{32,24},{40,32},{48,40},{56,48},{64,5... | collective-permute-start | bytes 36872 | tf_op jit(solution)/shard_map/ppermute | solution.py:413
  74.2 8.3 %copy-start.8 = (s32[24,128]{1,0:T(8,128)S(1)}, s32[24,128]{1,0:T(8,128)}, u32[]{:S(2)}) copy-start(s32[24,128]{1,0:T(8,128)} %get-tuple-element.27.idx_ref) | copy-start | bytes 36868
  (2 other events, 2.4 us)

commit v9 on v7

--- a/solution.py
+++ b/solution.py
@@ -32,11 +32,36 @@
 
 FIRST, SECOND = tables(2 * PARTS)
 MIXED = (SECOND + damping * FIRST).astype(np.float32)
-SPREAD = np.kron(FIRST, np.eye(3)).astype(np.float32)
+
+
+def rate_tables():
+    table = np.zeros((PARTS, 2, 16, PARTS, 16), np.float32)
+    for me in range(PARTS):
+        for odd in range(2):
+            for row in range(16):
+                channel = row if row < 8 else row - 4 * odd
+                if channel < 8 and row >= 8 or channel >= 12:
+                    continue
+                field, s, c = channel // 6, channel // 3 % 2, channel % 3
+                for t in range(2):
+                    table[me, odd, 6 * field + 3 * t + c, :, row] = FIRST[2 * me + t, s::2]
+    return table.reshape(PARTS, 2, 16, 16 * PARTS)
+
+
+RATES = rate_tables()
 
 
 def far_place(offset):
     return 8 + (offset - 3) // 3, SEG * ((offset - 3) % 3)
+
+
+def fold(rows):
+    return jnp.concatenate([rows[0:4], rows[4:8], rows[8:12]], axis=1)
+
+
+def unfold(rows):
+    width = rows.shape[1] // 3
+    return jnp.concatenate([rows[:, width * k : width * (k + 1)] for k in range(3)], axis=0)
 
 
 def lane_roll(x, shift):
@@ -197,8 +222,8 @@
         move.wait()
 
 
-def gap_kernel(p_ref, chunk_ref, up_ref, down_ref, self_ref, parts_ref, after_ref,
-               idx_ref, kind_ref, gap_ref, here_ref):
+def gap_kernel(p_ref, chunk_ref, up_ref, down_ref, self_ref, parts_ref, after1, after2, after3,
+               idx_ref, kind_ref, gap_hbm, here_ref, gap_ref, sems):
     p = p_ref[0]
 
     def asked(d):
@@ -211,60 +236,68 @@
     idx_ref[...] = jnp.concatenate(rows + [jnp.full((7, 128), -1.0, f32)], axis=0).astype(i32)
     kind_ref[...] = jnp.concatenate([t[13:14] for t in tiles] + [jnp.zeros((7, 128), f32)], axis=0)
     gather_rows(parts_ref, idx_ref, here_ref)
-    for tile in range(24):
-        gap = tiles[tile][0:12] - here_ref[tile] if tile < 17 else jnp.zeros((12, 128), f32)
-        gap_ref[tile // 3, :, 128 * (tile % 3) : 128 * (tile % 3 + 1)] = gap
-
-
-def force_kernel(me_ref, kind_ref, spread_ref, gap_ref, after_ref, out_ref, r_ref, d_ref, f_ref, t_ref):
+    for m in range(9):
+        low = []
+        for tile in (2 * m, 2 * m + 1):
+            gap = tiles[tile][0:12] - here_ref[tile] if tile < 17 else jnp.zeros((12, 128), f32)
+            low.append(gap[8:12])
+            if tile < 17:
+                gap_ref[8 * tile : 8 * tile + 8] = gap[0:8]
+        gap_ref[8 * (17 + m) : 8 * (18 + m)] = jnp.concatenate(low, axis=0)
+    copies = [pltpu.make_async_copy(gap_ref, gap_hbm.at[k], sems.at[k]) for k in range(PARTS)]
+    for copy in copies:
+        copy.start()
+    for copy in copies:
+        copy.wait()
+
+
+def force_kernel(p_ref, me_ref, kind_ref, rates_ref, gap_ref, after1, after2,
+                 val_ref, chunk_ref, up_ref, down_ref, self_ref, all_ref):
+    p = p_ref[0]
     me = me_ref[0]
-    for k in range(PARTS):
-        r_ref[6 * k : 6 * k + 6] = gap_ref[k, 0:6, :]
-        d_ref[6 * k : 6 * k + 6] = gap_ref[k, 6:12, :]
-    r = r_ref[...]
-    dr = d_ref[...]
-    w = jnp.dot(spread_ref[...], r, precision=lax.Precision.HIGHEST, preferred_element_type=f32)
-    dw = jnp.dot(spread_ref[...], dr, precision=lax.Precision.HIGHEST, preferred_element_type=f32)
-    bolted = jnp.concatenate([kind_ref[pl.ds(3 * me + k, 1), :] for k in range(3)], axis=1)
-    slide = jnp.tanh(w / slip_speed)
-    opened = jnp.tanh(r / clearance)
-    friction = bolt_stiff * r + slip_force * slide
-    contact = stop_stiff * (r - clearance * opened)
-    f_ref[...] = bolted * friction + (1.0 - bolted) * contact
-    tangent_friction = bolt_stiff * dr + slip_force * (1.0 - slide * slide) / slip_speed * dw
-    tangent_contact = stop_stiff * opened * opened * dr
-    t_ref[...] = bolted * tangent_friction + (1.0 - bolted) * tangent_contact
-    for k in range(PARTS):
-        out_ref[k, 0:6, :] = f_ref[6 * k : 6 * k + 6]
-        out_ref[k, 6:12, :] = t_ref[6 * k : 6 * k + 6]
-
-
-def reply_kernel(p_ref, force_ref, chunk_ref, up_ref, down_ref, self_ref):
-    p = p_ref[0]
-
-    def force(tile):
-        return force_ref[tile // 3, :, 128 * (tile % 3) : 128 * (tile % 3 + 1)]
-
+    for odd in range(2):
+        count = 9 - odd
+        for m in range(count):
+            for k in range(PARTS):
+                tile = 2 * m + odd
+                all_ref[16 * k : 16 * k + 8, 128 * m : 128 * (m + 1)] = gap_ref[k, 8 * tile : 8 * tile + 8]
+                all_ref[16 * k + 8 : 16 * k + 16, 128 * m : 128 * (m + 1)] = gap_ref[k, 8 * (17 + m) : 8 * (18 + m)]
+        width = 128 * count
+        rates = jnp.dot(
+            rates_ref[me, odd], all_ref[:, :width], precision=lax.Precision.HIGHEST, preferred_element_type=f32
+        )
+        mine = all_ref[pl.ds(pl.multiple_of(16 * me, 16), 16), :width]
+        mine = jnp.concatenate([mine[0:8], mine[8 + 4 * odd : 12 + 4 * odd]], axis=0)
+        r, dr, w, dw = mine[0:6], mine[6:12], rates[0:6], rates[6:12]
+        bolted = jnp.concatenate([kind_ref[2 * m + odd : 2 * m + odd + 1] for m in range(count)], axis=1)
+        slide = jnp.tanh(w / slip_speed)
+        opened = jnp.tanh(r / clearance)
+        friction = bolt_stiff * r + slip_force * slide
+        contact = stop_stiff * (r - clearance * opened)
+        force = bolted * friction + (1.0 - bolted) * contact
+        tangent_friction = bolt_stiff * dr + slip_force * (1.0 - slide * slide) / slip_speed * dw
+        tangent_contact = stop_stiff * opened * opened * dr
+        tangent = bolted * tangent_friction + (1.0 - bolted) * tangent_contact
+        both = jnp.concatenate([force, tangent], axis=0)
+        for m in range(count):
+            val_ref[2 * m + odd] = both[:, 128 * m : 128 * (m + 1)]
+    val_ref[17] = jnp.zeros((12, 128), f32)
     for d in (0, 1, SLABS - 1):
-        chunk_ref[(p - d) & (SLABS - 1)] = jnp.zeros((12, 128), f32)
+        chunk_ref[(p - d) & (SLABS - 1)] = jnp.zeros((4, 384), f32)
     for d, tile in ((2, 6), (SLABS - 2, 7)):
-        chunk_ref[(p - d) & (SLABS - 1)] = force(tile)
+        chunk_ref[(p - d) & (SLABS - 1)] = fold(val_ref[tile])
     for d in range(3, SLABS - 2):
         tile, seg = far_place(d)
-        chunk_ref[(p - d) & (SLABS - 1)] = lane_roll(force(tile), -seg)
-    for k in range(2):
-        self_ref[k] = force(k)
-        down_ref[k] = force(2 + k)
-        up_ref[k] = force(4 + k)
-
-
-def partner_kernel(idx_ref, force_ref, lin_ref, out_ref, val_ref, sum_ref):
-    for tile in range(17):
-        val_ref[tile] = -force_ref[tile // 3, :, 128 * (tile % 3) : 128 * (tile % 3 + 1)]
-    val_ref[17] = jnp.zeros((12, 128), f32)
+        chunk_ref[(p - d) & (SLABS - 1)] = fold(lane_roll(val_ref[tile], -seg))
+    self_ref[...] = val_ref[0:2]
+    down_ref[...] = val_ref[2:4]
+    up_ref[...] = val_ref[4:6]
+
+
+def partner_kernel(idx_ref, val_ref, lin_ref, out_ref, sum_ref):
     scatter_rows(val_ref, idx_ref, sum_ref)
     for x in range(4):
-        out_ref[:, x] = lin_ref[:, x] + sum_ref[:, 128 * x : 128 * (x + 1)].reshape(12, 32, 128)
+        out_ref[:, x] = lin_ref[:, x] - sum_ref[:, 128 * x : 128 * (x + 1)].reshape(12, 32, 128)
 
 
 def final_kernel(p_ref, me_ref, idx_ref, chunk_ref, up_ref, down_ref, self_ref, part_ref, mass_ref,
@@ -278,7 +311,7 @@
         copy.start()
 
     def listed(d):
-        return chunk_ref[(p + d) & (SLABS - 1)]
+        return unfold(chunk_ref[(p + d) & (SLABS - 1)])
 
     tiles = [self_ref[0], self_ref[1], down_ref[0], down_ref[1], up_ref[0], up_ref[1], listed(2), listed(SLABS - 2)]
     tiles += merge_far(listed, 12, 0.0) + [jnp.zeros((12, 128), f32)]
@@ -306,7 +339,7 @@
         out_ref[k] = ref[1]
 
 
-def time_kernel(me_ref, same_ref, other_ref, y1_ref, y2_ref, y3_ref, *refs):
+def time_kernel(me_ref, same_ref, other_ref, y1_ref, y2_ref, y3_ref, after_ref, *refs):
     outs, in_ref, out_ref, sems = refs[:4], refs[4], refs[5], refs[6]
     me = me_ref[0]
     pairs = [(same_ref.at[0], in_ref.at[0]), (other_ref.at[0], in_ref.at[1])]
@@ -389,7 +422,7 @@
         kernel,
         out_shape=[jax.ShapeDtypeStruct(s, d) for s, d in outs],
         in_specs=specs,
-        out_specs=[pl.BlockSpec(memory_space=pl.ANY if k in kept else pltpu.VMEM) for k in range(len(outs))],
+        out_specs=[pl.BlockSpec(memory_space=pltpu.HBM if k in kept else pltpu.VMEM) for k in range(len(outs))],
         scratch_shapes=list(scratch),
         compiler_params=pltpu.CompilerParams(vmem_limit_bytes=limit),
     )(*args)
@@ -400,17 +433,13 @@
     return lax.ppermute(x, "mesh", pairs)
 
 
-def exchange(chunk, *near):
-    near = [shift(x, by) for x, by in zip(near, (1, -1))]
-    return lax.all_to_all(chunk, "mesh", split_axis=0, concat_axis=0, tiled=True), *near
+def exchange(chunk, up, down):
+    up, down = shift(up, 1), shift(down, -1)
+    return lax.all_to_all(chunk, "mesh", split_axis=0, concat_axis=0, tiled=True), up, down
 
 
 def swap(x, bit):
     return lax.ppermute(x, "inst", [(i, i ^ bit) for i in range(PARTS)])
-
-
-def inst_split(x):
-    return lax.all_to_all(x, "inst", split_axis=0, concat_axis=0, tiled=True)
 
 
 def on_device(displacement, direction, forcing, material_ids, materials, joint_owner, joint_local, joint_remote, joint_kind):
@@ -455,30 +484,22 @@
     other = swap(other, 1)
     joined = call(join_kernel, [pair] * 3, same, other, smem=())
     turned = [swap(x, 2 * k + 2) for k, x in enumerate(joined)]
-    blocks = [pltpu.VMEM((PARTS, 12, 16, 128), f32)] * 2
-    inertia = call(time_kernel, [pair] * 4, me, same, other, *turned, away=range(1, 6), scratch=blocks + [pltpu.SemaphoreType.DMA((5,))])
-
-    part = ((PARTS, 12, 384), f32)
     fields_parts = call(split_kernel, [(parts, bf16)], disp, dire, smem=())[0]
     far_idx, kind, gap = call(
         gap_kernel,
-        [index, ((24, 128), f32), part],
-        p, chunk, up, down, own, fields_parts, joined[0],
-        away=(6,),
-        scratch=[pltpu.VMEM((SIDE, 12, 128), f32)],
+        [index, ((24, 128), f32), ((PARTS, 8 * 26, 128), f32)],
+        p, chunk, up, down, own, fields_parts, *turned,
+        away=(6, 7, 8),
+        kept=(2,),
+        scratch=[
+            pltpu.VMEM((SIDE, 12, 128), f32),
+            pltpu.VMEM((8 * 26, 128), f32),
+            pltpu.SemaphoreType.DMA((PARTS,)),
+        ],
     )
-    force = call(
-        force_kernel,
-        [part],
-        me, kind, jnp.asarray(SPREAD), inst_split(gap), inertia[0],
-        away=(4,),
-        scratch=[pltpu.VMEM((48, 384), f32)] * 4,
-    )[0]
-    force = inst_split(force)
-    turned = [inertia[0]] + [swap(inertia[k], 2 * k) for k in (1, 2, 3)]
-    two = ((2, 12, 128), f32)
-    chunk, *replies, own = call(reply_kernel, [((SLABS, 12, 128), f32), two, two, two], p, force)
-    chunk, *replies = exchange(chunk, *replies)
+    gap = lax.all_to_all(gap, "inst", split_axis=0, concat_axis=0, tiled=True)
+    blocks = [pltpu.VMEM((PARTS, 12, 16, 128), f32)] * 2
+    inertia = call(time_kernel, [pair] * 4, me, same, other, *turned, far_idx, away=range(1, 7), scratch=blocks + [pltpu.SemaphoreType.DMA((5,))])
 
     lin, mass = call(
         lambda *refs: stiff_kernel(*refs, materials=materials.shape[0]),
@@ -486,13 +507,25 @@
         p, materials, material_ids, disp, dire, forcing.reshape(fields), shift(high, 1, False), shift(low, -1, False),
         smem=(0, 1),
     )
+    two = ((2, 12, 128), f32)
+    force, chunk, up2, down2, own = call(
+        force_kernel,
+        [((SIDE, 12, 128), f32), ((SLABS, 4, 384), f32), two, two, two],
+        p, me, kind, jnp.asarray(RATES), gap, inertia[0], mass,
+        smem=(0, 1),
+        away=(5, 6),
+        scratch=[pltpu.VMEM((16 * PARTS, 9 * 128), f32)],
+    )
+    turned = [inertia[0]] + [swap(inertia[k], 2 * k) for k in (1, 2, 3)]
+    chunk, up2, down2 = exchange(chunk, up2, down2)
+
     other = swap(call(turn_kernel, [half], *turned, smem=())[0], 1)
     adding = [pltpu.VMEM((SIDE, 12, 128), f32), pltpu.VMEM((384, 512), f32)]
-    partial = call(partner_kernel, [(whole, f32)], far_idx, force, lin, smem=(), scratch=adding)[0]
+    partial = call(partner_kernel, [(whole, f32)], far_idx, force, lin, smem=(), scratch=adding[1:])[0]
     residual, jacobian = call(
         final_kernel,
         [(fields, f32)] * 2,
-        p, me, own_idx, chunk, *replies, own, partial, mass, *turned, other,
+        p, me, own_idx, chunk, up2, down2, own, partial, mass, *turned, other,
         smem=(0, 1),
         away=range(9, 14),
         scratch=adding + blocks[:1] + [pltpu.SemaphoreType.DMA((PARTS,))],

time: 96.8 us -> 104 us (1.074)
  the two profiles are of different devices: /device:TPU:4 before, /device:TPU:1 now
where the time goes in v9:
time: 104 us; the launch traced here: 103 us
  starting transfers between devices  48.1 us (46%)
  waiting for transfers between devices  27 us (26%)
  Pallas kernels  22.3 us (21%)
  local copies, waits for them, and re-layouts  4.61 us (4%)
    all_to_all x2, starting transfers between devices, exchange(): lax.all_to_all(chunk, 'mesh', split_axis=0, concat_axis=0, tiled=True)  22.8 us
    pallas_call x10, Pallas kernels, call(): pl.pallas_call(kernel, out_shape=[jax.ShapeDtypeStruct(s, d) for s, d in...  22.3 us
    ppermute x8, waiting for transfers between devices, swap(): return lax.ppermute(x, 'inst', [(i, i ^ bit) for i in range(PARTS)])  13.7 us
    ppermute x6, starting transfers between devices, shift(): return lax.ppermute(x, 'mesh', pairs)  11 us
    ppermute x8, starting transfers between devices, swap(): return lax.ppermute(x, 'inst', [(i, i ^ bit) for i in range(PARTS)])  10.7 us
    all_to_all x2, waiting for transfers between devices, exchange(): lax.all_to_all(chunk, 'mesh', split_axis=0, concat_axis=0, tiled=True)  7.39 us
    ppermute x6, waiting for transfers between devices, shift(): return lax.ppermute(x, 'mesh', pairs)  5.91 us
    unnamed x33, local copies, waits for them, and re-layouts  4.61 us
  transfers between devices with their start and end apart: 17, of which 10 were waited for; matrix products, arithmetic and copies ran while one was open for 1% of the time, Pallas kernels for 9%

profile of v9, /device:TPU:1, one launch (start us, length us, event | category | flops | bytes accessed | tf_op | source)
XLA Modules:
  0.0 102.9 jit_solution(409184111623051168)
XLA Ops:
  0.6 4.9 %shard_map.113 = (s32[24,128]{1,0:T(8,128)}, f32[32,16,128]{2,1,0:T(8,128)}, f32[2,16,128]{2,1,0:T(8,128)}, f32[2,16,128]{2,1,0:T(8,128)}, f32[2,16,128]{2,1,0:T...) custom-call(s32[1]{0:T(128)} %bitcast.p_ref.refs_0_, ...), custom_call_target="tpu_custom_call" | custom-call | tf_op jit(solution)/shard_map/pallas_call | solution.py:421
  5.6 2.1 %collective-permute-start.2 = (f32[4,12,16,128]{3,2,1,0:T(8,128)}, f32[4,12,16,128]{3,2,1,0:T(8,128)S(1)}, u32[]{:S(2)}, u32[]{:S(2)}) collective-permute-start(f32[4,12,16,128]{3,2,1,0:T(8,128)} %get-tuple-element.36), channel_id=1, source_target_pairs={{0,1},{1,0},{2,3},{3,2},{4,5},{5,4},{6,7},{7,6},{8,9},{9,8},{10,11... | collective-permute-start | bytes 1179656 | tf_op jit(solution)/shard_map/ppermute | solution.py:442
  7.7 11.9 %all-to-all-start = ((f32[32,16,128]{2,1,0:T(8,128)}), f32[32,16,128]{2,1,0:T(8,128)S(1)}, u32[]{:S(2)}, u32[]{:S(2)}) async-start(f32[32,16,128]{2,1,0:T(8,128)} %get-tuple-element.31), calls=%async_computation | async-start | bytes 524288 | tf_op jit(solution)/shard_map/all_to_all | solution.py:438
  21.7 2.6 %collective-permute-start.4 = (f32[2,12,16,128]{3,2,1,0:T(8,128)}, f32[2,12,16,128]{3,2,1,0:T(8,128)S(1)}, u32[]{:S(2)}, u32[]{:S(2)}) collective-permute-start(f32[2,12,16,128]{3,2,1,0:T(8,128)} %get-tuple-element.38), channel_id=1, source_target_pairs={{0,4},{1,5},{2,6},{3,7},{4,0},{5,1},{6,2},{7,3},{8,12},{9,13},{10,... | collective-permute-start | bytes 589832 | tf_op jit(solution)/shard_map/ppermute | solution.py:442
  24.3 2.4 %collective-permute-start = (f32[2,16,128]{2,1,0:T(8,128)S(1)}, f32[2,16,128]{2,1,0:T(8,128)S(1)}, u32[]{:S(2)}, u32[]{:S(2)}) collective-permute-start(f32[2,16,128]{2,1,0:T(8,128)S(1)} %copy-done.15), channel_id=1, source_target_pairs={{0,8},{8,16},{16,24},{24,32},{32,40},{40,48},{48,56},{56,64},{64,7... | collective-permute-start | bytes 49160 | tf_op jit(solution)/shard_map/ppermute | solution.py:433
  27.6 2.6 %collective-permute-done.1.down_ref = f32[2,16,128]{2,1,0:T(8,128)S(1)} collective-permute-done((f32[2,16,128]{2,1,0:T(8,128)S(1)}, f32[2,16,128]{2,1,0:T(8,128)S(1)}, u32[]{:S(2)}, u32[]{:S(2)}) %collective-permute-start.1) | collective-permute-done | bytes 16416 | tf_op jit(solution)/shard_map/ppermute | solution.py:433
  30.2 2.8 %all-to-all-done.chunk_ref = f32[32,16,128]{2,1,0:T(8,128)S(1)} async-done(((f32[32,16,128]{2,1,0:T(8,128)}), f32[32,16,128]{2,1,0:T(8,128)S(1)}, u32[]{:S(2)}, u32[]{:S(2)}) %all-to-all-start) | async-done | bytes 262176 | tf_op jit(solution)/shard_map/all_to_all | solution.py:438
  33.6 1.9 %collective-permute-done.5.after3.y3_ref = f32[2,12,16,128]{3,2,1,0:T(8,128)S(1)} collective-permute-done((f32[2,12,16,128]{3,2,1,0:T(8,128)S(1)}, f32[2,12,16,128]{3,2,1,0:T(8,128)S(1)}, u32[]{:S(2)}, u32[]{:S(2)}) %collective-permute-start.5) | collective-permute-done | bytes 196640 | tf_op jit(solution)/shard_map/ppermute | solution.py:442
  35.5 3.5 %shard_map.116 = (s32[24,128]{1,0:T(8,128)S(1)}, f32[24,128]{1,0:T(8,128)S(1)}, f32[8,208,128]{2,1,0:T(8,128)}) custom-call(s32[1]{0:T(128)} %bitcast.p_ref.refs_0_, f32[32,16,128]{2,1,0:T(8,128)S(1)} %all-to-all-done.chunk_ref, f32[2,16,128]{2,1,0:T(8,128)S(1)} %collective-permute-done.up_ref, f32[2,16,128]{2,1,0:T(8,128)S(1)} %collective-permute-done.1.down_ref, ...), custom_call_target="tpu_custom_call" | custom-call | tf_op jit(solution)/shard_map/pallas_call | solution.py:421
  39.6 3.5 %all-to-all-start.1 = ((f32[8,208,128]{2,1,0:T(8,128)}), f32[8,208,128]{2,1,0:T(8,128)S(1)}, u32[]{:S(2)}, u32[]{:S(2)}) async-start(f32[8,208,128]{2,1,0:T(8,128)} %get-tuple-element.41), calls=%async_computation.1 | async-start | bytes 1703936 | tf_op jit(solution)/shard_map/all_to_all | solution.py:500
  43.1 4.8 %collective-permute-start.6 = (f32[13,32,128]{2,1,0:T(8,128)}, f32[13,32,128]{2,1,0:T(8,128)S(1)}, u32[]{:S(2)}, u32[]{:S(2)}) collective-permute-start(f32[13,32,128]{2,1,0:T(8,128)} %get-tuple-element.44), channel_id=1, source_target_pairs={{0,8},{8,16},{16,24},{24,32},{32,40},{40,48},{48,56},{56,64},{64,7... | collective-permute-start | bytes 638984 | tf_op jit(solution)/shard_map/ppermute | solution.py:433
  47.9 1.9 %collective-permute-start.7 = (f32[13,32,128]{2,1,0:T(8,128)}, f32[13,32,128]{2,1,0:T(8,128)}, u32[]{:S(2)}, u32[]{:S(2)}) collective-permute-start(f32[13,32,128]{2,1,0:T(8,128)} %get-tuple-element.45), channel_id=1, source_target_pairs={{8,0},{16,8},{24,16},{32,24},{40,32},{48,40},{56,48},{64,56},{72,6... | collective-permute-start | bytes 638984 | tf_op jit(solution)/shard_map/ppermute | solution.py:433
  49.9 2.0 %shard_map.117 = (f32[2,12,16,128]{3,2,1,0:T(8,128)S(1)}, f32[2,12,16,128]{3,2,1,0:T(8,128)S(1)}, f32[2,12,16,128]{3,2,1,0:T(8,128)S(1)}, f32[2,12,16,128]{3,2,1,0:T(8,128)S(1)}) custom-call(s32[1]{0:T(128)} %bitcast.1.me_ref, f32[4,12,16,128]{3,2,1,0:T(8,128)S(1)} %copy-done.2, f32[4,12,16,128]{3,2,1,0:T(8,128)S(1)} %collective-permute-done.2.other_ref, ...), custom_call_target="tpu_custom_call" | custom-call | tf_op jit(solution)/shard_map/pallas_call | solution.py:421
  53.6 2.4 %collective-permute-start.11 = (f32[2,12,16,128]{3,2,1,0:T(8,128)S(1)}, f32[2,12,16,128]{3,2,1,0:T(8,128)S(1)}, u32[]{:S(2)}, u32[]{:S(2)}) collective-permute-start(f32[2,12,16,128]{3,2,1,0:T(8,128)S(1)} %get-tuple-element.54), channel_id=1, source_target_pairs={{0,4},{1,5},{2,6},{3,7},{4,0},{5,1},{6,2},{7,3},{8,12},{9,13},{10,... | collective-permute-start | bytes 589832 | tf_op jit(solution)/shard_map/ppermute | solution.py:442
  56.1 3.1 %collective-permute-done.10.y1_ref = f32[2,12,16,128]{3,2,1,0:T(8,128)S(1)} collective-permute-done((f32[2,12,16,128]{3,2,1,0:T(8,128)S(1)}, f32[2,12,16,128]{3,2,1,0:T(8,128)S(1)}, u32[]{:S(2)}, u32[]{:S(2)}) %collective-permute-start.10) | collective-permute-done | bytes 196640 | tf_op jit(solution)/shard_map/ppermute | solution.py:442
  59.2 5.6 %collective-permute-done.11.y2_ref = f32[2,12,16,128]{3,2,1,0:T(8,128)S(1)} collective-permute-done((f32[2,12,16,128]{3,2,1,0:T(8,128)S(1)}, f32[2,12,16,128]{3,2,1,0:T(8,128)S(1)}, u32[]{:S(2)}, u32[]{:S(2)}) %collective-permute-start.11) | collective-permute-done | bytes 196640 | tf_op jit(solution)/shard_map/ppermute | solution.py:442
  64.8 2.6 %collective-permute-done.12.y3_ref = f32[2,12,16,128]{3,2,1,0:T(8,128)S(1)} collective-permute-done((f32[2,12,16,128]{3,2,1,0:T(8,128)S(1)}, f32[2,12,16,128]{3,2,1,0:T(8,128)S(1)}, u32[]{:S(2)}, u32[]{:S(2)}) %collective-permute-start.12) | collective-permute-done | bytes 196640 | tf_op jit(solution)/shard_map/ppermute | solution.py:442
  71.0 1.9 %shard_map.118 = (f32[12,4,32,128]{3,2,1,0:T(8,128)S(1)}, f32[4,32,128]{2,1,0:T(8,128)S(1)}) custom-call(s32[1]{0:T(128)} %bitcast.p_ref.refs_0_, f32[16,4]{1,0:T(8,128)S(1)} %copy-done.8, s32[4,32,128]{2,1,0:T(8,128)S(1)} %copy-done.4, f32[6,4,32,128]{3,2,1,0:T(8,128)S(1)} %bitcast.13, f32[6,4,32,128]{3,2,1,0:T(8,128)S(1)} %bitcast.16, ...), custom_call_target="tpu_custom_call" | custom-call | tf_op jit(solution)/shard_map/pallas_call | solution.py:421
  76.0 10.9 %all-to-all-start.2 = ((f32[32,4,384]{2,1,0:T(4,128)}), f32[32,4,384]{2,1,0:T(4,128)S(1)}, u32[]{:S(2)}, u32[]{:S(2)}) async-start(f32[32,4,384]{2,1,0:T(4,128)} %get-tuple-element.47), calls=%async_computation.2 | async-start | bytes 393216 | tf_op jit(solution)/shard_map/all_to_all | solution.py:438
  86.9 1.9 %collective-permute-start.8 = (f32[2,12,128]{2,1,0:T(8,128)S(1)}, f32[2,12,128]{2,1,0:T(8,128)S(1)}, u32[]{:S(2)}, u32[]{:S(2)}) collective-permute-start(f32[2,12,128]{2,1,0:T(8,128)S(1)} %get-tuple-element.48), channel_id=1, source_target_pairs={{0,8},{8,16},{16,24},{24,32},{32,40},{40,48},{48,56},{56,64},{64,7... | collective-permute-start | bytes 36872 | tf_op jit(solution)/shard_map/ppermute | solution.py:433
  88.8 2.6 %shard_map.120.part_ref = f32[12,4,32,128]{3,2,1,0:T(8,128)S(1)} custom-call(s32[24,128]{1,0:T(8,128)S(1)} %copy-done.7, f32[18,12,128]{2,1,0:T(8,128)S(1)} %get-tuple-element.51.val_ref, f32[12,4,32,128]{3,2,1,0:T(8,128)S(1)} %get-tuple-element.52.lin_ref), custom_call_target="tpu_custom_call" | custom-call | tf_op jit(solution)/shard_map/pallas_call | solution.py:421
  91.4 2.6 %collective-permute-done.9.down_ref = f32[2,12,128]{2,1,0:T(8,128)S(1)} collective-permute-done((f32[2,12,128]{2,1,0:T(8,128)S(1)}, f32[2,12,128]{2,1,0:T(8,128)S(1)}, u32[]{:S(2)}, u32[]{:S(2)}) %collective-permute-start.9) | collective-permute-done | bytes 12320 | tf_op jit(solution)/shard_map/ppermute | solution.py:433
  94.0 4.6 %all-to-all-done.2.chunk_ref = f32[32,4,384]{2,1,0:T(4,128)S(1)} async-done(((f32[32,4,384]{2,1,0:T(4,128)}), f32[32,4,384]{2,1,0:T(4,128)S(1)}, u32[]{:S(2)}, u32[]{:S(2)}) %all-to-all-start.2) | async-done | bytes 196640 | tf_op jit(solution)/shard_map/all_to_all | solution.py:438
  98.6 4.1 %shard_map.122 = (f32[6,4,32,128]{3,2,1,0:T(8,128)}, f32[6,4,32,128]{3,2,1,0:T(8,128)}) custom-call(s32[1]{0:T(128)} %bitcast.p_ref.refs_0_, s32[1]{0:T(128)} %bitcast.1.me_ref, s32[24,128]{1,0:T(8,128)S(1)} %copy-done.10, f32[32,4,384]{2,1,0:T(4,128)S(1)} %all-to-all-done.2.chunk_ref, f32[2,12,128]{2,1,0:T(8,128)S(1)} %collective-permute-done.8.up_ref, ...), custom_call_target="tpu_custom_call" | custom-call | tf_op jit(solution)/shard_map/pallas_call | solution.py:421
  (53 shorter events, 12.7 us)
Async XLA Ops:
  5.6 14.0 %copy-start.2 = (f32[4,12,16,128]{3,2,1,0:T(8,128)S(1)}, f32[4,12,16,128]{3,2,1,0:T(8,128)}, u32[]{:S(2)}) copy-start(f32[4,12,16,128]{3,2,1,0:T(8,128)} %get-tuple-element.35.same_ref) | copy-start | bytes 1179652
  5.6 14.0 %collective-permute-start.2 = (f32[4,12,16,128]{3,2,1,0:T(8,128)}, f32[4,12,16,128]{3,2,1,0:T(8,128)S(1)}, u32[]{:S(2)}, u32[]{:S(2)}) collective-permute-start(f32[4,12,16,128]{3,2,1,0:T(8,128)} %get-tuple-element.36), channel_id=1, source_target_pairs={{0,1},{1,0},{2,3},{3,2},{4,5},{5,4},{6,7},{7,6},{8,9},{9,8},{10,11... | collective-permute-start | bytes 1179656 | tf_op jit(solution)/shard_map/ppermute | solution.py:442
  7.7 16.6 %copy-start.15 = (f32[2,16,128]{2,1,0:T(8,128)S(1)}, f32[2,16,128]{2,1,0:T(8,128)}, u32[]{:S(2)}) copy-start(f32[2,16,128]{2,1,0:T(8,128)} %get-tuple-element.32) | copy-start | bytes 49156
  7.7 19.0 %copy-start.14 = (f32[2,16,128]{2,1,0:T(8,128)S(1)}, f32[2,16,128]{2,1,0:T(8,128)}, u32[]{:S(2)}) copy-start(f32[2,16,128]{2,1,0:T(8,128)} %get-tuple-element.33) | copy-start | bytes 49156
  7.7 25.3 %all-to-all-start = ((f32[32,16,128]{2,1,0:T(8,128)}), f32[32,16,128]{2,1,0:T(8,128)S(1)}, u32[]{:S(2)}, u32[]{:S(2)}) async-start(f32[32,16,128]{2,1,0:T(8,128)} %get-tuple-element.31), calls=%async_computation | async-start | bytes 524288 | tf_op jit(solution)/shard_map/all_to_all | solution.py:438
  20.4 12.6 %collective-permute-start.3 = (f32[2,12,16,128]{3,2,1,0:T(8,128)}, f32[2,12,16,128]{3,2,1,0:T(8,128)S(1)}, u32[]{:S(2)}, u32[]{:S(2)}) collective-permute-start(f32[2,12,16,128]{3,2,1,0:T(8,128)} %get-tuple-element.37), channel_id=1, source_target_pairs={{0,2},{1,3},{2,0},{3,1},{4,6},{5,7},{6,4},{7,5},{8,10},{9,11},{10,... | collective-permute-start | bytes 589832 | tf_op jit(solution)/shard_map/ppermute | solution.py:442
  21.7 11.9 %collective-permute-start.4 = (f32[2,12,16,128]{3,2,1,0:T(8,128)}, f32[2,12,16,128]{3,2,1,0:T(8,128)S(1)}, u32[]{:S(2)}, u32[]{:S(2)}) collective-permute-start(f32[2,12,16,128]{3,2,1,0:T(8,128)} %get-tuple-element.38), channel_id=1, source_target_pairs={{0,4},{1,5},{2,6},{3,7},{4,0},{5,1},{6,2},{7,3},{8,12},{9,13},{10,... | collective-permute-start | bytes 589832 | tf_op jit(solution)/shard_map/ppermute | solution.py:442
  24.3 11.1 %collective-permute-start.5 = (f32[2,12,16,128]{3,2,1,0:T(8,128)S(1)}, f32[2,12,16,128]{3,2,1,0:T(8,128)S(1)}, u32[]{:S(2)}, u32[]{:S(2)}) collective-permute-start(f32[2,12,16,128]{3,2,1,0:T(8,128)S(1)} %get-tuple-element.39), channel_id=1, source_target_pairs={{0,6},{1,7},{2,4},{3,5},{4,2},{5,3},{6,0},{7,1},{8,14},{9,15},{10,... | collective-permute-start | bytes 589832 | tf_op jit(solution)/shard_map/ppermute | solution.py:442
  24.3 3.3 %collective-permute-start = (f32[2,16,128]{2,1,0:T(8,128)S(1)}, f32[2,16,128]{2,1,0:T(8,128)S(1)}, u32[]{:S(2)}, u32[]{:S(2)}) collective-permute-start(f32[2,16,128]{2,1,0:T(8,128)S(1)} %copy-done.15), channel_id=1, source_target_pairs={{0,8},{8,16},{16,24},{24,32},{32,40},{40,48},{48,56},{56,64},{64,7... | collective-permute-start | bytes 49160 | tf_op jit(solution)/shard_map/ppermute | solution.py:433
  26.8 8.7 %copy-start.9 = (f32[2,16,128]{2,1,0:T(8,128)S(1)}, f32[2,16,128]{2,1,0:T(8,128)}, u32[]{:S(2)}) copy-start(f32[2,16,128]{2,1,0:T(8,128)} %get-tuple-element.34.self_ref) | copy-start | bytes 49156
  26.8 3.5 %collective-permute-start.1 = (f32[2,16,128]{2,1,0:T(8,128)S(1)}, f32[2,16,128]{2,1,0:T(8,128)S(1)}, u32[]{:S(2)}, u32[]{:S(2)}) collective-permute-start(f32[2,16,128]{2,1,0:T(8,128)S(1)} %copy-done.14), channel_id=1, source_target_pairs={{0,248},{8,0},{16,8},{24,16},{32,24},{40,32},{48,40},{56,48},{64,5... | collective-permute-start | bytes 49160 | tf_op jit(solution)/shard_map/ppermute | solution.py:433
  39.6 10.3 %copy-start.6 = (s32[24,128]{1,0:T(8,128)}, s32[24,128]{1,0:T(8,128)S(1)}, u32[]{:S(2)}) copy-start(s32[24,128]{1,0:T(8,128)S(1)} %get-tuple-element.42.after_ref.idx_ref) | copy-start | bytes 36868
  39.6 33.3 %all-to-all-start.1 = ((f32[8,208,128]{2,1,0:T(8,128)}), f32[8,208,128]{2,1,0:T(8,128)S(1)}, u32[]{:S(2)}, u32[]{:S(2)}) async-start(f32[8,208,128]{2,1,0:T(8,128)} %get-tuple-element.41), calls=%async_computation.1 | async-start | bytes 1703936 | tf_op jit(solution)/shard_map/all_to_all | solution.py:500
  43.1 26.1 %collective-permute-start.6 = (f32[13,32,128]{2,1,0:T(8,128)}, f32[13,32,128]{2,1,0:T(8,128)S(1)}, u32[]{:S(2)}, u32[]{:S(2)}) collective-permute-start(f32[13,32,128]{2,1,0:T(8,128)} %get-tuple-element.44), channel_id=1, source_target_pairs={{0,8},{8,16},{16,24},{24,32},{32,40},{40,48},{48,56},{56,64},{64,7... | collective-permute-start | bytes 638984 | tf_op jit(solution)/shard_map/ppermute | solution.py:433
  47.9 21.3 %collective-permute-start.7 = (f32[13,32,128]{2,1,0:T(8,128)}, f32[13,32,128]{2,1,0:T(8,128)}, u32[]{:S(2)}, u32[]{:S(2)}) collective-permute-start(f32[13,32,128]{2,1,0:T(8,128)} %get-tuple-element.45), channel_id=1, source_target_pairs={{8,0},{16,8},{24,16},{32,24},{40,32},{48,40},{56,48},{64,56},{72,6... | collective-permute-start | bytes 638984 | tf_op jit(solution)/shard_map/ppermute | solution.py:433
  51.9 7.3 %collective-permute-start.10 = (f32[2,12,16,128]{3,2,1,0:T(8,128)S(1)}, f32[2,12,16,128]{3,2,1,0:T(8,128)S(1)}, u32[]{:S(2)}, u32[]{:S(2)}) collective-permute-start(f32[2,12,16,128]{3,2,1,0:T(8,128)S(1)} %get-tuple-element.53), channel_id=1, source_target_pairs={{0,2},{1,3},{2,0},{3,1},{4,6},{5,7},{6,4},{7,5},{8,10},{9,11},{10,... | collective-permute-start | bytes 589832 | tf_op jit(solution)/shard_map/ppermute | solution.py:442
  53.6 11.2 %collective-permute-start.11 = (f32[2,12,16,128]{3,2,1,0:T(8,128)S(1)}, f32[2,12,16,128]{3,2,1,0:T(8,128)S(1)}, u32[]{:S(2)}, u32[]{:S(2)}) collective-permute-start(f32[2,12,16,128]{3,2,1,0:T(8,128)S(1)} %get-tuple-element.54), channel_id=1, source_target_pairs={{0,4},{1,5},{2,6},{3,7},{4,0},{5,1},{6,2},{7,3},{8,12},{9,13},{10,... | collective-permute-start | bytes 589832 | tf_op jit(solution)/shard_map/ppermute | solution.py:442
  56.1 11.3 %collective-permute-start.12 = (f32[2,12,16,128]{3,2,1,0:T(8,128)S(1)}, f32[2,12,16,128]{3,2,1,0:T(8,128)S(1)}, u32[]{:S(2)}, u32[]{:S(2)}) collective-permute-start(f32[2,12,16,128]{3,2,1,0:T(8,128)S(1)} %get-tuple-element.55), channel_id=1, source_target_pairs={{0,6},{1,7},{2,4},{3,5},{4,2},{5,3},{6,0},{7,1},{8,14},{9,15},{10,... | collective-permute-start | bytes 589832 | tf_op jit(solution)/shard_map/ppermute | solution.py:442
  68.1 23.3 %collective-permute-start.13 = (f32[4,12,16,128]{3,2,1,0:T(8,128)}, f32[4,12,16,128]{3,2,1,0:T(8,128)}, u32[]{:S(2)}, u32[]{:S(2)}) collective-permute-start(f32[4,12,16,128]{3,2,1,0:T(8,128)} %shard_map.121), channel_id=1, source_target_pairs={{0,1},{1,0},{2,3},{3,2},{4,5},{5,4},{6,7},{7,6},{8,9},{9,8},{10,11... | collective-permute-start | bytes 1179656 | tf_op jit(solution)/shard_map/ppermute | solution.py:442
  76.0 12.8 %copy-start.7 = (s32[24,128]{1,0:T(8,128)S(1)}, s32[24,128]{1,0:T(8,128)}, u32[]{:S(2)}) copy-start(s32[24,128]{1,0:T(8,128)} %copy-done.6) | copy-start | bytes 36868
  76.0 22.6 %all-to-all-start.2 = ((f32[32,4,384]{2,1,0:T(4,128)}), f32[32,4,384]{2,1,0:T(4,128)S(1)}, u32[]{:S(2)}, u32[]{:S(2)}) async-start(f32[32,4,384]{2,1,0:T(4,128)} %get-tuple-element.47), calls=%async_computation.2 | async-start | bytes 393216 | tf_op jit(solution)/shard_map/all_to_all | solution.py:438
  86.9 4.5 %collective-permute-start.8 = (f32[2,12,128]{2,1,0:T(8,128)S(1)}, f32[2,12,128]{2,1,0:T(8,128)S(1)}, u32[]{:S(2)}, u32[]{:S(2)}) collective-permute-start(f32[2,12,128]{2,1,0:T(8,128)S(1)} %get-tuple-element.48), channel_id=1, source_target_pairs={{0,8},{8,16},{16,24},{24,32},{32,40},{40,48},{48,56},{56,64},{64,7... | collective-permute-start | bytes 36872 | tf_op jit(solution)/shard_map/ppermute | solution.py:433
  88.8 5.2 %collective-permute-start.9 = (f32[2,12,128]{2,1,0:T(8,128)S(1)}, f32[2,12,128]{2,1,0:T(8,128)S(1)}, u32[]{:S(2)}, u32[]{:S(2)}) collective-permute-start(f32[2,12,128]{2,1,0:T(8,128)S(1)} %get-tuple-element.49), channel_id=1, source_target_pairs={{0,248},{8,0},{16,8},{24,16},{32,24},{40,32},{48,40},{56,48},{64,5... | collective-permute-start | bytes 36872 | tf_op jit(solution)/shard_map/ppermute | solution.py:433
  88.8 9.8 %copy-start.10 = (s32[24,128]{1,0:T(8,128)S(1)}, s32[24,128]{1,0:T(8,128)}, u32[]{:S(2)}) copy-start(s32[24,128]{1,0:T(8,128)} %get-tuple-element.30.idx_ref) | copy-start | bytes 36868
  (9 other events, 21.4 us)

commit v10 on v8

--- a/solution.py
+++ b/solution.py
@@ -257,7 +257,7 @@
         out_ref[k] = fold(jnp.concatenate([f_ref[6 * k : 6 * k + 6], t_ref[6 * k : 6 * k + 6]], axis=0))
 
 
-def reply_kernel(p_ref, force_ref, chunk_ref, up_ref, down_ref, self_ref):
+def reply_kernel(p_ref, force_ref, after_ref, chunk_ref, up_ref, down_ref, self_ref):
     p = p_ref[0]
     for d in (0, 1, SLABS - 1):
         chunk_ref[(p - d) & (SLABS - 1)] = jnp.zeros((4, 384), f32)
@@ -282,11 +282,11 @@
 
 
 def final_kernel(p_ref, me_ref, idx_ref, chunk_ref, up_ref, down_ref, self_ref, part_ref, mass_ref,
-                 own_ref, y1_ref, y2_ref, y3_ref, x_ref, res_ref, jac_ref, val_ref, sum_ref, acc_ref, sems):
+                 keep_ref, cross_ref, y1_ref, y2_ref, y3_ref, res_ref, jac_ref, val_ref, sum_ref, acc_ref, sems):
     p = p_ref[0]
     copies = []
     for k in range(PARTS):
-        source = x_ref.at[k // 2] if k % 2 else (own_ref, y1_ref, y2_ref, y3_ref)[k // 2].at[0]
+        source = (y1_ref, y2_ref, y3_ref)[k // 2 - 1].at[k % 2] if k > 1 else (keep_ref, cross_ref)[k].at[0]
         copies.append(pltpu.make_async_copy(source, acc_ref.at[me_ref[0] ^ k], sems.at[k]))
     for copy in copies:
         copy.start()
@@ -315,13 +315,8 @@
         out[1] = other_ref[k + 1]
 
 
-def turn_kernel(own_ref, y1_ref, y2_ref, y3_ref, out_ref):
-    for k, ref in enumerate((own_ref, y1_ref, y2_ref, y3_ref)):
-        out_ref[k] = ref[1]
-
-
 def time_kernel(me_ref, same_ref, other_ref, y1_ref, y2_ref, y3_ref, *refs):
-    outs, in_ref, out_ref, sems = refs[:4], refs[4], refs[5], refs[6]
+    keep_ref, cross_ref, in_ref, out_ref, sems = refs
     me = me_ref[0]
     pairs = [(same_ref.at[0], in_ref.at[0]), (other_ref.at[0], in_ref.at[1])]
     pairs += [(ref, in_ref.at[pl.ds(2 * k + 2, 2)]) for k, ref in enumerate((y1_ref, y2_ref, y3_ref))]
@@ -345,8 +340,8 @@
         return carry
 
     lax.fori_loop(0, 6, step, 0)
-    for k, out in enumerate(outs):
-        out[...] = out_ref[2 * k : 2 * k + 2]
+    for k in range(PARTS):
+        (keep_ref, cross_ref)[k % 2][k // 2] = out_ref[k]
 
 
 def lookup(ids, mat_ref, column, count):
@@ -469,7 +464,7 @@
     joined = call(join_kernel, [pair] * 3, same, other, smem=())
     turned = [swap(x, 2 * k + 2) for k, x in enumerate(joined)]
     blocks = [pltpu.VMEM((PARTS, 12, 16, 128), f32)] * 2
-    inertia = call(time_kernel, [pair] * 4, me, same, other, *turned, away=range(1, 6), scratch=blocks + [pltpu.SemaphoreType.DMA((5,))])
+    keep, cross = call(time_kernel, [half] * 2, me, same, other, *turned, away=range(1, 6), scratch=blocks + [pltpu.SemaphoreType.DMA((5,))])
 
     part = ((PARTS, 4, 1152), f32)
     fields_parts = call(split_kernel, [(parts, bf16)], disp, dire, smem=())[0]
@@ -483,29 +478,30 @@
     force = call(
         force_kernel,
         [part],
-        me, kind, jnp.asarray(SPREAD), inst_split(gap), inertia[0],
+        me, kind, jnp.asarray(SPREAD), inst_split(gap), keep,
         away=(4,),
         scratch=[pltpu.VMEM((48, 384), f32)] * 4,
     )[0]
     force = inst_split(force)
-    turned = [inertia[0]] + [swap(inertia[k], 2 * k) for k in (1, 2, 3)]
-    two = ((2, 12, 128), f32)
-    chunk, up2, down2, own = call(reply_kernel, [((SLABS, 4, 384), f32), two, two, two], p, force)
-    chunk, up2, down2 = exchange(chunk, up2, down2)
-
+    cross = swap(cross, 1)
+    joined = call(join_kernel, [pair] * 3, keep, cross, smem=())
+    turned = [swap(x, 2 * k + 2) for k, x in enumerate(joined)]
     lin, mass = call(
         lambda *refs: stiff_kernel(*refs, materials=materials.shape[0]),
         [(whole, f32), ((4, 32, 128), f32)],
         p, materials, material_ids, disp, dire, forcing.reshape(fields), up, down,
         smem=(0, 1),
     )
-    other = swap(call(turn_kernel, [half], *turned, smem=())[0], 1)
+    two = ((2, 12, 128), f32)
+    chunk, up2, down2, own = call(reply_kernel, [((SLABS, 4, 384), f32), two, two, two], p, force, mass, away=(2,))
+    chunk, up2, down2 = exchange(chunk, up2, down2)
+
     adding = [pltpu.VMEM((SIDE, 12, 128), f32), pltpu.VMEM((384, 512), f32)]
     partial = call(partner_kernel, [(whole, f32)], far_idx, force, lin, smem=(), scratch=adding)[0]
     residual, jacobian = call(
         final_kernel,
         [(fields, f32)] * 2,
-        p, me, own_idx, chunk, up2, down2, own, partial, mass, *turned, other,
+        p, me, own_idx, chunk, up2, down2, own, partial, mass, keep, cross, *turned,
         smem=(0, 1),
         away=range(9, 14),
         scratch=adding + blocks[:1] + [pltpu.SemaphoreType.DMA((PARTS,))],

time: 87.3 us -> 86.7 us (level)
  starting transfers between devices: 45.6 us -> 43.6 us
  Pallas kernels: 22.4 us -> 24.2 us
  waiting for transfers between devices: 17 us -> 15.8 us
    all_to_all x2, waiting for transfers between devices: 0.01 us -> 4.44 us  [inst_split(): return lax.all_to_all(x, 'inst', split_axis=0, concat_axis=0, tiled=True)]
    all_to_all x2, waiting for transfers between devices: 7.22 us -> 3.69 us  [exchange(): lax.all_to_all(chunk, 'mesh', split_axis=0, concat_axis=0, tiled=True)]
    ppermute x8, waiting for transfers between devices: 4.62 us -> 2.48 us  [swap(): return lax.ppermute(x, 'inst', [(i, i ^ bit) for i in range(PARTS)])]
    pallas_call x11, Pallas kernels: 22.4 us -> 24.2 us  [call(): pl.pallas_call(kernel, out_shape=[jax.ShapeDtypeStruct(s, d) for s, d in...]
    all_to_all x2, starting transfers between devices: 8.95 us -> 7.7 us  [inst_split(): return lax.all_to_all(x, 'inst', split_axis=0, concat_axis=0, tiled=True)]
    all_to_all x2, starting transfers between devices: 21.6 us -> 20.5 us  [exchange(): lax.all_to_all(chunk, 'mesh', split_axis=0, concat_axis=0, tiled=True)]
  transfers between devices with their start and end apart: 16 -> 16, of which waited for: 7 -> 9; matrix products, arithmetic and copies ran while one was open for 0% -> 0% of each run, Pallas kernels for 15% -> 17%
where the time goes in v10:
time: 86.7 us; the launch traced here: 85.6 us
  starting transfers between devices  43.6 us (50%)
  Pallas kernels  24.2 us (28%)
  waiting for transfers between devices  15.8 us (18%)
  local copies, waits for them, and re-layouts  1.12 us (1%)
    pallas_call x11, Pallas kernels, call(): pl.pallas_call(kernel, out_shape=[jax.ShapeDtypeStruct(s, d) for s, d in...  24.2 us
    all_to_all x2, starting transfers between devices, exchange(): lax.all_to_all(chunk, 'mesh', split_axis=0, concat_axis=0, tiled=True)  20.5 us
    ppermute x8, starting transfers between devices, swap(): return lax.ppermute(x, 'inst', [(i, i ^ bit) for i in range(PARTS)])  11.2 us
    all_to_all x2, starting transfers between devices, inst_split(): return lax.all_to_all(x, 'inst', split_axis=0, concat_axis=0, tiled=True)  7.7 us
    ppermute x4, waiting for transfers between devices, shift(): lax.ppermute(x, 'mesh', [(i, (i + by) % SLABS) for i in range(SLABS)])  5.2 us
    all_to_all x2, waiting for transfers between devices, inst_split(): return lax.all_to_all(x, 'inst', split_axis=0, concat_axis=0, tiled=True)  4.44 us
    ppermute x4, starting transfers between devices, shift(): lax.ppermute(x, 'mesh', [(i, (i + by) % SLABS) for i in range(SLABS)])  4.19 us
    all_to_all x2, waiting for transfers between devices, exchange(): lax.all_to_all(chunk, 'mesh', split_axis=0, concat_axis=0, tiled=True)  3.69 us
  transfers between devices with their start and end apart: 16, of which 9 were waited for; matrix products, arithmetic and copies ran while one was open for 0% of the time, Pallas kernels for 17%

profile of v10, /device:TPU:1, one launch (start us, length us, event | category | flops | bytes accessed | tf_op | source)
XLA Modules:
  0.0 85.6 jit_solution(10094583155493558224)
XLA Ops:
  0.6 5.4 %shard_map.113 = (s32[24,128]{1,0:T(8,128)}, f32[32,16,128]{2,1,0:T(8,128)}, f32[14,32,128]{2,1,0:T(8,128)}, f32[14,32,128]{2,1,0:T(8,128)}, f32[2,16,128]{2,1,0...) custom-call(s32[1]{0:T(128)} %bitcast.p_ref.refs_0_, s32[1]{0:T(128)} %bitcast.1.me_ref, ...), custom_call_target="tpu_custom_call" | custom-call | tf_op jit(solution)/shard_map/pallas_call | solution.py:397
  6.1 2.1 %collective-permute-start.2 = (f32[4,12,16,128]{3,2,1,0:T(8,128)}, f32[4,12,16,128]{3,2,1,0:T(8,128)S(1)}, u32[]{:S(2)}, u32[]{:S(2)}) collective-permute-start(f32[4,12,16,128]{3,2,1,0:T(8,128)} %get-tuple-element.34), channel_id=1, source_target_pairs={{0,1},{1,0},{2,3},{3,2},{4,5},{5,4},{6,7},{7,6},{8,9},{9,8},{10,11... | collective-permute-start | bytes 1179656 | tf_op jit(solution)/shard_map/ppermute | solution.py:417
  8.2 11.7 %all-to-all-start = ((f32[32,16,128]{2,1,0:T(8,128)}), f32[32,16,128]{2,1,0:T(8,128)S(1)}, u32[]{:S(2)}, u32[]{:S(2)}) async-start(f32[32,16,128]{2,1,0:T(8,128)} %get-tuple-element.29), calls=%async_computation | async-start | bytes 524288 | tf_op jit(solution)/shard_map/all_to_all | solution.py:413
  19.9 1.7 %collective-permute-start = (f32[14,32,128]{2,1,0:T(8,128)}, f32[14,32,128]{2,1,0:T(8,128)S(1)}, u32[]{:S(2)}, u32[]{:S(2)}) collective-permute-start(f32[14,32,128]{2,1,0:T(8,128)} %get-tuple-element.30), channel_id=1, source_target_pairs={{0,8},{8,16},{16,24},{24,32},{32,40},{40,48},{48,56},{56,64},{64,7... | collective-permute-start | bytes 688136 | tf_op jit(solution)/shard_map/ppermute | solution.py:408
  22.6 2.9 %collective-permute-start.4 = (f32[2,12,16,128]{3,2,1,0:T(8,128)}, f32[2,12,16,128]{3,2,1,0:T(8,128)S(1)}, u32[]{:S(2)}, u32[]{:S(2)}) collective-permute-start(f32[2,12,16,128]{3,2,1,0:T(8,128)} %get-tuple-element.38), channel_id=1, source_target_pairs={{0,4},{1,5},{2,6},{3,7},{4,0},{5,1},{6,2},{7,3},{8,12},{9,13},{10,... | collective-permute-start | bytes 589832 | tf_op jit(solution)/shard_map/ppermute | solution.py:417
  26.4 2.3 %collective-permute-done.up_ref.refs_6_ = f32[14,32,128]{2,1,0:T(8,128)S(1)} collective-permute-done((f32[14,32,128]{2,1,0:T(8,128)}, f32[14,32,128]{2,1,0:T(8,128)S(1)}, u32[]{:S(2)}, u32[]{:S(2)}) %collective-permute-start) | collective-permute-done | bytes 229408 | tf_op jit(solution)/shard_map/ppermute | solution.py:408
  28.7 2.1 %collective-permute-done.1.down_ref.refs_7_ = f32[14,32,128]{2,1,0:T(8,128)S(1)} collective-permute-done((f32[14,32,128]{2,1,0:T(8,128)}, f32[14,32,128]{2,1,0:T(8,128)S(1)}, u32[]{:S(2)}, u32[]{:S(2)}) %collective-permute-start.1) | collective-permute-done | bytes 229408 | tf_op jit(solution)/shard_map/ppermute | solution.py:408
  30.7 2.6 %all-to-all-done.chunk_ref = f32[32,16,128]{2,1,0:T(8,128)S(1)} async-done(((f32[32,16,128]{2,1,0:T(8,128)}), f32[32,16,128]{2,1,0:T(8,128)S(1)}, u32[]{:S(2)}, u32[]{:S(2)}) %all-to-all-start) | async-done | bytes 262176 | tf_op jit(solution)/shard_map/all_to_all | solution.py:413
  33.4 3.2 %shard_map.116 = (s32[24,128]{1,0:T(8,128)S(1)}, f32[24,128]{1,0:T(8,128)S(1)}, f32[8,4,1152]{2,1,0:T(4,128)}) custom-call(s32[1]{0:T(128)} %bitcast.p_ref.refs_0_, f32[32,16,128]{2,1,0:T(8,128)S(1)} %all-to-all-done.chunk_ref, f32[14,32,128]{2,1,0:T(8,128)S(1)} %collective-permute-done.up_ref.refs_6_, ...), custom_call_target="tpu_custom_call" | custom-call | tf_op jit(solution)/shard_map/pallas_call | solution.py:397
  36.5 4.2 %all-to-all-start.1 = ((f32[8,4,1152]{2,1,0:T(4,128)}), f32[8,4,1152]{2,1,0:T(4,128)S(1)}, u32[]{:S(2)}, u32[]{:S(2)}) async-start(f32[8,4,1152]{2,1,0:T(4,128)} %get-tuple-element.37), calls=%async_computation.1 | async-start | bytes 294912 | tf_op jit(solution)/shard_map/all_to_all | solution.py:421
  40.8 3.2 %shard_map.117 = (f32[4,12,16,128]{3,2,1,0:T(8,128)S(1)}, f32[4,12,16,128]{3,2,1,0:T(8,128)}) custom-call(s32[1]{0:T(128)} %bitcast.1.me_ref, f32[4,12,16,128]{3,2,1,0:T(8,128)S(1)} %copy-done.2, f32[4,12,16,128]{3,2,1,0:T(8,128)S(1)} %collective-permute-done.2.other_ref, f32[2,12,16,128]{3,2,1,0:T(8,128)} %collective-permute-done.3.y1_ref, ...), custom_call_target="tpu_custom_call" | custom-call | tf_op jit(solution)/shard_map/pallas_call | solution.py:397
  44.0 1.5 %collective-permute-start.8 = (f32[4,12,16,128]{3,2,1,0:T(8,128)}, f32[4,12,16,128]{3,2,1,0:T(8,128)S(1)}, u32[]{:S(2)}, u32[]{:S(2)}) collective-permute-start(f32[4,12,16,128]{3,2,1,0:T(8,128)} %get-tuple-element.48), channel_id=1, source_target_pairs={{0,1},{1,0},{2,3},{3,2},{4,5},{5,4},{6,7},{7,6},{8,9},{9,8},{10,11... | collective-permute-start | bytes 1179656 | tf_op jit(solution)/shard_map/ppermute | solution.py:417
  47.3 3.5 %all-to-all-start.2 = ((f32[8,4,1152]{2,1,0:T(4,128)}), f32[8,4,1152]{2,1,0:T(4,128)S(1)}, u32[]{:S(2)}, u32[]{:S(2)}) async-start(f32[8,4,1152]{2,1,0:T(4,128)} %shard_map.118), calls=%async_computation.2 | async-start | bytes 294912 | tf_op jit(solution)/shard_map/all_to_all | solution.py:421
  50.9 1.0 %copy-done.3 = f32[2,3,4,32,128]{4,3,2,1,0:T(8,128)S(1)} copy-done((f32[2,3,4,32,128]{4,3,2,1,0:T(8,128)S(1)}, f32[2,3,4,32,128]{4,3,2,1,0:T(8,128)}, u32[]{:S(2)}) %copy-start.3) | copy-done | bytes 393240
  51.9 1.6 %shard_map.119 = (f32[12,4,32,128]{3,2,1,0:T(8,128)S(1)}, f32[4,32,128]{2,1,0:T(8,128)S(1)}) custom-call(s32[1]{0:T(128)} %bitcast.p_ref.refs_0_, f32[16,4]{1,0:T(8,128)S(1)} %copy.12.refs_1_, s32[4,32,128]{2,1,0:T(8,128)S(1)} %copy-done.4, f32[6,4,32,128]{3,2,1,0:T(8,128)S(1)} %bitcast.13, f32[6,4,32,128]{3,2,1,0:T(8,128)S(1)} %bitcast.16, ...), custom_call_target="tpu_custom_call" | custom-call | tf_op jit(solution)/shard_map/pallas_call | solution.py:397
  53.6 3.6 %all-to-all-done.2.force_ref = f32[8,4,1152]{2,1,0:T(4,128)S(1)} async-done(((f32[8,4,1152]{2,1,0:T(4,128)}), f32[8,4,1152]{2,1,0:T(4,128)S(1)}, u32[]{:S(2)}, u32[]{:S(2)}) %all-to-all-start.2) | async-done | bytes 147488 | tf_op jit(solution)/shard_map/all_to_all | solution.py:421
  57.9 8.8 %all-to-all-start.3 = ((f32[32,4,384]{2,1,0:T(4,128)}), f32[32,4,384]{2,1,0:T(4,128)S(1)}, u32[]{:S(2)}, u32[]{:S(2)}) async-start(f32[32,4,384]{2,1,0:T(4,128)} %get-tuple-element.42), calls=%async_computation.3 | async-start | bytes 393216 | tf_op jit(solution)/shard_map/all_to_all | solution.py:413
  67.7 1.8 %collective-permute-start.10 = (f32[2,12,16,128]{3,2,1,0:T(8,128)}, f32[2,12,16,128]{3,2,1,0:T(8,128)S(1)}, u32[]{:S(2)}, u32[]{:S(2)}) collective-permute-start(f32[2,12,16,128]{3,2,1,0:T(8,128)} %get-tuple-element.50), channel_id=1, source_target_pairs={{0,4},{1,5},{2,6},{3,7},{4,0},{5,1},{6,2},{7,3},{8,12},{9,13},{10,... | collective-permute-start | bytes 589832 | tf_op jit(solution)/shard_map/ppermute | solution.py:417
  69.5 2.0 %collective-permute-start.11 = (f32[2,12,16,128]{3,2,1,0:T(8,128)}, f32[2,12,16,128]{3,2,1,0:T(8,128)S(1)}, u32[]{:S(2)}, u32[]{:S(2)}) collective-permute-start(f32[2,12,16,128]{3,2,1,0:T(8,128)} %get-tuple-element.51), channel_id=1, source_target_pairs={{0,6},{1,7},{2,4},{3,5},{4,2},{5,3},{6,0},{7,1},{8,14},{9,15},{10,... | collective-permute-start | bytes 589832 | tf_op jit(solution)/shard_map/ppermute | solution.py:417
  71.4 2.5 %collective-permute-start.6 = (f32[2,12,128]{2,1,0:T(8,128)S(1)}, f32[2,12,128]{2,1,0:T(8,128)S(1)}, u32[]{:S(2)}, u32[]{:S(2)}) collective-permute-start(f32[2,12,128]{2,1,0:T(8,128)S(1)} %get-tuple-element.43), channel_id=1, source_target_pairs={{0,8},{8,16},{16,24},{24,32},{32,40},{40,48},{48,56},{56,64},{64,7... | collective-permute-start | bytes 36872 | tf_op jit(solution)/shard_map/ppermute | solution.py:408
  73.9 2.6 %shard_map.121.part_ref = f32[12,4,32,128]{3,2,1,0:T(8,128)S(1)} custom-call(s32[24,128]{1,0:T(8,128)S(1)} %get-tuple-element.46.idx_ref, f32[8,4,1152]{2,1,0:T(4,128)S(1)} %all-to-all-done.2.force_ref, f32[12,4,32,128]{3,2,1,0:T(8,128)S(1)} %get-tuple-element.47.lin_ref), custom_call_target="tpu_custom_call" | custom-call | tf_op jit(solution)/shard_map/pallas_call | solution.py:397
  77.4 1.1 %all-to-all-done.3.chunk_ref = f32[32,4,384]{2,1,0:T(4,128)S(1)} async-done(((f32[32,4,384]{2,1,0:T(4,128)}), f32[32,4,384]{2,1,0:T(4,128)S(1)}, u32[]{:S(2)}, u32[]{:S(2)}) %all-to-all-start.3) | async-done | bytes 196640 | tf_op jit(solution)/shard_map/all_to_all | solution.py:413
  78.7 2.2 %collective-permute-done.11.y3_ref = f32[2,12,16,128]{3,2,1,0:T(8,128)S(1)} collective-permute-done((f32[2,12,16,128]{3,2,1,0:T(8,128)}, f32[2,12,16,128]{3,2,1,0:T(8,128)S(1)}, u32[]{:S(2)}, u32[]{:S(2)}) %collective-permute-start.11) | collective-permute-done | bytes 196640 | tf_op jit(solution)/shard_map/ppermute | solution.py:417
  80.9 4.6 %shard_map.123 = (f32[6,4,32,128]{3,2,1,0:T(8,128)}, f32[6,4,32,128]{3,2,1,0:T(8,128)}) custom-call(s32[1]{0:T(128)} %bitcast.p_ref.refs_0_, s32[1]{0:T(128)} %bitcast.1.me_ref, s32[24,128]{1,0:T(8,128)S(1)} %copy-done.7, f32[32,4,384]{2,1,0:T(4,128)S(1)} %all-to-all-done.3.chunk_ref, f32[2,12,128]{2,1,0:T(8,128)S(1)} %collective-permute-done.6.up_ref, ...), custom_call_target="tpu_custom_call" | custom-call | tf_op jit(solution)/shard_map/pallas_call | solution.py:397
  (38 shorter events, 6.6 us)
Async XLA Ops:
  6.1 15.6 %copy-start.2 = (f32[4,12,16,128]{3,2,1,0:T(8,128)S(1)}, f32[4,12,16,128]{3,2,1,0:T(8,128)}, u32[]{:S(2)}) copy-start(f32[4,12,16,128]{3,2,1,0:T(8,128)} %get-tuple-element.33.same_ref) | copy-start | bytes 1179652
  6.1 15.6 %collective-permute-start.2 = (f32[4,12,16,128]{3,2,1,0:T(8,128)}, f32[4,12,16,128]{3,2,1,0:T(8,128)S(1)}, u32[]{:S(2)}, u32[]{:S(2)}) collective-permute-start(f32[4,12,16,128]{3,2,1,0:T(8,128)} %get-tuple-element.34), channel_id=1, source_target_pairs={{0,1},{1,0},{2,3},{3,2},{4,5},{5,4},{6,7},{7,6},{8,9},{9,8},{10,11... | collective-permute-start | bytes 1179656 | tf_op jit(solution)/shard_map/ppermute | solution.py:417
  8.2 25.2 %all-to-all-start = ((f32[32,16,128]{2,1,0:T(8,128)}), f32[32,16,128]{2,1,0:T(8,128)S(1)}, u32[]{:S(2)}, u32[]{:S(2)}) async-start(f32[32,16,128]{2,1,0:T(8,128)} %get-tuple-element.29), calls=%async_computation | async-start | bytes 524288 | tf_op jit(solution)/shard_map/all_to_all | solution.py:413
  19.9 8.7 %collective-permute-start = (f32[14,32,128]{2,1,0:T(8,128)}, f32[14,32,128]{2,1,0:T(8,128)S(1)}, u32[]{:S(2)}, u32[]{:S(2)}) collective-permute-start(f32[14,32,128]{2,1,0:T(8,128)} %get-tuple-element.30), channel_id=1, source_target_pairs={{0,8},{8,16},{16,24},{24,32},{32,40},{40,48},{48,56},{56,64},{64,7... | collective-permute-start | bytes 688136 | tf_op jit(solution)/shard_map/ppermute | solution.py:408
  21.7 9.1 %collective-permute-start.1 = (f32[14,32,128]{2,1,0:T(8,128)}, f32[14,32,128]{2,1,0:T(8,128)S(1)}, u32[]{:S(2)}, u32[]{:S(2)}) collective-permute-start(f32[14,32,128]{2,1,0:T(8,128)} %get-tuple-element.31), channel_id=1, source_target_pairs={{0,248},{8,0},{16,8},{24,16},{32,24},{40,32},{48,40},{56,48},{64,5... | collective-permute-start | bytes 688136 | tf_op jit(solution)/shard_map/ppermute | solution.py:408
  21.7 4.6 %copy-start = (f32[2,3,4,32,128]{4,3,2,1,0:T(8,128)S(1)}, f32[2,3,4,32,128]{4,3,2,1,0:T(8,128)}, u32[]{:S(2)}) copy-start(f32[2,3,4,32,128]{4,3,2,1,0:T(8,128)} %param.10) | copy-start | bytes 1179652
  21.7 4.6 %copy-start.1 = (f32[2,3,4,32,128]{4,3,2,1,0:T(8,128)S(1)}, f32[2,3,4,32,128]{4,3,2,1,0:T(8,128)}, u32[]{:S(2)}) copy-start(f32[2,3,4,32,128]{4,3,2,1,0:T(8,128)} %param.11) | copy-start | bytes 1179652
  22.6 18.2 %collective-permute-start.4 = (f32[2,12,16,128]{3,2,1,0:T(8,128)}, f32[2,12,16,128]{3,2,1,0:T(8,128)S(1)}, u32[]{:S(2)}, u32[]{:S(2)}) collective-permute-start(f32[2,12,16,128]{3,2,1,0:T(8,128)} %get-tuple-element.38), channel_id=1, source_target_pairs={{0,4},{1,5},{2,6},{3,7},{4,0},{5,1},{6,2},{7,3},{8,12},{9,13},{10,... | collective-permute-start | bytes 589832 | tf_op jit(solution)/shard_map/ppermute | solution.py:417
  25.5 15.3 %collective-permute-start.5 = (f32[2,12,16,128]{3,2,1,0:T(8,128)}, f32[2,12,16,128]{3,2,1,0:T(8,128)}, u32[]{:S(2)}, u32[]{:S(2)}) collective-permute-start(f32[2,12,16,128]{3,2,1,0:T(8,128)} %get-tuple-element.39), channel_id=1, source_target_pairs={{0,6},{1,7},{2,4},{3,5},{4,2},{5,3},{6,0},{7,1},{8,14},{9,15},{10,... | collective-permute-start | bytes 589832 | tf_op jit(solution)/shard_map/ppermute | solution.py:417
  26.2 7.1 %copy-start.6 = (f32[2,16,128]{2,1,0:T(8,128)S(1)}, f32[2,16,128]{2,1,0:T(8,128)}, u32[]{:S(2)}) copy-start(f32[2,16,128]{2,1,0:T(8,128)} %get-tuple-element.32.self_ref) | copy-start | bytes 49156
  26.2 14.5 %collective-permute-start.3 = (f32[2,12,16,128]{3,2,1,0:T(8,128)}, f32[2,12,16,128]{3,2,1,0:T(8,128)}, u32[]{:S(2)}, u32[]{:S(2)}) collective-permute-start(f32[2,12,16,128]{3,2,1,0:T(8,128)} %get-tuple-element.35.after_ref), channel_id=1, source_target_pairs={{0,2},{1,3},{2,0},{3,1},{4,6},{5,7},{6,4},{7,5},{8,10},{9,11},{10,... | collective-permute-start | bytes 589832 | tf_op jit(solution)/shard_map/ppermute | solution.py:417
  36.5 9.8 %all-to-all-start.1 = ((f32[8,4,1152]{2,1,0:T(4,128)}), f32[8,4,1152]{2,1,0:T(4,128)S(1)}, u32[]{:S(2)}, u32[]{:S(2)}) async-start(f32[8,4,1152]{2,1,0:T(4,128)} %get-tuple-element.37), calls=%async_computation.1 | async-start | bytes 294912 | tf_op jit(solution)/shard_map/all_to_all | solution.py:421
  40.7 5.6 %copy-start.5 = (f32[48,48]{1,0:T(8,128)S(1)}, f32[48,48]{1,0:T(8,128)}, u32[]{:S(2)}) copy-start(f32[48,48]{1,0:T(8,128)} %constant.11.clone.spread_ref) | copy-start | bytes 27652
  44.0 22.8 %collective-permute-start.8 = (f32[4,12,16,128]{3,2,1,0:T(8,128)}, f32[4,12,16,128]{3,2,1,0:T(8,128)S(1)}, u32[]{:S(2)}, u32[]{:S(2)}) collective-permute-start(f32[4,12,16,128]{3,2,1,0:T(8,128)} %get-tuple-element.48), channel_id=1, source_target_pairs={{0,1},{1,0},{2,3},{3,2},{4,5},{5,4},{6,7},{7,6},{8,9},{9,8},{10,11... | collective-permute-start | bytes 1179656 | tf_op jit(solution)/shard_map/ppermute | solution.py:417
  47.3 3.5 %copy-start.8 = (f32[16,4]{0,1:T(4,128)S(1)}, f32[16,4]{0,1:T(4,128)}, u32[]{:S(2)}) copy-start(f32[16,4]{0,1:T(4,128)} %param.14) | copy-start | bytes 772
  47.3 3.6 %copy-start.4 = (s32[4,32,128]{2,1,0:T(8,128)S(1)}, s32[4,32,128]{2,1,0:T(8,128)}, u32[]{:S(2)}) copy-start(s32[4,32,128]{2,1,0:T(8,128)} %refs_2_.1) | copy-start | bytes 196612
  47.3 9.8 %all-to-all-start.2 = ((f32[8,4,1152]{2,1,0:T(4,128)}), f32[8,4,1152]{2,1,0:T(4,128)S(1)}, u32[]{:S(2)}, u32[]{:S(2)}) async-start(f32[8,4,1152]{2,1,0:T(4,128)} %shard_map.118), calls=%async_computation.2 | async-start | bytes 294912 | tf_op jit(solution)/shard_map/all_to_all | solution.py:421
  57.9 20.5 %all-to-all-start.3 = ((f32[32,4,384]{2,1,0:T(4,128)}), f32[32,4,384]{2,1,0:T(4,128)S(1)}, u32[]{:S(2)}, u32[]{:S(2)}) async-start(f32[32,4,384]{2,1,0:T(4,128)} %get-tuple-element.42), calls=%async_computation.3 | async-start | bytes 393216 | tf_op jit(solution)/shard_map/all_to_all | solution.py:413
  67.6 10.9 %collective-permute-start.9 = (f32[2,12,16,128]{3,2,1,0:T(8,128)}, f32[2,12,16,128]{3,2,1,0:T(8,128)S(1)}, u32[]{:S(2)}, u32[]{:S(2)}) collective-permute-start(f32[2,12,16,128]{3,2,1,0:T(8,128)} %get-tuple-element.49), channel_id=1, source_target_pairs={{0,2},{1,3},{2,0},{3,1},{4,6},{5,7},{6,4},{7,5},{8,10},{9,11},{10,... | collective-permute-start | bytes 589832 | tf_op jit(solution)/shard_map/ppermute | solution.py:417
  67.7 11.1 %collective-permute-start.10 = (f32[2,12,16,128]{3,2,1,0:T(8,128)}, f32[2,12,16,128]{3,2,1,0:T(8,128)S(1)}, u32[]{:S(2)}, u32[]{:S(2)}) collective-permute-start(f32[2,12,16,128]{3,2,1,0:T(8,128)} %get-tuple-element.50), channel_id=1, source_target_pairs={{0,4},{1,5},{2,6},{3,7},{4,0},{5,1},{6,2},{7,3},{8,12},{9,13},{10,... | collective-permute-start | bytes 589832 | tf_op jit(solution)/shard_map/ppermute | solution.py:417
  69.5 11.4 %collective-permute-start.11 = (f32[2,12,16,128]{3,2,1,0:T(8,128)}, f32[2,12,16,128]{3,2,1,0:T(8,128)S(1)}, u32[]{:S(2)}, u32[]{:S(2)}) collective-permute-start(f32[2,12,16,128]{3,2,1,0:T(8,128)} %get-tuple-element.51), channel_id=1, source_target_pairs={{0,6},{1,7},{2,4},{3,5},{4,2},{5,3},{6,0},{7,1},{8,14},{9,15},{10,... | collective-permute-start | bytes 589832 | tf_op jit(solution)/shard_map/ppermute | solution.py:417
  71.4 5.1 %collective-permute-start.6 = (f32[2,12,128]{2,1,0:T(8,128)S(1)}, f32[2,12,128]{2,1,0:T(8,128)S(1)}, u32[]{:S(2)}, u32[]{:S(2)}) collective-permute-start(f32[2,12,128]{2,1,0:T(8,128)S(1)} %get-tuple-element.43), channel_id=1, source_target_pairs={{0,8},{8,16},{16,24},{24,32},{32,40},{40,48},{48,56},{56,64},{64,7... | collective-permute-start | bytes 36872 | tf_op jit(solution)/shard_map/ppermute | solution.py:408
  73.9 3.5 %collective-permute-start.7 = (f32[2,12,128]{2,1,0:T(8,128)S(1)}, f32[2,12,128]{2,1,0:T(8,128)S(1)}, u32[]{:S(2)}, u32[]{:S(2)}) collective-permute-start(f32[2,12,128]{2,1,0:T(8,128)S(1)} %get-tuple-element.44), channel_id=1, source_target_pairs={{0,248},{8,0},{16,8},{24,16},{32,24},{40,32},{48,40},{56,48},{64,5... | collective-permute-start | bytes 36872 | tf_op jit(solution)/shard_map/ppermute | solution.py:408
  73.9 7.0 %copy-start.7 = (s32[24,128]{1,0:T(8,128)S(1)}, s32[24,128]{1,0:T(8,128)}, u32[]{:S(2)}) copy-start(s32[24,128]{1,0:T(8,128)} %get-tuple-element.28.idx_ref) | copy-start | bytes 36868
  (1 other events, 1.0 us)

commit v11 on v10

--- a/solution.py
+++ b/solution.py
@@ -139,28 +139,28 @@
 
 
 def scatter_rows(val_ref, idx_ref, sum_ref):
-    sum_ref[...] = jnp.zeros(sum_ref.shape, f32)
     dims = (((1,), (1,)), ((), ()))
-
-    def step(k, carry):
-        pick, in_y = picks(idx_ref, k)
-        value = jnp.concatenate([val_ref[2 * k], val_ref[2 * k + 1]], axis=1)
-        hi = value.astype(bf16).astype(f32)
-        spread = [
-            jnp.where(in_y[None], part[:, None, :], 0.0).reshape(384, 256).astype(bf16) for part in (hi, value - hi)
-        ]
-        got = lax.dot_general(spread[0], pick, dims, preferred_element_type=f32)
-        got = got + lax.dot_general(spread[1], pick, dims, preferred_element_type=f32)
-        sum_ref[...] = sum_ref[...] + got
-        return carry
-
-    lax.fori_loop(0, SIDE // 2, step, 0, unroll=3)
+    total = None
+    for group in range(3):
+        held, high, low = [], [], []
+        for k in range(group * SIDE // 2 // 3, (group + 1) * SIDE // 2 // 3):
+            pick, in_y = picks(idx_ref, k)
+            value = jnp.concatenate([val_ref[2 * k], val_ref[2 * k + 1]], axis=1)
+            hi = value.astype(bf16).astype(f32)
+            held.append(pick)
+            for out, part in ((high, hi), (low, value - hi)):
+                out.append(jnp.where(in_y[None], part[:, None, :], 0.0).reshape(384, 256).astype(bf16))
+        held = jnp.concatenate(held, axis=1)
+        got = lax.dot_general(jnp.concatenate(high, axis=1), held, dims, preferred_element_type=f32)
+        got = got + lax.dot_general(jnp.concatenate(low, axis=1), held, dims, preferred_element_type=f32)
+        total = got if total is None else total + got
+    sum_ref[...] = total
 
 
 def list_kernel(p_ref, me_ref, owner_hbm, local_hbm, remote_hbm, kind_hbm, disp_hbm, dir_hbm, ids_hbm,
-                idx_ref, chunk_ref, up_hbm, down_hbm, self_ref, same_hbm, other_hbm,
+                idx_ref, chunk_hbm, up_hbm, down_hbm, self_ref, same_hbm, other_hbm,
                 parts_ref, rows_ref, owner_ref, local_ref, remote_ref, kind_ref, disp_ref, dir_ref, ids_ref, near_ref,
-                sems, more_sems):
+                chunk_ref, sems, more_sems):
     p = p_ref[0]
     pairs = ((owner_hbm, owner_ref), (local_hbm, local_ref), (remote_hbm, remote_ref), (kind_hbm, kind_ref),
              (disp_hbm, disp_ref), (dir_hbm, dir_ref), (ids_hbm, ids_ref))
@@ -207,6 +207,8 @@
     for d in range(3, SLABS - 2):
         tile, seg = far_place(d)
         chunk_ref[(p + d) & (SLABS - 1)] = lane_roll(rows_ref[tile], -seg)
+    ends.append(pltpu.make_async_copy(chunk_ref, chunk_hbm, sems.at[11]))
+    ends[-1].start()
     self_ref[...] = rows_ref[0:2]
     for move in moves + ends:
         move.wait()
@@ -282,14 +284,11 @@
 
 
 def final_kernel(p_ref, me_ref, idx_ref, chunk_ref, up_ref, down_ref, self_ref, part_ref, mass_ref,
-                 keep_ref, cross_ref, y1_ref, y2_ref, y3_ref, res_ref, jac_ref, val_ref, sum_ref, acc_ref, sems):
+                 keep_ref, cross_ref, y1_ref, y2_ref, y3_ref, res_ref, jac_ref, val_ref, sum_ref, acc_ref):
     p = p_ref[0]
-    copies = []
     for k in range(PARTS):
-        source = (y1_ref, y2_ref, y3_ref)[k // 2 - 1].at[k % 2] if k > 1 else (keep_ref, cross_ref)[k].at[0]
-        copies.append(pltpu.make_async_copy(source, acc_ref.at[me_ref[0] ^ k], sems.at[k]))
-    for copy in copies:
-        copy.start()
+        acc = (y1_ref, y2_ref, y3_ref)[k // 2 - 1][k % 2] if k > 1 else (keep_ref, cross_ref)[k][0]
+        acc_ref[me_ref[0] ^ k] = acc
 
     def listed(d):
         return unfold(chunk_ref[(p + d) & (SLABS - 1)])
@@ -299,8 +298,6 @@
     for k, tile in enumerate(tiles):
         val_ref[k] = tile
     scatter_rows(val_ref, idx_ref, sum_ref)
-    for copy in copies:
-        copy.wait()
     for x in range(4):
         acc = jnp.concatenate([acc_ref[2 * x], acc_ref[2 * x + 1]], axis=1)
         added = sum_ref[:, 128 * x : 128 * (x + 1)].reshape(12, 32, 128)
@@ -316,15 +313,12 @@
 
 
 def time_kernel(me_ref, same_ref, other_ref, y1_ref, y2_ref, y3_ref, *refs):
-    keep_ref, cross_ref, in_ref, out_ref, sems = refs
+    keep_ref, cross_ref, in_ref, out_ref = refs
     me = me_ref[0]
-    pairs = [(same_ref.at[0], in_ref.at[0]), (other_ref.at[0], in_ref.at[1])]
-    pairs += [(ref, in_ref.at[pl.ds(2 * k + 2, 2)]) for k, ref in enumerate((y1_ref, y2_ref, y3_ref))]
-    copies = [pltpu.make_async_copy(a, b, sems.at[k]) for k, (a, b) in enumerate(pairs)]
-    for copy in copies:
-        copy.start()
-    for copy in copies:
-        copy.wait()
+    in_ref[0] = same_ref[0]
+    in_ref[1] = other_ref[0]
+    for k, ref in enumerate((y1_ref, y2_ref, y3_ref)):
+        in_ref[2 * k + 2 : 2 * k + 4] = ref[...]
     at = [me ^ ((me + k) & (PARTS - 1)) for k in range(PARTS)]
     count = 2 * PARTS
 
@@ -450,12 +444,12 @@
         smem=(0, 1),
         away=range(2, 9),
         limit=60 * 1024 * 1024,
-        kept=(2, 3, 5, 6),
+        kept=(1, 2, 3, 5, 6),
         scratch=[pltpu.VMEM(parts, bf16), pltpu.VMEM((SIDE, 16, 128), f32)]
         + [pltpu.VMEM((1, count), i32)] * 4
         + [pltpu.VMEM(fields, f32)] * 2
         + [pltpu.VMEM((4, 32, 128), i32), pltpu.VMEM((4, 32, 128), f32)]
-        + [pltpu.SemaphoreType.DMA((11,)), pltpu.SemaphoreType.DMA((20,))],
+        + [pltpu.VMEM((SLABS, 16, 128), f32), pltpu.SemaphoreType.DMA((12,)), pltpu.SemaphoreType.DMA((20,))],
     )
     chunk, up, down = exchange(chunk, up, down)
 
@@ -464,7 +458,7 @@
     joined = call(join_kernel, [pair] * 3, same, other, smem=())
     turned = [swap(x, 2 * k + 2) for k, x in enumerate(joined)]
     blocks = [pltpu.VMEM((PARTS, 12, 16, 128), f32)] * 2
-    keep, cross = call(time_kernel, [half] * 2, me, same, other, *turned, away=range(1, 6), scratch=blocks + [pltpu.SemaphoreType.DMA((5,))])
+    keep, cross = call(time_kernel, [half] * 2, me, same, other, *turned, scratch=blocks)
 
     part = ((PARTS, 4, 1152), f32)
     fields_parts = call(split_kernel, [(parts, bf16)], disp, dire, smem=())[0]
@@ -503,8 +497,7 @@
         [(fields, f32)] * 2,
         p, me, own_idx, chunk, up2, down2, own, partial, mass, keep, cross, *turned,
         smem=(0, 1),
-        away=range(9, 14),
-        scratch=adding + blocks[:1] + [pltpu.SemaphoreType.DMA((PARTS,))],
+        scratch=adding + blocks[:1],
     )
     return residual.reshape(shape), jacobian.reshape(shape)
 

time: 86.7 us -> 84.6 us (0.976)
  Pallas kernels: 24.2 us -> 21.7 us
  waiting for transfers between devices: 15.8 us -> 16.8 us
    pallas_call x11, Pallas kernels: 24.2 us -> 21.7 us  [call(): pl.pallas_call(kernel, out_shape=[jax.ShapeDtypeStruct(s, d) for s, d in...]
  transfers between devices with their start and end apart: 16 -> 16, of which waited for: 9 -> 9; matrix products, arithmetic and copies ran while one was open for 0% -> 0% of each run, Pallas kernels for 17% -> 16%
where the time goes in v11:
time: 84.6 us; the launch traced here: 83.4 us
  starting transfers between devices  43 us (51%)
  Pallas kernels  21.7 us (26%)
  waiting for transfers between devices  16.8 us (20%)
  local copies, waits for them, and re-layouts  1.12 us (1%)
    pallas_call x11, Pallas kernels, call(): pl.pallas_call(kernel, out_shape=[jax.ShapeDtypeStruct(s, d) for s, d in...  21.7 us
    all_to_all x2, starting transfers between devices, exchange(): lax.all_to_all(chunk, 'mesh', split_axis=0, concat_axis=0, tiled=True)  20 us
    ppermute x8, starting transfers between devices, swap(): return lax.ppermute(x, 'inst', [(i, i ^ bit) for i in range(PARTS)])  11.1 us
    all_to_all x2, starting transfers between devices, inst_split(): return lax.all_to_all(x, 'inst', split_axis=0, concat_axis=0, tiled=True)  7.7 us
    ppermute x4, waiting for transfers between devices, shift(): lax.ppermute(x, 'mesh', [(i, (i + by) % SLABS) for i in range(SLABS)])  5.7 us
    all_to_all x2, waiting for transfers between devices, inst_split(): return lax.all_to_all(x, 'inst', split_axis=0, concat_axis=0, tiled=True)  4.95 us
    ppermute x4, starting transfers between devices, shift(): lax.ppermute(x, 'mesh', [(i, (i + by) % SLABS) for i in range(SLABS)])  4.19 us
    all_to_all x2, waiting for transfers between devices, exchange(): lax.all_to_all(chunk, 'mesh', split_axis=0, concat_axis=0, tiled=True)  3.69 us
  transfers between devices with their start and end apart: 16, of which 9 were waited for; matrix products, arithmetic and copies ran while one was open for 0% of the time, Pallas kernels for 16%

profile of v11, /device:TPU:1, one launch (start us, length us, event | category | flops | bytes accessed | tf_op | source)
XLA Modules:
  0.0 83.4 jit_solution(3801278297168806360)
XLA Ops:
  0.6 5.5 %shard_map.113 = (s32[24,128]{1,0:T(8,128)}, f32[32,16,128]{2,1,0:T(8,128)}, f32[14,32,128]{2,1,0:T(8,128)}, f32[14,32,128]{2,1,0:T(8,128)}, f32[2,16,128]{2,1,0...) custom-call(s32[1]{0:T(128)} %bitcast.p_ref.refs_0_, s32[1]{0:T(128)} %bitcast.1.me_ref, ...), custom_call_target="tpu_custom_call" | custom-call | tf_op jit(solution)/shard_map/pallas_call | solution.py:391
  6.1 2.1 %collective-permute-start.2 = (f32[4,12,16,128]{3,2,1,0:T(8,128)}, f32[4,12,16,128]{3,2,1,0:T(8,128)S(1)}, u32[]{:S(2)}, u32[]{:S(2)}) collective-permute-start(f32[4,12,16,128]{3,2,1,0:T(8,128)} %get-tuple-element.34), channel_id=1, source_target_pairs={{0,1},{1,0},{2,3},{3,2},{4,5},{5,4},{6,7},{7,6},{8,9},{9,8},{10,11... | collective-permute-start | bytes 1179656 | tf_op jit(solution)/shard_map/ppermute | solution.py:411
  8.3 11.7 %all-to-all-start = ((f32[32,16,128]{2,1,0:T(8,128)}), f32[32,16,128]{2,1,0:T(8,128)S(1)}, u32[]{:S(2)}, u32[]{:S(2)}) async-start(f32[32,16,128]{2,1,0:T(8,128)} %get-tuple-element.29), calls=%async_computation | async-start | bytes 524288 | tf_op jit(solution)/shard_map/all_to_all | solution.py:407
  20.0 1.7 %collective-permute-start = (f32[14,32,128]{2,1,0:T(8,128)}, f32[14,32,128]{2,1,0:T(8,128)S(1)}, u32[]{:S(2)}, u32[]{:S(2)}) collective-permute-start(f32[14,32,128]{2,1,0:T(8,128)} %get-tuple-element.30), channel_id=1, source_target_pairs={{0,8},{8,16},{16,24},{24,32},{32,40},{40,48},{48,56},{56,64},{64,7... | collective-permute-start | bytes 688136 | tf_op jit(solution)/shard_map/ppermute | solution.py:402
  22.6 2.9 %collective-permute-start.4 = (f32[2,12,16,128]{3,2,1,0:T(8,128)}, f32[2,12,16,128]{3,2,1,0:T(8,128)S(1)}, u32[]{:S(2)}, u32[]{:S(2)}) collective-permute-start(f32[2,12,16,128]{3,2,1,0:T(8,128)} %get-tuple-element.38), channel_id=1, source_target_pairs={{0,4},{1,5},{2,6},{3,7},{4,0},{5,1},{6,2},{7,3},{8,12},{9,13},{10,... | collective-permute-start | bytes 589832 | tf_op jit(solution)/shard_map/ppermute | solution.py:411
  26.5 2.3 %collective-permute-done.up_ref.refs_6_ = f32[14,32,128]{2,1,0:T(8,128)S(1)} collective-permute-done((f32[14,32,128]{2,1,0:T(8,128)}, f32[14,32,128]{2,1,0:T(8,128)S(1)}, u32[]{:S(2)}, u32[]{:S(2)}) %collective-permute-start) | collective-permute-done | bytes 229408 | tf_op jit(solution)/shard_map/ppermute | solution.py:402
  28.8 2.1 %collective-permute-done.1.down_ref.refs_7_ = f32[14,32,128]{2,1,0:T(8,128)S(1)} collective-permute-done((f32[14,32,128]{2,1,0:T(8,128)}, f32[14,32,128]{2,1,0:T(8,128)S(1)}, u32[]{:S(2)}, u32[]{:S(2)}) %collective-permute-start.1) | collective-permute-done | bytes 229408 | tf_op jit(solution)/shard_map/ppermute | solution.py:402
  30.8 2.6 %all-to-all-done.chunk_ref = f32[32,16,128]{2,1,0:T(8,128)S(1)} async-done(((f32[32,16,128]{2,1,0:T(8,128)}), f32[32,16,128]{2,1,0:T(8,128)S(1)}, u32[]{:S(2)}, u32[]{:S(2)}) %all-to-all-start) | async-done | bytes 262176 | tf_op jit(solution)/shard_map/all_to_all | solution.py:407
  33.5 3.2 %shard_map.116 = (s32[24,128]{1,0:T(8,128)S(1)}, f32[24,128]{1,0:T(8,128)S(1)}, f32[8,4,1152]{2,1,0:T(4,128)}) custom-call(s32[1]{0:T(128)} %bitcast.p_ref.refs_0_, f32[32,16,128]{2,1,0:T(8,128)S(1)} %all-to-all-done.chunk_ref, f32[14,32,128]{2,1,0:T(8,128)S(1)} %collective-permute-done.up_ref.refs_6_, ...), custom_call_target="tpu_custom_call" | custom-call | tf_op jit(solution)/shard_map/pallas_call | solution.py:391
  36.6 4.2 %all-to-all-start.1 = ((f32[8,4,1152]{2,1,0:T(4,128)}), f32[8,4,1152]{2,1,0:T(4,128)S(1)}, u32[]{:S(2)}, u32[]{:S(2)}) async-start(f32[8,4,1152]{2,1,0:T(4,128)} %get-tuple-element.37), calls=%async_computation.1 | async-start | bytes 294912 | tf_op jit(solution)/shard_map/all_to_all | solution.py:415
  40.9 2.8 %shard_map.117 = (f32[4,12,16,128]{3,2,1,0:T(8,128)S(1)}, f32[4,12,16,128]{3,2,1,0:T(8,128)}) custom-call(s32[1]{0:T(128)} %bitcast.1.me_ref, f32[4,12,16,128]{3,2,1,0:T(8,128)S(1)} %copy-done.2, f32[4,12,16,128]{3,2,1,0:T(8,128)S(1)} %collective-permute-done.2.other_ref, f32[2,12,16,128]{3,2,1,0:T(8,128)} %collective-permute-done.3.y1_ref, ...), custom_call_target="tpu_custom_call" | custom-call | tf_op jit(solution)/shard_map/pallas_call | solution.py:391
  43.6 1.5 %collective-permute-start.8 = (f32[4,12,16,128]{3,2,1,0:T(8,128)}, f32[4,12,16,128]{3,2,1,0:T(8,128)S(1)}, u32[]{:S(2)}, u32[]{:S(2)}) collective-permute-start(f32[4,12,16,128]{3,2,1,0:T(8,128)} %get-tuple-element.48), channel_id=1, source_target_pairs={{0,1},{1,0},{2,3},{3,2},{4,5},{5,4},{6,7},{7,6},{8,9},{9,8},{10,11... | collective-permute-start | bytes 1179656 | tf_op jit(solution)/shard_map/ppermute | solution.py:411
  45.1 1.4 %all-to-all-done.1.gap_ref = f32[8,4,1152]{2,1,0:T(4,128)S(1)} async-done(((f32[8,4,1152]{2,1,0:T(4,128)}), f32[8,4,1152]{2,1,0:T(4,128)S(1)}, u32[]{:S(2)}, u32[]{:S(2)}) %all-to-all-start.1) | async-done | bytes 147488 | tf_op jit(solution)/shard_map/all_to_all | solution.py:415
  47.4 3.5 %all-to-all-start.2 = ((f32[8,4,1152]{2,1,0:T(4,128)}), f32[8,4,1152]{2,1,0:T(4,128)S(1)}, u32[]{:S(2)}, u32[]{:S(2)}) async-start(f32[8,4,1152]{2,1,0:T(4,128)} %shard_map.118), calls=%async_computation.2 | async-start | bytes 294912 | tf_op jit(solution)/shard_map/all_to_all | solution.py:415
  52.0 1.6 %shard_map.119 = (f32[12,4,32,128]{3,2,1,0:T(8,128)S(1)}, f32[4,32,128]{2,1,0:T(8,128)S(1)}) custom-call(s32[1]{0:T(128)} %bitcast.p_ref.refs_0_, f32[16,4]{1,0:T(8,128)S(1)} %copy.12.refs_1_, s32[4,32,128]{2,1,0:T(8,128)S(1)} %copy-done.4, f32[6,4,32,128]{3,2,1,0:T(8,128)S(1)} %bitcast.13, f32[6,4,32,128]{3,2,1,0:T(8,128)S(1)} %bitcast.16, ...), custom_call_target="tpu_custom_call" | custom-call | tf_op jit(solution)/shard_map/pallas_call | solution.py:391
  53.6 3.6 %all-to-all-done.2.force_ref = f32[8,4,1152]{2,1,0:T(4,128)S(1)} async-done(((f32[8,4,1152]{2,1,0:T(4,128)}), f32[8,4,1152]{2,1,0:T(4,128)S(1)}, u32[]{:S(2)}, u32[]{:S(2)}) %all-to-all-start.2) | async-done | bytes 147488 | tf_op jit(solution)/shard_map/all_to_all | solution.py:415
  58.0 8.3 %all-to-all-start.3 = ((f32[32,4,384]{2,1,0:T(4,128)}), f32[32,4,384]{2,1,0:T(4,128)S(1)}, u32[]{:S(2)}, u32[]{:S(2)}) async-start(f32[32,4,384]{2,1,0:T(4,128)} %get-tuple-element.42), calls=%async_computation.3 | async-start | bytes 393216 | tf_op jit(solution)/shard_map/all_to_all | solution.py:407
  67.3 1.8 %collective-permute-start.10 = (f32[2,12,16,128]{3,2,1,0:T(8,128)}, f32[2,12,16,128]{3,2,1,0:T(8,128)S(1)}, u32[]{:S(2)}, u32[]{:S(2)}) collective-permute-start(f32[2,12,16,128]{3,2,1,0:T(8,128)} %get-tuple-element.50), channel_id=1, source_target_pairs={{0,4},{1,5},{2,6},{3,7},{4,0},{5,1},{6,2},{7,3},{8,12},{9,13},{10,... | collective-permute-start | bytes 589832 | tf_op jit(solution)/shard_map/ppermute | solution.py:411
  69.0 2.0 %collective-permute-start.11 = (f32[2,12,16,128]{3,2,1,0:T(8,128)}, f32[2,12,16,128]{3,2,1,0:T(8,128)S(1)}, u32[]{:S(2)}, u32[]{:S(2)}) collective-permute-start(f32[2,12,16,128]{3,2,1,0:T(8,128)} %get-tuple-element.51), channel_id=1, source_target_pairs={{0,6},{1,7},{2,4},{3,5},{4,2},{5,3},{6,0},{7,1},{8,14},{9,15},{10,... | collective-permute-start | bytes 589832 | tf_op jit(solution)/shard_map/ppermute | solution.py:411
  71.0 2.5 %collective-permute-start.6 = (f32[2,12,128]{2,1,0:T(8,128)S(1)}, f32[2,12,128]{2,1,0:T(8,128)S(1)}, u32[]{:S(2)}, u32[]{:S(2)}) collective-permute-start(f32[2,12,128]{2,1,0:T(8,128)S(1)} %get-tuple-element.43), channel_id=1, source_target_pairs={{0,8},{8,16},{16,24},{24,32},{32,40},{40,48},{48,56},{56,64},{64,7... | collective-permute-start | bytes 36872 | tf_op jit(solution)/shard_map/ppermute | solution.py:402
  73.5 2.1 %shard_map.121.part_ref = f32[12,4,32,128]{3,2,1,0:T(8,128)S(1)} custom-call(s32[24,128]{1,0:T(8,128)S(1)} %get-tuple-element.46.idx_ref, f32[8,4,1152]{2,1,0:T(4,128)S(1)} %all-to-all-done.2.force_ref, f32[12,4,32,128]{3,2,1,0:T(8,128)S(1)} %get-tuple-element.47.lin_ref), custom_call_target="tpu_custom_call" | custom-call | tf_op jit(solution)/shard_map/pallas_call | solution.py:391
  75.6 1.4 %collective-permute-done.7.down_ref = f32[2,12,128]{2,1,0:T(8,128)S(1)} collective-permute-done((f32[2,12,128]{2,1,0:T(8,128)S(1)}, f32[2,12,128]{2,1,0:T(8,128)S(1)}, u32[]{:S(2)}, u32[]{:S(2)}) %collective-permute-start.7) | collective-permute-done | bytes 12320 | tf_op jit(solution)/shard_map/ppermute | solution.py:402
  78.3 2.2 %collective-permute-done.11.y3_ref = f32[2,12,16,128]{3,2,1,0:T(8,128)S(1)} collective-permute-done((f32[2,12,16,128]{3,2,1,0:T(8,128)}, f32[2,12,16,128]{3,2,1,0:T(8,128)S(1)}, u32[]{:S(2)}, u32[]{:S(2)}) %collective-permute-start.11) | collective-permute-done | bytes 196640 | tf_op jit(solution)/shard_map/ppermute | solution.py:411
  80.5 2.9 %shard_map.123 = (f32[6,4,32,128]{3,2,1,0:T(8,128)}, f32[6,4,32,128]{3,2,1,0:T(8,128)}) custom-call(s32[1]{0:T(128)} %bitcast.p_ref.refs_0_, s32[1]{0:T(128)} %bitcast.1.me_ref, s32[24,128]{1,0:T(8,128)S(1)} %copy-done.7, f32[32,4,384]{2,1,0:T(4,128)S(1)} %all-to-all-done.3.chunk_ref, f32[2,12,128]{2,1,0:T(8,128)S(1)} %collective-permute-done.6.up_ref, ...), custom_call_target="tpu_custom_call" | custom-call | tf_op jit(solution)/shard_map/pallas_call | solution.py:391
  (38 shorter events, 7.0 us)
Async XLA Ops:
  6.1 15.6 %copy-start.2 = (f32[4,12,16,128]{3,2,1,0:T(8,128)S(1)}, f32[4,12,16,128]{3,2,1,0:T(8,128)}, u32[]{:S(2)}) copy-start(f32[4,12,16,128]{3,2,1,0:T(8,128)} %get-tuple-element.33.same_ref) | copy-start | bytes 1179652
  6.1 15.6 %collective-permute-start.2 = (f32[4,12,16,128]{3,2,1,0:T(8,128)}, f32[4,12,16,128]{3,2,1,0:T(8,128)S(1)}, u32[]{:S(2)}, u32[]{:S(2)}) collective-permute-start(f32[4,12,16,128]{3,2,1,0:T(8,128)} %get-tuple-element.34), channel_id=1, source_target_pairs={{0,1},{1,0},{2,3},{3,2},{4,5},{5,4},{6,7},{7,6},{8,9},{9,8},{10,11... | collective-permute-start | bytes 1179656 | tf_op jit(solution)/shard_map/ppermute | solution.py:411
  8.3 25.2 %all-to-all-start = ((f32[32,16,128]{2,1,0:T(8,128)}), f32[32,16,128]{2,1,0:T(8,128)S(1)}, u32[]{:S(2)}, u32[]{:S(2)}) async-start(f32[32,16,128]{2,1,0:T(8,128)} %get-tuple-element.29), calls=%async_computation | async-start | bytes 524288 | tf_op jit(solution)/shard_map/all_to_all | solution.py:407
  20.0 8.7 %collective-permute-start = (f32[14,32,128]{2,1,0:T(8,128)}, f32[14,32,128]{2,1,0:T(8,128)S(1)}, u32[]{:S(2)}, u32[]{:S(2)}) collective-permute-start(f32[14,32,128]{2,1,0:T(8,128)} %get-tuple-element.30), channel_id=1, source_target_pairs={{0,8},{8,16},{16,24},{24,32},{32,40},{40,48},{48,56},{56,64},{64,7... | collective-permute-start | bytes 688136 | tf_op jit(solution)/shard_map/ppermute | solution.py:402
  21.7 9.1 %collective-permute-start.1 = (f32[14,32,128]{2,1,0:T(8,128)}, f32[14,32,128]{2,1,0:T(8,128)S(1)}, u32[]{:S(2)}, u32[]{:S(2)}) collective-permute-start(f32[14,32,128]{2,1,0:T(8,128)} %get-tuple-element.31), channel_id=1, source_target_pairs={{0,248},{8,0},{16,8},{24,16},{32,24},{40,32},{48,40},{56,48},{64,5... | collective-permute-start | bytes 688136 | tf_op jit(solution)/shard_map/ppermute | solution.py:402
  21.7 4.6 %copy-start = (f32[2,3,4,32,128]{4,3,2,1,0:T(8,128)S(1)}, f32[2,3,4,32,128]{4,3,2,1,0:T(8,128)}, u32[]{:S(2)}) copy-start(f32[2,3,4,32,128]{4,3,2,1,0:T(8,128)} %param.10) | copy-start | bytes 1179652
  21.8 4.6 %copy-start.1 = (f32[2,3,4,32,128]{4,3,2,1,0:T(8,128)S(1)}, f32[2,3,4,32,128]{4,3,2,1,0:T(8,128)}, u32[]{:S(2)}) copy-start(f32[2,3,4,32,128]{4,3,2,1,0:T(8,128)} %param.11) | copy-start | bytes 1179652
  22.6 18.2 %collective-permute-start.4 = (f32[2,12,16,128]{3,2,1,0:T(8,128)}, f32[2,12,16,128]{3,2,1,0:T(8,128)S(1)}, u32[]{:S(2)}, u32[]{:S(2)}) collective-permute-start(f32[2,12,16,128]{3,2,1,0:T(8,128)} %get-tuple-element.38), channel_id=1, source_target_pairs={{0,4},{1,5},{2,6},{3,7},{4,0},{5,1},{6,2},{7,3},{8,12},{9,13},{10,... | collective-permute-start | bytes 589832 | tf_op jit(solution)/shard_map/ppermute | solution.py:411
  25.5 15.3 %collective-permute-start.5 = (f32[2,12,16,128]{3,2,1,0:T(8,128)}, f32[2,12,16,128]{3,2,1,0:T(8,128)}, u32[]{:S(2)}, u32[]{:S(2)}) collective-permute-start(f32[2,12,16,128]{3,2,1,0:T(8,128)} %get-tuple-element.39), channel_id=1, source_target_pairs={{0,6},{1,7},{2,4},{3,5},{4,2},{5,3},{6,0},{7,1},{8,14},{9,15},{10,... | collective-permute-start | bytes 589832 | tf_op jit(solution)/shard_map/ppermute | solution.py:411
  26.3 7.1 %copy-start.6 = (f32[2,16,128]{2,1,0:T(8,128)S(1)}, f32[2,16,128]{2,1,0:T(8,128)}, u32[]{:S(2)}) copy-start(f32[2,16,128]{2,1,0:T(8,128)} %get-tuple-element.32.self_ref) | copy-start | bytes 49156
  26.3 14.5 %collective-permute-start.3 = (f32[2,12,16,128]{3,2,1,0:T(8,128)}, f32[2,12,16,128]{3,2,1,0:T(8,128)}, u32[]{:S(2)}, u32[]{:S(2)}) collective-permute-start(f32[2,12,16,128]{3,2,1,0:T(8,128)} %get-tuple-element.35.after_ref), channel_id=1, source_target_pairs={{0,2},{1,3},{2,0},{3,1},{4,6},{5,7},{6,4},{7,5},{8,10},{9,11},{10,... | collective-permute-start | bytes 589832 | tf_op jit(solution)/shard_map/ppermute | solution.py:411
  36.6 9.8 %all-to-all-start.1 = ((f32[8,4,1152]{2,1,0:T(4,128)}), f32[8,4,1152]{2,1,0:T(4,128)S(1)}, u32[]{:S(2)}, u32[]{:S(2)}) async-start(f32[8,4,1152]{2,1,0:T(4,128)} %get-tuple-element.37), calls=%async_computation.1 | async-start | bytes 294912 | tf_op jit(solution)/shard_map/all_to_all | solution.py:415
  40.8 5.6 %copy-start.5 = (f32[48,48]{1,0:T(8,128)S(1)}, f32[48,48]{1,0:T(8,128)}, u32[]{:S(2)}) copy-start(f32[48,48]{1,0:T(8,128)} %constant.11.clone.spread_ref) | copy-start | bytes 27652
  43.6 22.7 %collective-permute-start.8 = (f32[4,12,16,128]{3,2,1,0:T(8,128)}, f32[4,12,16,128]{3,2,1,0:T(8,128)S(1)}, u32[]{:S(2)}, u32[]{:S(2)}) collective-permute-start(f32[4,12,16,128]{3,2,1,0:T(8,128)} %get-tuple-element.48), channel_id=1, source_target_pairs={{0,1},{1,0},{2,3},{3,2},{4,5},{5,4},{6,7},{7,6},{8,9},{9,8},{10,11... | collective-permute-start | bytes 1179656 | tf_op jit(solution)/shard_map/ppermute | solution.py:411
  47.4 3.5 %copy-start.8 = (f32[16,4]{0,1:T(4,128)S(1)}, f32[16,4]{0,1:T(4,128)}, u32[]{:S(2)}) copy-start(f32[16,4]{0,1:T(4,128)} %param.14) | copy-start | bytes 772
  47.4 3.6 %copy-start.4 = (s32[4,32,128]{2,1,0:T(8,128)S(1)}, s32[4,32,128]{2,1,0:T(8,128)}, u32[]{:S(2)}) copy-start(s32[4,32,128]{2,1,0:T(8,128)} %refs_2_.1) | copy-start | bytes 196612
  47.4 9.8 %all-to-all-start.2 = ((f32[8,4,1152]{2,1,0:T(4,128)}), f32[8,4,1152]{2,1,0:T(4,128)S(1)}, u32[]{:S(2)}, u32[]{:S(2)}) async-start(f32[8,4,1152]{2,1,0:T(4,128)} %shard_map.118), calls=%async_computation.2 | async-start | bytes 294912 | tf_op jit(solution)/shard_map/all_to_all | solution.py:415
  58.0 20.0 %all-to-all-start.3 = ((f32[32,4,384]{2,1,0:T(4,128)}), f32[32,4,384]{2,1,0:T(4,128)S(1)}, u32[]{:S(2)}, u32[]{:S(2)}) async-start(f32[32,4,384]{2,1,0:T(4,128)} %get-tuple-element.42), calls=%async_computation.3 | async-start | bytes 393216 | tf_op jit(solution)/shard_map/all_to_all | solution.py:407
  67.2 10.9 %collective-permute-start.9 = (f32[2,12,16,128]{3,2,1,0:T(8,128)}, f32[2,12,16,128]{3,2,1,0:T(8,128)S(1)}, u32[]{:S(2)}, u32[]{:S(2)}) collective-permute-start(f32[2,12,16,128]{3,2,1,0:T(8,128)} %get-tuple-element.49), channel_id=1, source_target_pairs={{0,2},{1,3},{2,0},{3,1},{4,6},{5,7},{6,4},{7,5},{8,10},{9,11},{10,... | collective-permute-start | bytes 589832 | tf_op jit(solution)/shard_map/ppermute | solution.py:411
  67.3 11.1 %collective-permute-start.10 = (f32[2,12,16,128]{3,2,1,0:T(8,128)}, f32[2,12,16,128]{3,2,1,0:T(8,128)S(1)}, u32[]{:S(2)}, u32[]{:S(2)}) collective-permute-start(f32[2,12,16,128]{3,2,1,0:T(8,128)} %get-tuple-element.50), channel_id=1, source_target_pairs={{0,4},{1,5},{2,6},{3,7},{4,0},{5,1},{6,2},{7,3},{8,12},{9,13},{10,... | collective-permute-start | bytes 589832 | tf_op jit(solution)/shard_map/ppermute | solution.py:411
  69.0 11.4 %collective-permute-start.11 = (f32[2,12,16,128]{3,2,1,0:T(8,128)}, f32[2,12,16,128]{3,2,1,0:T(8,128)S(1)}, u32[]{:S(2)}, u32[]{:S(2)}) collective-permute-start(f32[2,12,16,128]{3,2,1,0:T(8,128)} %get-tuple-element.51), channel_id=1, source_target_pairs={{0,6},{1,7},{2,4},{3,5},{4,2},{5,3},{6,0},{7,1},{8,14},{9,15},{10,... | collective-permute-start | bytes 589832 | tf_op jit(solution)/shard_map/ppermute | solution.py:411
  71.0 4.6 %collective-permute-start.6 = (f32[2,12,128]{2,1,0:T(8,128)S(1)}, f32[2,12,128]{2,1,0:T(8,128)S(1)}, u32[]{:S(2)}, u32[]{:S(2)}) collective-permute-start(f32[2,12,128]{2,1,0:T(8,128)S(1)} %get-tuple-element.43), channel_id=1, source_target_pairs={{0,8},{8,16},{16,24},{24,32},{32,40},{40,48},{48,56},{56,64},{64,7... | collective-permute-start | bytes 36872 | tf_op jit(solution)/shard_map/ppermute | solution.py:402
  73.5 3.5 %collective-permute-start.7 = (f32[2,12,128]{2,1,0:T(8,128)S(1)}, f32[2,12,128]{2,1,0:T(8,128)S(1)}, u32[]{:S(2)}, u32[]{:S(2)}) collective-permute-start(f32[2,12,128]{2,1,0:T(8,128)S(1)} %get-tuple-element.44), channel_id=1, source_target_pairs={{0,248},{8,0},{16,8},{24,16},{32,24},{40,32},{48,40},{56,48},{64,5... | collective-permute-start | bytes 36872 | tf_op jit(solution)/shard_map/ppermute | solution.py:402
  73.5 7.0 %copy-start.7 = (s32[24,128]{1,0:T(8,128)S(1)}, s32[24,128]{1,0:T(8,128)}, u32[]{:S(2)}) copy-start(s32[24,128]{1,0:T(8,128)} %get-tuple-element.28.idx_ref) | copy-start | bytes 36868
  (1 other events, 1.0 us)

commit v12 on v11

--- a/solution.py
+++ b/solution.py
@@ -125,7 +125,7 @@
     split_fields(disp_ref, dir_ref, parts_ref)
 
 
-def gather_rows(parts_ref, idx_ref, here_ref):
+def gather_rows(parts_ref, idx_ref, here_ref, first, last):
     def step(k, carry):
         pick, in_y = picks(idx_ref, k)
         rows = jnp.dot(parts_ref[...], pick, preferred_element_type=f32)
@@ -135,7 +135,7 @@
         here_ref[2 * k + 1, 0:12, :] = got[:, 128:]
         return carry
 
-    lax.fori_loop(0, SIDE // 2, step, 0, unroll=3)
+    lax.fori_loop(first, last, step, 0, unroll=3)
 
 
 def scatter_rows(val_ref, idx_ref, sum_ref):
@@ -192,30 +192,31 @@
     split_fields(disp_ref, dir_ref, parts_ref)
     near_ref[2] = (ids_ref[3] + 1).astype(f32)
     near_ref[3] = (ids_ref[0] + 1).astype(f32)
-    gather_rows(parts_ref, idx_ref, rows_ref)
-    for k in range(2):
-        near_ref[k] = rows_ref[2 + 2 * k : 4 + 2 * k].reshape(32, 128)
-    ends = ((near_ref.at[0], up_hbm.at[0]), (near_ref.at[1], down_hbm.at[0]),
-            (near_ref.at[2], up_hbm.at[13]), (near_ref.at[3], down_hbm.at[13]))
-    ends = [pltpu.make_async_copy(a, b, sems.at[7 + k]) for k, (a, b) in enumerate(ends)]
-    for end in ends:
-        end.start()
     for d in (0, 1, SLABS - 1):
         chunk_ref[(p + d) & (SLABS - 1)] = jnp.zeros((16, 128), f32)
+    gather_rows(parts_ref, idx_ref, rows_ref, 3, SIDE // 2)
     for d, tile in ((2, 6), (SLABS - 2, 7)):
         chunk_ref[(p + d) & (SLABS - 1)] = rows_ref[tile]
     for d in range(3, SLABS - 2):
         tile, seg = far_place(d)
         chunk_ref[(p + d) & (SLABS - 1)] = lane_roll(rows_ref[tile], -seg)
-    ends.append(pltpu.make_async_copy(chunk_ref, chunk_hbm, sems.at[11]))
-    ends[-1].start()
+    ends = [pltpu.make_async_copy(chunk_ref, chunk_hbm, sems.at[11])]
+    ends[0].start()
+    gather_rows(parts_ref, idx_ref, rows_ref, 0, 3)
+    for k in range(2):
+        near_ref[k] = rows_ref[2 + 2 * k : 4 + 2 * k].reshape(32, 128)
+    pairs = ((near_ref.at[0], up_hbm.at[0]), (near_ref.at[1], down_hbm.at[0]),
+             (near_ref.at[2], up_hbm.at[13]), (near_ref.at[3], down_hbm.at[13]))
+    for k, (a, b) in enumerate(pairs):
+        ends.append(pltpu.make_async_copy(a, b, sems.at[7 + k]))
+        ends[-1].start()
     self_ref[...] = rows_ref[0:2]
     for move in moves + ends:
         move.wait()
 
 
 def gap_kernel(p_ref, chunk_ref, up_ref, down_ref, self_ref, parts_ref, after_ref,
-               idx_ref, kind_ref, gap_ref, here_ref):
+               idx_ref, kind_ref, gap_hbm, here_ref, gap_ref, sems):
     p = p_ref[0]
 
     def asked(d):
@@ -228,12 +229,19 @@
     rows = [t[12:13] for t in tiles[:8]] + [jnp.where(beyond, -1.0, t[12:13]) for t in tiles[8:]]
     idx_ref[...] = jnp.concatenate(rows + [jnp.full((7, 128), -1.0, f32)], axis=0).astype(i32)
     kind_ref[...] = jnp.concatenate([t[13:14] for t in tiles] + [jnp.zeros((7, 128), f32)], axis=0)
-    gather_rows(parts_ref, idx_ref, here_ref)
-    for tile in range(24):
-        gap = tiles[tile][0:12] - here_ref[tile] if tile < 17 else jnp.zeros((12, 128), f32)
-        at = 128 * (tile % 3)
-        for k in range(3):
-            gap_ref[tile // 3, :, 384 * k + at : 384 * k + at + 128] = gap[4 * k : 4 * k + 4]
+    copies = [pltpu.make_async_copy(gap_ref.at[pl.ds(2 * g, 2)], gap_hbm.at[pl.ds(2 * g, 2)], sems.at[g]) for g in range(4)]
+    gap_ref[6:8] = jnp.zeros((2, 4, 1152), f32)
+    copies[3].start()
+    for g in range(3):
+        gather_rows(parts_ref, idx_ref, here_ref, 3 * g, 3 * g + 3)
+        for tile in range(6 * g, 6 * g + 6):
+            gap = tiles[tile][0:12] - here_ref[tile] if tile < 17 else jnp.zeros((12, 128), f32)
+            at = 128 * (tile % 3)
+            for k in range(3):
+                gap_ref[tile // 3, :, 384 * k + at : 384 * k + at + 128] = gap[4 * k : 4 * k + 4]
+        copies[g].start()
+    for copy in copies:
+        copy.wait()
 
 
 def force_kernel(me_ref, kind_ref, spread_ref, gap_ref, after_ref, out_ref, r_ref, d_ref, f_ref, t_ref):
@@ -312,8 +320,14 @@
         out[1] = other_ref[k + 1]
 
 
+def rejoin_kernel(keep_ref, cross1_ref, cross2_ref, *out_refs):
+    for k, out in enumerate(out_refs):
+        out[0] = keep_ref[k + 1]
+        out[1] = (cross1_ref, cross2_ref)[(k + 1) // 2][(k + 1) % 2]
+
+
 def time_kernel(me_ref, same_ref, other_ref, y1_ref, y2_ref, y3_ref, *refs):
-    keep_ref, cross_ref, in_ref, out_ref = refs
+    keep_ref, cross1_ref, cross2_ref, in_ref, out_ref = refs
     me = me_ref[0]
     in_ref[0] = same_ref[0]
     in_ref[1] = other_ref[0]
@@ -335,7 +349,8 @@
 
     lax.fori_loop(0, 6, step, 0)
     for k in range(PARTS):
-        (keep_ref, cross_ref)[k % 2][k // 2] = out_ref[k]
+        ref, at = (keep_ref, k // 2) if k % 2 == 0 else ((cross1_ref, cross2_ref)[k // 4], k // 2 % 2)
+        ref[at] = out_ref[k]
 
 
 def lookup(ids, mat_ref, column, count):
@@ -345,7 +360,7 @@
     return out
 
 
-def stiff_kernel(p_ref, mat_ref, ids_ref, disp_ref, dir_ref, forcing_ref, up_ref, down_ref, out_ref, mass_ref, *, materials):
+def stiff_kernel(p_ref, mat_ref, ids_ref, disp_ref, dir_ref, forcing_ref, up_ref, down_ref, after_ref, out_ref, mass_ref, *, materials):
     p = p_ref[0]
     low = jnp.where(p > 0, up_ref[1:14], 0.0)
     high = jnp.where(p < SLABS - 1, down_ref[1:14], 0.0)
@@ -392,7 +407,7 @@
         kernel,
         out_shape=[jax.ShapeDtypeStruct(s, d) for s, d in outs],
         in_specs=specs,
-        out_specs=[pl.BlockSpec(memory_space=pl.ANY if k in kept else pltpu.VMEM) for k in range(len(outs))],
+        out_specs=[pl.BlockSpec(memory_space=pltpu.HBM if k in kept else pltpu.VMEM) for k in range(len(outs))],
         scratch_shapes=list(scratch),
         compiler_params=pltpu.CompilerParams(vmem_limit_bytes=limit),
     )(*args)
@@ -458,7 +473,7 @@
     joined = call(join_kernel, [pair] * 3, same, other, smem=())
     turned = [swap(x, 2 * k + 2) for k, x in enumerate(joined)]
     blocks = [pltpu.VMEM((PARTS, 12, 16, 128), f32)] * 2
-    keep, cross = call(time_kernel, [half] * 2, me, same, other, *turned, scratch=blocks)
+    keep, *cross = call(time_kernel, [half, pair, pair], me, same, other, *turned, scratch=blocks)
 
     part = ((PARTS, 4, 1152), f32)
     fields_parts = call(split_kernel, [(parts, bf16)], disp, dire, smem=())[0]
@@ -467,7 +482,8 @@
         [index, ((24, 128), f32), part],
         p, chunk, up, down, own, fields_parts, joined[0],
         away=(6,),
-        scratch=[pltpu.VMEM((SIDE, 12, 128), f32)],
+        kept=(2,),
+        scratch=[pltpu.VMEM((SIDE, 12, 128), f32), pltpu.VMEM(part[0], f32), pltpu.SemaphoreType.DMA((4,))],
     )
     force = call(
         force_kernel,
@@ -477,14 +493,15 @@
         scratch=[pltpu.VMEM((48, 384), f32)] * 4,
     )[0]
     force = inst_split(force)
-    cross = swap(cross, 1)
-    joined = call(join_kernel, [pair] * 3, keep, cross, smem=())
+    cross = [swap(x, 1) for x in cross]
+    joined = call(rejoin_kernel, [pair] * 3, keep, *cross, smem=())
     turned = [swap(x, 2 * k + 2) for k, x in enumerate(joined)]
     lin, mass = call(
         lambda *refs: stiff_kernel(*refs, materials=materials.shape[0]),
         [(whole, f32), ((4, 32, 128), f32)],
-        p, materials, material_ids, disp, dire, forcing.reshape(fields), up, down,
+        p, materials, material_ids, disp, dire, forcing.reshape(fields), up, down, joined[0],
         smem=(0, 1),
+        away=(8,),
     )
     two = ((2, 12, 128), f32)
     chunk, up2, down2, own = call(reply_kernel, [((SLABS, 4, 384), f32), two, two, two], p, force, mass, away=(2,))
@@ -495,7 +512,7 @@
     residual, jacobian = call(
         final_kernel,
         [(fields, f32)] * 2,
-        p, me, own_idx, chunk, up2, down2, own, partial, mass, keep, cross, *turned,
+        p, me, own_idx, chunk, up2, down2, own, partial, mass, keep, cross[0], *turned,
         smem=(0, 1),
         scratch=adding + blocks[:1],
     )

time: 84.6 us -> 83.5 us (0.987)
  waiting for transfers between devices: 16.8 us -> 17.8 us
    ppermute x8 -> x9, waiting for transfers between devices: 2.48 us -> 6.07 us  [swap(): return lax.ppermute(x, 'inst', [(i, i ^ bit) for i in range(PARTS)])]
    all_to_all x2, waiting for transfers between devices: 4.95 us -> 3.42 us  [inst_split(): return lax.all_to_all(x, 'inst', split_axis=0, concat_axis=0, tiled=True)]
    all_to_all x2, waiting for transfers between devices: 3.69 us -> 2.63 us  [exchange(): lax.all_to_all(chunk, 'mesh', split_axis=0, concat_axis=0, tiled=True)]
    ppermute x8 -> x9, starting transfers between devices: 11.1 us -> 10.2 us  [swap(): return lax.ppermute(x, 'inst', [(i, i ^ bit) for i in range(PARTS)])]
  transfers between devices with their start and end apart: 16 -> 17, of which waited for: 9 -> 8; matrix products, arithmetic and copies ran while one was open for 0% -> 0% of each run, Pallas kernels for 16% -> 15%
where the time goes in v12:
time: 83.5 us; the launch traced here: 83.1 us
  starting transfers between devices  42.3 us (51%)
  Pallas kernels  21.3 us (26%)
  waiting for transfers between devices  17.8 us (21%)
    pallas_call x11, Pallas kernels, call(): pl.pallas_call(kernel, out_shape=[jax.ShapeDtypeStruct(s, d) for s, d in...  21.3 us
    all_to_all x2, starting transfers between devices, exchange(): lax.all_to_all(chunk, 'mesh', split_axis=0, concat_axis=0, tiled=True)  19.9 us
    ppermute x9, starting transfers between devices, swap(): return lax.ppermute(x, 'inst', [(i, i ^ bit) for i in range(PARTS)])  10.2 us
    all_to_all x2, starting transfers between devices, inst_split(): return lax.all_to_all(x, 'inst', split_axis=0, concat_axis=0, tiled=True)  8.01 us
    ppermute x9, waiting for transfers between devices, swap(): return lax.ppermute(x, 'inst', [(i, i ^ bit) for i in range(PARTS)])  6.07 us
    ppermute x4, waiting for transfers between devices, shift(): lax.ppermute(x, 'mesh', [(i, (i + by) % SLABS) for i in range(SLABS)])  5.71 us
    ppermute x4, starting transfers between devices, shift(): lax.ppermute(x, 'mesh', [(i, (i + by) % SLABS) for i in range(SLABS)])  4.19 us
    all_to_all x2, waiting for transfers between devices, inst_split(): return lax.all_to_all(x, 'inst', split_axis=0, concat_axis=0, tiled=True)  3.42 us
  transfers between devices with their start and end apart: 17, of which 8 were waited for; matrix products, arithmetic and copies ran while one was open for 0% of the time, Pallas kernels for 15%

profile of v12, /device:TPU:1, one launch (start us, length us, event | category | flops | bytes accessed | tf_op | source)
XLA Modules:
  0.0 83.1 jit_solution(13450889587064358801)
XLA Ops:
  0.6 5.4 %shard_map.113 = (s32[24,128]{1,0:T(8,128)}, f32[32,16,128]{2,1,0:T(8,128)}, f32[14,32,128]{2,1,0:T(8,128)}, f32[14,32,128]{2,1,0:T(8,128)}, f32[2,16,128]{2,1,0...) custom-call(s32[1]{0:T(128)} %bitcast.p_ref.refs_0_, s32[1]{0:T(128)} %bitcast.1.me_ref, ...), custom_call_target="tpu_custom_call" | custom-call | tf_op jit(solution)/shard_map/pallas_call | solution.py:406
  6.0 2.1 %collective-permute-start.2 = (f32[4,12,16,128]{3,2,1,0:T(8,128)}, f32[4,12,16,128]{3,2,1,0:T(8,128)S(1)}, u32[]{:S(2)}, u32[]{:S(2)}) collective-permute-start(f32[4,12,16,128]{3,2,1,0:T(8,128)} %get-tuple-element.35), channel_id=1, source_target_pairs={{0,1},{1,0},{2,3},{3,2},{4,5},{5,4},{6,7},{7,6},{8,9},{9,8},{10,11... | collective-permute-start | bytes 1179656 | tf_op jit(solution)/shard_map/ppermute | solution.py:426
  8.1 11.7 %all-to-all-start = ((f32[32,16,128]{2,1,0:T(8,128)}), f32[32,16,128]{2,1,0:T(8,128)S(1)}, u32[]{:S(2)}, u32[]{:S(2)}) async-start(f32[32,16,128]{2,1,0:T(8,128)} %get-tuple-element.30), calls=%async_computation | async-start | bytes 524288 | tf_op jit(solution)/shard_map/all_to_all | solution.py:422
  19.9 1.7 %collective-permute-start = (f32[14,32,128]{2,1,0:T(8,128)}, f32[14,32,128]{2,1,0:T(8,128)S(1)}, u32[]{:S(2)}, u32[]{:S(2)}) collective-permute-start(f32[14,32,128]{2,1,0:T(8,128)} %get-tuple-element.31), channel_id=1, source_target_pairs={{0,8},{8,16},{16,24},{24,32},{32,40},{40,48},{48,56},{56,64},{64,7... | collective-permute-start | bytes 688136 | tf_op jit(solution)/shard_map/ppermute | solution.py:417
  22.5 2.9 %collective-permute-start.4 = (f32[2,12,16,128]{3,2,1,0:T(8,128)}, f32[2,12,16,128]{3,2,1,0:T(8,128)S(1)}, u32[]{:S(2)}, u32[]{:S(2)}) collective-permute-start(f32[2,12,16,128]{3,2,1,0:T(8,128)} %get-tuple-element.39), channel_id=1, source_target_pairs={{0,4},{1,5},{2,6},{3,7},{4,0},{5,1},{6,2},{7,3},{8,12},{9,13},{10,... | collective-permute-start | bytes 589832 | tf_op jit(solution)/shard_map/ppermute | solution.py:426
  26.3 2.3 %collective-permute-done.up_ref.refs_6_ = f32[14,32,128]{2,1,0:T(8,128)S(1)} collective-permute-done((f32[14,32,128]{2,1,0:T(8,128)}, f32[14,32,128]{2,1,0:T(8,128)S(1)}, u32[]{:S(2)}, u32[]{:S(2)}) %collective-permute-start) | collective-permute-done | bytes 229408 | tf_op jit(solution)/shard_map/ppermute | solution.py:417
  28.6 2.1 %collective-permute-done.1.down_ref.refs_7_ = f32[14,32,128]{2,1,0:T(8,128)S(1)} collective-permute-done((f32[14,32,128]{2,1,0:T(8,128)}, f32[14,32,128]{2,1,0:T(8,128)S(1)}, u32[]{:S(2)}, u32[]{:S(2)}) %collective-permute-start.1) | collective-permute-done | bytes 229408 | tf_op jit(solution)/shard_map/ppermute | solution.py:417
  30.7 2.6 %all-to-all-done.chunk_ref = f32[32,16,128]{2,1,0:T(8,128)S(1)} async-done(((f32[32,16,128]{2,1,0:T(8,128)}), f32[32,16,128]{2,1,0:T(8,128)S(1)}, u32[]{:S(2)}, u32[]{:S(2)}) %all-to-all-start) | async-done | bytes 262176 | tf_op jit(solution)/shard_map/all_to_all | solution.py:422
  33.3 3.2 %shard_map.116 = (s32[24,128]{1,0:T(8,128)S(1)}, f32[24,128]{1,0:T(8,128)S(1)}, f32[8,4,1152]{2,1,0:T(4,128)S(1)}) custom-call(s32[1]{0:T(128)} %bitcast.p_ref.refs_0_, f32[32,16,128]{2,1,0:T(8,128)S(1)} %all-to-all-done.chunk_ref, f32[14,32,128]{2,1,0:T(8,128)S(1)} %collective-permute-done.up_ref.refs_6_, ...), custom_call_target="tpu_custom_call" | custom-call | tf_op jit(solution)/shard_map/pallas_call | solution.py:406
  37.1 4.2 %all-to-all-start.1 = ((f32[8,4,1152]{2,1,0:T(4,128)}), f32[8,4,1152]{2,1,0:T(4,128)S(1)}, u32[]{:S(2)}, u32[]{:S(2)}) async-start(f32[8,4,1152]{2,1,0:T(4,128)} %copy-done.5), calls=%async_computation.1 | async-start | bytes 294912 | tf_op jit(solution)/shard_map/all_to_all | solution.py:430
  41.4 2.7 %shard_map.117 = (f32[4,12,16,128]{3,2,1,0:T(8,128)S(1)}, f32[2,12,16,128]{3,2,1,0:T(8,128)}, f32[2,12,16,128]{3,2,1,0:T(8,128)}) custom-call(s32[1]{0:T(128)} %bitcast.1.me_ref, f32[4,12,16,128]{3,2,1,0:T(8,128)S(1)} %copy-done.2, f32[4,12,16,128]{3,2,1,0:T(8,128)S(1)} %collective-permute-done.2.other_ref, ...), custom_call_target="tpu_custom_call" | custom-call | tf_op jit(solution)/shard_map/pallas_call | solution.py:406
  44.0 1.5 %collective-permute-start.6 = (f32[2,12,16,128]{3,2,1,0:T(8,128)}, f32[2,12,16,128]{3,2,1,0:T(8,128)S(1)}, u32[]{:S(2)}, u32[]{:S(2)}) collective-permute-start(f32[2,12,16,128]{3,2,1,0:T(8,128)} %get-tuple-element.42), channel_id=1, source_target_pairs={{0,1},{1,0},{2,3},{3,2},{4,5},{5,4},{6,7},{7,6},{8,9},{9,8},{10,11... | collective-permute-start | bytes 589832 | tf_op jit(solution)/shard_map/ppermute | solution.py:426
  45.5 1.4 %all-to-all-done.1.gap_ref = f32[8,4,1152]{2,1,0:T(4,128)S(1)} async-done(((f32[8,4,1152]{2,1,0:T(4,128)}), f32[8,4,1152]{2,1,0:T(4,128)S(1)}, u32[]{:S(2)}, u32[]{:S(2)}) %all-to-all-start.1) | async-done | bytes 147488 | tf_op jit(solution)/shard_map/all_to_all | solution.py:430
  47.9 3.8 %all-to-all-start.2 = ((f32[8,4,1152]{2,1,0:T(4,128)}), f32[8,4,1152]{2,1,0:T(4,128)S(1)}, u32[]{:S(2)}, u32[]{:S(2)}) async-start(f32[8,4,1152]{2,1,0:T(4,128)} %shard_map.118), calls=%async_computation.2 | async-start | bytes 294912 | tf_op jit(solution)/shard_map/all_to_all | solution.py:430
  51.8 1.9 %collective-permute-done.7.cross2_ref = f32[2,12,16,128]{3,2,1,0:T(8,128)S(1)} collective-permute-done((f32[2,12,16,128]{3,2,1,0:T(8,128)}, f32[2,12,16,128]{3,2,1,0:T(8,128)S(1)}, u32[]{:S(2)}, u32[]{:S(2)}) %collective-permute-start.7) | collective-permute-done | bytes 196640 | tf_op jit(solution)/shard_map/ppermute | solution.py:426
  54.5 1.6 %shard_map.120 = (f32[12,4,32,128]{3,2,1,0:T(8,128)S(1)}, f32[4,32,128]{2,1,0:T(8,128)S(1)}) custom-call(s32[1]{0:T(128)} %bitcast.p_ref.refs_0_, f32[16,4]{1,0:T(8,128)S(1)} %copy.12.refs_1_, s32[4,32,128]{2,1,0:T(8,128)S(1)} %copy-done.4, f32[6,4,32,128]{3,2,1,0:T(8,128)S(1)} %bitcast.13, f32[6,4,32,128]{3,2,1,0:T(8,128)S(1)} %bitcast.16, ...), custom_call_target="tpu_custom_call" | custom-call | tf_op jit(solution)/shard_map/pallas_call | solution.py:406
  56.1 2.0 %all-to-all-done.2.force_ref = f32[8,4,1152]{2,1,0:T(4,128)S(1)} async-done(((f32[8,4,1152]{2,1,0:T(4,128)}), f32[8,4,1152]{2,1,0:T(4,128)S(1)}, u32[]{:S(2)}, u32[]{:S(2)}) %all-to-all-start.2) | async-done | bytes 147488 | tf_op jit(solution)/shard_map/all_to_all | solution.py:430
  58.9 8.2 %all-to-all-start.3 = ((f32[32,4,384]{2,1,0:T(4,128)}), f32[32,4,384]{2,1,0:T(4,128)S(1)}, u32[]{:S(2)}, u32[]{:S(2)}) async-start(f32[32,4,384]{2,1,0:T(4,128)} %get-tuple-element.46), calls=%async_computation.3 | async-start | bytes 393216 | tf_op jit(solution)/shard_map/all_to_all | solution.py:422
  67.1 1.9 %collective-permute-start.11 = (f32[2,12,16,128]{3,2,1,0:T(8,128)}, f32[2,12,16,128]{3,2,1,0:T(8,128)S(1)}, u32[]{:S(2)}, u32[]{:S(2)}) collective-permute-start(f32[2,12,16,128]{3,2,1,0:T(8,128)} %get-tuple-element.52), channel_id=1, source_target_pairs={{0,4},{1,5},{2,6},{3,7},{4,0},{5,1},{6,2},{7,3},{8,12},{9,13},{10,... | collective-permute-start | bytes 589832 | tf_op jit(solution)/shard_map/ppermute | solution.py:426
  70.0 2.5 %collective-permute-start.8 = (f32[2,12,128]{2,1,0:T(8,128)S(1)}, f32[2,12,128]{2,1,0:T(8,128)S(1)}, u32[]{:S(2)}, u32[]{:S(2)}) collective-permute-start(f32[2,12,128]{2,1,0:T(8,128)S(1)} %get-tuple-element.47), channel_id=1, source_target_pairs={{0,8},{8,16},{16,24},{24,32},{32,40},{40,48},{48,56},{56,64},{64,7... | collective-permute-start | bytes 36872 | tf_op jit(solution)/shard_map/ppermute | solution.py:417
  72.5 2.1 %shard_map.122.part_ref = f32[12,4,32,128]{3,2,1,0:T(8,128)S(1)} custom-call(s32[24,128]{1,0:T(8,128)S(1)} %get-tuple-element.50.idx_ref, f32[8,4,1152]{2,1,0:T(4,128)S(1)} %all-to-all-done.2.force_ref, f32[12,4,32,128]{3,2,1,0:T(8,128)S(1)} %get-tuple-element.51.lin_ref), custom_call_target="tpu_custom_call" | custom-call | tf_op jit(solution)/shard_map/pallas_call | solution.py:406
  74.6 1.4 %collective-permute-done.9.down_ref = f32[2,12,128]{2,1,0:T(8,128)S(1)} collective-permute-done((f32[2,12,128]{2,1,0:T(8,128)S(1)}, f32[2,12,128]{2,1,0:T(8,128)S(1)}, u32[]{:S(2)}, u32[]{:S(2)}) %collective-permute-start.9) | collective-permute-done | bytes 12320 | tf_op jit(solution)/shard_map/ppermute | solution.py:417
  75.9 4.2 %collective-permute-done.12.y3_ref = f32[2,12,16,128]{3,2,1,0:T(8,128)S(1)} collective-permute-done((f32[2,12,16,128]{3,2,1,0:T(8,128)}, f32[2,12,16,128]{3,2,1,0:T(8,128)S(1)}, u32[]{:S(2)}, u32[]{:S(2)}) %collective-permute-start.12) | collective-permute-done | bytes 196640 | tf_op jit(solution)/shard_map/ppermute | solution.py:426
  80.1 2.9 %shard_map.123 = (f32[6,4,32,128]{3,2,1,0:T(8,128)}, f32[6,4,32,128]{3,2,1,0:T(8,128)}) custom-call(s32[1]{0:T(128)} %bitcast.p_ref.refs_0_, s32[1]{0:T(128)} %bitcast.1.me_ref, s32[24,128]{1,0:T(8,128)S(1)} %copy-done.8, f32[32,4,384]{2,1,0:T(4,128)S(1)} %all-to-all-done.3.chunk_ref, f32[2,12,128]{2,1,0:T(8,128)S(1)} %collective-permute-done.8.up_ref, ...), custom_call_target="tpu_custom_call" | custom-call | tf_op jit(solution)/shard_map/pallas_call | solution.py:406
  (42 shorter events, 6.1 us)
Async XLA Ops:
  6.0 15.6 %copy-start.2 = (f32[4,12,16,128]{3,2,1,0:T(8,128)S(1)}, f32[4,12,16,128]{3,2,1,0:T(8,128)}, u32[]{:S(2)}) copy-start(f32[4,12,16,128]{3,2,1,0:T(8,128)} %get-tuple-element.34.same_ref) | copy-start | bytes 1179652
  6.0 15.6 %collective-permute-start.2 = (f32[4,12,16,128]{3,2,1,0:T(8,128)}, f32[4,12,16,128]{3,2,1,0:T(8,128)S(1)}, u32[]{:S(2)}, u32[]{:S(2)}) collective-permute-start(f32[4,12,16,128]{3,2,1,0:T(8,128)} %get-tuple-element.35), channel_id=1, source_target_pairs={{0,1},{1,0},{2,3},{3,2},{4,5},{5,4},{6,7},{7,6},{8,9},{9,8},{10,11... | collective-permute-start | bytes 1179656 | tf_op jit(solution)/shard_map/ppermute | solution.py:426
  8.1 25.2 %all-to-all-start = ((f32[32,16,128]{2,1,0:T(8,128)}), f32[32,16,128]{2,1,0:T(8,128)S(1)}, u32[]{:S(2)}, u32[]{:S(2)}) async-start(f32[32,16,128]{2,1,0:T(8,128)} %get-tuple-element.30), calls=%async_computation | async-start | bytes 524288 | tf_op jit(solution)/shard_map/all_to_all | solution.py:422
  19.9 8.7 %collective-permute-start = (f32[14,32,128]{2,1,0:T(8,128)}, f32[14,32,128]{2,1,0:T(8,128)S(1)}, u32[]{:S(2)}, u32[]{:S(2)}) collective-permute-start(f32[14,32,128]{2,1,0:T(8,128)} %get-tuple-element.31), channel_id=1, source_target_pairs={{0,8},{8,16},{16,24},{24,32},{32,40},{40,48},{48,56},{56,64},{64,7... | collective-permute-start | bytes 688136 | tf_op jit(solution)/shard_map/ppermute | solution.py:417
  21.6 9.1 %collective-permute-start.1 = (f32[14,32,128]{2,1,0:T(8,128)}, f32[14,32,128]{2,1,0:T(8,128)S(1)}, u32[]{:S(2)}, u32[]{:S(2)}) collective-permute-start(f32[14,32,128]{2,1,0:T(8,128)} %get-tuple-element.32), channel_id=1, source_target_pairs={{0,248},{8,0},{16,8},{24,16},{32,24},{40,32},{48,40},{56,48},{64,5... | collective-permute-start | bytes 688136 | tf_op jit(solution)/shard_map/ppermute | solution.py:417
  21.6 4.6 %copy-start = (f32[2,3,4,32,128]{4,3,2,1,0:T(8,128)S(1)}, f32[2,3,4,32,128]{4,3,2,1,0:T(8,128)}, u32[]{:S(2)}) copy-start(f32[2,3,4,32,128]{4,3,2,1,0:T(8,128)} %param.10) | copy-start | bytes 1179652
  21.6 4.6 %copy-start.1 = (f32[2,3,4,32,128]{4,3,2,1,0:T(8,128)S(1)}, f32[2,3,4,32,128]{4,3,2,1,0:T(8,128)}, u32[]{:S(2)}) copy-start(f32[2,3,4,32,128]{4,3,2,1,0:T(8,128)} %param.11) | copy-start | bytes 1179652
  22.5 18.8 %collective-permute-start.4 = (f32[2,12,16,128]{3,2,1,0:T(8,128)}, f32[2,12,16,128]{3,2,1,0:T(8,128)S(1)}, u32[]{:S(2)}, u32[]{:S(2)}) collective-permute-start(f32[2,12,16,128]{3,2,1,0:T(8,128)} %get-tuple-element.39), channel_id=1, source_target_pairs={{0,4},{1,5},{2,6},{3,7},{4,0},{5,1},{6,2},{7,3},{8,12},{9,13},{10,... | collective-permute-start | bytes 589832 | tf_op jit(solution)/shard_map/ppermute | solution.py:426
  25.4 15.9 %collective-permute-start.5 = (f32[2,12,16,128]{3,2,1,0:T(8,128)}, f32[2,12,16,128]{3,2,1,0:T(8,128)S(1)}, u32[]{:S(2)}, u32[]{:S(2)}) collective-permute-start(f32[2,12,16,128]{3,2,1,0:T(8,128)} %get-tuple-element.40), channel_id=1, source_target_pairs={{0,6},{1,7},{2,4},{3,5},{4,2},{5,3},{6,0},{7,1},{8,14},{9,15},{10,... | collective-permute-start | bytes 589832 | tf_op jit(solution)/shard_map/ppermute | solution.py:426
  26.2 7.1 %copy-start.7 = (f32[2,16,128]{2,1,0:T(8,128)S(1)}, f32[2,16,128]{2,1,0:T(8,128)}, u32[]{:S(2)}) copy-start(f32[2,16,128]{2,1,0:T(8,128)} %get-tuple-element.33.self_ref) | copy-start | bytes 49156
  26.2 15.2 %collective-permute-start.3 = (f32[2,12,16,128]{3,2,1,0:T(8,128)}, f32[2,12,16,128]{3,2,1,0:T(8,128)}, u32[]{:S(2)}, u32[]{:S(2)}) collective-permute-start(f32[2,12,16,128]{3,2,1,0:T(8,128)} %get-tuple-element.36.after_ref), channel_id=1, source_target_pairs={{0,2},{1,3},{2,0},{3,1},{4,6},{5,7},{6,4},{7,5},{8,10},{9,11},{10,... | collective-permute-start | bytes 589832 | tf_op jit(solution)/shard_map/ppermute | solution.py:426
  37.1 9.8 %all-to-all-start.1 = ((f32[8,4,1152]{2,1,0:T(4,128)}), f32[8,4,1152]{2,1,0:T(4,128)S(1)}, u32[]{:S(2)}, u32[]{:S(2)}) async-start(f32[8,4,1152]{2,1,0:T(4,128)} %copy-done.5), calls=%async_computation.1 | async-start | bytes 294912 | tf_op jit(solution)/shard_map/all_to_all | solution.py:430
  41.4 5.6 %copy-start.6 = (f32[48,48]{1,0:T(8,128)S(1)}, f32[48,48]{1,0:T(8,128)}, u32[]{:S(2)}) copy-start(f32[48,48]{1,0:T(8,128)} %constant.11.clone.spread_ref) | copy-start | bytes 27652
  44.0 7.8 %collective-permute-start.6 = (f32[2,12,16,128]{3,2,1,0:T(8,128)}, f32[2,12,16,128]{3,2,1,0:T(8,128)S(1)}, u32[]{:S(2)}, u32[]{:S(2)}) collective-permute-start(f32[2,12,16,128]{3,2,1,0:T(8,128)} %get-tuple-element.42), channel_id=1, source_target_pairs={{0,1},{1,0},{2,3},{3,2},{4,5},{5,4},{6,7},{7,6},{8,9},{9,8},{10,11... | collective-permute-start | bytes 589832 | tf_op jit(solution)/shard_map/ppermute | solution.py:426
  45.5 8.2 %collective-permute-start.7 = (f32[2,12,16,128]{3,2,1,0:T(8,128)}, f32[2,12,16,128]{3,2,1,0:T(8,128)S(1)}, u32[]{:S(2)}, u32[]{:S(2)}) collective-permute-start(f32[2,12,16,128]{3,2,1,0:T(8,128)} %get-tuple-element.43), channel_id=1, source_target_pairs={{0,1},{1,0},{2,3},{3,2},{4,5},{5,4},{6,7},{7,6},{8,9},{9,8},{10,11... | collective-permute-start | bytes 589832 | tf_op jit(solution)/shard_map/ppermute | solution.py:426
  47.9 3.8 %copy-start.9 = (f32[16,4]{0,1:T(4,128)S(1)}, f32[16,4]{0,1:T(4,128)}, u32[]{:S(2)}) copy-start(f32[16,4]{0,1:T(4,128)} %param.14) | copy-start | bytes 772
  47.9 10.2 %all-to-all-start.2 = ((f32[8,4,1152]{2,1,0:T(4,128)}), f32[8,4,1152]{2,1,0:T(4,128)S(1)}, u32[]{:S(2)}, u32[]{:S(2)}) async-start(f32[8,4,1152]{2,1,0:T(4,128)} %shard_map.118), calls=%async_computation.2 | async-start | bytes 294912 | tf_op jit(solution)/shard_map/all_to_all | solution.py:430
  58.9 21.2 %all-to-all-start.3 = ((f32[32,4,384]{2,1,0:T(4,128)}), f32[32,4,384]{2,1,0:T(4,128)S(1)}, u32[]{:S(2)}, u32[]{:S(2)}) async-start(f32[32,4,384]{2,1,0:T(4,128)} %get-tuple-element.46), calls=%async_computation.3 | async-start | bytes 393216 | tf_op jit(solution)/shard_map/all_to_all | solution.py:422
  67.1 8.9 %collective-permute-start.11 = (f32[2,12,16,128]{3,2,1,0:T(8,128)}, f32[2,12,16,128]{3,2,1,0:T(8,128)S(1)}, u32[]{:S(2)}, u32[]{:S(2)}) collective-permute-start(f32[2,12,16,128]{3,2,1,0:T(8,128)} %get-tuple-element.52), channel_id=1, source_target_pairs={{0,4},{1,5},{2,6},{3,7},{4,0},{5,1},{6,2},{7,3},{8,12},{9,13},{10,... | collective-permute-start | bytes 589832 | tf_op jit(solution)/shard_map/ppermute | solution.py:426
  69.0 11.1 %collective-permute-start.12 = (f32[2,12,16,128]{3,2,1,0:T(8,128)}, f32[2,12,16,128]{3,2,1,0:T(8,128)S(1)}, u32[]{:S(2)}, u32[]{:S(2)}) collective-permute-start(f32[2,12,16,128]{3,2,1,0:T(8,128)} %get-tuple-element.53), channel_id=1, source_target_pairs={{0,6},{1,7},{2,4},{3,5},{4,2},{5,3},{6,0},{7,1},{8,14},{9,15},{10,... | collective-permute-start | bytes 589832 | tf_op jit(solution)/shard_map/ppermute | solution.py:426
  69.9 10.2 %collective-permute-start.10 = (f32[2,12,16,128]{3,2,1,0:T(8,128)S(1)}, f32[2,12,16,128]{3,2,1,0:T(8,128)S(1)}, u32[]{:S(2)}, u32[]{:S(2)}) collective-permute-start(f32[2,12,16,128]{3,2,1,0:T(8,128)S(1)} %get-tuple-element.44.refs_8_), channel_id=1, source_target_pairs={{0,2},{1,3},{2,0},{3,1},{4,6},{5,7},{6,4},{7,5},{8,10},{9,11},{10,... | collective-permute-start | bytes 589832 | tf_op jit(solution)/shard_map/ppermute | solution.py:426
  70.0 4.6 %collective-permute-start.8 = (f32[2,12,128]{2,1,0:T(8,128)S(1)}, f32[2,12,128]{2,1,0:T(8,128)S(1)}, u32[]{:S(2)}, u32[]{:S(2)}) collective-permute-start(f32[2,12,128]{2,1,0:T(8,128)S(1)} %get-tuple-element.47), channel_id=1, source_target_pairs={{0,8},{8,16},{16,24},{24,32},{32,40},{40,48},{48,56},{56,64},{64,7... | collective-permute-start | bytes 36872 | tf_op jit(solution)/shard_map/ppermute | solution.py:417
  72.5 3.5 %collective-permute-start.9 = (f32[2,12,128]{2,1,0:T(8,128)S(1)}, f32[2,12,128]{2,1,0:T(8,128)S(1)}, u32[]{:S(2)}, u32[]{:S(2)}) collective-permute-start(f32[2,12,128]{2,1,0:T(8,128)S(1)} %get-tuple-element.48), channel_id=1, source_target_pairs={{0,248},{8,0},{16,8},{24,16},{32,24},{40,32},{48,40},{56,48},{64,5... | collective-permute-start | bytes 36872 | tf_op jit(solution)/shard_map/ppermute | solution.py:417
  72.5 7.6 %copy-start.8 = (s32[24,128]{1,0:T(8,128)S(1)}, s32[24,128]{1,0:T(8,128)}, u32[]{:S(2)}) copy-start(s32[24,128]{1,0:T(8,128)} %get-tuple-element.29.idx_ref) | copy-start | bytes 36868
  (3 other events, 6.0 us)

commit v13 on v12

--- a/solution.py
+++ b/solution.py
@@ -35,8 +35,8 @@
 SPREAD = np.kron(FIRST, np.eye(3)).astype(np.float32)
 
 
-def far_place(offset):
-    return 8 + (offset - 3) // 3, SEG * ((offset - 3) % 3)
+def far_tile(offset):
+    return 8 + (offset - 3) // 3
 
 
 def fold(rows):
@@ -51,11 +51,6 @@
 def part_tile(ref, tile):
     at = 128 * (tile % 3)
     return jnp.concatenate([ref[tile // 3, :, 384 * k + at : 384 * k + at + 128] for k in range(3)], axis=0)
-
-
-def lane_roll(x, shift):
-    shift = shift % 128
-    return pltpu.roll(x, shift, x.ndim - 1) if shift else x
 
 
 def lanes(rows):
@@ -66,7 +61,7 @@
     lane = lanes(rows)
     tiles = []
     for k in range(9):
-        parts = [lane_roll(read(3 + 3 * k + s), SEG * s) for s in range(3)]
+        parts = [read(3 + 3 * k + s) for s in range(3)]
         tile = jnp.where(lane < SEG, parts[0], jnp.where(lane < 2 * SEG, parts[1], parts[2]))
         tiles.append(jnp.where(lane < 3 * SEG, tile, fill))
     return tiles
@@ -198,8 +193,8 @@
     for d, tile in ((2, 6), (SLABS - 2, 7)):
         chunk_ref[(p + d) & (SLABS - 1)] = rows_ref[tile]
     for d in range(3, SLABS - 2):
-        tile, seg = far_place(d)
-        chunk_ref[(p + d) & (SLABS - 1)] = lane_roll(rows_ref[tile], -seg)
+        tile = far_tile(d)
+        chunk_ref[(p + d) & (SLABS - 1)] = rows_ref[tile]
     ends = [pltpu.make_async_copy(chunk_ref, chunk_hbm, sems.at[11])]
     ends[0].start()
     gather_rows(parts_ref, idx_ref, rows_ref, 0, 3)
@@ -216,7 +211,7 @@
 
 
 def gap_kernel(p_ref, chunk_ref, up_ref, down_ref, self_ref, parts_ref, after_ref,
-               idx_ref, kind_ref, gap_hbm, here_ref, gap_ref, sems):
+               idx_ref, kind_ref, gap_ref, here_ref):
     p = p_ref[0]
 
     def asked(d):
@@ -229,19 +224,12 @@
     rows = [t[12:13] for t in tiles[:8]] + [jnp.where(beyond, -1.0, t[12:13]) for t in tiles[8:]]
     idx_ref[...] = jnp.concatenate(rows + [jnp.full((7, 128), -1.0, f32)], axis=0).astype(i32)
     kind_ref[...] = jnp.concatenate([t[13:14] for t in tiles] + [jnp.zeros((7, 128), f32)], axis=0)
-    copies = [pltpu.make_async_copy(gap_ref.at[pl.ds(2 * g, 2)], gap_hbm.at[pl.ds(2 * g, 2)], sems.at[g]) for g in range(4)]
-    gap_ref[6:8] = jnp.zeros((2, 4, 1152), f32)
-    copies[3].start()
-    for g in range(3):
-        gather_rows(parts_ref, idx_ref, here_ref, 3 * g, 3 * g + 3)
-        for tile in range(6 * g, 6 * g + 6):
-            gap = tiles[tile][0:12] - here_ref[tile] if tile < 17 else jnp.zeros((12, 128), f32)
-            at = 128 * (tile % 3)
-            for k in range(3):
-                gap_ref[tile // 3, :, 384 * k + at : 384 * k + at + 128] = gap[4 * k : 4 * k + 4]
-        copies[g].start()
-    for copy in copies:
-        copy.wait()
+    gather_rows(parts_ref, idx_ref, here_ref, 0, SIDE // 2)
+    for tile in range(24):
+        gap = tiles[tile][0:12] - here_ref[tile] if tile < 17 else jnp.zeros((12, 128), f32)
+        at = 128 * (tile % 3)
+        for k in range(3):
+            gap_ref[tile // 3, :, 384 * k + at : 384 * k + at + 128] = gap[4 * k : 4 * k + 4]
 
 
 def force_kernel(me_ref, kind_ref, spread_ref, gap_ref, after_ref, out_ref, r_ref, d_ref, f_ref, t_ref):
@@ -274,8 +262,8 @@
     for d, tile in ((2, 6), (SLABS - 2, 7)):
         chunk_ref[(p - d) & (SLABS - 1)] = fold(part_tile(force_ref, tile))
     for d in range(3, SLABS - 2):
-        tile, seg = far_place(d)
-        chunk_ref[(p - d) & (SLABS - 1)] = fold(lane_roll(part_tile(force_ref, tile), -seg))
+        tile = far_tile(d)
+        chunk_ref[(p - d) & (SLABS - 1)] = fold(part_tile(force_ref, tile))
     for k in range(2):
         self_ref[k] = part_tile(force_ref, k)
         down_ref[k] = part_tile(force_ref, 2 + k)
@@ -482,8 +470,7 @@
         [index, ((24, 128), f32), part],
         p, chunk, up, down, own, fields_parts, joined[0],
         away=(6,),
-        kept=(2,),
-        scratch=[pltpu.VMEM((SIDE, 12, 128), f32), pltpu.VMEM(part[0], f32), pltpu.SemaphoreType.DMA((4,))],
+        scratch=[pltpu.VMEM((SIDE, 12, 128), f32)],
     )
     force = call(
         force_kernel,

time: 83.5 us -> 82.5 us (0.988)
  transfers between devices with their start and end apart: 17 -> 17, of which waited for: 8 -> 8; matrix products, arithmetic and copies ran while one was open for 0% -> 0% of each run, Pallas kernels for 15% -> 14%
where the time goes in v13:
time: 82.5 us; the launch traced here: 82 us
  starting transfers between devices  42.2 us (51%)
  Pallas kernels  20.5 us (25%)
  waiting for transfers between devices  17.8 us (22%)
    pallas_call x11, Pallas kernels, call(): pl.pallas_call(kernel, out_shape=[jax.ShapeDtypeStruct(s, d) for s, d in...  20.5 us
    all_to_all x2, starting transfers between devices, exchange(): lax.all_to_all(chunk, 'mesh', split_axis=0, concat_axis=0, tiled=True)  19.9 us
    ppermute x9, starting transfers between devices, swap(): return lax.ppermute(x, 'inst', [(i, i ^ bit) for i in range(PARTS)])  10 us
    all_to_all x2, starting transfers between devices, inst_split(): return lax.all_to_all(x, 'inst', split_axis=0, concat_axis=0, tiled=True)  8.01 us
    ppermute x9, waiting for transfers between devices, swap(): return lax.ppermute(x, 'inst', [(i, i ^ bit) for i in range(PARTS)])  6.06 us
    ppermute x4, waiting for transfers between devices, shift(): lax.ppermute(x, 'mesh', [(i, (i + by) % SLABS) for i in range(SLABS)])  5.71 us
    ppermute x4, starting transfers between devices, shift(): lax.ppermute(x, 'mesh', [(i, (i + by) % SLABS) for i in range(SLABS)])  4.19 us
    all_to_all x2, waiting for transfers between devices, inst_split(): return lax.all_to_all(x, 'inst', split_axis=0, concat_axis=0, tiled=True)  3.43 us
  transfers between devices with their start and end apart: 17, of which 8 were waited for; matrix products, arithmetic and copies ran while one was open for 0% of the time, Pallas kernels for 14%

profile of v13, /device:TPU:1, one launch (start us, length us, event | category | flops | bytes accessed | tf_op | source)
XLA Modules:
  0.0 82.0 jit_solution(1077028444948066763)
XLA Ops:
  0.6 5.4 %shard_map.113 = (s32[24,128]{1,0:T(8,128)}, f32[32,16,128]{2,1,0:T(8,128)}, f32[14,32,128]{2,1,0:T(8,128)}, f32[14,32,128]{2,1,0:T(8,128)}, f32[2,16,128]{2,1,0...) custom-call(s32[1]{0:T(128)} %bitcast.p_ref.refs_0_, s32[1]{0:T(128)} %bitcast.1.me_ref, ...), custom_call_target="tpu_custom_call" | custom-call | tf_op jit(solution)/shard_map/pallas_call | solution.py:394
  6.0 2.1 %collective-permute-start.2 = (f32[4,12,16,128]{3,2,1,0:T(8,128)}, f32[4,12,16,128]{3,2,1,0:T(8,128)S(1)}, u32[]{:S(2)}, u32[]{:S(2)}) collective-permute-start(f32[4,12,16,128]{3,2,1,0:T(8,128)} %get-tuple-element.35), channel_id=1, source_target_pairs={{0,1},{1,0},{2,3},{3,2},{4,5},{5,4},{6,7},{7,6},{8,9},{9,8},{10,11... | collective-permute-start | bytes 1179656 | tf_op jit(solution)/shard_map/ppermute | solution.py:414
  8.1 11.7 %all-to-all-start = ((f32[32,16,128]{2,1,0:T(8,128)}), f32[32,16,128]{2,1,0:T(8,128)S(1)}, u32[]{:S(2)}, u32[]{:S(2)}) async-start(f32[32,16,128]{2,1,0:T(8,128)} %get-tuple-element.30), calls=%async_computation | async-start | bytes 524288 | tf_op jit(solution)/shard_map/all_to_all | solution.py:410
  19.9 1.7 %collective-permute-start = (f32[14,32,128]{2,1,0:T(8,128)}, f32[14,32,128]{2,1,0:T(8,128)S(1)}, u32[]{:S(2)}, u32[]{:S(2)}) collective-permute-start(f32[14,32,128]{2,1,0:T(8,128)} %get-tuple-element.31), channel_id=1, source_target_pairs={{0,8},{8,16},{16,24},{24,32},{32,40},{40,48},{48,56},{56,64},{64,7... | collective-permute-start | bytes 688136 | tf_op jit(solution)/shard_map/ppermute | solution.py:405
  22.5 2.9 %collective-permute-start.4 = (f32[2,12,16,128]{3,2,1,0:T(8,128)}, f32[2,12,16,128]{3,2,1,0:T(8,128)S(1)}, u32[]{:S(2)}, u32[]{:S(2)}) collective-permute-start(f32[2,12,16,128]{3,2,1,0:T(8,128)} %get-tuple-element.39), channel_id=1, source_target_pairs={{0,4},{1,5},{2,6},{3,7},{4,0},{5,1},{6,2},{7,3},{8,12},{9,13},{10,... | collective-permute-start | bytes 589832 | tf_op jit(solution)/shard_map/ppermute | solution.py:414
  26.3 2.3 %collective-permute-done.up_ref.refs_6_ = f32[14,32,128]{2,1,0:T(8,128)S(1)} collective-permute-done((f32[14,32,128]{2,1,0:T(8,128)}, f32[14,32,128]{2,1,0:T(8,128)S(1)}, u32[]{:S(2)}, u32[]{:S(2)}) %collective-permute-start) | collective-permute-done | bytes 229408 | tf_op jit(solution)/shard_map/ppermute | solution.py:405
  28.6 2.1 %collective-permute-done.1.down_ref.refs_7_ = f32[14,32,128]{2,1,0:T(8,128)S(1)} collective-permute-done((f32[14,32,128]{2,1,0:T(8,128)}, f32[14,32,128]{2,1,0:T(8,128)S(1)}, u32[]{:S(2)}, u32[]{:S(2)}) %collective-permute-start.1) | collective-permute-done | bytes 229408 | tf_op jit(solution)/shard_map/ppermute | solution.py:405
  30.7 2.6 %all-to-all-done.chunk_ref = f32[32,16,128]{2,1,0:T(8,128)S(1)} async-done(((f32[32,16,128]{2,1,0:T(8,128)}), f32[32,16,128]{2,1,0:T(8,128)S(1)}, u32[]{:S(2)}, u32[]{:S(2)}) %all-to-all-start) | async-done | bytes 262176 | tf_op jit(solution)/shard_map/all_to_all | solution.py:410
  33.3 2.4 %shard_map.116 = (s32[24,128]{1,0:T(8,128)S(1)}, f32[24,128]{1,0:T(8,128)S(1)}, f32[8,4,1152]{2,1,0:T(4,128)S(1)}) custom-call(s32[1]{0:T(128)} %bitcast.p_ref.refs_0_, f32[32,16,128]{2,1,0:T(8,128)S(1)} %all-to-all-done.chunk_ref, f32[14,32,128]{2,1,0:T(8,128)S(1)} %collective-permute-done.up_ref.refs_6_, ...), custom_call_target="tpu_custom_call" | custom-call | tf_op jit(solution)/shard_map/pallas_call | solution.py:394
  36.4 4.2 %all-to-all-start.1 = ((f32[8,4,1152]{2,1,0:T(4,128)}), f32[8,4,1152]{2,1,0:T(4,128)S(1)}, u32[]{:S(2)}, u32[]{:S(2)}) async-start(f32[8,4,1152]{2,1,0:T(4,128)} %copy-done.5), calls=%async_computation.1 | async-start | bytes 294912 | tf_op jit(solution)/shard_map/all_to_all | solution.py:418
  40.6 2.7 %shard_map.117 = (f32[4,12,16,128]{3,2,1,0:T(8,128)S(1)}, f32[2,12,16,128]{3,2,1,0:T(8,128)}, f32[2,12,16,128]{3,2,1,0:T(8,128)}) custom-call(s32[1]{0:T(128)} %bitcast.1.me_ref, f32[4,12,16,128]{3,2,1,0:T(8,128)S(1)} %copy-done.2, f32[4,12,16,128]{3,2,1,0:T(8,128)S(1)} %collective-permute-done.2.other_ref, ...), custom_call_target="tpu_custom_call" | custom-call | tf_op jit(solution)/shard_map/pallas_call | solution.py:394
  43.3 1.5 %collective-permute-start.6 = (f32[2,12,16,128]{3,2,1,0:T(8,128)}, f32[2,12,16,128]{3,2,1,0:T(8,128)S(1)}, u32[]{:S(2)}, u32[]{:S(2)}) collective-permute-start(f32[2,12,16,128]{3,2,1,0:T(8,128)} %get-tuple-element.42), channel_id=1, source_target_pairs={{0,1},{1,0},{2,3},{3,2},{4,5},{5,4},{6,7},{7,6},{8,9},{9,8},{10,11... | collective-permute-start | bytes 589832 | tf_op jit(solution)/shard_map/ppermute | solution.py:414
  44.8 1.4 %all-to-all-done.1.gap_ref = f32[8,4,1152]{2,1,0:T(4,128)S(1)} async-done(((f32[8,4,1152]{2,1,0:T(4,128)}), f32[8,4,1152]{2,1,0:T(4,128)S(1)}, u32[]{:S(2)}, u32[]{:S(2)}) %all-to-all-start.1) | async-done | bytes 147488 | tf_op jit(solution)/shard_map/all_to_all | solution.py:418
  47.2 3.8 %all-to-all-start.2 = ((f32[8,4,1152]{2,1,0:T(4,128)}), f32[8,4,1152]{2,1,0:T(4,128)S(1)}, u32[]{:S(2)}, u32[]{:S(2)}) async-start(f32[8,4,1152]{2,1,0:T(4,128)} %shard_map.118), calls=%async_computation.2 | async-start | bytes 294912 | tf_op jit(solution)/shard_map/all_to_all | solution.py:418
  51.1 1.9 %collective-permute-done.7.cross2_ref = f32[2,12,16,128]{3,2,1,0:T(8,128)S(1)} collective-permute-done((f32[2,12,16,128]{3,2,1,0:T(8,128)}, f32[2,12,16,128]{3,2,1,0:T(8,128)S(1)}, u32[]{:S(2)}, u32[]{:S(2)}) %collective-permute-start.7) | collective-permute-done | bytes 196640 | tf_op jit(solution)/shard_map/ppermute | solution.py:414
  53.8 1.6 %shard_map.120 = (f32[12,4,32,128]{3,2,1,0:T(8,128)S(1)}, f32[4,32,128]{2,1,0:T(8,128)S(1)}) custom-call(s32[1]{0:T(128)} %bitcast.p_ref.refs_0_, f32[16,4]{1,0:T(8,128)S(1)} %copy.12.refs_1_, s32[4,32,128]{2,1,0:T(8,128)S(1)} %copy-done.4, f32[6,4,32,128]{3,2,1,0:T(8,128)S(1)} %bitcast.13, f32[6,4,32,128]{3,2,1,0:T(8,128)S(1)} %bitcast.16, ...), custom_call_target="tpu_custom_call" | custom-call | tf_op jit(solution)/shard_map/pallas_call | solution.py:394
  55.4 2.0 %all-to-all-done.2.force_ref = f32[8,4,1152]{2,1,0:T(4,128)S(1)} async-done(((f32[8,4,1152]{2,1,0:T(4,128)}), f32[8,4,1152]{2,1,0:T(4,128)S(1)}, u32[]{:S(2)}, u32[]{:S(2)}) %all-to-all-start.2) | async-done | bytes 147488 | tf_op jit(solution)/shard_map/all_to_all | solution.py:418
  58.1 8.2 %all-to-all-start.3 = ((f32[32,4,384]{2,1,0:T(4,128)}), f32[32,4,384]{2,1,0:T(4,128)S(1)}, u32[]{:S(2)}, u32[]{:S(2)}) async-start(f32[32,4,384]{2,1,0:T(4,128)} %get-tuple-element.46), calls=%async_computation.3 | async-start | bytes 393216 | tf_op jit(solution)/shard_map/all_to_all | solution.py:410
  66.3 1.7 %collective-permute-start.11 = (f32[2,12,16,128]{3,2,1,0:T(8,128)}, f32[2,12,16,128]{3,2,1,0:T(8,128)S(1)}, u32[]{:S(2)}, u32[]{:S(2)}) collective-permute-start(f32[2,12,16,128]{3,2,1,0:T(8,128)} %get-tuple-element.52), channel_id=1, source_target_pairs={{0,4},{1,5},{2,6},{3,7},{4,0},{5,1},{6,2},{7,3},{8,12},{9,13},{10,... | collective-permute-start | bytes 589832 | tf_op jit(solution)/shard_map/ppermute | solution.py:414
  69.0 2.5 %collective-permute-start.8 = (f32[2,12,128]{2,1,0:T(8,128)S(1)}, f32[2,12,128]{2,1,0:T(8,128)S(1)}, u32[]{:S(2)}, u32[]{:S(2)}) collective-permute-start(f32[2,12,128]{2,1,0:T(8,128)S(1)} %get-tuple-element.47), channel_id=1, source_target_pairs={{0,8},{8,16},{16,24},{24,32},{32,40},{40,48},{48,56},{56,64},{64,7... | collective-permute-start | bytes 36872 | tf_op jit(solution)/shard_map/ppermute | solution.py:405
  71.5 2.1 %shard_map.122.part_ref = f32[12,4,32,128]{3,2,1,0:T(8,128)S(1)} custom-call(s32[24,128]{1,0:T(8,128)S(1)} %get-tuple-element.50.idx_ref, f32[8,4,1152]{2,1,0:T(4,128)S(1)} %all-to-all-done.2.force_ref, f32[12,4,32,128]{3,2,1,0:T(8,128)S(1)} %get-tuple-element.51.lin_ref), custom_call_target="tpu_custom_call" | custom-call | tf_op jit(solution)/shard_map/pallas_call | solution.py:394
  73.6 1.4 %collective-permute-done.9.down_ref = f32[2,12,128]{2,1,0:T(8,128)S(1)} collective-permute-done((f32[2,12,128]{2,1,0:T(8,128)S(1)}, f32[2,12,128]{2,1,0:T(8,128)S(1)}, u32[]{:S(2)}, u32[]{:S(2)}) %collective-permute-start.9) | collective-permute-done | bytes 12320 | tf_op jit(solution)/shard_map/ppermute | solution.py:405
  74.9 4.2 %collective-permute-done.12.y3_ref = f32[2,12,16,128]{3,2,1,0:T(8,128)S(1)} collective-permute-done((f32[2,12,16,128]{3,2,1,0:T(8,128)}, f32[2,12,16,128]{3,2,1,0:T(8,128)S(1)}, u32[]{:S(2)}, u32[]{:S(2)}) %collective-permute-start.12) | collective-permute-done | bytes 196640 | tf_op jit(solution)/shard_map/ppermute | solution.py:414
  79.1 2.9 %shard_map.123 = (f32[6,4,32,128]{3,2,1,0:T(8,128)}, f32[6,4,32,128]{3,2,1,0:T(8,128)}) custom-call(s32[1]{0:T(128)} %bitcast.p_ref.refs_0_, s32[1]{0:T(128)} %bitcast.1.me_ref, s32[24,128]{1,0:T(8,128)S(1)} %copy-done.8, f32[32,4,384]{2,1,0:T(4,128)S(1)} %all-to-all-done.3.chunk_ref, f32[2,12,128]{2,1,0:T(8,128)S(1)} %collective-permute-done.8.up_ref, ...), custom_call_target="tpu_custom_call" | custom-call | tf_op jit(solution)/shard_map/pallas_call | solution.py:394
  (42 shorter events, 6.0 us)
Async XLA Ops:
  6.0 15.6 %copy-start.2 = (f32[4,12,16,128]{3,2,1,0:T(8,128)S(1)}, f32[4,12,16,128]{3,2,1,0:T(8,128)}, u32[]{:S(2)}) copy-start(f32[4,12,16,128]{3,2,1,0:T(8,128)} %get-tuple-element.34.same_ref) | copy-start | bytes 1179652
  6.0 15.6 %collective-permute-start.2 = (f32[4,12,16,128]{3,2,1,0:T(8,128)}, f32[4,12,16,128]{3,2,1,0:T(8,128)S(1)}, u32[]{:S(2)}, u32[]{:S(2)}) collective-permute-start(f32[4,12,16,128]{3,2,1,0:T(8,128)} %get-tuple-element.35), channel_id=1, source_target_pairs={{0,1},{1,0},{2,3},{3,2},{4,5},{5,4},{6,7},{7,6},{8,9},{9,8},{10,11... | collective-permute-start | bytes 1179656 | tf_op jit(solution)/shard_map/ppermute | solution.py:414
  8.1 25.2 %all-to-all-start = ((f32[32,16,128]{2,1,0:T(8,128)}), f32[32,16,128]{2,1,0:T(8,128)S(1)}, u32[]{:S(2)}, u32[]{:S(2)}) async-start(f32[32,16,128]{2,1,0:T(8,128)} %get-tuple-element.30), calls=%async_computation | async-start | bytes 524288 | tf_op jit(solution)/shard_map/all_to_all | solution.py:410
  19.9 8.7 %collective-permute-start = (f32[14,32,128]{2,1,0:T(8,128)}, f32[14,32,128]{2,1,0:T(8,128)S(1)}, u32[]{:S(2)}, u32[]{:S(2)}) collective-permute-start(f32[14,32,128]{2,1,0:T(8,128)} %get-tuple-element.31), channel_id=1, source_target_pairs={{0,8},{8,16},{16,24},{24,32},{32,40},{40,48},{48,56},{56,64},{64,7... | collective-permute-start | bytes 688136 | tf_op jit(solution)/shard_map/ppermute | solution.py:405
  21.6 9.1 %collective-permute-start.1 = (f32[14,32,128]{2,1,0:T(8,128)}, f32[14,32,128]{2,1,0:T(8,128)S(1)}, u32[]{:S(2)}, u32[]{:S(2)}) collective-permute-start(f32[14,32,128]{2,1,0:T(8,128)} %get-tuple-element.32), channel_id=1, source_target_pairs={{0,248},{8,0},{16,8},{24,16},{32,24},{40,32},{48,40},{56,48},{64,5... | collective-permute-start | bytes 688136 | tf_op jit(solution)/shard_map/ppermute | solution.py:405
  21.6 4.6 %copy-start = (f32[2,3,4,32,128]{4,3,2,1,0:T(8,128)S(1)}, f32[2,3,4,32,128]{4,3,2,1,0:T(8,128)}, u32[]{:S(2)}) copy-start(f32[2,3,4,32,128]{4,3,2,1,0:T(8,128)} %param.10) | copy-start | bytes 1179652
  21.6 4.6 %copy-start.1 = (f32[2,3,4,32,128]{4,3,2,1,0:T(8,128)S(1)}, f32[2,3,4,32,128]{4,3,2,1,0:T(8,128)}, u32[]{:S(2)}) copy-start(f32[2,3,4,32,128]{4,3,2,1,0:T(8,128)} %param.11) | copy-start | bytes 1179652
  22.5 18.1 %collective-permute-start.4 = (f32[2,12,16,128]{3,2,1,0:T(8,128)}, f32[2,12,16,128]{3,2,1,0:T(8,128)S(1)}, u32[]{:S(2)}, u32[]{:S(2)}) collective-permute-start(f32[2,12,16,128]{3,2,1,0:T(8,128)} %get-tuple-element.39), channel_id=1, source_target_pairs={{0,4},{1,5},{2,6},{3,7},{4,0},{5,1},{6,2},{7,3},{8,12},{9,13},{10,... | collective-permute-start | bytes 589832 | tf_op jit(solution)/shard_map/ppermute | solution.py:414
  25.4 15.2 %collective-permute-start.5 = (f32[2,12,16,128]{3,2,1,0:T(8,128)}, f32[2,12,16,128]{3,2,1,0:T(8,128)S(1)}, u32[]{:S(2)}, u32[]{:S(2)}) collective-permute-start(f32[2,12,16,128]{3,2,1,0:T(8,128)} %get-tuple-element.40), channel_id=1, source_target_pairs={{0,6},{1,7},{2,4},{3,5},{4,2},{5,3},{6,0},{7,1},{8,14},{9,15},{10,... | collective-permute-start | bytes 589832 | tf_op jit(solution)/shard_map/ppermute | solution.py:414
  26.2 7.1 %copy-start.7 = (f32[2,16,128]{2,1,0:T(8,128)S(1)}, f32[2,16,128]{2,1,0:T(8,128)}, u32[]{:S(2)}) copy-start(f32[2,16,128]{2,1,0:T(8,128)} %get-tuple-element.33.self_ref) | copy-start | bytes 49156
  26.2 14.4 %collective-permute-start.3 = (f32[2,12,16,128]{3,2,1,0:T(8,128)}, f32[2,12,16,128]{3,2,1,0:T(8,128)}, u32[]{:S(2)}, u32[]{:S(2)}) collective-permute-start(f32[2,12,16,128]{3,2,1,0:T(8,128)} %get-tuple-element.36.after_ref), channel_id=1, source_target_pairs={{0,2},{1,3},{2,0},{3,1},{4,6},{5,7},{6,4},{7,5},{8,10},{9,11},{10,... | collective-permute-start | bytes 589832 | tf_op jit(solution)/shard_map/ppermute | solution.py:414
  36.4 9.8 %all-to-all-start.1 = ((f32[8,4,1152]{2,1,0:T(4,128)}), f32[8,4,1152]{2,1,0:T(4,128)S(1)}, u32[]{:S(2)}, u32[]{:S(2)}) async-start(f32[8,4,1152]{2,1,0:T(4,128)} %copy-done.5), calls=%async_computation.1 | async-start | bytes 294912 | tf_op jit(solution)/shard_map/all_to_all | solution.py:418
  40.6 5.6 %copy-start.6 = (f32[48,48]{1,0:T(8,128)S(1)}, f32[48,48]{1,0:T(8,128)}, u32[]{:S(2)}) copy-start(f32[48,48]{1,0:T(8,128)} %constant.11.clone.spread_ref) | copy-start | bytes 27652
  43.3 7.8 %collective-permute-start.6 = (f32[2,12,16,128]{3,2,1,0:T(8,128)}, f32[2,12,16,128]{3,2,1,0:T(8,128)S(1)}, u32[]{:S(2)}, u32[]{:S(2)}) collective-permute-start(f32[2,12,16,128]{3,2,1,0:T(8,128)} %get-tuple-element.42), channel_id=1, source_target_pairs={{0,1},{1,0},{2,3},{3,2},{4,5},{5,4},{6,7},{7,6},{8,9},{9,8},{10,11... | collective-permute-start | bytes 589832 | tf_op jit(solution)/shard_map/ppermute | solution.py:414
  44.8 8.2 %collective-permute-start.7 = (f32[2,12,16,128]{3,2,1,0:T(8,128)}, f32[2,12,16,128]{3,2,1,0:T(8,128)S(1)}, u32[]{:S(2)}, u32[]{:S(2)}) collective-permute-start(f32[2,12,16,128]{3,2,1,0:T(8,128)} %get-tuple-element.43), channel_id=1, source_target_pairs={{0,1},{1,0},{2,3},{3,2},{4,5},{5,4},{6,7},{7,6},{8,9},{9,8},{10,11... | collective-permute-start | bytes 589832 | tf_op jit(solution)/shard_map/ppermute | solution.py:414
  47.2 3.8 %copy-start.9 = (f32[16,4]{0,1:T(4,128)S(1)}, f32[16,4]{0,1:T(4,128)}, u32[]{:S(2)}) copy-start(f32[16,4]{0,1:T(4,128)} %param.14) | copy-start | bytes 772
  47.2 10.2 %all-to-all-start.2 = ((f32[8,4,1152]{2,1,0:T(4,128)}), f32[8,4,1152]{2,1,0:T(4,128)S(1)}, u32[]{:S(2)}, u32[]{:S(2)}) async-start(f32[8,4,1152]{2,1,0:T(4,128)} %shard_map.118), calls=%async_computation.2 | async-start | bytes 294912 | tf_op jit(solution)/shard_map/all_to_all | solution.py:418
  58.1 21.0 %all-to-all-start.3 = ((f32[32,4,384]{2,1,0:T(4,128)}), f32[32,4,384]{2,1,0:T(4,128)S(1)}, u32[]{:S(2)}, u32[]{:S(2)}) async-start(f32[32,4,384]{2,1,0:T(4,128)} %get-tuple-element.46), calls=%async_computation.3 | async-start | bytes 393216 | tf_op jit(solution)/shard_map/all_to_all | solution.py:410
  66.3 8.7 %collective-permute-start.11 = (f32[2,12,16,128]{3,2,1,0:T(8,128)}, f32[2,12,16,128]{3,2,1,0:T(8,128)S(1)}, u32[]{:S(2)}, u32[]{:S(2)}) collective-permute-start(f32[2,12,16,128]{3,2,1,0:T(8,128)} %get-tuple-element.52), channel_id=1, source_target_pairs={{0,4},{1,5},{2,6},{3,7},{4,0},{5,1},{6,2},{7,3},{8,12},{9,13},{10,... | collective-permute-start | bytes 589832 | tf_op jit(solution)/shard_map/ppermute | solution.py:414
  68.0 11.1 %collective-permute-start.12 = (f32[2,12,16,128]{3,2,1,0:T(8,128)}, f32[2,12,16,128]{3,2,1,0:T(8,128)S(1)}, u32[]{:S(2)}, u32[]{:S(2)}) collective-permute-start(f32[2,12,16,128]{3,2,1,0:T(8,128)} %get-tuple-element.53), channel_id=1, source_target_pairs={{0,6},{1,7},{2,4},{3,5},{4,2},{5,3},{6,0},{7,1},{8,14},{9,15},{10,... | collective-permute-start | bytes 589832 | tf_op jit(solution)/shard_map/ppermute | solution.py:414
  68.9 10.2 %collective-permute-start.10 = (f32[2,12,16,128]{3,2,1,0:T(8,128)S(1)}, f32[2,12,16,128]{3,2,1,0:T(8,128)S(1)}, u32[]{:S(2)}, u32[]{:S(2)}) collective-permute-start(f32[2,12,16,128]{3,2,1,0:T(8,128)S(1)} %get-tuple-element.44.refs_8_), channel_id=1, source_target_pairs={{0,2},{1,3},{2,0},{3,1},{4,6},{5,7},{6,4},{7,5},{8,10},{9,11},{10,... | collective-permute-start | bytes 589832 | tf_op jit(solution)/shard_map/ppermute | solution.py:414
  69.0 4.6 %collective-permute-start.8 = (f32[2,12,128]{2,1,0:T(8,128)S(1)}, f32[2,12,128]{2,1,0:T(8,128)S(1)}, u32[]{:S(2)}, u32[]{:S(2)}) collective-permute-start(f32[2,12,128]{2,1,0:T(8,128)S(1)} %get-tuple-element.47), channel_id=1, source_target_pairs={{0,8},{8,16},{16,24},{24,32},{32,40},{40,48},{48,56},{56,64},{64,7... | collective-permute-start | bytes 36872 | tf_op jit(solution)/shard_map/ppermute | solution.py:405
  71.5 3.5 %collective-permute-start.9 = (f32[2,12,128]{2,1,0:T(8,128)S(1)}, f32[2,12,128]{2,1,0:T(8,128)S(1)}, u32[]{:S(2)}, u32[]{:S(2)}) collective-permute-start(f32[2,12,128]{2,1,0:T(8,128)S(1)} %get-tuple-element.48), channel_id=1, source_target_pairs={{0,248},{8,0},{16,8},{24,16},{32,24},{40,32},{48,40},{56,48},{64,5... | collective-permute-start | bytes 36872 | tf_op jit(solution)/shard_map/ppermute | solution.py:405
  71.5 7.6 %copy-start.8 = (s32[24,128]{1,0:T(8,128)S(1)}, s32[24,128]{1,0:T(8,128)}, u32[]{:S(2)}) copy-start(s32[24,128]{1,0:T(8,128)} %get-tuple-element.29.idx_ref) | copy-start | bytes 36868
  (3 other events, 6.0 us)

commit v14 on v13

--- a/solution.py
+++ b/solution.py
@@ -280,11 +280,11 @@
 
 
 def final_kernel(p_ref, me_ref, idx_ref, chunk_ref, up_ref, down_ref, self_ref, part_ref, mass_ref,
-                 keep_ref, cross_ref, y1_ref, y2_ref, y3_ref, res_ref, jac_ref, val_ref, sum_ref, acc_ref):
+                 keep_ref, cross_ref, early_ref, y1_ref, y2_ref, y3_ref, res_ref, jac_ref, val_ref, sum_ref, acc_ref):
     p = p_ref[0]
     for k in range(PARTS):
-        acc = (y1_ref, y2_ref, y3_ref)[k // 2 - 1][k % 2] if k > 1 else (keep_ref, cross_ref)[k][0]
-        acc_ref[me_ref[0] ^ k] = acc
+        acc = ((keep_ref, 0), (cross_ref, 0), (y1_ref, 0), (y1_ref, 1), (early_ref, ...), (y2_ref, ...), (y3_ref, 0), (y3_ref, 1))[k]
+        acc_ref[me_ref[0] ^ k] = acc[0][acc[1]]
 
     def listed(d):
         return unfold(chunk_ref[(p + d) & (SLABS - 1)])
@@ -308,14 +308,16 @@
         out[1] = other_ref[k + 1]
 
 
-def rejoin_kernel(keep_ref, cross1_ref, cross2_ref, *out_refs):
-    for k, out in enumerate(out_refs):
-        out[0] = keep_ref[k + 1]
-        out[1] = (cross1_ref, cross2_ref)[(k + 1) // 2][(k + 1) % 2]
+def rejoin_kernel(keep_ref, cross1_ref, cross2_ref, out1_ref, out2_ref, out3_ref):
+    out1_ref[0] = keep_ref[1]
+    out1_ref[1] = cross1_ref[1]
+    out2_ref[...] = cross2_ref[0]
+    out3_ref[0] = keep_ref[3]
+    out3_ref[1] = cross2_ref[1]
 
 
 def time_kernel(me_ref, same_ref, other_ref, y1_ref, y2_ref, y3_ref, *refs):
-    keep_ref, cross1_ref, cross2_ref, in_ref, out_ref = refs
+    keep_ref, cross1_ref, cross2_ref, early_ref, in_ref, out_ref = refs
     me = me_ref[0]
     in_ref[0] = same_ref[0]
     in_ref[1] = other_ref[0]
@@ -339,6 +341,7 @@
     for k in range(PARTS):
         ref, at = (keep_ref, k // 2) if k % 2 == 0 else ((cross1_ref, cross2_ref)[k // 4], k // 2 % 2)
         ref[at] = out_ref[k]
+    early_ref[...] = out_ref[4]
 
 
 def lookup(ids, mat_ref, column, count):
@@ -348,7 +351,7 @@
     return out
 
 
-def stiff_kernel(p_ref, mat_ref, ids_ref, disp_ref, dir_ref, forcing_ref, up_ref, down_ref, after_ref, out_ref, mass_ref, *, materials):
+def stiff_kernel(p_ref, mat_ref, ids_ref, disp_ref, dir_ref, forcing_ref, up_ref, down_ref, after1, after2, out_ref, mass_ref, *, materials):
     p = p_ref[0]
     low = jnp.where(p > 0, up_ref[1:14], 0.0)
     high = jnp.where(p < SLABS - 1, down_ref[1:14], 0.0)
@@ -457,11 +460,12 @@
     chunk, up, down = exchange(chunk, up, down)
 
     pair = ((2, 12, 16, 128), f32)
+    block = ((12, 16, 128), f32)
     other = swap(other, 1)
     joined = call(join_kernel, [pair] * 3, same, other, smem=())
     turned = [swap(x, 2 * k + 2) for k, x in enumerate(joined)]
     blocks = [pltpu.VMEM((PARTS, 12, 16, 128), f32)] * 2
-    keep, *cross = call(time_kernel, [half, pair, pair], me, same, other, *turned, scratch=blocks)
+    keep, *cross, early = call(time_kernel, [half, pair, pair, block], me, same, other, *turned, scratch=blocks)
 
     part = ((PARTS, 4, 1152), f32)
     fields_parts = call(split_kernel, [(parts, bf16)], disp, dire, smem=())[0]
@@ -481,14 +485,15 @@
     )[0]
     force = inst_split(force)
     cross = [swap(x, 1) for x in cross]
-    joined = call(rejoin_kernel, [pair] * 3, keep, *cross, smem=())
+    early = swap(early, 4)
+    joined = call(rejoin_kernel, [pair, block, pair], keep, *cross, smem=())
     turned = [swap(x, 2 * k + 2) for k, x in enumerate(joined)]
     lin, mass = call(
         lambda *refs: stiff_kernel(*refs, materials=materials.shape[0]),
         [(whole, f32), ((4, 32, 128), f32)],
-        p, materials, material_ids, disp, dire, forcing.reshape(fields), up, down, joined[0],
+        p, materials, material_ids, disp, dire, forcing.reshape(fields), up, down, joined[0], early,
         smem=(0, 1),
-        away=(8,),
+        away=(8, 9),
     )
     two = ((2, 12, 128), f32)
     chunk, up2, down2, own = call(reply_kernel, [((SLABS, 4, 384), f32), two, two, two], p, force, mass, away=(2,))
@@ -499,7 +504,7 @@
     residual, jacobian = call(
         final_kernel,
         [(fields, f32)] * 2,
-        p, me, own_idx, chunk, up2, down2, own, partial, mass, keep, cross[0], *turned,
+        p, me, own_idx, chunk, up2, down2, own, partial, mass, keep, cross[0], early, *turned,
         smem=(0, 1),
         scratch=adding + blocks[:1],
     )

time: 82.5 us -> 84.2 us (1.021)
  starting transfers between devices: 42.2 us -> 48.2 us
  waiting for transfers between devices: 17.8 us -> 12.8 us
    ppermute x9 -> x10, starting transfers between devices: 10 us -> 14.2 us  [swap(): return lax.ppermute(x, 'inst', [(i, i ^ bit) for i in range(PARTS)])]
    ppermute x9 -> x10, waiting for transfers between devices: 6.06 us -> 2.52 us  [swap(): return lax.ppermute(x, 'inst', [(i, i ^ bit) for i in range(PARTS)])]
    all_to_all x2, waiting for transfers between devices: 3.43 us -> 0.79 us  [inst_split(): return lax.all_to_all(x, 'inst', split_axis=0, concat_axis=0, tiled=True)]
    all_to_all x2, starting transfers between devices: 19.9 us -> 21.1 us  [exchange(): lax.all_to_all(chunk, 'mesh', split_axis=0, concat_axis=0, tiled=True)]
    all_to_all x2, waiting for transfers between devices: 2.63 us -> 3.79 us  [exchange(): lax.all_to_all(chunk, 'mesh', split_axis=0, concat_axis=0, tiled=True)]
  transfers between devices with their start and end apart: 17 -> 18, of which waited for: 8 -> 8; matrix products, arithmetic and copies ran while one was open for 0% -> 0% of each run, Pallas kernels for 14% -> 14%
where the time goes in v14:
time: 84.2 us; the launch traced here: 83.7 us
  starting transfers between devices  48.2 us (57%)
  Pallas kernels  20.5 us (24%)
  waiting for transfers between devices  12.8 us (15%)
  local copies, waits for them, and re-layouts  1.42 us (2%)
    all_to_all x2, starting transfers between devices, exchange(): lax.all_to_all(chunk, 'mesh', split_axis=0, concat_axis=0, tiled=True)  21.1 us
    pallas_call x11, Pallas kernels, call(): pl.pallas_call(kernel, out_shape=[jax.ShapeDtypeStruct(s, d) for s, d in...  20.5 us
    ppermute x10, starting transfers between devices, swap(): return lax.ppermute(x, 'inst', [(i, i ^ bit) for i in range(PARTS)])  14.2 us
    all_to_all x2, starting transfers between devices, inst_split(): return lax.all_to_all(x, 'inst', split_axis=0, concat_axis=0, tiled=True)  8.64 us
    ppermute x4, waiting for transfers between devices, shift(): lax.ppermute(x, 'mesh', [(i, (i + by) % SLABS) for i in range(SLABS)])  5.71 us
    ppermute x4, starting transfers between devices, shift(): lax.ppermute(x, 'mesh', [(i, (i + by) % SLABS) for i in range(SLABS)])  4.19 us
    all_to_all x2, waiting for transfers between devices, exchange(): lax.all_to_all(chunk, 'mesh', split_axis=0, concat_axis=0, tiled=True)  3.79 us
    ppermute x10, waiting for transfers between devices, swap(): return lax.ppermute(x, 'inst', [(i, i ^ bit) for i in range(PARTS)])  2.52 us
  transfers between devices with their start and end apart: 18, of which 8 were waited for; matrix products, arithmetic and copies ran while one was open for 0% of the time, Pallas kernels for 14%

profile of v14, /device:TPU:1, one launch (start us, length us, event | category | flops | bytes accessed | tf_op | source)
XLA Modules:
  0.0 83.7 jit_solution(6488923129122858285)
XLA Ops:
  0.6 5.4 %shard_map.113 = (s32[24,128]{1,0:T(8,128)}, f32[32,16,128]{2,1,0:T(8,128)}, f32[14,32,128]{2,1,0:T(8,128)}, f32[14,32,128]{2,1,0:T(8,128)}, f32[2,16,128]{2,1,0...) custom-call(s32[1]{0:T(128)} %bitcast.p_ref.refs_0_, s32[1]{0:T(128)} %bitcast.1.me_ref, ...), custom_call_target="tpu_custom_call" | custom-call | tf_op jit(solution)/shard_map/pallas_call | solution.py:397
  6.0 2.1 %collective-permute-start.2 = (f32[4,12,16,128]{3,2,1,0:T(8,128)}, f32[4,12,16,128]{3,2,1,0:T(8,128)S(1)}, u32[]{:S(2)}, u32[]{:S(2)}) collective-permute-start(f32[4,12,16,128]{3,2,1,0:T(8,128)} %get-tuple-element.36), channel_id=1, source_target_pairs={{0,1},{1,0},{2,3},{3,2},{4,5},{5,4},{6,7},{7,6},{8,9},{9,8},{10,11... | collective-permute-start | bytes 1179656 | tf_op jit(solution)/shard_map/ppermute | solution.py:417
  8.1 11.7 %all-to-all-start = ((f32[32,16,128]{2,1,0:T(8,128)}), f32[32,16,128]{2,1,0:T(8,128)S(1)}, u32[]{:S(2)}, u32[]{:S(2)}) async-start(f32[32,16,128]{2,1,0:T(8,128)} %get-tuple-element.31), calls=%async_computation | async-start | bytes 524288 | tf_op jit(solution)/shard_map/all_to_all | solution.py:413
  19.9 1.7 %collective-permute-start = (f32[14,32,128]{2,1,0:T(8,128)}, f32[14,32,128]{2,1,0:T(8,128)S(1)}, u32[]{:S(2)}, u32[]{:S(2)}) collective-permute-start(f32[14,32,128]{2,1,0:T(8,128)} %get-tuple-element.32), channel_id=1, source_target_pairs={{0,8},{8,16},{16,24},{24,32},{32,40},{40,48},{48,56},{56,64},{64,7... | collective-permute-start | bytes 688136 | tf_op jit(solution)/shard_map/ppermute | solution.py:408
  22.5 2.9 %collective-permute-start.4 = (f32[2,12,16,128]{3,2,1,0:T(8,128)}, f32[2,12,16,128]{3,2,1,0:T(8,128)S(1)}, u32[]{:S(2)}, u32[]{:S(2)}) collective-permute-start(f32[2,12,16,128]{3,2,1,0:T(8,128)} %get-tuple-element.40), channel_id=1, source_target_pairs={{0,4},{1,5},{2,6},{3,7},{4,0},{5,1},{6,2},{7,3},{8,12},{9,13},{10,... | collective-permute-start | bytes 589832 | tf_op jit(solution)/shard_map/ppermute | solution.py:417
  26.3 2.3 %collective-permute-done.up_ref.refs_6_ = f32[14,32,128]{2,1,0:T(8,128)S(1)} collective-permute-done((f32[14,32,128]{2,1,0:T(8,128)}, f32[14,32,128]{2,1,0:T(8,128)S(1)}, u32[]{:S(2)}, u32[]{:S(2)}) %collective-permute-start) | collective-permute-done | bytes 229408 | tf_op jit(solution)/shard_map/ppermute | solution.py:408
  28.6 2.1 %collective-permute-done.1.down_ref.refs_7_ = f32[14,32,128]{2,1,0:T(8,128)S(1)} collective-permute-done((f32[14,32,128]{2,1,0:T(8,128)}, f32[14,32,128]{2,1,0:T(8,128)S(1)}, u32[]{:S(2)}, u32[]{:S(2)}) %collective-permute-start.1) | collective-permute-done | bytes 229408 | tf_op jit(solution)/shard_map/ppermute | solution.py:408
  30.7 2.6 %all-to-all-done.chunk_ref = f32[32,16,128]{2,1,0:T(8,128)S(1)} async-done(((f32[32,16,128]{2,1,0:T(8,128)}), f32[32,16,128]{2,1,0:T(8,128)S(1)}, u32[]{:S(2)}, u32[]{:S(2)}) %all-to-all-start) | async-done | bytes 262176 | tf_op jit(solution)/shard_map/all_to_all | solution.py:413
  33.3 2.4 %shard_map.116 = (s32[24,128]{1,0:T(8,128)S(1)}, f32[24,128]{1,0:T(8,128)S(1)}, f32[8,4,1152]{2,1,0:T(4,128)S(1)}) custom-call(s32[1]{0:T(128)} %bitcast.p_ref.refs_0_, f32[32,16,128]{2,1,0:T(8,128)S(1)} %all-to-all-done.chunk_ref, f32[14,32,128]{2,1,0:T(8,128)S(1)} %collective-permute-done.up_ref.refs_6_, ...), custom_call_target="tpu_custom_call" | custom-call | tf_op jit(solution)/shard_map/pallas_call | solution.py:397
  36.4 4.2 %all-to-all-start.1 = ((f32[8,4,1152]{2,1,0:T(4,128)}), f32[8,4,1152]{2,1,0:T(4,128)S(1)}, u32[]{:S(2)}, u32[]{:S(2)}) async-start(f32[8,4,1152]{2,1,0:T(4,128)} %copy-done.5), calls=%async_computation.1 | async-start | bytes 294912 | tf_op jit(solution)/shard_map/all_to_all | solution.py:421
  40.7 2.7 %shard_map.117 = (f32[4,12,16,128]{3,2,1,0:T(8,128)S(1)}, f32[2,12,16,128]{3,2,1,0:T(8,128)}, f32[2,12,16,128]{3,2,1,0:T(8,128)}, f32[12,16,128]{2,1,0:T(8,128)S(1)}) custom-call(s32[1]{0:T(128)} %bitcast.1.me_ref, f32[4,12,16,128]{3,2,1,0:T(8,128)S(1)} %copy-done.2, f32[4,12,16,128]{3,2,1,0:T(8,128)S(1)} %collective-permute-done.2.other_ref, ...), custom_call_target="tpu_custom_call" | custom-call | tf_op jit(solution)/shard_map/pallas_call | solution.py:397
  44.0 1.5 %collective-permute-start.6 = (f32[2,12,16,128]{3,2,1,0:T(8,128)}, f32[2,12,16,128]{3,2,1,0:T(8,128)S(1)}, u32[]{:S(2)}, u32[]{:S(2)}) collective-permute-start(f32[2,12,16,128]{3,2,1,0:T(8,128)} %get-tuple-element.43), channel_id=1, source_target_pairs={{0,1},{1,0},{2,3},{3,2},{4,5},{5,4},{6,7},{7,6},{8,9},{9,8},{10,11... | collective-permute-start | bytes 589832 | tf_op jit(solution)/shard_map/ppermute | solution.py:417
  47.2 4.4 %all-to-all-start.2 = ((f32[8,4,1152]{2,1,0:T(4,128)}), f32[8,4,1152]{2,1,0:T(4,128)S(1)}, u32[]{:S(2)}, u32[]{:S(2)}) async-start(f32[8,4,1152]{2,1,0:T(4,128)} %shard_map.118), calls=%async_computation.2 | async-start | bytes 294912 | tf_op jit(solution)/shard_map/all_to_all | solution.py:421
  51.7 3.0 %collective-permute-start.8 = (f32[12,16,128]{2,1,0:T(8,128)S(1)}, f32[12,16,128]{2,1,0:T(8,128)S(1)}, u32[]{:S(2)}, u32[]{:S(2)}) collective-permute-start(f32[12,16,128]{2,1,0:T(8,128)S(1)} %copy-done.10), channel_id=1, source_target_pairs={{0,4},{1,5},{2,6},{3,7},{4,0},{5,1},{6,2},{7,3},{8,12},{9,13},{10,... | collective-permute-start | bytes 294920 | tf_op jit(solution)/shard_map/ppermute | solution.py:417
  55.5 1.8 %collective-permute-done.8.refs_9_.early_ref = f32[12,16,128]{2,1,0:T(8,128)S(1)} collective-permute-done((f32[12,16,128]{2,1,0:T(8,128)S(1)}, f32[12,16,128]{2,1,0:T(8,128)S(1)}, u32[]{:S(2)}, u32[]{:S(2)}) %collective-permute-start.8) | collective-permute-done | bytes 98336 | tf_op jit(solution)/shard_map/ppermute | solution.py:417
  57.3 1.6 %shard_map.120 = (f32[12,4,32,128]{3,2,1,0:T(8,128)S(1)}, f32[4,32,128]{2,1,0:T(8,128)S(1)}) custom-call(s32[1]{0:T(128)} %bitcast.p_ref.refs_0_, f32[16,4]{1,0:T(8,128)S(1)} %copy.12.refs_1_, s32[4,32,128]{2,1,0:T(8,128)S(1)} %copy-done.4, f32[6,4,32,128]{3,2,1,0:T(8,128)S(1)} %bitcast.13, f32[6,4,32,128]{3,2,1,0:T(8,128)S(1)} %bitcast.16, ...), custom_call_target="tpu_custom_call" | custom-call | tf_op jit(solution)/shard_map/pallas_call | solution.py:397
  59.7 9.4 %all-to-all-start.3 = ((f32[32,4,384]{2,1,0:T(4,128)}), f32[32,4,384]{2,1,0:T(4,128)S(1)}, u32[]{:S(2)}, u32[]{:S(2)}) async-start(f32[32,4,384]{2,1,0:T(4,128)} %get-tuple-element.48), calls=%async_computation.3 | async-start | bytes 393216 | tf_op jit(solution)/shard_map/all_to_all | solution.py:413
  69.1 1.9 %collective-permute-start.13 = (f32[2,12,16,128]{3,2,1,0:T(8,128)}, f32[2,12,16,128]{3,2,1,0:T(8,128)S(1)}, u32[]{:S(2)}, u32[]{:S(2)}) collective-permute-start(f32[2,12,16,128]{3,2,1,0:T(8,128)} %get-tuple-element.55), channel_id=1, source_target_pairs={{0,6},{1,7},{2,4},{3,5},{4,2},{5,3},{6,0},{7,1},{8,14},{9,15},{10,... | collective-permute-start | bytes 589832 | tf_op jit(solution)/shard_map/ppermute | solution.py:417
  71.0 2.0 %collective-permute-start.12 = (f32[12,16,128]{2,1,0:T(8,128)}, f32[12,16,128]{2,1,0:T(8,128)S(1)}, u32[]{:S(2)}, u32[]{:S(2)}) collective-permute-start(f32[12,16,128]{2,1,0:T(8,128)} %get-tuple-element.54), channel_id=1, source_target_pairs={{0,4},{1,5},{2,6},{3,7},{4,0},{5,1},{6,2},{7,3},{8,12},{9,13},{10,... | collective-permute-start | bytes 294920 | tf_op jit(solution)/shard_map/ppermute | solution.py:417
  73.0 2.5 %collective-permute-start.9 = (f32[2,12,128]{2,1,0:T(8,128)S(1)}, f32[2,12,128]{2,1,0:T(8,128)S(1)}, u32[]{:S(2)}, u32[]{:S(2)}) collective-permute-start(f32[2,12,128]{2,1,0:T(8,128)S(1)} %get-tuple-element.49), channel_id=1, source_target_pairs={{0,8},{8,16},{16,24},{24,32},{32,40},{40,48},{48,56},{56,64},{64,7... | collective-permute-start | bytes 36872 | tf_op jit(solution)/shard_map/ppermute | solution.py:408
  75.5 2.1 %shard_map.122.part_ref = f32[12,4,32,128]{3,2,1,0:T(8,128)S(1)} custom-call(s32[24,128]{1,0:T(8,128)S(1)} %get-tuple-element.52.idx_ref, f32[8,4,1152]{2,1,0:T(4,128)S(1)} %all-to-all-done.2.force_ref, f32[12,4,32,128]{3,2,1,0:T(8,128)S(1)} %get-tuple-element.53.lin_ref), custom_call_target="tpu_custom_call" | custom-call | tf_op jit(solution)/shard_map/pallas_call | solution.py:397
  77.6 1.4 %collective-permute-done.10.down_ref = f32[2,12,128]{2,1,0:T(8,128)S(1)} collective-permute-done((f32[2,12,128]{2,1,0:T(8,128)S(1)}, f32[2,12,128]{2,1,0:T(8,128)S(1)}, u32[]{:S(2)}, u32[]{:S(2)}) %collective-permute-start.10) | collective-permute-done | bytes 12320 | tf_op jit(solution)/shard_map/ppermute | solution.py:408
  79.6 1.2 %all-to-all-done.3.chunk_ref = f32[32,4,384]{2,1,0:T(4,128)S(1)} async-done(((f32[32,4,384]{2,1,0:T(4,128)}), f32[32,4,384]{2,1,0:T(4,128)S(1)}, u32[]{:S(2)}, u32[]{:S(2)}) %all-to-all-start.3) | async-done | bytes 196640 | tf_op jit(solution)/shard_map/all_to_all | solution.py:413
  80.8 2.9 %shard_map.123 = (f32[6,4,32,128]{3,2,1,0:T(8,128)}, f32[6,4,32,128]{3,2,1,0:T(8,128)}) custom-call(s32[1]{0:T(128)} %bitcast.p_ref.refs_0_, s32[1]{0:T(128)} %bitcast.1.me_ref, s32[24,128]{1,0:T(8,128)S(1)} %copy-done.8, f32[32,4,384]{2,1,0:T(4,128)S(1)} %all-to-all-done.3.chunk_ref, f32[2,12,128]{2,1,0:T(8,128)S(1)} %collective-permute-done.9.up_ref, ...), custom_call_target="tpu_custom_call" | custom-call | tf_op jit(solution)/shard_map/pallas_call | solution.py:397
  (48 shorter events, 7.1 us)
Async XLA Ops:
  6.0 15.6 %copy-start.2 = (f32[4,12,16,128]{3,2,1,0:T(8,128)S(1)}, f32[4,12,16,128]{3,2,1,0:T(8,128)}, u32[]{:S(2)}) copy-start(f32[4,12,16,128]{3,2,1,0:T(8,128)} %get-tuple-element.35.same_ref) | copy-start | bytes 1179652
  6.0 15.6 %collective-permute-start.2 = (f32[4,12,16,128]{3,2,1,0:T(8,128)}, f32[4,12,16,128]{3,2,1,0:T(8,128)S(1)}, u32[]{:S(2)}, u32[]{:S(2)}) collective-permute-start(f32[4,12,16,128]{3,2,1,0:T(8,128)} %get-tuple-element.36), channel_id=1, source_target_pairs={{0,1},{1,0},{2,3},{3,2},{4,5},{5,4},{6,7},{7,6},{8,9},{9,8},{10,11... | collective-permute-start | bytes 1179656 | tf_op jit(solution)/shard_map/ppermute | solution.py:417
  8.1 25.2 %all-to-all-start = ((f32[32,16,128]{2,1,0:T(8,128)}), f32[32,16,128]{2,1,0:T(8,128)S(1)}, u32[]{:S(2)}, u32[]{:S(2)}) async-start(f32[32,16,128]{2,1,0:T(8,128)} %get-tuple-element.31), calls=%async_computation | async-start | bytes 524288 | tf_op jit(solution)/shard_map/all_to_all | solution.py:413
  19.9 8.7 %collective-permute-start = (f32[14,32,128]{2,1,0:T(8,128)}, f32[14,32,128]{2,1,0:T(8,128)S(1)}, u32[]{:S(2)}, u32[]{:S(2)}) collective-permute-start(f32[14,32,128]{2,1,0:T(8,128)} %get-tuple-element.32), channel_id=1, source_target_pairs={{0,8},{8,16},{16,24},{24,32},{32,40},{40,48},{48,56},{56,64},{64,7... | collective-permute-start | bytes 688136 | tf_op jit(solution)/shard_map/ppermute | solution.py:408
  21.6 9.1 %collective-permute-start.1 = (f32[14,32,128]{2,1,0:T(8,128)}, f32[14,32,128]{2,1,0:T(8,128)S(1)}, u32[]{:S(2)}, u32[]{:S(2)}) collective-permute-start(f32[14,32,128]{2,1,0:T(8,128)} %get-tuple-element.33), channel_id=1, source_target_pairs={{0,248},{8,0},{16,8},{24,16},{32,24},{40,32},{48,40},{56,48},{64,5... | collective-permute-start | bytes 688136 | tf_op jit(solution)/shard_map/ppermute | solution.py:408
  21.6 4.6 %copy-start = (f32[2,3,4,32,128]{4,3,2,1,0:T(8,128)S(1)}, f32[2,3,4,32,128]{4,3,2,1,0:T(8,128)}, u32[]{:S(2)}) copy-start(f32[2,3,4,32,128]{4,3,2,1,0:T(8,128)} %param.10) | copy-start | bytes 1179652
  22.5 18.1 %collective-permute-start.4 = (f32[2,12,16,128]{3,2,1,0:T(8,128)}, f32[2,12,16,128]{3,2,1,0:T(8,128)S(1)}, u32[]{:S(2)}, u32[]{:S(2)}) collective-permute-start(f32[2,12,16,128]{3,2,1,0:T(8,128)} %get-tuple-element.40), channel_id=1, source_target_pairs={{0,4},{1,5},{2,6},{3,7},{4,0},{5,1},{6,2},{7,3},{8,12},{9,13},{10,... | collective-permute-start | bytes 589832 | tf_op jit(solution)/shard_map/ppermute | solution.py:417
  25.4 15.2 %collective-permute-start.5 = (f32[2,12,16,128]{3,2,1,0:T(8,128)}, f32[2,12,16,128]{3,2,1,0:T(8,128)S(1)}, u32[]{:S(2)}, u32[]{:S(2)}) collective-permute-start(f32[2,12,16,128]{3,2,1,0:T(8,128)} %get-tuple-element.41), channel_id=1, source_target_pairs={{0,6},{1,7},{2,4},{3,5},{4,2},{5,3},{6,0},{7,1},{8,14},{9,15},{10,... | collective-permute-start | bytes 589832 | tf_op jit(solution)/shard_map/ppermute | solution.py:417
  26.2 7.1 %copy-start.7 = (f32[2,16,128]{2,1,0:T(8,128)S(1)}, f32[2,16,128]{2,1,0:T(8,128)}, u32[]{:S(2)}) copy-start(f32[2,16,128]{2,1,0:T(8,128)} %get-tuple-element.34.self_ref) | copy-start | bytes 49156
  26.2 14.4 %collective-permute-start.3 = (f32[2,12,16,128]{3,2,1,0:T(8,128)}, f32[2,12,16,128]{3,2,1,0:T(8,128)}, u32[]{:S(2)}, u32[]{:S(2)}) collective-permute-start(f32[2,12,16,128]{3,2,1,0:T(8,128)} %get-tuple-element.37.after_ref), channel_id=1, source_target_pairs={{0,2},{1,3},{2,0},{3,1},{4,6},{5,7},{6,4},{7,5},{8,10},{9,11},{10,... | collective-permute-start | bytes 589832 | tf_op jit(solution)/shard_map/ppermute | solution.py:417
  36.4 9.8 %all-to-all-start.1 = ((f32[8,4,1152]{2,1,0:T(4,128)}), f32[8,4,1152]{2,1,0:T(4,128)S(1)}, u32[]{:S(2)}, u32[]{:S(2)}) async-start(f32[8,4,1152]{2,1,0:T(4,128)} %copy-done.5), calls=%async_computation.1 | async-start | bytes 294912 | tf_op jit(solution)/shard_map/all_to_all | solution.py:421
  40.6 5.6 %copy-start.6 = (f32[48,48]{1,0:T(8,128)S(1)}, f32[48,48]{1,0:T(8,128)}, u32[]{:S(2)}) copy-start(f32[48,48]{1,0:T(8,128)} %constant.11.clone.spread_ref) | copy-start | bytes 27652
  44.0 10.8 %collective-permute-start.6 = (f32[2,12,16,128]{3,2,1,0:T(8,128)}, f32[2,12,16,128]{3,2,1,0:T(8,128)S(1)}, u32[]{:S(2)}, u32[]{:S(2)}) collective-permute-start(f32[2,12,16,128]{3,2,1,0:T(8,128)} %get-tuple-element.43), channel_id=1, source_target_pairs={{0,1},{1,0},{2,3},{3,2},{4,5},{5,4},{6,7},{7,6},{8,9},{9,8},{10,11... | collective-permute-start | bytes 589832 | tf_op jit(solution)/shard_map/ppermute | solution.py:417
  45.4 9.3 %collective-permute-start.7 = (f32[2,12,16,128]{3,2,1,0:T(8,128)}, f32[2,12,16,128]{3,2,1,0:T(8,128)S(1)}, u32[]{:S(2)}, u32[]{:S(2)}) collective-permute-start(f32[2,12,16,128]{3,2,1,0:T(8,128)} %get-tuple-element.44), channel_id=1, source_target_pairs={{0,1},{1,0},{2,3},{3,2},{4,5},{5,4},{6,7},{7,6},{8,9},{9,8},{10,11... | collective-permute-start | bytes 589832 | tf_op jit(solution)/shard_map/ppermute | solution.py:417
  47.2 7.4 %copy-start.11 = (f32[16,4]{0,1:T(4,128)S(1)}, f32[16,4]{0,1:T(4,128)}, u32[]{:S(2)}) copy-start(f32[16,4]{0,1:T(4,128)} %param.14) | copy-start | bytes 772
  47.2 11.7 %all-to-all-start.2 = ((f32[8,4,1152]{2,1,0:T(4,128)}), f32[8,4,1152]{2,1,0:T(4,128)S(1)}, u32[]{:S(2)}, u32[]{:S(2)}) async-start(f32[8,4,1152]{2,1,0:T(4,128)} %shard_map.118), calls=%async_computation.2 | async-start | bytes 294912 | tf_op jit(solution)/shard_map/all_to_all | solution.py:421
  51.7 5.6 %collective-permute-start.8 = (f32[12,16,128]{2,1,0:T(8,128)S(1)}, f32[12,16,128]{2,1,0:T(8,128)S(1)}, u32[]{:S(2)}, u32[]{:S(2)}) collective-permute-start(f32[12,16,128]{2,1,0:T(8,128)S(1)} %copy-done.10), channel_id=1, source_target_pairs={{0,4},{1,5},{2,6},{3,7},{4,0},{5,1},{6,2},{7,3},{8,12},{9,13},{10,... | collective-permute-start | bytes 294920 | tf_op jit(solution)/shard_map/ppermute | solution.py:417
  59.7 21.1 %all-to-all-start.3 = ((f32[32,4,384]{2,1,0:T(4,128)}), f32[32,4,384]{2,1,0:T(4,128)S(1)}, u32[]{:S(2)}, u32[]{:S(2)}) async-start(f32[32,4,384]{2,1,0:T(4,128)} %get-tuple-element.48), calls=%async_computation.3 | async-start | bytes 393216 | tf_op jit(solution)/shard_map/all_to_all | solution.py:413
  69.1 10.5 %collective-permute-start.13 = (f32[2,12,16,128]{3,2,1,0:T(8,128)}, f32[2,12,16,128]{3,2,1,0:T(8,128)S(1)}, u32[]{:S(2)}, u32[]{:S(2)}) collective-permute-start(f32[2,12,16,128]{3,2,1,0:T(8,128)} %get-tuple-element.55), channel_id=1, source_target_pairs={{0,6},{1,7},{2,4},{3,5},{4,2},{5,3},{6,0},{7,1},{8,14},{9,15},{10,... | collective-permute-start | bytes 589832 | tf_op jit(solution)/shard_map/ppermute | solution.py:417
  71.0 8.6 %collective-permute-start.11 = (f32[2,12,16,128]{3,2,1,0:T(8,128)S(1)}, f32[2,12,16,128]{3,2,1,0:T(8,128)S(1)}, u32[]{:S(2)}, u32[]{:S(2)}) collective-permute-start(f32[2,12,16,128]{3,2,1,0:T(8,128)S(1)} %get-tuple-element.45.refs_8_), channel_id=1, source_target_pairs={{0,2},{1,3},{2,0},{3,1},{4,6},{5,7},{6,4},{7,5},{8,10},{9,11},{10,... | collective-permute-start | bytes 589832 | tf_op jit(solution)/shard_map/ppermute | solution.py:417
  71.0 8.6 %collective-permute-start.12 = (f32[12,16,128]{2,1,0:T(8,128)}, f32[12,16,128]{2,1,0:T(8,128)S(1)}, u32[]{:S(2)}, u32[]{:S(2)}) collective-permute-start(f32[12,16,128]{2,1,0:T(8,128)} %get-tuple-element.54), channel_id=1, source_target_pairs={{0,4},{1,5},{2,6},{3,7},{4,0},{5,1},{6,2},{7,3},{8,12},{9,13},{10,... | collective-permute-start | bytes 294920 | tf_op jit(solution)/shard_map/ppermute | solution.py:417
  73.0 4.6 %collective-permute-start.9 = (f32[2,12,128]{2,1,0:T(8,128)S(1)}, f32[2,12,128]{2,1,0:T(8,128)S(1)}, u32[]{:S(2)}, u32[]{:S(2)}) collective-permute-start(f32[2,12,128]{2,1,0:T(8,128)S(1)} %get-tuple-element.49), channel_id=1, source_target_pairs={{0,8},{8,16},{16,24},{24,32},{32,40},{40,48},{48,56},{56,64},{64,7... | collective-permute-start | bytes 36872 | tf_op jit(solution)/shard_map/ppermute | solution.py:408
  75.5 3.5 %collective-permute-start.10 = (f32[2,12,128]{2,1,0:T(8,128)S(1)}, f32[2,12,128]{2,1,0:T(8,128)S(1)}, u32[]{:S(2)}, u32[]{:S(2)}) collective-permute-start(f32[2,12,128]{2,1,0:T(8,128)S(1)} %get-tuple-element.50), channel_id=1, source_target_pairs={{0,248},{8,0},{16,8},{24,16},{32,24},{40,32},{48,40},{56,48},{64,5... | collective-permute-start | bytes 36872 | tf_op jit(solution)/shard_map/ppermute | solution.py:408
  75.5 5.3 %copy-start.8 = (s32[24,128]{1,0:T(8,128)S(1)}, s32[24,128]{1,0:T(8,128)}, u32[]{:S(2)}) copy-start(s32[24,128]{1,0:T(8,128)} %get-tuple-element.30.idx_ref) | copy-start | bytes 36868
  (6 other events, 15.5 us)

commit v15 on v13

--- a/solution.py
+++ b/solution.py
@@ -279,12 +279,8 @@
         out_ref[:, x] = lin_ref[:, x] + sum_ref[:, 128 * x : 128 * (x + 1)].reshape(12, 32, 128)
 
 
-def final_kernel(p_ref, me_ref, idx_ref, chunk_ref, up_ref, down_ref, self_ref, part_ref, mass_ref,
-                 keep_ref, cross_ref, y1_ref, y2_ref, y3_ref, res_ref, jac_ref, val_ref, sum_ref, acc_ref):
+def listed_kernel(p_ref, idx_ref, chunk_ref, up_ref, down_ref, self_ref, part_ref, out_ref, val_ref, sum_ref):
     p = p_ref[0]
-    for k in range(PARTS):
-        acc = (y1_ref, y2_ref, y3_ref)[k // 2 - 1][k % 2] if k > 1 else (keep_ref, cross_ref)[k][0]
-        acc_ref[me_ref[0] ^ k] = acc
 
     def listed(d):
         return unfold(chunk_ref[(p + d) & (SLABS - 1)])
@@ -295,11 +291,18 @@
         val_ref[k] = tile
     scatter_rows(val_ref, idx_ref, sum_ref)
     for x in range(4):
-        acc = jnp.concatenate([acc_ref[2 * x], acc_ref[2 * x + 1]], axis=1)
-        added = sum_ref[:, 128 * x : 128 * (x + 1)].reshape(12, 32, 128)
-        out = part_ref[:, x] + mass_ref[x][None] * acc + added
-        res_ref[:, x] = out[0:6]
-        jac_ref[:, x] = out[6:12]
+        out_ref[:, x] = part_ref[:, x] + sum_ref[:, 128 * x : 128 * (x + 1)].reshape(12, 32, 128)
+
+
+def final_kernel(me_ref, part_ref, mass_ref, keep_ref, cross_ref, y1_ref, y2_ref, y3_ref, res_ref, jac_ref):
+    for k in range(PARTS):
+        acc = (y1_ref, y2_ref, y3_ref)[k // 2 - 1][k % 2] if k > 1 else (keep_ref, cross_ref)[k][0]
+        block = me_ref[0] ^ k
+        x = block >> 1
+        rows = pl.ds(pl.multiple_of(16 * (block & 1), 16), 16)
+        out = part_ref[:, x, rows, :] + mass_ref[x, rows, :][None] * acc
+        res_ref[:, x, rows, :] = out[0:6]
+        jac_ref[:, x, rows, :] = out[6:12]
 
 
 def join_kernel(same_ref, other_ref, *out_refs):
@@ -496,13 +499,10 @@
 
     adding = [pltpu.VMEM((SIDE, 12, 128), f32), pltpu.VMEM((384, 512), f32)]
     partial = call(partner_kernel, [(whole, f32)], far_idx, force, lin, smem=(), scratch=adding)[0]
-    residual, jacobian = call(
-        final_kernel,
-        [(fields, f32)] * 2,
-        p, me, own_idx, chunk, up2, down2, own, partial, mass, keep, cross[0], *turned,
-        smem=(0, 1),
-        scratch=adding + blocks[:1],
-    )
+    partial = call(
+        listed_kernel, [(whole, f32)], p, own_idx, chunk, up2, down2, own, partial, scratch=adding
+    )[0]
+    residual, jacobian = call(final_kernel, [(fields, f32)] * 2, me, partial, mass, keep, cross[0], *turned)
     return residual.reshape(shape), jacobian.reshape(shape)
 
 

time: 82.5 us -> 81.6 us (0.989)
    ppermute x9, waiting for transfers between devices: 6.06 us -> 2.44 us  [swap(): return lax.ppermute(x, 'inst', [(i, i ^ bit) for i in range(PARTS)])]
    all_to_all x2, waiting for transfers between devices: 2.63 us -> 5.67 us  [exchange(): lax.all_to_all(chunk, 'mesh', split_axis=0, concat_axis=0, tiled=True)]
    pallas_call x11 -> x12, Pallas kernels: 20.5 us -> 20.7 us  [call(): pl.pallas_call(kernel, out_shape=[jax.ShapeDtypeStruct(s, d) for s, d in...]
  transfers between devices with their start and end apart: 17 -> 17, of which waited for: 8 -> 8; matrix products, arithmetic and copies ran while one was open for 0% -> 0% of each run, Pallas kernels for 14% -> 17%
where the time goes in v15:
time: 81.6 us; the launch traced here: 81.1 us
  starting transfers between devices  42.4 us (52%)
  Pallas kernels  20.7 us (25%)
  waiting for transfers between devices  17.1 us (21%)
  between operations  0.83 us (1%)
    pallas_call x12, Pallas kernels, call(): pl.pallas_call(kernel, out_shape=[jax.ShapeDtypeStruct(s, d) for s, d in...  20.7 us
    all_to_all x2, starting transfers between devices, exchange(): lax.all_to_all(chunk, 'mesh', split_axis=0, concat_axis=0, tiled=True)  20.3 us
    ppermute x9, starting transfers between devices, swap(): return lax.ppermute(x, 'inst', [(i, i ^ bit) for i in range(PARTS)])  10.2 us
    all_to_all x2, starting transfers between devices, inst_split(): return lax.all_to_all(x, 'inst', split_axis=0, concat_axis=0, tiled=True)  7.7 us
    ppermute x4, waiting for transfers between devices, shift(): lax.ppermute(x, 'mesh', [(i, (i + by) % SLABS) for i in range(SLABS)])  5.71 us
    all_to_all x2, waiting for transfers between devices, exchange(): lax.all_to_all(chunk, 'mesh', split_axis=0, concat_axis=0, tiled=True)  5.67 us
    ppermute x4, starting transfers between devices, shift(): lax.ppermute(x, 'mesh', [(i, (i + by) % SLABS) for i in range(SLABS)])  4.19 us
    all_to_all x2, waiting for transfers between devices, inst_split(): return lax.all_to_all(x, 'inst', split_axis=0, concat_axis=0, tiled=True)  3.27 us
  transfers between devices with their start and end apart: 17, of which 8 were waited for; matrix products, arithmetic and copies ran while one was open for 0% of the time, Pallas kernels for 17%

profile of v15, /device:TPU:1, one launch (start us, length us, event | category | flops | bytes accessed | tf_op | source)
XLA Modules:
  0.0 81.1 jit_solution(2566338593360631292)
XLA Ops:
  0.6 5.4 %shard_map.113 = (s32[24,128]{1,0:T(8,128)}, f32[32,16,128]{2,1,0:T(8,128)}, f32[14,32,128]{2,1,0:T(8,128)}, f32[14,32,128]{2,1,0:T(8,128)}, f32[2,16,128]{2,1,0...) custom-call(s32[1]{0:T(128)} %bitcast.1.p_ref.refs_0_, s32[1]{0:T(128)} %bitcast.me_ref, ...), custom_call_target="tpu_custom_call" | custom-call | tf_op jit(solution)/shard_map/pallas_call | solution.py:397
  6.0 2.1 %collective-permute-start.2 = (f32[4,12,16,128]{3,2,1,0:T(8,128)}, f32[4,12,16,128]{3,2,1,0:T(8,128)S(1)}, u32[]{:S(2)}, u32[]{:S(2)}) collective-permute-start(f32[4,12,16,128]{3,2,1,0:T(8,128)} %get-tuple-element.35), channel_id=1, source_target_pairs={{0,1},{1,0},{2,3},{3,2},{4,5},{5,4},{6,7},{7,6},{8,9},{9,8},{10,11... | collective-permute-start | bytes 1179656 | tf_op jit(solution)/shard_map/ppermute | solution.py:417
  8.2 11.7 %all-to-all-start = ((f32[32,16,128]{2,1,0:T(8,128)}), f32[32,16,128]{2,1,0:T(8,128)S(1)}, u32[]{:S(2)}, u32[]{:S(2)}) async-start(f32[32,16,128]{2,1,0:T(8,128)} %get-tuple-element.30), calls=%async_computation | async-start | bytes 524288 | tf_op jit(solution)/shard_map/all_to_all | solution.py:413
  19.9 1.7 %collective-permute-start = (f32[14,32,128]{2,1,0:T(8,128)}, f32[14,32,128]{2,1,0:T(8,128)S(1)}, u32[]{:S(2)}, u32[]{:S(2)}) collective-permute-start(f32[14,32,128]{2,1,0:T(8,128)} %get-tuple-element.31), channel_id=1, source_target_pairs={{0,8},{8,16},{16,24},{24,32},{32,40},{40,48},{48,56},{56,64},{64,7... | collective-permute-start | bytes 688136 | tf_op jit(solution)/shard_map/ppermute | solution.py:408
  22.5 2.9 %collective-permute-start.4 = (f32[2,12,16,128]{3,2,1,0:T(8,128)}, f32[2,12,16,128]{3,2,1,0:T(8,128)S(1)}, u32[]{:S(2)}, u32[]{:S(2)}) collective-permute-start(f32[2,12,16,128]{3,2,1,0:T(8,128)} %get-tuple-element.39), channel_id=1, source_target_pairs={{0,4},{1,5},{2,6},{3,7},{4,0},{5,1},{6,2},{7,3},{8,12},{9,13},{10,... | collective-permute-start | bytes 589832 | tf_op jit(solution)/shard_map/ppermute | solution.py:417
  26.4 2.3 %collective-permute-done.up_ref.refs_6_ = f32[14,32,128]{2,1,0:T(8,128)S(1)} collective-permute-done((f32[14,32,128]{2,1,0:T(8,128)}, f32[14,32,128]{2,1,0:T(8,128)S(1)}, u32[]{:S(2)}, u32[]{:S(2)}) %collective-permute-start) | collective-permute-done | bytes 229408 | tf_op jit(solution)/shard_map/ppermute | solution.py:408
  28.6 2.1 %collective-permute-done.1.down_ref.refs_7_ = f32[14,32,128]{2,1,0:T(8,128)S(1)} collective-permute-done((f32[14,32,128]{2,1,0:T(8,128)}, f32[14,32,128]{2,1,0:T(8,128)S(1)}, u32[]{:S(2)}, u32[]{:S(2)}) %collective-permute-start.1) | collective-permute-done | bytes 229408 | tf_op jit(solution)/shard_map/ppermute | solution.py:408
  30.7 2.6 %all-to-all-done.chunk_ref = f32[32,16,128]{2,1,0:T(8,128)S(1)} async-done(((f32[32,16,128]{2,1,0:T(8,128)}), f32[32,16,128]{2,1,0:T(8,128)S(1)}, u32[]{:S(2)}, u32[]{:S(2)}) %all-to-all-start) | async-done | bytes 262176 | tf_op jit(solution)/shard_map/all_to_all | solution.py:413
  33.4 3.1 %shard_map.116 = (s32[24,128]{1,0:T(8,128)S(1)}, f32[24,128]{1,0:T(8,128)S(1)}, f32[8,4,1152]{2,1,0:T(4,128)}) custom-call(s32[1]{0:T(128)} %bitcast.1.p_ref.refs_0_, f32[32,16,128]{2,1,0:T(8,128)S(1)} %all-to-all-done.chunk_ref, f32[14,32,128]{2,1,0:T(8,128)S(1)} %collective-permute-done.up_ref.refs_6_, ...), custom_call_target="tpu_custom_call" | custom-call | tf_op jit(solution)/shard_map/pallas_call | solution.py:397
  36.4 4.2 %all-to-all-start.1 = ((f32[8,4,1152]{2,1,0:T(4,128)}), f32[8,4,1152]{2,1,0:T(4,128)S(1)}, u32[]{:S(2)}, u32[]{:S(2)}) async-start(f32[8,4,1152]{2,1,0:T(4,128)} %get-tuple-element.38), calls=%async_computation.1 | async-start | bytes 294912 | tf_op jit(solution)/shard_map/all_to_all | solution.py:421
  40.7 2.0 %shard_map.117 = (f32[4,12,16,128]{3,2,1,0:T(8,128)S(1)}, f32[2,12,16,128]{3,2,1,0:T(8,128)S(1)}, f32[2,12,16,128]{3,2,1,0:T(8,128)S(1)}) custom-call(s32[1]{0:T(128)} %bitcast.me_ref, f32[4,12,16,128]{3,2,1,0:T(8,128)S(1)} %copy-done.2, f32[4,12,16,128]{3,2,1,0:T(8,128)S(1)} %collective-permute-done.2.other_ref, ...), custom_call_target="tpu_custom_call" | custom-call | tf_op jit(solution)/shard_map/pallas_call | solution.py:397
  42.7 1.5 %collective-permute-start.6 = (f32[2,12,16,128]{3,2,1,0:T(8,128)S(1)}, f32[2,12,16,128]{3,2,1,0:T(8,128)S(1)}, u32[]{:S(2)}, u32[]{:S(2)}) collective-permute-start(f32[2,12,16,128]{3,2,1,0:T(8,128)S(1)} %get-tuple-element.42), channel_id=1, source_target_pairs={{0,1},{1,0},{2,3},{3,2},{4,5},{5,4},{6,7},{7,6},{8,9},{9,8},{10,11... | collective-permute-start | bytes 589832 | tf_op jit(solution)/shard_map/ppermute | solution.py:417
  44.4 1.9 %all-to-all-done.1.gap_ref = f32[8,4,1152]{2,1,0:T(4,128)S(1)} async-done(((f32[8,4,1152]{2,1,0:T(4,128)}), f32[8,4,1152]{2,1,0:T(4,128)S(1)}, u32[]{:S(2)}, u32[]{:S(2)}) %all-to-all-start.1) | async-done | bytes 147488 | tf_op jit(solution)/shard_map/all_to_all | solution.py:421
  47.2 3.5 %all-to-all-start.2 = ((f32[8,4,1152]{2,1,0:T(4,128)}), f32[8,4,1152]{2,1,0:T(4,128)S(1)}, u32[]{:S(2)}, u32[]{:S(2)}) async-start(f32[8,4,1152]{2,1,0:T(4,128)} %shard_map.118), calls=%async_computation.2 | async-start | bytes 294912 | tf_op jit(solution)/shard_map/all_to_all | solution.py:421
  50.8 2.4 %collective-permute-done.7.cross2_ref = f32[2,12,16,128]{3,2,1,0:T(8,128)S(1)} collective-permute-done((f32[2,12,16,128]{3,2,1,0:T(8,128)S(1)}, f32[2,12,16,128]{3,2,1,0:T(8,128)S(1)}, u32[]{:S(2)}, u32[]{:S(2)}) %collective-permute-start.7) | collective-permute-done | bytes 196640 | tf_op jit(solution)/shard_map/ppermute | solution.py:417
  54.0 1.6 %shard_map.120 = (f32[12,4,32,128]{3,2,1,0:T(8,128)S(1)}, f32[4,32,128]{2,1,0:T(8,128)S(1)}) custom-call(s32[1]{0:T(128)} %bitcast.1.p_ref.refs_0_, f32[16,4]{1,0:T(8,128)S(1)} %copy.12.refs_1_, s32[4,32,128]{2,1,0:T(8,128)S(1)} %copy-done.4, f32[6,4,32,128]{3,2,1,0:T(8,128)S(1)} %bitcast.13, f32[6,4,32,128]{3,2,1,0:T(8,128)S(1)} %bitcast.16, ...), custom_call_target="tpu_custom_call" | custom-call | tf_op jit(solution)/shard_map/pallas_call | solution.py:397
  55.6 1.4 %all-to-all-done.2.force_ref = f32[8,4,1152]{2,1,0:T(4,128)S(1)} async-done(((f32[8,4,1152]{2,1,0:T(4,128)}), f32[8,4,1152]{2,1,0:T(4,128)S(1)}, u32[]{:S(2)}, u32[]{:S(2)}) %all-to-all-start.2) | async-done | bytes 147488 | tf_op jit(solution)/shard_map/all_to_all | solution.py:421
  57.7 8.6 %all-to-all-start.3 = ((f32[32,4,384]{2,1,0:T(4,128)}), f32[32,4,384]{2,1,0:T(4,128)S(1)}, u32[]{:S(2)}, u32[]{:S(2)}) async-start(f32[32,4,384]{2,1,0:T(4,128)} %get-tuple-element.46), calls=%async_computation.3 | async-start | bytes 393216 | tf_op jit(solution)/shard_map/all_to_all | solution.py:413
  67.3 1.6 %collective-permute-start.12 = (f32[2,12,16,128]{3,2,1,0:T(8,128)}, f32[2,12,16,128]{3,2,1,0:T(8,128)S(1)}, u32[]{:S(2)}, u32[]{:S(2)}) collective-permute-start(f32[2,12,16,128]{3,2,1,0:T(8,128)} %get-tuple-element.53), channel_id=1, source_target_pairs={{0,6},{1,7},{2,4},{3,5},{4,2},{5,3},{6,0},{7,1},{8,14},{9,15},{10,... | collective-permute-start | bytes 589832 | tf_op jit(solution)/shard_map/ppermute | solution.py:417
  69.0 2.5 %collective-permute-start.8 = (f32[2,12,128]{2,1,0:T(8,128)S(1)}, f32[2,12,128]{2,1,0:T(8,128)S(1)}, u32[]{:S(2)}, u32[]{:S(2)}) collective-permute-start(f32[2,12,128]{2,1,0:T(8,128)S(1)} %get-tuple-element.47), channel_id=1, source_target_pairs={{0,8},{8,16},{16,24},{24,32},{32,40},{40,48},{48,56},{56,64},{64,7... | collective-permute-start | bytes 36872 | tf_op jit(solution)/shard_map/ppermute | solution.py:408
  71.5 2.1 %shard_map.122.part_ref = f32[12,4,32,128]{3,2,1,0:T(8,128)S(1)} custom-call(s32[24,128]{1,0:T(8,128)S(1)} %get-tuple-element.50.idx_ref, f32[8,4,1152]{2,1,0:T(4,128)S(1)} %all-to-all-done.2.force_ref, f32[12,4,32,128]{3,2,1,0:T(8,128)S(1)} %get-tuple-element.51.lin_ref), custom_call_target="tpu_custom_call" | custom-call | tf_op jit(solution)/shard_map/pallas_call | solution.py:397
  73.6 1.4 %collective-permute-done.9.down_ref = f32[2,12,128]{2,1,0:T(8,128)S(1)} collective-permute-done((f32[2,12,128]{2,1,0:T(8,128)S(1)}, f32[2,12,128]{2,1,0:T(8,128)S(1)}, u32[]{:S(2)}, u32[]{:S(2)}) %collective-permute-start.9) | collective-permute-done | bytes 12320 | tf_op jit(solution)/shard_map/ppermute | solution.py:408
  75.0 3.0 %all-to-all-done.3.chunk_ref = f32[32,4,384]{2,1,0:T(4,128)S(1)} async-done(((f32[32,4,384]{2,1,0:T(4,128)}), f32[32,4,384]{2,1,0:T(4,128)S(1)}, u32[]{:S(2)}, u32[]{:S(2)}) %all-to-all-start.3) | async-done | bytes 196640 | tf_op jit(solution)/shard_map/all_to_all | solution.py:413
  78.0 2.1 %shard_map.123.part_ref = f32[12,4,32,128]{3,2,1,0:T(8,128)S(1)} custom-call(s32[1]{0:T(128)} %bitcast.1.p_ref.refs_0_, s32[24,128]{1,0:T(8,128)S(1)} %copy-done.7, f32[32,4,384]{2,1,0:T(4,128)S(1)} %all-to-all-done.3.chunk_ref, f32[2,12,128]{2,1,0:T(8,128)S(1)} %collective-permute-done.8.up_ref, f32[2,12,128]{2,1,0:T(8,128)S(1)} %collective-permute-done.9.down_ref, ...), custom_call_target="tpu_custom_call" | custom-call | tf_op jit(solution)/shard_map/pallas_call | solution.py:397
  (41 shorter events, 6.6 us)
Async XLA Ops:
  6.0 15.6 %copy-start.2 = (f32[4,12,16,128]{3,2,1,0:T(8,128)S(1)}, f32[4,12,16,128]{3,2,1,0:T(8,128)}, u32[]{:S(2)}) copy-start(f32[4,12,16,128]{3,2,1,0:T(8,128)} %get-tuple-element.34.same_ref) | copy-start | bytes 1179652
  6.0 15.6 %collective-permute-start.2 = (f32[4,12,16,128]{3,2,1,0:T(8,128)}, f32[4,12,16,128]{3,2,1,0:T(8,128)S(1)}, u32[]{:S(2)}, u32[]{:S(2)}) collective-permute-start(f32[4,12,16,128]{3,2,1,0:T(8,128)} %get-tuple-element.35), channel_id=1, source_target_pairs={{0,1},{1,0},{2,3},{3,2},{4,5},{5,4},{6,7},{7,6},{8,9},{9,8},{10,11... | collective-permute-start | bytes 1179656 | tf_op jit(solution)/shard_map/ppermute | solution.py:417
  8.2 25.2 %all-to-all-start = ((f32[32,16,128]{2,1,0:T(8,128)}), f32[32,16,128]{2,1,0:T(8,128)S(1)}, u32[]{:S(2)}, u32[]{:S(2)}) async-start(f32[32,16,128]{2,1,0:T(8,128)} %get-tuple-element.30), calls=%async_computation | async-start | bytes 524288 | tf_op jit(solution)/shard_map/all_to_all | solution.py:413
  19.9 8.7 %collective-permute-start = (f32[14,32,128]{2,1,0:T(8,128)}, f32[14,32,128]{2,1,0:T(8,128)S(1)}, u32[]{:S(2)}, u32[]{:S(2)}) collective-permute-start(f32[14,32,128]{2,1,0:T(8,128)} %get-tuple-element.31), channel_id=1, source_target_pairs={{0,8},{8,16},{16,24},{24,32},{32,40},{40,48},{48,56},{56,64},{64,7... | collective-permute-start | bytes 688136 | tf_op jit(solution)/shard_map/ppermute | solution.py:408
  21.6 9.1 %collective-permute-start.1 = (f32[14,32,128]{2,1,0:T(8,128)}, f32[14,32,128]{2,1,0:T(8,128)S(1)}, u32[]{:S(2)}, u32[]{:S(2)}) collective-permute-start(f32[14,32,128]{2,1,0:T(8,128)} %get-tuple-element.32), channel_id=1, source_target_pairs={{0,248},{8,0},{16,8},{24,16},{32,24},{40,32},{48,40},{56,48},{64,5... | collective-permute-start | bytes 688136 | tf_op jit(solution)/shard_map/ppermute | solution.py:408
  21.6 4.6 %copy-start = (f32[2,3,4,32,128]{4,3,2,1,0:T(8,128)S(1)}, f32[2,3,4,32,128]{4,3,2,1,0:T(8,128)}, u32[]{:S(2)}) copy-start(f32[2,3,4,32,128]{4,3,2,1,0:T(8,128)} %param.10) | copy-start | bytes 1179652
  21.6 4.6 %copy-start.1 = (f32[2,3,4,32,128]{4,3,2,1,0:T(8,128)S(1)}, f32[2,3,4,32,128]{4,3,2,1,0:T(8,128)}, u32[]{:S(2)}) copy-start(f32[2,3,4,32,128]{4,3,2,1,0:T(8,128)} %param.11) | copy-start | bytes 1179652
  22.5 18.1 %collective-permute-start.4 = (f32[2,12,16,128]{3,2,1,0:T(8,128)}, f32[2,12,16,128]{3,2,1,0:T(8,128)S(1)}, u32[]{:S(2)}, u32[]{:S(2)}) collective-permute-start(f32[2,12,16,128]{3,2,1,0:T(8,128)} %get-tuple-element.39), channel_id=1, source_target_pairs={{0,4},{1,5},{2,6},{3,7},{4,0},{5,1},{6,2},{7,3},{8,12},{9,13},{10,... | collective-permute-start | bytes 589832 | tf_op jit(solution)/shard_map/ppermute | solution.py:417
  25.4 15.2 %collective-permute-start.5 = (f32[2,12,16,128]{3,2,1,0:T(8,128)}, f32[2,12,16,128]{3,2,1,0:T(8,128)}, u32[]{:S(2)}, u32[]{:S(2)}) collective-permute-start(f32[2,12,16,128]{3,2,1,0:T(8,128)} %get-tuple-element.40), channel_id=1, source_target_pairs={{0,6},{1,7},{2,4},{3,5},{4,2},{5,3},{6,0},{7,1},{8,14},{9,15},{10,... | collective-permute-start | bytes 589832 | tf_op jit(solution)/shard_map/ppermute | solution.py:417
  26.2 7.1 %copy-start.6 = (f32[2,16,128]{2,1,0:T(8,128)S(1)}, f32[2,16,128]{2,1,0:T(8,128)}, u32[]{:S(2)}) copy-start(f32[2,16,128]{2,1,0:T(8,128)} %get-tuple-element.33.self_ref) | copy-start | bytes 49156
  26.2 14.4 %collective-permute-start.3 = (f32[2,12,16,128]{3,2,1,0:T(8,128)}, f32[2,12,16,128]{3,2,1,0:T(8,128)}, u32[]{:S(2)}, u32[]{:S(2)}) collective-permute-start(f32[2,12,16,128]{3,2,1,0:T(8,128)} %get-tuple-element.36.after_ref), channel_id=1, source_target_pairs={{0,2},{1,3},{2,0},{3,1},{4,6},{5,7},{6,4},{7,5},{8,10},{9,11},{10,... | collective-permute-start | bytes 589832 | tf_op jit(solution)/shard_map/ppermute | solution.py:417
  36.4 9.8 %all-to-all-start.1 = ((f32[8,4,1152]{2,1,0:T(4,128)}), f32[8,4,1152]{2,1,0:T(4,128)S(1)}, u32[]{:S(2)}, u32[]{:S(2)}) async-start(f32[8,4,1152]{2,1,0:T(4,128)} %get-tuple-element.38), calls=%async_computation.1 | async-start | bytes 294912 | tf_op jit(solution)/shard_map/all_to_all | solution.py:421
  40.7 5.6 %copy-start.5 = (f32[48,48]{1,0:T(8,128)S(1)}, f32[48,48]{1,0:T(8,128)}, u32[]{:S(2)}) copy-start(f32[48,48]{1,0:T(8,128)} %constant.11.clone.spread_ref) | copy-start | bytes 27652
  42.7 8.1 %collective-permute-start.6 = (f32[2,12,16,128]{3,2,1,0:T(8,128)S(1)}, f32[2,12,16,128]{3,2,1,0:T(8,128)S(1)}, u32[]{:S(2)}, u32[]{:S(2)}) collective-permute-start(f32[2,12,16,128]{3,2,1,0:T(8,128)S(1)} %get-tuple-element.42), channel_id=1, source_target_pairs={{0,1},{1,0},{2,3},{3,2},{4,5},{5,4},{6,7},{7,6},{8,9},{9,8},{10,11... | collective-permute-start | bytes 589832 | tf_op jit(solution)/shard_map/ppermute | solution.py:417
  44.3 9.0 %collective-permute-start.7 = (f32[2,12,16,128]{3,2,1,0:T(8,128)S(1)}, f32[2,12,16,128]{3,2,1,0:T(8,128)S(1)}, u32[]{:S(2)}, u32[]{:S(2)}) collective-permute-start(f32[2,12,16,128]{3,2,1,0:T(8,128)S(1)} %get-tuple-element.43), channel_id=1, source_target_pairs={{0,1},{1,0},{2,3},{3,2},{4,5},{5,4},{6,7},{7,6},{8,9},{9,8},{10,11... | collective-permute-start | bytes 589832 | tf_op jit(solution)/shard_map/ppermute | solution.py:417
  47.2 3.5 %copy-start.8 = (f32[16,4]{0,1:T(4,128)S(1)}, f32[16,4]{0,1:T(4,128)}, u32[]{:S(2)}) copy-start(f32[16,4]{0,1:T(4,128)} %param.14) | copy-start | bytes 772
  47.2 9.8 %all-to-all-start.2 = ((f32[8,4,1152]{2,1,0:T(4,128)}), f32[8,4,1152]{2,1,0:T(4,128)S(1)}, u32[]{:S(2)}, u32[]{:S(2)}) async-start(f32[8,4,1152]{2,1,0:T(4,128)} %shard_map.118), calls=%async_computation.2 | async-start | bytes 294912 | tf_op jit(solution)/shard_map/all_to_all | solution.py:421
  57.7 20.3 %all-to-all-start.3 = ((f32[32,4,384]{2,1,0:T(4,128)}), f32[32,4,384]{2,1,0:T(4,128)S(1)}, u32[]{:S(2)}, u32[]{:S(2)}) async-start(f32[32,4,384]{2,1,0:T(4,128)} %get-tuple-element.46), calls=%async_computation.3 | async-start | bytes 393216 | tf_op jit(solution)/shard_map/all_to_all | solution.py:413
  66.3 13.8 %collective-permute-start.11 = (f32[2,12,16,128]{3,2,1,0:T(8,128)}, f32[2,12,16,128]{3,2,1,0:T(8,128)S(1)}, u32[]{:S(2)}, u32[]{:S(2)}) collective-permute-start(f32[2,12,16,128]{3,2,1,0:T(8,128)} %get-tuple-element.52), channel_id=1, source_target_pairs={{0,4},{1,5},{2,6},{3,7},{4,0},{5,1},{6,2},{7,3},{8,12},{9,13},{10,... | collective-permute-start | bytes 589832 | tf_op jit(solution)/shard_map/ppermute | solution.py:417
  67.3 12.8 %collective-permute-start.12 = (f32[2,12,16,128]{3,2,1,0:T(8,128)}, f32[2,12,16,128]{3,2,1,0:T(8,128)S(1)}, u32[]{:S(2)}, u32[]{:S(2)}) collective-permute-start(f32[2,12,16,128]{3,2,1,0:T(8,128)} %get-tuple-element.53), channel_id=1, source_target_pairs={{0,6},{1,7},{2,4},{3,5},{4,2},{5,3},{6,0},{7,1},{8,14},{9,15},{10,... | collective-permute-start | bytes 589832 | tf_op jit(solution)/shard_map/ppermute | solution.py:417
  68.9 11.2 %collective-permute-start.10 = (f32[2,12,16,128]{3,2,1,0:T(8,128)S(1)}, f32[2,12,16,128]{3,2,1,0:T(8,128)S(1)}, u32[]{:S(2)}, u32[]{:S(2)}) collective-permute-start(f32[2,12,16,128]{3,2,1,0:T(8,128)S(1)} %get-tuple-element.44.refs_8_), channel_id=1, source_target_pairs={{0,2},{1,3},{2,0},{3,1},{4,6},{5,7},{6,4},{7,5},{8,10},{9,11},{10,... | collective-permute-start | bytes 589832 | tf_op jit(solution)/shard_map/ppermute | solution.py:417
  69.0 4.6 %collective-permute-start.8 = (f32[2,12,128]{2,1,0:T(8,128)S(1)}, f32[2,12,128]{2,1,0:T(8,128)S(1)}, u32[]{:S(2)}, u32[]{:S(2)}) collective-permute-start(f32[2,12,128]{2,1,0:T(8,128)S(1)} %get-tuple-element.47), channel_id=1, source_target_pairs={{0,8},{8,16},{16,24},{24,32},{32,40},{40,48},{48,56},{56,64},{64,7... | collective-permute-start | bytes 36872 | tf_op jit(solution)/shard_map/ppermute | solution.py:408
  71.5 3.5 %collective-permute-start.9 = (f32[2,12,128]{2,1,0:T(8,128)S(1)}, f32[2,12,128]{2,1,0:T(8,128)S(1)}, u32[]{:S(2)}, u32[]{:S(2)}) collective-permute-start(f32[2,12,128]{2,1,0:T(8,128)S(1)} %get-tuple-element.48), channel_id=1, source_target_pairs={{0,248},{8,0},{16,8},{24,16},{32,24},{40,32},{48,40},{56,48},{64,5... | collective-permute-start | bytes 36872 | tf_op jit(solution)/shard_map/ppermute | solution.py:408
  71.5 6.5 %copy-start.7 = (s32[24,128]{1,0:T(8,128)S(1)}, s32[24,128]{1,0:T(8,128)}, u32[]{:S(2)}) copy-start(s32[24,128]{1,0:T(8,128)} %get-tuple-element.29.idx_ref) | copy-start | bytes 36868
  (2 other events, 6.4 us)

commit v16 on v15

--- a/solution.py
+++ b/solution.py
@@ -130,7 +130,7 @@
         here_ref[2 * k + 1, 0:12, :] = got[:, 128:]
         return carry
 
-    lax.fori_loop(first, last, step, 0, unroll=3)
+    lax.fori_loop(first, last, step, 0, unroll=True)
 
 
 def scatter_rows(val_ref, idx_ref, sum_ref):

time: 81.6 us -> 80.9 us (level)
  no operation moved by 1% of the time
where the time goes in v16:
time: 80.9 us; the launch traced here: 80.4 us
  starting transfers between devices  42.4 us (52%)
  Pallas kernels  20 us (25%)
  waiting for transfers between devices  17.1 us (21%)
  between operations  0.83 us (1%)
    all_to_all x2, starting transfers between devices, exchange(): lax.all_to_all(chunk, 'mesh', split_axis=0, concat_axis=0, tiled=True)  20.3 us
    pallas_call x12, Pallas kernels, call(): pl.pallas_call(kernel, out_shape=[jax.ShapeDtypeStruct(s, d) for s, d in...  20 us
    ppermute x9, starting transfers between devices, swap(): return lax.ppermute(x, 'inst', [(i, i ^ bit) for i in range(PARTS)])  10.2 us
    all_to_all x2, starting transfers between devices, inst_split(): return lax.all_to_all(x, 'inst', split_axis=0, concat_axis=0, tiled=True)  7.7 us
    ppermute x4, waiting for transfers between devices, shift(): lax.ppermute(x, 'mesh', [(i, (i + by) % SLABS) for i in range(SLABS)])  5.71 us
    all_to_all x2, waiting for transfers between devices, exchange(): lax.all_to_all(chunk, 'mesh', split_axis=0, concat_axis=0, tiled=True)  5.67 us
    ppermute x4, starting transfers between devices, shift(): lax.ppermute(x, 'mesh', [(i, (i + by) % SLABS) for i in range(SLABS)])  4.19 us
    all_to_all x2, waiting for transfers between devices, inst_split(): return lax.all_to_all(x, 'inst', split_axis=0, concat_axis=0, tiled=True)  3.29 us
  transfers between devices with their start and end apart: 17, of which 8 were waited for; matrix products, arithmetic and copies ran while one was open for 0% of the time, Pallas kernels for 17%

profile of v16, /device:TPU:1, one launch (start us, length us, event | category | flops | bytes accessed | tf_op | source)
XLA Modules:
  0.0 80.4 jit_solution(1016496356841600026)
XLA Ops:
  0.6 5.1 %shard_map.113 = (s32[24,128]{1,0:T(8,128)}, f32[32,16,128]{2,1,0:T(8,128)}, f32[14,32,128]{2,1,0:T(8,128)}, f32[14,32,128]{2,1,0:T(8,128)}, f32[2,16,128]{2,1,0...) custom-call(s32[1]{0:T(128)} %bitcast.1.p_ref.refs_0_, s32[1]{0:T(128)} %bitcast.me_ref, ...), custom_call_target="tpu_custom_call" | custom-call | tf_op jit(solution)/shard_map/pallas_call | solution.py:397
  5.7 2.1 %collective-permute-start.2 = (f32[4,12,16,128]{3,2,1,0:T(8,128)}, f32[4,12,16,128]{3,2,1,0:T(8,128)S(1)}, u32[]{:S(2)}, u32[]{:S(2)}) collective-permute-start(f32[4,12,16,128]{3,2,1,0:T(8,128)} %get-tuple-element.35), channel_id=1, source_target_pairs={{0,1},{1,0},{2,3},{3,2},{4,5},{5,4},{6,7},{7,6},{8,9},{9,8},{10,11... | collective-permute-start | bytes 1179656 | tf_op jit(solution)/shard_map/ppermute | solution.py:417
  7.9 11.7 %all-to-all-start = ((f32[32,16,128]{2,1,0:T(8,128)}), f32[32,16,128]{2,1,0:T(8,128)S(1)}, u32[]{:S(2)}, u32[]{:S(2)}) async-start(f32[32,16,128]{2,1,0:T(8,128)} %get-tuple-element.30), calls=%async_computation | async-start | bytes 524288 | tf_op jit(solution)/shard_map/all_to_all | solution.py:413
  19.6 1.7 %collective-permute-start = (f32[14,32,128]{2,1,0:T(8,128)}, f32[14,32,128]{2,1,0:T(8,128)S(1)}, u32[]{:S(2)}, u32[]{:S(2)}) collective-permute-start(f32[14,32,128]{2,1,0:T(8,128)} %get-tuple-element.31), channel_id=1, source_target_pairs={{0,8},{8,16},{16,24},{24,32},{32,40},{40,48},{48,56},{56,64},{64,7... | collective-permute-start | bytes 688136 | tf_op jit(solution)/shard_map/ppermute | solution.py:408
  22.2 2.9 %collective-permute-start.4 = (f32[2,12,16,128]{3,2,1,0:T(8,128)}, f32[2,12,16,128]{3,2,1,0:T(8,128)S(1)}, u32[]{:S(2)}, u32[]{:S(2)}) collective-permute-start(f32[2,12,16,128]{3,2,1,0:T(8,128)} %get-tuple-element.39), channel_id=1, source_target_pairs={{0,4},{1,5},{2,6},{3,7},{4,0},{5,1},{6,2},{7,3},{8,12},{9,13},{10,... | collective-permute-start | bytes 589832 | tf_op jit(solution)/shard_map/ppermute | solution.py:417
  26.1 2.3 %collective-permute-done.up_ref.refs_6_ = f32[14,32,128]{2,1,0:T(8,128)S(1)} collective-permute-done((f32[14,32,128]{2,1,0:T(8,128)}, f32[14,32,128]{2,1,0:T(8,128)S(1)}, u32[]{:S(2)}, u32[]{:S(2)}) %collective-permute-start) | collective-permute-done | bytes 229408 | tf_op jit(solution)/shard_map/ppermute | solution.py:408
  28.3 2.1 %collective-permute-done.1.down_ref.refs_7_ = f32[14,32,128]{2,1,0:T(8,128)S(1)} collective-permute-done((f32[14,32,128]{2,1,0:T(8,128)}, f32[14,32,128]{2,1,0:T(8,128)S(1)}, u32[]{:S(2)}, u32[]{:S(2)}) %collective-permute-start.1) | collective-permute-done | bytes 229408 | tf_op jit(solution)/shard_map/ppermute | solution.py:408
  30.4 2.6 %all-to-all-done.chunk_ref = f32[32,16,128]{2,1,0:T(8,128)S(1)} async-done(((f32[32,16,128]{2,1,0:T(8,128)}), f32[32,16,128]{2,1,0:T(8,128)S(1)}, u32[]{:S(2)}, u32[]{:S(2)}) %all-to-all-start) | async-done | bytes 262176 | tf_op jit(solution)/shard_map/all_to_all | solution.py:413
  33.0 2.7 %shard_map.116 = (s32[24,128]{1,0:T(8,128)S(1)}, f32[24,128]{1,0:T(8,128)S(1)}, f32[8,4,1152]{2,1,0:T(4,128)}) custom-call(s32[1]{0:T(128)} %bitcast.1.p_ref.refs_0_, f32[32,16,128]{2,1,0:T(8,128)S(1)} %all-to-all-done.chunk_ref, f32[14,32,128]{2,1,0:T(8,128)S(1)} %collective-permute-done.up_ref.refs_6_, ...), custom_call_target="tpu_custom_call" | custom-call | tf_op jit(solution)/shard_map/pallas_call | solution.py:397
  35.8 4.2 %all-to-all-start.1 = ((f32[8,4,1152]{2,1,0:T(4,128)}), f32[8,4,1152]{2,1,0:T(4,128)S(1)}, u32[]{:S(2)}, u32[]{:S(2)}) async-start(f32[8,4,1152]{2,1,0:T(4,128)} %get-tuple-element.38), calls=%async_computation.1 | async-start | bytes 294912 | tf_op jit(solution)/shard_map/all_to_all | solution.py:421
  40.0 2.0 %shard_map.117 = (f32[4,12,16,128]{3,2,1,0:T(8,128)S(1)}, f32[2,12,16,128]{3,2,1,0:T(8,128)S(1)}, f32[2,12,16,128]{3,2,1,0:T(8,128)S(1)}) custom-call(s32[1]{0:T(128)} %bitcast.me_ref, f32[4,12,16,128]{3,2,1,0:T(8,128)S(1)} %copy-done.2, f32[4,12,16,128]{3,2,1,0:T(8,128)S(1)} %collective-permute-done.2.other_ref, ...), custom_call_target="tpu_custom_call" | custom-call | tf_op jit(solution)/shard_map/pallas_call | solution.py:397
  42.1 1.5 %collective-permute-start.6 = (f32[2,12,16,128]{3,2,1,0:T(8,128)S(1)}, f32[2,12,16,128]{3,2,1,0:T(8,128)S(1)}, u32[]{:S(2)}, u32[]{:S(2)}) collective-permute-start(f32[2,12,16,128]{3,2,1,0:T(8,128)S(1)} %get-tuple-element.42), channel_id=1, source_target_pairs={{0,1},{1,0},{2,3},{3,2},{4,5},{5,4},{6,7},{7,6},{8,9},{9,8},{10,11... | collective-permute-start | bytes 589832 | tf_op jit(solution)/shard_map/ppermute | solution.py:417
  43.7 1.9 %all-to-all-done.1.gap_ref = f32[8,4,1152]{2,1,0:T(4,128)S(1)} async-done(((f32[8,4,1152]{2,1,0:T(4,128)}), f32[8,4,1152]{2,1,0:T(4,128)S(1)}, u32[]{:S(2)}, u32[]{:S(2)}) %all-to-all-start.1) | async-done | bytes 147488 | tf_op jit(solution)/shard_map/all_to_all | solution.py:421
  46.6 3.5 %all-to-all-start.2 = ((f32[8,4,1152]{2,1,0:T(4,128)}), f32[8,4,1152]{2,1,0:T(4,128)S(1)}, u32[]{:S(2)}, u32[]{:S(2)}) async-start(f32[8,4,1152]{2,1,0:T(4,128)} %shard_map.118), calls=%async_computation.2 | async-start | bytes 294912 | tf_op jit(solution)/shard_map/all_to_all | solution.py:421
  50.2 2.4 %collective-permute-done.7.cross2_ref = f32[2,12,16,128]{3,2,1,0:T(8,128)S(1)} collective-permute-done((f32[2,12,16,128]{3,2,1,0:T(8,128)S(1)}, f32[2,12,16,128]{3,2,1,0:T(8,128)S(1)}, u32[]{:S(2)}, u32[]{:S(2)}) %collective-permute-start.7) | collective-permute-done | bytes 196640 | tf_op jit(solution)/shard_map/ppermute | solution.py:417
  53.4 1.6 %shard_map.120 = (f32[12,4,32,128]{3,2,1,0:T(8,128)S(1)}, f32[4,32,128]{2,1,0:T(8,128)S(1)}) custom-call(s32[1]{0:T(128)} %bitcast.1.p_ref.refs_0_, f32[16,4]{1,0:T(8,128)S(1)} %copy.12.refs_1_, s32[4,32,128]{2,1,0:T(8,128)S(1)} %copy-done.4, f32[6,4,32,128]{3,2,1,0:T(8,128)S(1)} %bitcast.13, f32[6,4,32,128]{3,2,1,0:T(8,128)S(1)} %bitcast.16, ...), custom_call_target="tpu_custom_call" | custom-call | tf_op jit(solution)/shard_map/pallas_call | solution.py:397
  55.0 1.4 %all-to-all-done.2.force_ref = f32[8,4,1152]{2,1,0:T(4,128)S(1)} async-done(((f32[8,4,1152]{2,1,0:T(4,128)}), f32[8,4,1152]{2,1,0:T(4,128)S(1)}, u32[]{:S(2)}, u32[]{:S(2)}) %all-to-all-start.2) | async-done | bytes 147488 | tf_op jit(solution)/shard_map/all_to_all | solution.py:421
  57.1 8.5 %all-to-all-start.3 = ((f32[32,4,384]{2,1,0:T(4,128)}), f32[32,4,384]{2,1,0:T(4,128)S(1)}, u32[]{:S(2)}, u32[]{:S(2)}) async-start(f32[32,4,384]{2,1,0:T(4,128)} %get-tuple-element.46), calls=%async_computation.3 | async-start | bytes 393216 | tf_op jit(solution)/shard_map/all_to_all | solution.py:413
  66.6 1.6 %collective-permute-start.12 = (f32[2,12,16,128]{3,2,1,0:T(8,128)}, f32[2,12,16,128]{3,2,1,0:T(8,128)S(1)}, u32[]{:S(2)}, u32[]{:S(2)}) collective-permute-start(f32[2,12,16,128]{3,2,1,0:T(8,128)} %get-tuple-element.53), channel_id=1, source_target_pairs={{0,6},{1,7},{2,4},{3,5},{4,2},{5,3},{6,0},{7,1},{8,14},{9,15},{10,... | collective-permute-start | bytes 589832 | tf_op jit(solution)/shard_map/ppermute | solution.py:417
  68.4 2.5 %collective-permute-start.8 = (f32[2,12,128]{2,1,0:T(8,128)S(1)}, f32[2,12,128]{2,1,0:T(8,128)S(1)}, u32[]{:S(2)}, u32[]{:S(2)}) collective-permute-start(f32[2,12,128]{2,1,0:T(8,128)S(1)} %get-tuple-element.47), channel_id=1, source_target_pairs={{0,8},{8,16},{16,24},{24,32},{32,40},{40,48},{48,56},{56,64},{64,7... | collective-permute-start | bytes 36872 | tf_op jit(solution)/shard_map/ppermute | solution.py:408
  70.8 2.1 %shard_map.122.part_ref = f32[12,4,32,128]{3,2,1,0:T(8,128)S(1)} custom-call(s32[24,128]{1,0:T(8,128)S(1)} %get-tuple-element.50.idx_ref, f32[8,4,1152]{2,1,0:T(4,128)S(1)} %all-to-all-done.2.force_ref, f32[12,4,32,128]{3,2,1,0:T(8,128)S(1)} %get-tuple-element.51.lin_ref), custom_call_target="tpu_custom_call" | custom-call | tf_op jit(solution)/shard_map/pallas_call | solution.py:397
  72.9 1.4 %collective-permute-done.9.down_ref = f32[2,12,128]{2,1,0:T(8,128)S(1)} collective-permute-done((f32[2,12,128]{2,1,0:T(8,128)S(1)}, f32[2,12,128]{2,1,0:T(8,128)S(1)}, u32[]{:S(2)}, u32[]{:S(2)}) %collective-permute-start.9) | collective-permute-done | bytes 12320 | tf_op jit(solution)/shard_map/ppermute | solution.py:408
  74.3 3.0 %all-to-all-done.3.chunk_ref = f32[32,4,384]{2,1,0:T(4,128)S(1)} async-done(((f32[32,4,384]{2,1,0:T(4,128)}), f32[32,4,384]{2,1,0:T(4,128)S(1)}, u32[]{:S(2)}, u32[]{:S(2)}) %all-to-all-start.3) | async-done | bytes 196640 | tf_op jit(solution)/shard_map/all_to_all | solution.py:413
  77.3 2.1 %shard_map.123.part_ref = f32[12,4,32,128]{3,2,1,0:T(8,128)S(1)} custom-call(s32[1]{0:T(128)} %bitcast.1.p_ref.refs_0_, s32[24,128]{1,0:T(8,128)S(1)} %copy-done.7, f32[32,4,384]{2,1,0:T(4,128)S(1)} %all-to-all-done.3.chunk_ref, f32[2,12,128]{2,1,0:T(8,128)S(1)} %collective-permute-done.8.up_ref, f32[2,12,128]{2,1,0:T(8,128)S(1)} %collective-permute-done.9.down_ref, ...), custom_call_target="tpu_custom_call" | custom-call | tf_op jit(solution)/shard_map/pallas_call | solution.py:397
  (41 shorter events, 6.6 us)
Async XLA Ops:
  5.7 15.6 %copy-start.2 = (f32[4,12,16,128]{3,2,1,0:T(8,128)S(1)}, f32[4,12,16,128]{3,2,1,0:T(8,128)}, u32[]{:S(2)}) copy-start(f32[4,12,16,128]{3,2,1,0:T(8,128)} %get-tuple-element.34.same_ref) | copy-start | bytes 1179652
  5.7 15.6 %collective-permute-start.2 = (f32[4,12,16,128]{3,2,1,0:T(8,128)}, f32[4,12,16,128]{3,2,1,0:T(8,128)S(1)}, u32[]{:S(2)}, u32[]{:S(2)}) collective-permute-start(f32[4,12,16,128]{3,2,1,0:T(8,128)} %get-tuple-element.35), channel_id=1, source_target_pairs={{0,1},{1,0},{2,3},{3,2},{4,5},{5,4},{6,7},{7,6},{8,9},{9,8},{10,11... | collective-permute-start | bytes 1179656 | tf_op jit(solution)/shard_map/ppermute | solution.py:417
  7.9 25.2 %all-to-all-start = ((f32[32,16,128]{2,1,0:T(8,128)}), f32[32,16,128]{2,1,0:T(8,128)S(1)}, u32[]{:S(2)}, u32[]{:S(2)}) async-start(f32[32,16,128]{2,1,0:T(8,128)} %get-tuple-element.30), calls=%async_computation | async-start | bytes 524288 | tf_op jit(solution)/shard_map/all_to_all | solution.py:413
  19.6 8.7 %collective-permute-start = (f32[14,32,128]{2,1,0:T(8,128)}, f32[14,32,128]{2,1,0:T(8,128)S(1)}, u32[]{:S(2)}, u32[]{:S(2)}) collective-permute-start(f32[14,32,128]{2,1,0:T(8,128)} %get-tuple-element.31), channel_id=1, source_target_pairs={{0,8},{8,16},{16,24},{24,32},{32,40},{40,48},{48,56},{56,64},{64,7... | collective-permute-start | bytes 688136 | tf_op jit(solution)/shard_map/ppermute | solution.py:408
  21.3 9.1 %collective-permute-start.1 = (f32[14,32,128]{2,1,0:T(8,128)}, f32[14,32,128]{2,1,0:T(8,128)S(1)}, u32[]{:S(2)}, u32[]{:S(2)}) collective-permute-start(f32[14,32,128]{2,1,0:T(8,128)} %get-tuple-element.32), channel_id=1, source_target_pairs={{0,248},{8,0},{16,8},{24,16},{32,24},{40,32},{48,40},{56,48},{64,5... | collective-permute-start | bytes 688136 | tf_op jit(solution)/shard_map/ppermute | solution.py:408
  21.3 4.6 %copy-start = (f32[2,3,4,32,128]{4,3,2,1,0:T(8,128)S(1)}, f32[2,3,4,32,128]{4,3,2,1,0:T(8,128)}, u32[]{:S(2)}) copy-start(f32[2,3,4,32,128]{4,3,2,1,0:T(8,128)} %param.10) | copy-start | bytes 1179652
  21.3 4.6 %copy-start.1 = (f32[2,3,4,32,128]{4,3,2,1,0:T(8,128)S(1)}, f32[2,3,4,32,128]{4,3,2,1,0:T(8,128)}, u32[]{:S(2)}) copy-start(f32[2,3,4,32,128]{4,3,2,1,0:T(8,128)} %param.11) | copy-start | bytes 1179652
  22.2 17.7 %collective-permute-start.4 = (f32[2,12,16,128]{3,2,1,0:T(8,128)}, f32[2,12,16,128]{3,2,1,0:T(8,128)S(1)}, u32[]{:S(2)}, u32[]{:S(2)}) collective-permute-start(f32[2,12,16,128]{3,2,1,0:T(8,128)} %get-tuple-element.39), channel_id=1, source_target_pairs={{0,4},{1,5},{2,6},{3,7},{4,0},{5,1},{6,2},{7,3},{8,12},{9,13},{10,... | collective-permute-start | bytes 589832 | tf_op jit(solution)/shard_map/ppermute | solution.py:417
  25.1 14.8 %collective-permute-start.5 = (f32[2,12,16,128]{3,2,1,0:T(8,128)}, f32[2,12,16,128]{3,2,1,0:T(8,128)}, u32[]{:S(2)}, u32[]{:S(2)}) collective-permute-start(f32[2,12,16,128]{3,2,1,0:T(8,128)} %get-tuple-element.40), channel_id=1, source_target_pairs={{0,6},{1,7},{2,4},{3,5},{4,2},{5,3},{6,0},{7,1},{8,14},{9,15},{10,... | collective-permute-start | bytes 589832 | tf_op jit(solution)/shard_map/ppermute | solution.py:417
  25.9 7.1 %copy-start.6 = (f32[2,16,128]{2,1,0:T(8,128)S(1)}, f32[2,16,128]{2,1,0:T(8,128)}, u32[]{:S(2)}) copy-start(f32[2,16,128]{2,1,0:T(8,128)} %get-tuple-element.33.self_ref) | copy-start | bytes 49156
  25.9 14.1 %collective-permute-start.3 = (f32[2,12,16,128]{3,2,1,0:T(8,128)}, f32[2,12,16,128]{3,2,1,0:T(8,128)}, u32[]{:S(2)}, u32[]{:S(2)}) collective-permute-start(f32[2,12,16,128]{3,2,1,0:T(8,128)} %get-tuple-element.36.after_ref), channel_id=1, source_target_pairs={{0,2},{1,3},{2,0},{3,1},{4,6},{5,7},{6,4},{7,5},{8,10},{9,11},{10,... | collective-permute-start | bytes 589832 | tf_op jit(solution)/shard_map/ppermute | solution.py:417
  35.8 9.8 %all-to-all-start.1 = ((f32[8,4,1152]{2,1,0:T(4,128)}), f32[8,4,1152]{2,1,0:T(4,128)S(1)}, u32[]{:S(2)}, u32[]{:S(2)}) async-start(f32[8,4,1152]{2,1,0:T(4,128)} %get-tuple-element.38), calls=%async_computation.1 | async-start | bytes 294912 | tf_op jit(solution)/shard_map/all_to_all | solution.py:421
  40.0 5.6 %copy-start.5 = (f32[48,48]{1,0:T(8,128)S(1)}, f32[48,48]{1,0:T(8,128)}, u32[]{:S(2)}) copy-start(f32[48,48]{1,0:T(8,128)} %constant.11.clone.spread_ref) | copy-start | bytes 27652
  42.1 8.1 %collective-permute-start.6 = (f32[2,12,16,128]{3,2,1,0:T(8,128)S(1)}, f32[2,12,16,128]{3,2,1,0:T(8,128)S(1)}, u32[]{:S(2)}, u32[]{:S(2)}) collective-permute-start(f32[2,12,16,128]{3,2,1,0:T(8,128)S(1)} %get-tuple-element.42), channel_id=1, source_target_pairs={{0,1},{1,0},{2,3},{3,2},{4,5},{5,4},{6,7},{7,6},{8,9},{9,8},{10,11... | collective-permute-start | bytes 589832 | tf_op jit(solution)/shard_map/ppermute | solution.py:417
  43.6 9.0 %collective-permute-start.7 = (f32[2,12,16,128]{3,2,1,0:T(8,128)S(1)}, f32[2,12,16,128]{3,2,1,0:T(8,128)S(1)}, u32[]{:S(2)}, u32[]{:S(2)}) collective-permute-start(f32[2,12,16,128]{3,2,1,0:T(8,128)S(1)} %get-tuple-element.43), channel_id=1, source_target_pairs={{0,1},{1,0},{2,3},{3,2},{4,5},{5,4},{6,7},{7,6},{8,9},{9,8},{10,11... | collective-permute-start | bytes 589832 | tf_op jit(solution)/shard_map/ppermute | solution.py:417
  46.6 3.5 %copy-start.8 = (f32[16,4]{0,1:T(4,128)S(1)}, f32[16,4]{0,1:T(4,128)}, u32[]{:S(2)}) copy-start(f32[16,4]{0,1:T(4,128)} %param.14) | copy-start | bytes 772
  46.6 9.8 %all-to-all-start.2 = ((f32[8,4,1152]{2,1,0:T(4,128)}), f32[8,4,1152]{2,1,0:T(4,128)S(1)}, u32[]{:S(2)}, u32[]{:S(2)}) async-start(f32[8,4,1152]{2,1,0:T(4,128)} %shard_map.118), calls=%async_computation.2 | async-start | bytes 294912 | tf_op jit(solution)/shard_map/all_to_all | solution.py:421
  57.1 20.3 %all-to-all-start.3 = ((f32[32,4,384]{2,1,0:T(4,128)}), f32[32,4,384]{2,1,0:T(4,128)S(1)}, u32[]{:S(2)}, u32[]{:S(2)}) async-start(f32[32,4,384]{2,1,0:T(4,128)} %get-tuple-element.46), calls=%async_computation.3 | async-start | bytes 393216 | tf_op jit(solution)/shard_map/all_to_all | solution.py:413
  65.6 13.8 %collective-permute-start.11 = (f32[2,12,16,128]{3,2,1,0:T(8,128)}, f32[2,12,16,128]{3,2,1,0:T(8,128)S(1)}, u32[]{:S(2)}, u32[]{:S(2)}) collective-permute-start(f32[2,12,16,128]{3,2,1,0:T(8,128)} %get-tuple-element.52), channel_id=1, source_target_pairs={{0,4},{1,5},{2,6},{3,7},{4,0},{5,1},{6,2},{7,3},{8,12},{9,13},{10,... | collective-permute-start | bytes 589832 | tf_op jit(solution)/shard_map/ppermute | solution.py:417
  66.6 12.8 %collective-permute-start.12 = (f32[2,12,16,128]{3,2,1,0:T(8,128)}, f32[2,12,16,128]{3,2,1,0:T(8,128)S(1)}, u32[]{:S(2)}, u32[]{:S(2)}) collective-permute-start(f32[2,12,16,128]{3,2,1,0:T(8,128)} %get-tuple-element.53), channel_id=1, source_target_pairs={{0,6},{1,7},{2,4},{3,5},{4,2},{5,3},{6,0},{7,1},{8,14},{9,15},{10,... | collective-permute-start | bytes 589832 | tf_op jit(solution)/shard_map/ppermute | solution.py:417
  68.2 11.2 %collective-permute-start.10 = (f32[2,12,16,128]{3,2,1,0:T(8,128)S(1)}, f32[2,12,16,128]{3,2,1,0:T(8,128)S(1)}, u32[]{:S(2)}, u32[]{:S(2)}) collective-permute-start(f32[2,12,16,128]{3,2,1,0:T(8,128)S(1)} %get-tuple-element.44.refs_8_), channel_id=1, source_target_pairs={{0,2},{1,3},{2,0},{3,1},{4,6},{5,7},{6,4},{7,5},{8,10},{9,11},{10,... | collective-permute-start | bytes 589832 | tf_op jit(solution)/shard_map/ppermute | solution.py:417
  68.4 4.6 %collective-permute-start.8 = (f32[2,12,128]{2,1,0:T(8,128)S(1)}, f32[2,12,128]{2,1,0:T(8,128)S(1)}, u32[]{:S(2)}, u32[]{:S(2)}) collective-permute-start(f32[2,12,128]{2,1,0:T(8,128)S(1)} %get-tuple-element.47), channel_id=1, source_target_pairs={{0,8},{8,16},{16,24},{24,32},{32,40},{40,48},{48,56},{56,64},{64,7... | collective-permute-start | bytes 36872 | tf_op jit(solution)/shard_map/ppermute | solution.py:408
  70.8 3.5 %collective-permute-start.9 = (f32[2,12,128]{2,1,0:T(8,128)S(1)}, f32[2,12,128]{2,1,0:T(8,128)S(1)}, u32[]{:S(2)}, u32[]{:S(2)}) collective-permute-start(f32[2,12,128]{2,1,0:T(8,128)S(1)} %get-tuple-element.48), channel_id=1, source_target_pairs={{0,248},{8,0},{16,8},{24,16},{32,24},{40,32},{48,40},{56,48},{64,5... | collective-permute-start | bytes 36872 | tf_op jit(solution)/shard_map/ppermute | solution.py:408
  70.8 6.5 %copy-start.7 = (s32[24,128]{1,0:T(8,128)S(1)}, s32[24,128]{1,0:T(8,128)}, u32[]{:S(2)}) copy-start(s32[24,128]{1,0:T(8,128)} %get-tuple-element.29.idx_ref) | copy-start | bytes 36868
  (2 other events, 6.4 us)

commit v17 on v16

--- a/solution.py
+++ b/solution.py
@@ -189,7 +189,7 @@
     near_ref[3] = (ids_ref[0] + 1).astype(f32)
     for d in (0, 1, SLABS - 1):
         chunk_ref[(p + d) & (SLABS - 1)] = jnp.zeros((16, 128), f32)
-    gather_rows(parts_ref, idx_ref, rows_ref, 3, SIDE // 2)
+    gather_rows(parts_ref, idx_ref, rows_ref, 0, SIDE // 2)
     for d, tile in ((2, 6), (SLABS - 2, 7)):
         chunk_ref[(p + d) & (SLABS - 1)] = rows_ref[tile]
     for d in range(3, SLABS - 2):
@@ -197,7 +197,6 @@
         chunk_ref[(p + d) & (SLABS - 1)] = rows_ref[tile]
     ends = [pltpu.make_async_copy(chunk_ref, chunk_hbm, sems.at[11])]
     ends[0].start()
-    gather_rows(parts_ref, idx_ref, rows_ref, 0, 3)
     for k in range(2):
         near_ref[k] = rows_ref[2 + 2 * k : 4 + 2 * k].reshape(32, 128)
     pairs = ((near_ref.at[0], up_hbm.at[0]), (near_ref.at[1], down_hbm.at[0]),

time: 80.9 us -> 81.1 us (level)
  transfers between devices with their start and end apart: 17 -> 17, of which waited for: 8 -> 8; matrix products, arithmetic and copies ran while one was open for 0% -> 0% of each run, Pallas kernels for 17% -> 16%
where the time goes in v17:
time: 81.1 us; the launch traced here: 80.6 us
  starting transfers between devices  42.4 us (52%)
  Pallas kernels  20.2 us (25%)
  waiting for transfers between devices  17.1 us (21%)
  between operations  0.83 us (1%)
    all_to_all x2, starting transfers between devices, exchange(): lax.all_to_all(chunk, 'mesh', split_axis=0, concat_axis=0, tiled=True)  20.3 us
    pallas_call x12, Pallas kernels, call(): pl.pallas_call(kernel, out_shape=[jax.ShapeDtypeStruct(s, d) for s, d in...  20.2 us
    ppermute x9, starting transfers between devices, swap(): return lax.ppermute(x, 'inst', [(i, i ^ bit) for i in range(PARTS)])  10.2 us
    all_to_all x2, starting transfers between devices, inst_split(): return lax.all_to_all(x, 'inst', split_axis=0, concat_axis=0, tiled=True)  7.7 us
    ppermute x4, waiting for transfers between devices, shift(): lax.ppermute(x, 'mesh', [(i, (i + by) % SLABS) for i in range(SLABS)])  5.71 us
    all_to_all x2, waiting for transfers between devices, exchange(): lax.all_to_all(chunk, 'mesh', split_axis=0, concat_axis=0, tiled=True)  5.67 us
    ppermute x4, starting transfers between devices, shift(): lax.ppermute(x, 'mesh', [(i, (i + by) % SLABS) for i in range(SLABS)])  4.19 us
    all_to_all x2, waiting for transfers between devices, inst_split(): return lax.all_to_all(x, 'inst', split_axis=0, concat_axis=0, tiled=True)  3.28 us
  transfers between devices with their start and end apart: 17, of which 8 were waited for; matrix products, arithmetic and copies ran while one was open for 0% of the time, Pallas kernels for 16%

profile of v17, /device:TPU:1, one launch (start us, length us, event | category | flops | bytes accessed | tf_op | source)
XLA Modules:
  0.0 80.6 jit_solution(16691520595920053018)
XLA Ops:
  0.6 5.2 %shard_map.113 = (s32[24,128]{1,0:T(8,128)}, f32[32,16,128]{2,1,0:T(8,128)}, f32[14,32,128]{2,1,0:T(8,128)}, f32[14,32,128]{2,1,0:T(8,128)}, f32[2,16,128]{2,1,0...) custom-call(s32[1]{0:T(128)} %bitcast.1.p_ref.refs_0_, s32[1]{0:T(128)} %bitcast.me_ref, ...), custom_call_target="tpu_custom_call" | custom-call | tf_op jit(solution)/shard_map/pallas_call | solution.py:396
  5.9 2.1 %collective-permute-start.2 = (f32[4,12,16,128]{3,2,1,0:T(8,128)}, f32[4,12,16,128]{3,2,1,0:T(8,128)S(1)}, u32[]{:S(2)}, u32[]{:S(2)}) collective-permute-start(f32[4,12,16,128]{3,2,1,0:T(8,128)} %get-tuple-element.35), channel_id=1, source_target_pairs={{0,1},{1,0},{2,3},{3,2},{4,5},{5,4},{6,7},{7,6},{8,9},{9,8},{10,11... | collective-permute-start | bytes 1179656 | tf_op jit(solution)/shard_map/ppermute | solution.py:416
  8.0 11.7 %all-to-all-start = ((f32[32,16,128]{2,1,0:T(8,128)}), f32[32,16,128]{2,1,0:T(8,128)S(1)}, u32[]{:S(2)}, u32[]{:S(2)}) async-start(f32[32,16,128]{2,1,0:T(8,128)} %get-tuple-element.30), calls=%async_computation | async-start | bytes 524288 | tf_op jit(solution)/shard_map/all_to_all | solution.py:412
  19.8 1.7 %collective-permute-start = (f32[14,32,128]{2,1,0:T(8,128)}, f32[14,32,128]{2,1,0:T(8,128)S(1)}, u32[]{:S(2)}, u32[]{:S(2)}) collective-permute-start(f32[14,32,128]{2,1,0:T(8,128)} %get-tuple-element.31), channel_id=1, source_target_pairs={{0,8},{8,16},{16,24},{24,32},{32,40},{40,48},{48,56},{56,64},{64,7... | collective-permute-start | bytes 688136 | tf_op jit(solution)/shard_map/ppermute | solution.py:407
  22.4 2.9 %collective-permute-start.4 = (f32[2,12,16,128]{3,2,1,0:T(8,128)}, f32[2,12,16,128]{3,2,1,0:T(8,128)S(1)}, u32[]{:S(2)}, u32[]{:S(2)}) collective-permute-start(f32[2,12,16,128]{3,2,1,0:T(8,128)} %get-tuple-element.39), channel_id=1, source_target_pairs={{0,4},{1,5},{2,6},{3,7},{4,0},{5,1},{6,2},{7,3},{8,12},{9,13},{10,... | collective-permute-start | bytes 589832 | tf_op jit(solution)/shard_map/ppermute | solution.py:416
  26.2 2.3 %collective-permute-done.up_ref.refs_6_ = f32[14,32,128]{2,1,0:T(8,128)S(1)} collective-permute-done((f32[14,32,128]{2,1,0:T(8,128)}, f32[14,32,128]{2,1,0:T(8,128)S(1)}, u32[]{:S(2)}, u32[]{:S(2)}) %collective-permute-start) | collective-permute-done | bytes 229408 | tf_op jit(solution)/shard_map/ppermute | solution.py:407
  28.5 2.1 %collective-permute-done.1.down_ref.refs_7_ = f32[14,32,128]{2,1,0:T(8,128)S(1)} collective-permute-done((f32[14,32,128]{2,1,0:T(8,128)}, f32[14,32,128]{2,1,0:T(8,128)S(1)}, u32[]{:S(2)}, u32[]{:S(2)}) %collective-permute-start.1) | collective-permute-done | bytes 229408 | tf_op jit(solution)/shard_map/ppermute | solution.py:407
  30.6 2.6 %all-to-all-done.chunk_ref = f32[32,16,128]{2,1,0:T(8,128)S(1)} async-done(((f32[32,16,128]{2,1,0:T(8,128)}), f32[32,16,128]{2,1,0:T(8,128)S(1)}, u32[]{:S(2)}, u32[]{:S(2)}) %all-to-all-start) | async-done | bytes 262176 | tf_op jit(solution)/shard_map/all_to_all | solution.py:412
  33.2 2.7 %shard_map.116 = (s32[24,128]{1,0:T(8,128)S(1)}, f32[24,128]{1,0:T(8,128)S(1)}, f32[8,4,1152]{2,1,0:T(4,128)}) custom-call(s32[1]{0:T(128)} %bitcast.1.p_ref.refs_0_, f32[32,16,128]{2,1,0:T(8,128)S(1)} %all-to-all-done.chunk_ref, f32[14,32,128]{2,1,0:T(8,128)S(1)} %collective-permute-done.up_ref.refs_6_, ...), custom_call_target="tpu_custom_call" | custom-call | tf_op jit(solution)/shard_map/pallas_call | solution.py:396
  35.9 4.2 %all-to-all-start.1 = ((f32[8,4,1152]{2,1,0:T(4,128)}), f32[8,4,1152]{2,1,0:T(4,128)S(1)}, u32[]{:S(2)}, u32[]{:S(2)}) async-start(f32[8,4,1152]{2,1,0:T(4,128)} %get-tuple-element.38), calls=%async_computation.1 | async-start | bytes 294912 | tf_op jit(solution)/shard_map/all_to_all | solution.py:420
  40.2 2.0 %shard_map.117 = (f32[4,12,16,128]{3,2,1,0:T(8,128)S(1)}, f32[2,12,16,128]{3,2,1,0:T(8,128)S(1)}, f32[2,12,16,128]{3,2,1,0:T(8,128)S(1)}) custom-call(s32[1]{0:T(128)} %bitcast.me_ref, f32[4,12,16,128]{3,2,1,0:T(8,128)S(1)} %copy-done.2, f32[4,12,16,128]{3,2,1,0:T(8,128)S(1)} %collective-permute-done.2.other_ref, ...), custom_call_target="tpu_custom_call" | custom-call | tf_op jit(solution)/shard_map/pallas_call | solution.py:396
  42.2 1.5 %collective-permute-start.6 = (f32[2,12,16,128]{3,2,1,0:T(8,128)S(1)}, f32[2,12,16,128]{3,2,1,0:T(8,128)S(1)}, u32[]{:S(2)}, u32[]{:S(2)}) collective-permute-start(f32[2,12,16,128]{3,2,1,0:T(8,128)S(1)} %get-tuple-element.42), channel_id=1, source_target_pairs={{0,1},{1,0},{2,3},{3,2},{4,5},{5,4},{6,7},{7,6},{8,9},{9,8},{10,11... | collective-permute-start | bytes 589832 | tf_op jit(solution)/shard_map/ppermute | solution.py:416
  43.9 1.9 %all-to-all-done.1.gap_ref = f32[8,4,1152]{2,1,0:T(4,128)S(1)} async-done(((f32[8,4,1152]{2,1,0:T(4,128)}), f32[8,4,1152]{2,1,0:T(4,128)S(1)}, u32[]{:S(2)}, u32[]{:S(2)}) %all-to-all-start.1) | async-done | bytes 147488 | tf_op jit(solution)/shard_map/all_to_all | solution.py:420
  46.7 3.5 %all-to-all-start.2 = ((f32[8,4,1152]{2,1,0:T(4,128)}), f32[8,4,1152]{2,1,0:T(4,128)S(1)}, u32[]{:S(2)}, u32[]{:S(2)}) async-start(f32[8,4,1152]{2,1,0:T(4,128)} %shard_map.118), calls=%async_computation.2 | async-start | bytes 294912 | tf_op jit(solution)/shard_map/all_to_all | solution.py:420
  50.3 2.4 %collective-permute-done.7.cross2_ref = f32[2,12,16,128]{3,2,1,0:T(8,128)S(1)} collective-permute-done((f32[2,12,16,128]{3,2,1,0:T(8,128)S(1)}, f32[2,12,16,128]{3,2,1,0:T(8,128)S(1)}, u32[]{:S(2)}, u32[]{:S(2)}) %collective-permute-start.7) | collective-permute-done | bytes 196640 | tf_op jit(solution)/shard_map/ppermute | solution.py:416
  53.5 1.6 %shard_map.120 = (f32[12,4,32,128]{3,2,1,0:T(8,128)S(1)}, f32[4,32,128]{2,1,0:T(8,128)S(1)}) custom-call(s32[1]{0:T(128)} %bitcast.1.p_ref.refs_0_, f32[16,4]{1,0:T(8,128)S(1)} %copy.12.refs_1_, s32[4,32,128]{2,1,0:T(8,128)S(1)} %copy-done.4, f32[6,4,32,128]{3,2,1,0:T(8,128)S(1)} %bitcast.13, f32[6,4,32,128]{3,2,1,0:T(8,128)S(1)} %bitcast.16, ...), custom_call_target="tpu_custom_call" | custom-call | tf_op jit(solution)/shard_map/pallas_call | solution.py:396
  55.1 1.4 %all-to-all-done.2.force_ref = f32[8,4,1152]{2,1,0:T(4,128)S(1)} async-done(((f32[8,4,1152]{2,1,0:T(4,128)}), f32[8,4,1152]{2,1,0:T(4,128)S(1)}, u32[]{:S(2)}, u32[]{:S(2)}) %all-to-all-start.2) | async-done | bytes 147488 | tf_op jit(solution)/shard_map/all_to_all | solution.py:420
  57.2 8.6 %all-to-all-start.3 = ((f32[32,4,384]{2,1,0:T(4,128)}), f32[32,4,384]{2,1,0:T(4,128)S(1)}, u32[]{:S(2)}, u32[]{:S(2)}) async-start(f32[32,4,384]{2,1,0:T(4,128)} %get-tuple-element.46), calls=%async_computation.3 | async-start | bytes 393216 | tf_op jit(solution)/shard_map/all_to_all | solution.py:412
  66.8 1.6 %collective-permute-start.12 = (f32[2,12,16,128]{3,2,1,0:T(8,128)}, f32[2,12,16,128]{3,2,1,0:T(8,128)S(1)}, u32[]{:S(2)}, u32[]{:S(2)}) collective-permute-start(f32[2,12,16,128]{3,2,1,0:T(8,128)} %get-tuple-element.53), channel_id=1, source_target_pairs={{0,6},{1,7},{2,4},{3,5},{4,2},{5,3},{6,0},{7,1},{8,14},{9,15},{10,... | collective-permute-start | bytes 589832 | tf_op jit(solution)/shard_map/ppermute | solution.py:416
  68.5 2.5 %collective-permute-start.8 = (f32[2,12,128]{2,1,0:T(8,128)S(1)}, f32[2,12,128]{2,1,0:T(8,128)S(1)}, u32[]{:S(2)}, u32[]{:S(2)}) collective-permute-start(f32[2,12,128]{2,1,0:T(8,128)S(1)} %get-tuple-element.47), channel_id=1, source_target_pairs={{0,8},{8,16},{16,24},{24,32},{32,40},{40,48},{48,56},{56,64},{64,7... | collective-permute-start | bytes 36872 | tf_op jit(solution)/shard_map/ppermute | solution.py:407
  71.0 2.1 %shard_map.122.part_ref = f32[12,4,32,128]{3,2,1,0:T(8,128)S(1)} custom-call(s32[24,128]{1,0:T(8,128)S(1)} %get-tuple-element.50.idx_ref, f32[8,4,1152]{2,1,0:T(4,128)S(1)} %all-to-all-done.2.force_ref, f32[12,4,32,128]{3,2,1,0:T(8,128)S(1)} %get-tuple-element.51.lin_ref), custom_call_target="tpu_custom_call" | custom-call | tf_op jit(solution)/shard_map/pallas_call | solution.py:396
  73.1 1.4 %collective-permute-done.9.down_ref = f32[2,12,128]{2,1,0:T(8,128)S(1)} collective-permute-done((f32[2,12,128]{2,1,0:T(8,128)S(1)}, f32[2,12,128]{2,1,0:T(8,128)S(1)}, u32[]{:S(2)}, u32[]{:S(2)}) %collective-permute-start.9) | collective-permute-done | bytes 12320 | tf_op jit(solution)/shard_map/ppermute | solution.py:407
  74.5 3.0 %all-to-all-done.3.chunk_ref = f32[32,4,384]{2,1,0:T(4,128)S(1)} async-done(((f32[32,4,384]{2,1,0:T(4,128)}), f32[32,4,384]{2,1,0:T(4,128)S(1)}, u32[]{:S(2)}, u32[]{:S(2)}) %all-to-all-start.3) | async-done | bytes 196640 | tf_op jit(solution)/shard_map/all_to_all | solution.py:412
  77.5 2.1 %shard_map.123.part_ref = f32[12,4,32,128]{3,2,1,0:T(8,128)S(1)} custom-call(s32[1]{0:T(128)} %bitcast.1.p_ref.refs_0_, s32[24,128]{1,0:T(8,128)S(1)} %copy-done.7, f32[32,4,384]{2,1,0:T(4,128)S(1)} %all-to-all-done.3.chunk_ref, f32[2,12,128]{2,1,0:T(8,128)S(1)} %collective-permute-done.8.up_ref, f32[2,12,128]{2,1,0:T(8,128)S(1)} %collective-permute-done.9.down_ref, ...), custom_call_target="tpu_custom_call" | custom-call | tf_op jit(solution)/shard_map/pallas_call | solution.py:396
  (41 shorter events, 6.6 us)
Async XLA Ops:
  5.9 15.6 %copy-start.2 = (f32[4,12,16,128]{3,2,1,0:T(8,128)S(1)}, f32[4,12,16,128]{3,2,1,0:T(8,128)}, u32[]{:S(2)}) copy-start(f32[4,12,16,128]{3,2,1,0:T(8,128)} %get-tuple-element.34.same_ref) | copy-start | bytes 1179652
  5.9 15.6 %collective-permute-start.2 = (f32[4,12,16,128]{3,2,1,0:T(8,128)}, f32[4,12,16,128]{3,2,1,0:T(8,128)S(1)}, u32[]{:S(2)}, u32[]{:S(2)}) collective-permute-start(f32[4,12,16,128]{3,2,1,0:T(8,128)} %get-tuple-element.35), channel_id=1, source_target_pairs={{0,1},{1,0},{2,3},{3,2},{4,5},{5,4},{6,7},{7,6},{8,9},{9,8},{10,11... | collective-permute-start | bytes 1179656 | tf_op jit(solution)/shard_map/ppermute | solution.py:416
  8.0 25.2 %all-to-all-start = ((f32[32,16,128]{2,1,0:T(8,128)}), f32[32,16,128]{2,1,0:T(8,128)S(1)}, u32[]{:S(2)}, u32[]{:S(2)}) async-start(f32[32,16,128]{2,1,0:T(8,128)} %get-tuple-element.30), calls=%async_computation | async-start | bytes 524288 | tf_op jit(solution)/shard_map/all_to_all | solution.py:412
  19.8 8.7 %collective-permute-start = (f32[14,32,128]{2,1,0:T(8,128)}, f32[14,32,128]{2,1,0:T(8,128)S(1)}, u32[]{:S(2)}, u32[]{:S(2)}) collective-permute-start(f32[14,32,128]{2,1,0:T(8,128)} %get-tuple-element.31), channel_id=1, source_target_pairs={{0,8},{8,16},{16,24},{24,32},{32,40},{40,48},{48,56},{56,64},{64,7... | collective-permute-start | bytes 688136 | tf_op jit(solution)/shard_map/ppermute | solution.py:407
  21.5 9.1 %collective-permute-start.1 = (f32[14,32,128]{2,1,0:T(8,128)}, f32[14,32,128]{2,1,0:T(8,128)S(1)}, u32[]{:S(2)}, u32[]{:S(2)}) collective-permute-start(f32[14,32,128]{2,1,0:T(8,128)} %get-tuple-element.32), channel_id=1, source_target_pairs={{0,248},{8,0},{16,8},{24,16},{32,24},{40,32},{48,40},{56,48},{64,5... | collective-permute-start | bytes 688136 | tf_op jit(solution)/shard_map/ppermute | solution.py:407
  21.5 4.6 %copy-start = (f32[2,3,4,32,128]{4,3,2,1,0:T(8,128)S(1)}, f32[2,3,4,32,128]{4,3,2,1,0:T(8,128)}, u32[]{:S(2)}) copy-start(f32[2,3,4,32,128]{4,3,2,1,0:T(8,128)} %param.10) | copy-start | bytes 1179652
  21.5 4.6 %copy-start.1 = (f32[2,3,4,32,128]{4,3,2,1,0:T(8,128)S(1)}, f32[2,3,4,32,128]{4,3,2,1,0:T(8,128)}, u32[]{:S(2)}) copy-start(f32[2,3,4,32,128]{4,3,2,1,0:T(8,128)} %param.11) | copy-start | bytes 1179652
  22.4 17.7 %collective-permute-start.4 = (f32[2,12,16,128]{3,2,1,0:T(8,128)}, f32[2,12,16,128]{3,2,1,0:T(8,128)S(1)}, u32[]{:S(2)}, u32[]{:S(2)}) collective-permute-start(f32[2,12,16,128]{3,2,1,0:T(8,128)} %get-tuple-element.39), channel_id=1, source_target_pairs={{0,4},{1,5},{2,6},{3,7},{4,0},{5,1},{6,2},{7,3},{8,12},{9,13},{10,... | collective-permute-start | bytes 589832 | tf_op jit(solution)/shard_map/ppermute | solution.py:416
  25.3 14.8 %collective-permute-start.5 = (f32[2,12,16,128]{3,2,1,0:T(8,128)}, f32[2,12,16,128]{3,2,1,0:T(8,128)}, u32[]{:S(2)}, u32[]{:S(2)}) collective-permute-start(f32[2,12,16,128]{3,2,1,0:T(8,128)} %get-tuple-element.40), channel_id=1, source_target_pairs={{0,6},{1,7},{2,4},{3,5},{4,2},{5,3},{6,0},{7,1},{8,14},{9,15},{10,... | collective-permute-start | bytes 589832 | tf_op jit(solution)/shard_map/ppermute | solution.py:416
  26.1 7.1 %copy-start.6 = (f32[2,16,128]{2,1,0:T(8,128)S(1)}, f32[2,16,128]{2,1,0:T(8,128)}, u32[]{:S(2)}) copy-start(f32[2,16,128]{2,1,0:T(8,128)} %get-tuple-element.33.self_ref) | copy-start | bytes 49156
  26.1 14.1 %collective-permute-start.3 = (f32[2,12,16,128]{3,2,1,0:T(8,128)}, f32[2,12,16,128]{3,2,1,0:T(8,128)}, u32[]{:S(2)}, u32[]{:S(2)}) collective-permute-start(f32[2,12,16,128]{3,2,1,0:T(8,128)} %get-tuple-element.36.after_ref), channel_id=1, source_target_pairs={{0,2},{1,3},{2,0},{3,1},{4,6},{5,7},{6,4},{7,5},{8,10},{9,11},{10,... | collective-permute-start | bytes 589832 | tf_op jit(solution)/shard_map/ppermute | solution.py:416
  35.9 9.8 %all-to-all-start.1 = ((f32[8,4,1152]{2,1,0:T(4,128)}), f32[8,4,1152]{2,1,0:T(4,128)S(1)}, u32[]{:S(2)}, u32[]{:S(2)}) async-start(f32[8,4,1152]{2,1,0:T(4,128)} %get-tuple-element.38), calls=%async_computation.1 | async-start | bytes 294912 | tf_op jit(solution)/shard_map/all_to_all | solution.py:420
  40.2 5.6 %copy-start.5 = (f32[48,48]{1,0:T(8,128)S(1)}, f32[48,48]{1,0:T(8,128)}, u32[]{:S(2)}) copy-start(f32[48,48]{1,0:T(8,128)} %constant.11.clone.spread_ref) | copy-start | bytes 27652
  42.2 8.1 %collective-permute-start.6 = (f32[2,12,16,128]{3,2,1,0:T(8,128)S(1)}, f32[2,12,16,128]{3,2,1,0:T(8,128)S(1)}, u32[]{:S(2)}, u32[]{:S(2)}) collective-permute-start(f32[2,12,16,128]{3,2,1,0:T(8,128)S(1)} %get-tuple-element.42), channel_id=1, source_target_pairs={{0,1},{1,0},{2,3},{3,2},{4,5},{5,4},{6,7},{7,6},{8,9},{9,8},{10,11... | collective-permute-start | bytes 589832 | tf_op jit(solution)/shard_map/ppermute | solution.py:416
  43.8 9.0 %collective-permute-start.7 = (f32[2,12,16,128]{3,2,1,0:T(8,128)S(1)}, f32[2,12,16,128]{3,2,1,0:T(8,128)S(1)}, u32[]{:S(2)}, u32[]{:S(2)}) collective-permute-start(f32[2,12,16,128]{3,2,1,0:T(8,128)S(1)} %get-tuple-element.43), channel_id=1, source_target_pairs={{0,1},{1,0},{2,3},{3,2},{4,5},{5,4},{6,7},{7,6},{8,9},{9,8},{10,11... | collective-permute-start | bytes 589832 | tf_op jit(solution)/shard_map/ppermute | solution.py:416
  46.7 3.5 %copy-start.8 = (f32[16,4]{0,1:T(4,128)S(1)}, f32[16,4]{0,1:T(4,128)}, u32[]{:S(2)}) copy-start(f32[16,4]{0,1:T(4,128)} %param.14) | copy-start | bytes 772
  46.7 9.8 %all-to-all-start.2 = ((f32[8,4,1152]{2,1,0:T(4,128)}), f32[8,4,1152]{2,1,0:T(4,128)S(1)}, u32[]{:S(2)}, u32[]{:S(2)}) async-start(f32[8,4,1152]{2,1,0:T(4,128)} %shard_map.118), calls=%async_computation.2 | async-start | bytes 294912 | tf_op jit(solution)/shard_map/all_to_all | solution.py:420
  57.2 20.3 %all-to-all-start.3 = ((f32[32,4,384]{2,1,0:T(4,128)}), f32[32,4,384]{2,1,0:T(4,128)S(1)}, u32[]{:S(2)}, u32[]{:S(2)}) async-start(f32[32,4,384]{2,1,0:T(4,128)} %get-tuple-element.46), calls=%async_computation.3 | async-start | bytes 393216 | tf_op jit(solution)/shard_map/all_to_all | solution.py:412
  65.8 13.8 %collective-permute-start.11 = (f32[2,12,16,128]{3,2,1,0:T(8,128)}, f32[2,12,16,128]{3,2,1,0:T(8,128)S(1)}, u32[]{:S(2)}, u32[]{:S(2)}) collective-permute-start(f32[2,12,16,128]{3,2,1,0:T(8,128)} %get-tuple-element.52), channel_id=1, source_target_pairs={{0,4},{1,5},{2,6},{3,7},{4,0},{5,1},{6,2},{7,3},{8,12},{9,13},{10,... | collective-permute-start | bytes 589832 | tf_op jit(solution)/shard_map/ppermute | solution.py:416
  66.8 12.8 %collective-permute-start.12 = (f32[2,12,16,128]{3,2,1,0:T(8,128)}, f32[2,12,16,128]{3,2,1,0:T(8,128)S(1)}, u32[]{:S(2)}, u32[]{:S(2)}) collective-permute-start(f32[2,12,16,128]{3,2,1,0:T(8,128)} %get-tuple-element.53), channel_id=1, source_target_pairs={{0,6},{1,7},{2,4},{3,5},{4,2},{5,3},{6,0},{7,1},{8,14},{9,15},{10,... | collective-permute-start | bytes 589832 | tf_op jit(solution)/shard_map/ppermute | solution.py:416
  68.4 11.2 %collective-permute-start.10 = (f32[2,12,16,128]{3,2,1,0:T(8,128)S(1)}, f32[2,12,16,128]{3,2,1,0:T(8,128)S(1)}, u32[]{:S(2)}, u32[]{:S(2)}) collective-permute-start(f32[2,12,16,128]{3,2,1,0:T(8,128)S(1)} %get-tuple-element.44.refs_8_), channel_id=1, source_target_pairs={{0,2},{1,3},{2,0},{3,1},{4,6},{5,7},{6,4},{7,5},{8,10},{9,11},{10,... | collective-permute-start | bytes 589832 | tf_op jit(solution)/shard_map/ppermute | solution.py:416
  68.5 4.6 %collective-permute-start.8 = (f32[2,12,128]{2,1,0:T(8,128)S(1)}, f32[2,12,128]{2,1,0:T(8,128)S(1)}, u32[]{:S(2)}, u32[]{:S(2)}) collective-permute-start(f32[2,12,128]{2,1,0:T(8,128)S(1)} %get-tuple-element.47), channel_id=1, source_target_pairs={{0,8},{8,16},{16,24},{24,32},{32,40},{40,48},{48,56},{56,64},{64,7... | collective-permute-start | bytes 36872 | tf_op jit(solution)/shard_map/ppermute | solution.py:407
  71.0 3.5 %collective-permute-start.9 = (f32[2,12,128]{2,1,0:T(8,128)S(1)}, f32[2,12,128]{2,1,0:T(8,128)S(1)}, u32[]{:S(2)}, u32[]{:S(2)}) collective-permute-start(f32[2,12,128]{2,1,0:T(8,128)S(1)} %get-tuple-element.48), channel_id=1, source_target_pairs={{0,248},{8,0},{16,8},{24,16},{32,24},{40,32},{48,40},{56,48},{64,5... | collective-permute-start | bytes 36872 | tf_op jit(solution)/shard_map/ppermute | solution.py:407
  71.0 6.5 %copy-start.7 = (s32[24,128]{1,0:T(8,128)S(1)}, s32[24,128]{1,0:T(8,128)}, u32[]{:S(2)}) copy-start(s32[24,128]{1,0:T(8,128)} %get-tuple-element.29.idx_ref) | copy-start | bytes 36868
  (2 other events, 6.4 us)
